TPU v7x, 32 devices: a whole 2x2x4 slice. The times are simulated.
32 devices in a mesh: tm: 8 (over y, x, core), batch: 4 (over z).
Axes of the slice: x: 2, y: 2, z: 4, core: 2. Of those that a mesh axis runs over, the one named last changes fastest.
Arguments:
- features: bfloat16 [4, 896, 2, 1024], P('batch', 'tm'), may hold values from -52 to 52
- lengths: int32 [4, 24], P('batch'), may hold values from 8 to 63, as said below
- conv1_weight: bfloat16 [2048, 9, 1024], P('tm', None, 'batch'), may hold values from -0.0625 to 0.0625
- norm1_gain: float32 [2048], P('tm'), may hold values from 0.25 to 1.75
- norm1_bias: float32 [2048], P('tm'), may hold values from -2.5 to 2.5
- conv2_weight: bfloat16 [2048, 9, 2048], P('tm', None, 'batch'), may hold values from -0.046875 to 0.046875
- norm2_gain: float32 [2048], P('tm'), may hold values from 0.25 to 1.75
- norm2_bias: float32 [2048], P('tm'), may hold values from -2.5 to 2.5
- out_grad: bfloat16 [4, 896, 2, 2048], P('batch', 'tm'), may hold values from -6 to 6
Outputs:
- block_out: bfloat16 [4, 896, 2, 2048], P('batch', 'tm')
- input_grad: bfloat16 [4, 896, 2, 1024], P('batch', 'tm')
- conv1_grad: float32 [2048, 9, 1024], P('tm', None, 'batch')
- gain1_grad: float32 [2048], P('tm')
- bias1_grad: float32 [2048], P('tm')
- conv2_grad: float32 [2048, 9, 2048], P('tm', None, 'batch')
- gain2_grad: float32 [2048], P('tm')
- bias2_grad: float32 [2048], P('tm')
Inputs may be any that keep to these rules, and one draw needn't show every extreme that they name: `lengths`: clips 0 to 7 of a group are padded to 16 frames, the next 8 to 32 and the last 8 to 64; a clip's length is at least half of its padded frames and below them. In every group the first clip of each padded length has one frame less than its padded frames and the second exactly half of them.
All inputs are finite; a program needn't handle non-finite values.
Results may differ from a plain program's by a relative error of at most 0.019.
Values may be sent and summed in bfloat16 or wider, within the bound.
No kernel may reach another device: no remote copies, remote signals or barrier semaphores. Data moves between devices by JAX's collectives and lax.ppermute only.
A program may use at most 320 MiB of HBM per device.

v0:
```python
import jax
import jax.numpy as jnp
from jax import lax
from jax.sharding import PartitionSpec as P


def frame_valid(lengths_row, frame_total, clip_count):
    frame_ids = jnp.arange(frame_total, dtype=jnp.int32)
    first_end = 16 * clip_count
    second_end = 48 * clip_count
    clip_index = jnp.where(
        frame_ids < first_end,
        frame_ids // 16,
        jnp.where(
            frame_ids < second_end,
            clip_count + (frame_ids - first_end) // 32,
            2 * clip_count + (frame_ids - second_end) // 64,
        ),
    )
    offset = jnp.where(
        frame_ids < first_end,
        frame_ids % 16,
        jnp.where(
            frame_ids < second_end, (frame_ids - first_end) % 32, (frame_ids - second_end) % 64
        ),
    )
    clip_ids = jnp.arange(3 * clip_count, dtype=jnp.int32)
    picked = jnp.where(
        clip_index[:, None] == clip_ids[None, :], lengths_row[None, :], jnp.zeros((), jnp.int32)
    )
    length_here = jnp.sum(picked, axis=1)
    return offset < length_here


def silu_slope(value):
    sigma = jax.nn.sigmoid(value)
    return sigma * (1.0 + value * (1.0 - sigma))


def tap_weights(weight, tap_row, mel_count):
    row_blocks = []
    for mel_out in range(mel_count):
        col_blocks = []
        for mel_in in range(mel_count):
            offset = mel_in - mel_out + 1
            col_blocks.append(weight[:, 3 * tap_row + offset, :])
        row_blocks.append(jnp.concatenate(col_blocks, axis=1))
    return jnp.concatenate(row_blocks, axis=0)


def convolve(source, weight):
    frame_total, mel_count, width_in = source.shape
    width_out = weight.shape[0]
    flat_rows = jnp.pad(source.reshape(frame_total, mel_count * width_in), ((1, 1), (0, 0)))
    running = jnp.zeros((frame_total, mel_count * width_out), jnp.float32)
    for tap_row in range(3):
        running = running + lax.dot_general(
            flat_rows[tap_row : tap_row + frame_total],
            tap_weights(weight, tap_row, mel_count),
            (((1,), (1,)), ((), ())),
            preferred_element_type=jnp.float32,
        )
    return running.reshape(frame_total, mel_count, width_out)


def weight_grad(source, grad):
    frame_total, mel_count, width_in = source.shape
    width_out = grad.shape[2]
    flat_rows = jnp.pad(source.reshape(frame_total, mel_count * width_in), ((1, 1), (0, 0)))
    grad_flat = grad.reshape(frame_total, mel_count * width_out)
    tap_list = []
    for tap_row in range(3):
        product = lax.dot_general(
            grad_flat,
            flat_rows[tap_row : tap_row + frame_total],
            (((0,), (0,)), ((), ())),
            preferred_element_type=jnp.float32,
        )
        product = product.reshape(mel_count, width_out, mel_count, width_in)
        for offset in range(3):
            summed = jnp.zeros((width_out, width_in), jnp.float32)
            for mel_out in range(mel_count):
                mel_in = mel_out + offset - 1
                if 0 <= mel_in < mel_count:
                    summed = summed + product[mel_out, :, mel_in, :]
            tap_list.append(summed)
    return jnp.stack(tap_list, axis=1)


def transposed(grad_padded, weight, row_count, mel_count):
    width_in = weight.shape[2]
    running = jnp.zeros((row_count, mel_count * width_in), jnp.float32)
    for tap_row in range(3):
        running = running + jnp.dot(
            grad_padded[2 - tap_row : 2 - tap_row + row_count],
            tap_weights(weight, tap_row, mel_count),
            preferred_element_type=jnp.float32,
        )
    return running.reshape(row_count, mel_count, width_in)


def standardize(before, total_sum, total_square, pixel_total):
    average = total_sum / pixel_total
    variance = total_square / pixel_total - average * average
    inv_std = lax.rsqrt(variance + 1e-05)
    return ((before - average) * inv_std, inv_std)


def per_device(
    features,
    lengths,
    conv1_weight,
    norm1_gain,
    norm1_bias,
    conv2_weight,
    norm2_gain,
    norm2_bias,
    out_grad,
):
    tm_devices = lax.axis_size("tm")
    frames_dev = features.shape[1]
    mel_count = features.shape[2]
    frame_total = frames_dev * tm_devices
    clip_count = lengths.shape[1] // 3
    valid_mask = frame_valid(lengths[0], frame_total, clip_count).astype(jnp.float32)[:, None, None]
    valid_low = valid_mask.astype(jnp.bfloat16)

    def fetch_frames():
        return lax.all_gather(features, "tm", axis=1, tiled=True)[0] * valid_low

    def fetch_units(local_units):
        return lax.all_gather(local_units, "tm", axis=2, tiled=True)

    masked = fetch_frames()
    weight_one, weight_two = (
        lax.all_gather(conv1_weight, "batch", axis=2, tiled=True),
        lax.all_gather(conv2_weight, "batch", axis=2, tiled=True),
    )
    pre_one = convolve(masked, weight_one)
    local_total = jnp.sum(lengths.astype(jnp.float32)) * mel_count
    sum_one, square_one, pixel_total = lax.psum(
        (
            jnp.sum(pre_one * valid_mask, axis=(0, 1)),
            jnp.sum(pre_one * pre_one * valid_mask, axis=(0, 1)),
            local_total,
        ),
        "batch",
    )
    scaled_one, rstd_one = standardize(pre_one, sum_one, square_one, pixel_total)
    before_one = norm1_gain * scaled_one + norm1_bias
    hidden = (valid_mask * jax.nn.silu(before_one)).astype(jnp.bfloat16)
    hidden_all = fetch_units(hidden)
    pre_two = convolve(hidden_all, weight_two)
    sum_two, square_two = lax.psum(
        (
            jnp.sum(pre_two * valid_mask, axis=(0, 1)),
            jnp.sum(pre_two * pre_two * valid_mask, axis=(0, 1)),
        ),
        "batch",
    )
    scaled_two, rstd_two = standardize(pre_two, sum_two, square_two, pixel_total)
    before_two = norm2_gain * scaled_two + norm2_bias
    output_local = (valid_mask * jax.nn.silu(before_two)).astype(jnp.bfloat16)
    block_out = lax.all_to_all(output_local[None], "tm", split_axis=1, concat_axis=3, tiled=True)
    grad_local = lax.all_to_all(out_grad, "tm", split_axis=3, concat_axis=1, tiled=True)[0]
    delta_two = grad_local.astype(jnp.float32) * valid_mask * silu_slope(before_two)
    gain2_grad, bias2_grad = lax.psum(
        (jnp.sum(delta_two * scaled_two, axis=(0, 1)), jnp.sum(delta_two, axis=(0, 1))), "batch"
    )
    grad_two = (
        valid_mask
        * norm2_gain
        * rstd_two
        * (delta_two - (bias2_grad + scaled_two * gain2_grad) / pixel_total)
    ).astype(jnp.bfloat16)
    units_again = fetch_units(hidden)
    frames_again = fetch_frames()
    conv2_local = weight_grad(units_again, grad_two)
    padded_two = jnp.pad(grad_two.reshape(frame_total, -1), ((1, 1), (0, 0)))
    partial_terms = transposed(padded_two, weight_two, frame_total, mel_count)
    hidden_grad = lax.psum_scatter(
        partial_terms.astype(jnp.bfloat16), "tm", scatter_dimension=2, tiled=True
    ).astype(jnp.float32)
    delta_one = hidden_grad * valid_mask * silu_slope(before_one)
    gain1_grad, bias1_grad = lax.psum(
        (jnp.sum(delta_one * scaled_one, axis=(0, 1)), jnp.sum(delta_one, axis=(0, 1))), "batch"
    )
    grad_one = (
        valid_mask
        * norm1_gain
        * rstd_one
        * (delta_one - (bias1_grad + scaled_one * gain1_grad) / pixel_total)
    ).astype(jnp.bfloat16)
    conv1_local = weight_grad(frames_again, grad_one)
    conv1_grad, conv2_grad = (
        lax.psum_scatter(
            conv1_local.astype(jnp.bfloat16), "batch", scatter_dimension=2, tiled=True
        ).astype(jnp.float32),
        lax.psum_scatter(
            conv2_local.astype(jnp.bfloat16), "batch", scatter_dimension=2, tiled=True
        ).astype(jnp.float32),
    )
    padded_one = jnp.pad(grad_one.reshape(frame_total, -1), ((1, 1), (0, 0)))
    input_dev = lax.psum_scatter(
        transposed(padded_one, weight_one, frames_dev * lax.axis_size("tm"), mel_count).astype(
            jnp.bfloat16
        ),
        "tm",
        scatter_dimension=0,
        tiled=True,
    ).astype(jnp.float32)
    own_mask = lax.dynamic_slice_in_dim(
        valid_mask, lax.axis_index("tm") * frames_dev, frames_dev, 0
    )
    input_grad = (input_dev * own_mask).astype(jnp.bfloat16)[None]
    return (
        block_out,
        input_grad,
        conv1_grad,
        gain1_grad,
        bias1_grad,
        conv2_grad,
        gain2_grad,
        bias2_grad,
    )


def solution(mesh):
    return jax.shard_map(
        per_device,
        mesh=mesh,
        in_specs=(
            P("batch", "tm", None, None),
            P("batch", None),
            P("tm", None, "batch"),
            P("tm"),
            P("tm"),
            P("tm", None, "batch"),
            P("tm"),
            P("tm"),
            P("batch", "tm", None, None),
        ),
        out_specs=(
            P("batch", "tm", None, None),
            P("batch", "tm", None, None),
            P("tm", None, "batch"),
            P("tm"),
            P("tm"),
            P("tm", None, "batch"),
            P("tm"),
            P("tm"),
        ),
        check_vma=False,
    )
```

profile of v0, /device:TPU:0, one launch (start us, length us, event | category | flops | bytes accessed | tf_op | source)
XLA Modules:
  0.0 924.6 jit_solution(5918970099774436133)
XLA Ops:
  10.8 36.3 %all-gather.5.cloned.1.call-done = bf16[1,896,2,1024]{3,2,0,1:T(2,128)(2,1)} async-done(((bf16[1,112,2,1024]{3,2,0,1:T(2,128)(2,1)}), bf16[1,896,2,1024]{3,2,0,1:T(2,128)(2,1)}) %all-gather.5.cloned.1.call-update) | async-done | bytes 3670032 | tf_op jit(solution)/shard_map/all_gather | solution.py:129
  47.1 10.0 %copy.120 = bf16[1,896,2,1024]{1,3,2,0:T(8,128)(2,1)} copy(bf16[1,896,2,1024]{3,2,0,1:T(2,128)(2,1)} %all-gather.5.cloned.1.call-done) | data formatting | bytes 7340032 | tf_op jit(solution)/shard_map/squeeze | solution.py:129
  57.1 4.4 bitcast_multiply_fusion
  61.5 76.4 %all-gather.7.cloned.1.call-done = bf16[256,9,1024]{2,0,1:T(8,128)(2,1)} async-done(((bf16[256,9,256]{2,0,1:T(8,128)(2,1)}), bf16[256,9,1024]{2,0,1:T(8,128)(2,1)}) %all-gather.7.cloned.1.call-update) | async-done | bytes 4718608 | tf_op jit(solution)/shard_map/all_gather | solution.py:136
  137.9 3.0 slice_bitcast_fusion.22
  141.3 2.5 fusion.34
  143.9 2.3 fusion.33
  146.2 2.9 multiply_reduce_fusion.4
  149.2 9.7 %all-reduce.8 = (f32[256]{0:T(256)S(1)}, f32[]{:T(128)}, f32[256]{0:T(256)S(1)}) all-reduce(f32[256]{0:T(256)S(1)} %reduce_sum.123, f32[]{:T(128)S(6)} %mul.378, f32[256]{0:T(256)S(1)} %reduce_sum.127), channel_id=1, replica_groups=mesh['tm'=8,'batch'=4] {'batch'}, use_global_device_ids=true, to_apply=%region_3.4 | all-reduce | flops 513 | bytes 4104 | tf_op jit(solution)/shard_map/psum | solution.py:141
  159.6 2.2 multiply_convert_fusion.2
  161.9 3.0 copy.109
  165.0 3.7 all-to-all-start.1
  169.2 14.9 %all-to-all-done.1 = bf16[1,112,2,2048]{1,2,0,3:T(2,128)(2,1)S(1)} async-done(((bf16[1,112,2,2048]{1,2,0,3:T(2,128)(2,1)}), bf16[1,112,2,2048]{1,2,0,3:T(2,128)(2,1)S(1)}, u32[]{:S(2)}, u32[]{:S(2)}) %all-to-all-start.1) | async-done | bytes 917536 | tf_op jit(solution)/shard_map/all_to_all | solution.py:165
  189.4 3.0 copy.122
  192.4 2.9 reshape.489
  195.2 109.4 %all-gather.11.cloned.1.call-done = bf16[256,9,2048]{2,0,1:T(8,128)(2,1)} async-done(((bf16[256,9,512]{2,0,1:T(8,128)(2,1)}), bf16[256,9,2048]{2,0,1:T(8,128)(2,1)}) %all-gather.11.cloned.1.call-update) | async-done | bytes 9437200 | tf_op jit(solution)/shard_map/all_gather | solution.py:137
  304.7 6.8 slice_bitcast_fusion.7
  311.5 43.8 %all-gather.9.cloned.1.call-done = bf16[896,2,2048]{0,2,1:T(8,128)(2,1)} async-done(((bf16[896,2,256]{0,2,1:T(8,128)(2,1)}), bf16[896,2,2048]{0,2,1:T(8,128)(2,1)}) %all-gather.9.cloned.1.call-update) | async-done | bytes 7340048 | tf_op jit(solution)/shard_map/all_gather | solution.py:132
  355.2 9.1 fusion.9
  364.4 4.5 fusion.7
  368.9 6.2 multiply_reduce_fusion.2
  375.2 3.6 reshape.490
  378.8 3.1 copy.115
  381.9 11.7 %all-reduce.7 = (f32[256]{0:T(256)S(1)}, f32[256]{0:T(256)S(1)}) all-reduce(f32[256]{0:T(256)S(1)} %reduce_sum.130, f32[256]{0:T(256)S(1)} %reduce_sum.133), channel_id=1, replica_groups=mesh['tm'=8,'batch'=4] {'batch'}, use_global_device_ids=true, to_apply=%region_11.12 | all-reduce | flops 512 | bytes 4096 | tf_op jit(solution)/shard_map/psum | solution.py:154
  395.7 3.1 fusion.110
  398.8 8.4 all-reduce.6
  407.3 4.3 fusion.5
  411.6 11.7 %fusion.8 = f32[896,4096]{1,0:T(8,128)} fusion(bf16[256,2048]{1,0:T(8,128)(2,1)} %get-tuple-element.95, bf16[256,2048]{1,0:T(8,128)(2,1)} %get-tuple-element.93, bf16[256,2048]{1,0:T(8,128)(2,1)} %get-tuple-element.94, bf16[896,512]{0,1:T(8,128)(2,1)S(1)} %fusion.5), kind=kOutput, calls=%fused_computation.42 | convolution fusion | flops 3774873600 | bytes 18743296 | tf_op jit(solution)/shard_map/dot_general | solution.py:94
  423.3 21.1 %fusion.6 = f32[896,4096]{1,0:T(8,128)} fusion(bf16[896,512]{0,1:T(8,128)(2,1)S(1)} %fusion.5, bf16[256,2048]{1,0:T(8,128)(2,1)S(1)} %copy-done.12, bf16[256,2048]{1,0:T(8,128)(2,1)S(1)} %copy-done.8, bf16[256,2048]{1,0:T(8,128)(2,1)S(1)} %copy-done.10), kind=kOutput, calls=%fused_computation.40 | convolution fusion | flops 3774873600 | bytes 18743296 | tf_op jit(solution)/shard_map/dot_general | solution.py:94
  444.4 17.0 %add_convert_fusion = bf16[896,4096]{1,0:T(8,128)(2,1)} fusion(f32[896,4096]{1,0:T(8,128)} %fusion.8, f32[896,4096]{1,0:T(8,128)} %fusion.6, bf16[256,2048]{1,0:T(8,128)(2,1)} %get-tuple-element.89, bf16[256,2048]{1,0:T(8,128)(2,1)} %get-tuple-element.88, bf16[256,2048]{1,0:T(8,128)(2,1)} %copy-done.4, bf16[896,512]{0,1:T(8,128)(2,1)S(1)} %fusion.5), kind=kOutput, calls=%fused_computation | convolution fusion | flops 3785883648 | bytes 40763392 | tf_op jit(solution)/shard_map/dot_general | solution.py:94
  461.4 10.8 %copy.125 = bf16[896,4096]{0,1:T(8,128)(2,1)} copy(bf16[896,4096]{1,0:T(8,128)(2,1)} %add_convert_fusion) | data formatting | bytes 14680064 | tf_op jit(solution)/shard_map/convert_element_type | solution.py:182
  472.4 14.1 %pad_slice_fusion = (bf16[896,4096]{0,1:T(8,128)(2,1)S(1)}, bf16[896,4096]{0,1:T(8,128)(2,1)}) fusion(bf16[896,4096]{0,1:T(8,128)(2,1)} %bitcast.253), kind=kLoop, calls=%fused_computation.1 | loop fusion | bytes 22020096 | tf_op jit(solution)/shard_map/slice | solution.py:58
  486.5 11.2 %fusion.116 = (bf16[2,256,2,2048]{3,1,2,0:T(8,128)(2,1)}, f32[2,256,2,2048]{3,1,2,0:T(8,128)}) fusion(bf16[2,256,896,1]{2,1,3,0:T(8,128)(2,1)S(1)} %bitcast.248, bf16[2,2048,896,1]{2,1,0,3:T(8,128)(2,1)} %bitcast.259), kind=kOutput, calls=%fused_computation.228 | convolution fusion | flops 3760193536 | bytes 20840448 | tf_op jit(solution)/shard_map/dot_general | solution.py:73
  497.7 2.3 fusion.21
  500.1 3.4 fusion.11
  503.5 2.4 fusion.20
  505.9 7.4 fusion.117
  513.3 2.3 fusion.19
  515.6 3.5 fusion.13
  519.1 7.5 fusion.118
  526.6 11.4 %reduce-scatter.4.cloned.1.call-done = bf16[896,2,256]{0,2,1:T(8,128)(2,1)} async-done(((bf16[896,2,2048]{0,2,1:T(8,128)(2,1)}), bf16[896,2,256]{0,2,1:T(8,128)(2,1)}) %reduce-scatter.4.cloned.1.call-update) | async-done | bytes 917520 | tf_op jit(solution)/shard_map/reduce_scatter | solution.py:181
  538.0 2.4 multiply_multiply_fusion
  540.9 12.1 %all-reduce.5 = (f32[256]{0:T(256)S(1)}, f32[256]{0:T(256)S(1)}) all-reduce(f32[256]{0:T(256)S(1)} %get-tuple-element.69, f32[256]{0:T(256)S(1)} %get-tuple-element.68), channel_id=1, replica_groups=mesh['tm'=8,'batch'=4] {'batch'}, use_global_device_ids=true, to_apply=%region_23.24 | all-reduce | flops 512 | bytes 4096 | tf_op jit(solution)/shard_map/psum | solution.py:185
  553.0 3.6 multiply_convert_fusion
  556.7 3.9 fusion.25
  562.8 11.0 %add_convert_fusion.1 = bf16[896,2048]{1,0:T(8,128)(2,1)} fusion(f32[896,2048]{1,0:T(8,128)S(1)} %fusion.25, f32[896,2048]{1,0:T(8,128)S(1)} %fusion.32, bf16[896,512]{0,1:T(8,128)(2,1)S(1)} %bitcast.262, bf16[256,1024]{1,0:T(8,128)(2,1)S(1)} %copy-done.16, bf16[256,1024]{1,0:T(8,128)(2,1)S(1)} %copy-done.14, bf16[256,1024]{1,0:T(8,128)(2,1)S(1)} %get-tuple-element.98), kind=kOutput, calls=%fused_computation.5 | convolution fusion | flops 1892941824 | bytes 20840448 | tf_op jit(solution)/shard_map/dot_general | solution.py:94
  573.8 7.2 convert_element_type.117
  581.1 2.3 fusion.18
  583.4 2.5 fusion.17
  585.8 3.6 fusion.15
  589.4 2.4 fusion.16
  591.9 7.2 pad_slice_fusion.2
  599.1 2.4 fusion.113
  604.1 2.4 fusion.114
  609.1 2.4 fusion.115
  615.9 2.2 multiply_convert_fusion.1
  619.9 3.6 all-to-all-start
  624.8 15.1 %all-to-all-done = bf16[1,896,2,256]{3,2,0,1:T(2,128)(2,1)S(1)} async-done(((bf16[1,896,2,256]{3,2,0,1:T(2,128)(2,1)}), bf16[1,896,2,256]{3,2,0,1:T(2,128)(2,1)S(1)}, u32[]{:S(2)}, u32[]{:S(2)}) %all-to-all-start) | async-done | bytes 917536 | tf_op jit(solution)/shard_map/all_to_all | solution.py:164
  641.4 21.0 %all-reduce.11.cloned.1.call-done = bf16[896,2,1024]{2,1,0:T(2,128)(2,1)} async-done(((bf16[896,2,1024]{2,1,0:T(2,128)(2,1)}), bf16[896,2,1024]{2,1,0:T(2,128)(2,1)}) %all-reduce.11.cloned.1.call-update) | async-done | bytes 3670032
  662.5 2.2 fusion.47
  664.7 161.5 %reduce-scatter.8.cloned.1.call-done = bf16[256,9,512]{2,0,1:T(8,128)(2,1)} async-done(((bf16[256,9,2048]{2,0,1:T(8,128)(2,1)}), bf16[256,9,512]{2,0,1:T(8,128)(2,1)}) %reduce-scatter.8.cloned.1.call-update) | async-done | bytes 2359312 | tf_op jit(solution)/shard_map/reduce_scatter | solution.py:199
  826.2 4.5 convert_element_type.121
  830.7 84.0 %reduce-scatter.6.cloned.1.call-done = bf16[256,9,256]{2,0,1:T(8,128)(2,1)} async-done(((bf16[256,9,1024]{2,0,1:T(8,128)(2,1)}), bf16[256,9,256]{2,0,1:T(8,128)(2,1)}) %reduce-scatter.6.cloned.1.call-update) | async-done | bytes 1179664 | tf_op jit(solution)/shard_map/reduce_scatter | solution.py:196
  914.6 2.9 convert_element_type.120
  (144 shorter events, 28.6 us)
Async XLA Ops:
  7.2 2.3 copy-start.35
  7.2 40.0 %all-gather.5.cloned.1.call-start = ((), (), s32[]{:S(2)}) async-start(), calls=%async_computation.5 | async-start | bytes 4128768 | tf_op jit(solution)/shard_map/all_gather | solution.py:129
  7.9 130.0 %all-gather.7.cloned.1.call-start = ((), (), s32[]{:S(2)}) async-start(), calls=%async_computation.6 | async-start | bytes 5898240 | tf_op jit(solution)/shard_map/all_gather | solution.py:136
  8.7 296.0 %all-gather.11.cloned.1.call-start = ((), (), s32[]{:S(2)}) async-start(), calls=%async_computation.8 | async-start | bytes 11796480 | tf_op jit(solution)/shard_map/all_gather | solution.py:137
  9.4 345.8 %all-gather.9.cloned.1.call-start = ((), (), s32[]{:S(2)}) async-start(), calls=%async_computation.7 | async-start | bytes 8257536 | tf_op jit(solution)/shard_map/all_gather | solution.py:132
  137.9 3.5 copy-start.1
  140.9 2.9 copy-start.24
  140.9 2.9 copy-start.25
  140.9 2.9 copy-start.26
  140.9 2.9 copy-start.18
  140.9 2.9 copy-start.20
  140.9 2.9 copy-start.22
  140.9 5.2 copy-start.13
  141.0 5.2 copy-start.15
  146.2 13.4 %copy-start.27 = (f32[256]{0:T(256)S(1)}, f32[256]{0:T(256)}, u32[]{:S(2)}) copy-start(f32[256]{0:T(256)} %param.12) | copy-start | bytes 3076
  146.2 13.4 %copy-start.29 = (f32[256]{0:T(256)S(1)}, f32[256]{0:T(256)}, u32[]{:S(2)}) copy-start(f32[256]{0:T(256)} %param.13) | copy-start | bytes 3076
  149.1 12.8 %copy-start.17 = (bf16[1,112,2,2048]{3,2,1,0:T(2,128)(2,1)S(1)}, bf16[1,112,2,2048]{3,2,1,0:T(2,128)(2,1)}, u32[]{:S(2)}) copy-start(bf16[1,112,2,2048]{3,2,1,0:T(2,128)(2,1)} %param.17) | copy-start | bytes 2752516
  159.6 9.5 %copy-start.30 = (f32[256]{0:T(256)S(1)}, f32[256]{0:T(256)}, u32[]{:S(2)}) copy-start(f32[256]{0:T(256)} %param.16) | copy-start | bytes 3076
  159.6 9.5 %copy-start.28 = (f32[256]{0:T(256)S(1)}, f32[256]{0:T(256)}, u32[]{:S(2)}) copy-start(f32[256]{0:T(256)} %param.15) | copy-start | bytes 3076
  165.0 19.1 %all-to-all-start.1 = ((bf16[1,112,2,2048]{1,2,0,3:T(2,128)(2,1)}), bf16[1,112,2,2048]{1,2,0,3:T(2,128)(2,1)S(1)}, u32[]{:S(2)}, u32[]{:S(2)}) async-start(bf16[1,112,2,2048]{1,2,0,3:T(2,128)(2,1)} %copy.109), calls=%async_computation.1 | async-start | bytes 2097152 | tf_op jit(solution)/shard_map/all_to_all | solution.py:165
  168.7 369.4 %reduce-scatter.4.cloned.1.call-start = ((), (), s32[]{:S(2)}) async-start(), calls=%async_computation.9 | async-start | bytes 8257536 | tf_op jit(solution)/shard_map/reduce_scatter | solution.py:181
  311.4 57.5 %copy-start.4 = (bf16[256,2048]{1,0:T(8,128)(2,1)}, bf16[256,2048]{1,0:T(8,128)(2,1)S(1)}, u32[]{:S(2)}) copy-start(bf16[256,2048]{1,0:T(8,128)(2,1)S(1)} %get-tuple-element.87) | copy-start | bytes 3145732
  355.2 9.1 copy-start.3
  355.2 9.1 copy-start.7
  355.2 9.1 copy-start.9
  355.2 9.1 copy-start.11
  364.4 4.6 copy-start.5
  364.4 4.6 copy-start.6
  407.2 16.1 %copy-start.33 = (f32[256]{0:T(256)}, f32[256]{0:T(256)S(1)}, u32[]{:S(2)}) copy-start(f32[256]{0:T(256)S(1)} %get-tuple-element.74) | copy-start | bytes 3076
  407.2 16.1 %copy-start.34 = (f32[256]{0:T(256)}, f32[256]{0:T(256)S(1)}, u32[]{:S(2)}) copy-start(f32[256]{0:T(256)S(1)} %get-tuple-element.75) | copy-start | bytes 3076
  411.6 11.7 %copy-start.8 = (bf16[256,2048]{1,0:T(8,128)(2,1)S(1)}, bf16[256,2048]{1,0:T(8,128)(2,1)}, u32[]{:S(2)}) copy-start(bf16[256,2048]{1,0:T(8,128)(2,1)} %get-tuple-element.90) | copy-start | bytes 3145732
  411.6 11.7 %copy-start.10 = (bf16[256,2048]{1,0:T(8,128)(2,1)S(1)}, bf16[256,2048]{1,0:T(8,128)(2,1)}, u32[]{:S(2)}) copy-start(bf16[256,2048]{1,0:T(8,128)(2,1)} %get-tuple-element.91) | copy-start | bytes 3145732
  411.6 11.7 %copy-start.12 = (bf16[256,2048]{1,0:T(8,128)(2,1)S(1)}, bf16[256,2048]{1,0:T(8,128)(2,1)}, u32[]{:S(2)}) copy-start(bf16[256,2048]{1,0:T(8,128)(2,1)} %get-tuple-element.92) | copy-start | bytes 3145732
  472.3 190.2 %all-reduce.11.cloned.1.call-start = ((), (), s32[]{:S(2)}) async-start(), calls=%async_computation.12 | async-start | bytes 7340032
  472.3 33.5 %slice-start = ((s8[7340032]{0:T(1024)(128)(4,1)}), s8[4194304]{0:T(1024)(128)(4,1)S(1)}, s32[]{:S(2)}) async-start(s8[7340032]{0:T(1024)(128)(4,1)} %bitcast.256), calls=%async_computation.13 | async-start | bytes 8388608
  486.5 19.4 %slice-start.1 = ((s8[7340032]{0:T(1024)(128)(4,1)}), s8[3145728]{0:T(1024)(128)(4,1)S(1)}, s32[]{:S(2)}) async-start(s8[7340032]{0:T(1024)(128)(4,1)} %bitcast.256), calls=%async_computation.14 | async-start | bytes 6291456
  553.0 7.6 copy-start.31
  553.0 7.6 copy-start.32
  556.6 4.0 copy-start.19
  556.6 4.0 copy-start.21
  556.7 4.0 copy-start.23
  560.6 2.1 copy-start.14
  560.7 2.1 copy-start.16
  581.0 245.2 %reduce-scatter.8.cloned.1.call-start = ((), (), s32[]{:S(2)}) async-start(), calls=%async_computation.11 | async-start | bytes 11796480 | tf_op jit(solution)/shard_map/reduce_scatter | solution.py:199
  591.9 322.8 %reduce-scatter.6.cloned.1.call-start = ((), (), s32[]{:S(2)}) async-start(), calls=%async_computation.10 | async-start | bytes 5898240 | tf_op jit(solution)/shard_map/reduce_scatter | solution.py:196
  601.5 2.6 copy-start.2
  612.4 1.8 copy-start
  615.9 7.7 copy-start.36
  619.9 20.0 %all-to-all-start = ((bf16[1,896,2,256]{3,2,0,1:T(2,128)(2,1)}), bf16[1,896,2,256]{3,2,0,1:T(2,128)(2,1)S(1)}, u32[]{:S(2)}, u32[]{:S(2)}) async-start(bf16[1,896,2,256]{3,2,0,1:T(2,128)(2,1)} %copy.106), calls=%async_computation | async-start | bytes 1835008 | tf_op jit(solution)/shard_map/all_to_all | solution.py:164
Sparse Core Ops, SparseCore 0:
  9.9 37.2 all-gather.4
  48.7 89.1 all-gather.6
  139.4 165.1 all-gather.10
  307.0 48.1 all-gather.8
  472.4 65.5 reduce-scatter.3
  581.1 81.2 all-reduce.10
  664.8 161.3 reduce-scatter.7
  828.5 86.1 reduce-scatter.5
where the time goes:
time: 933 us; the launch traced here: 925 us
  waiting for transfers between devices  576 us (62%)
  matrix products  128 us (14%)
  local copies, waits for them, and re-layouts  104 us (11%)
  other arithmetic  50.5 us (5%)
  blocking collectives  41.9 us (4%)
  between operations  16.4 us (2%)
    reduce_scatter x1, waiting for transfers between devices, per_device(): lax.psum_scatter(conv2_local.astype(jnp.bfloat16), 'batch', scatter_dimen...  162 us
    all_gather x1, waiting for transfers between devices, per_device(): lax.all_gather(conv2_weight, 'batch', axis=2, tiled=True)  109 us
    reduce_scatter x1, waiting for transfers between devices, per_device(): lax.psum_scatter(conv1_local.astype(jnp.bfloat16), 'batch', scatter_dimen...  84 us
    all_gather x1, waiting for transfers between devices, per_device(): lax.all_gather(conv1_weight, 'batch', axis=2, tiled=True)  76.4 us
    dot_general x6, matrix products, transposed(): jnp.dot(grad_padded[2 - tap_row:2 - tap_row + row_count], tap_weights(wei...  66.9 us
    all_gather x1, waiting for transfers between devices, fetch_units(): return lax.all_gather(local_units, 'tm', axis=2, tiled=True)  43.8 us
    all_gather x1, waiting for transfers between devices, fetch_frames(): return lax.all_gather(features, 'tm', axis=1, tiled=True)[0] * valid_low  36.3 us
    dot_general x6, matrix products, weight_grad(): lax.dot_general(grad_flat, flat_rows[tap_row:tap_row + frame_total], (((0...  33.2 us
  transfers between devices with their start and end apart: 10, of which 10 were waited for; matrix products, arithmetic and copies ran while one was open for 16% of the time, Pallas kernels for 0%

commit v1 on v0

v1 whole, which is shorter than its diff:
```python
import jax
import jax.numpy as jnp
from jax import lax
from jax.sharding import PartitionSpec as P


def frame_valid(lengths_row, frame_total, clip_count):
    frame_ids = jnp.arange(frame_total, dtype=jnp.int32)
    first_end = 16 * clip_count
    second_end = 48 * clip_count
    clip_index = jnp.where(
        frame_ids < first_end,
        frame_ids // 16,
        jnp.where(
            frame_ids < second_end,
            clip_count + (frame_ids - first_end) // 32,
            2 * clip_count + (frame_ids - second_end) // 64,
        ),
    )
    offset = jnp.where(
        frame_ids < first_end,
        frame_ids % 16,
        jnp.where(
            frame_ids < second_end, (frame_ids - first_end) % 32, (frame_ids - second_end) % 64
        ),
    )
    clip_ids = jnp.arange(3 * clip_count, dtype=jnp.int32)
    picked = jnp.where(
        clip_index[:, None] == clip_ids[None, :], lengths_row[None, :], jnp.zeros((), jnp.int32)
    )
    length_here = jnp.sum(picked, axis=1)
    return offset < length_here


def silu_slope(value):
    sigma = jax.nn.sigmoid(value)
    return sigma * (1.0 + value * (1.0 - sigma))


def per_device(
    features,
    lengths,
    conv1_weight,
    norm1_gain,
    norm1_bias,
    conv2_weight,
    norm2_gain,
    norm2_bias,
    out_grad,
):
    f32, bf16 = jnp.float32, jnp.bfloat16
    n = lax.axis_size("tm")
    planes = lax.axis_size("batch")
    chips = n // 2
    square = chips == 4
    me = lax.axis_index("tm")
    plane = lax.axis_index("batch")
    chip, core = me // 2, me % 2
    own_frames, mels, width1 = features.shape[1:]
    frames = own_frames * n
    part = conv2_weight.shape[0]
    slice2 = conv2_weight.shape[2]
    per_plane = chips // planes
    half2 = slice2 // 2
    block = half2 // chips
    sub = width1 // (planes * chips)
    hz = planes // 2
    clip_count = lengths.shape[1] // 3
    same_core = [[c + 2 * p for p in range(chips)] for c in range(2)]
    groups = range(planes)

    def to_core(x):
        return lax.ppermute(x, "tm", [(i, i ^ 1) for i in range(n)])

    def to_chip(x, bits):
        return lax.ppermute(x, "tm", [(i, i ^ (2 * bits)) for i in range(n)])

    def to_right(x):
        return lax.ppermute(x, "batch", [(z, (z + 1) % planes) for z in range(planes)])

    def chip_order(x, axis):
        if not square:
            return x
        shape = x.shape
        x = x.reshape(shape[:axis] + (2, 2) + shape[axis + 1 :])
        x = jnp.where(chip // 2 == 1, jnp.flip(x, axis), x)
        x = jnp.where(chip % 2 == 1, jnp.flip(x, axis + 1), x)
        return x.reshape(shape)

    def core_order(x, axis):
        return jnp.where(core == 1, jnp.flip(x, axis), x)

    def gather_chips(x):
        if not square:
            return lax.all_gather(x, "tm", axis=1, tiled=True, axis_index_groups=same_core)
        return jnp.concatenate([x] + [to_chip(x, b) for b in (1, 2, 3)], axis=1)

    def scatter_chips(x):
        if not square:
            return lax.psum_scatter(
                x, "tm", scatter_dimension=1, tiled=True, axis_index_groups=same_core
            ).astype(f32)
        lanes = x.shape[1] // 4
        parts = [x[:, b * lanes : (b + 1) * lanes] for b in range(4)]
        got = [parts[0]] + [to_chip(parts[b], b) for b in (1, 2, 3)]
        got = [v.astype(f32) for v in got]
        return (got[0] + got[1]) + (got[2] + got[3])

    def plane_sum(x):
        terms = [x] + [
            lax.ppermute(x, "batch", [(z, z ^ s) for z in range(planes)])
            for s in range(1, planes)
        ]
        while len(terms) > 1:
            terms = [terms[k] + terms[k + 1] for k in range(0, len(terms), 2)]
        return terms[0]

    def ring_gather(x):
        out = [x]
        for _ in range(planes - 1):
            out.append(to_right(out[-1]))
        return out

    def ring_sum(make):
        total = make(1 % planes)
        for step in range(2, planes + 1):
            moved = to_right(total.astype(bf16))
            total = make(step % planes) + moved.astype(f32)
        return total

    def pad_rows(x):
        return jnp.pad(x, ((1, 1), (0, 0)))

    def contract(rows, matrix, dims):
        return lax.dot_general(rows, matrix, (dims, ((), ())), preferred_element_type=f32)

    def conv(x, taps):
        padded = pad_rows(x)
        total = None
        for a in range(3):
            term = contract(padded[a : a + frames], taps[a], ((1,), (1,)))
            total = term if total is None else total + term
        return total

    def conv_t(dy, taps):
        padded = pad_rows(dy)
        total = None
        for a in range(3):
            term = contract(padded[2 - a : 2 - a + frames], taps[a], ((1,), (0,)))
            total = term if total is None else total + term
        return total

    def conv_w(x, dy):
        padded = pad_rows(x)
        return [contract(dy, padded[a : a + frames], ((0,), (0,))) for a in range(3)]

    w1 = conv1_weight.reshape(part, 9, chips, sub).transpose(2, 0, 1, 3)
    w1 = lax.all_to_all(w1, "tm", 0, 0, tiled=True, axis_index_groups=same_core)
    w1 = lax.all_to_all(
        w1.reshape(planes, per_plane * part, 9, sub), "batch", 0, 0, tiled=True
    )
    w1 = w1.reshape(2, hz, chips, block, 9, sub).transpose(2, 3, 4, 0, 1, 5)
    w1 = core_order(chip_order(w1, 0), 3)

    def taps1():
        mats = []
        for a in range(3):
            outs = []
            for mo in range(mels):
                ins = [w1[:, :, 3 * a + mi - mo + 1] for mi in range(mels)]
                outs.append(jnp.stack(ins, axis=3))
            mat = jnp.stack(outs, axis=1)
            mats.append(mat.reshape(chips * mels * block, 2 * mels * hz * sub))
        return mats

    w2 = conv2_weight.reshape(part, 9, per_plane, 2, part).transpose(0, 1, 3, 2, 4)
    w2 = w2.reshape(part, 9, 2, chips, block)
    w2 = core_order(chip_order(w2, 3), 2)

    def taps2():
        mats = []
        for a in range(3):
            outs = []
            for mo in range(mels):
                ins = [w2[:, 3 * a + mi - mo + 1] for mi in range(mels)]
                outs.append(jnp.stack(ins, axis=3))
            mat = jnp.stack(outs, axis=0)
            mats.append(mat.reshape(mels * part, 2 * chips * mels * block))
        return mats

    weights1, weights2 = taps1(), taps2()

    all_lengths = lax.all_gather(lengths[0], "batch")
    count = jnp.sum(all_lengths.astype(f32)) * mels
    valid = [
        frame_valid(
            lax.dynamic_index_in_dim(all_lengths, (plane - r) % planes, 0, keepdims=False),
            frames,
            clip_count,
        ).astype(f32)[:, None]
        for r in groups
    ]
    own_valid = frame_valid(lengths[0], frames, clip_count).astype(bf16)
    here_valid = lax.dynamic_slice_in_dim(own_valid, me * own_frames, own_frames, 0)

    masked = features[0] * here_valid[:, None, None]
    masked = masked.reshape(own_frames, mels, 2, hz, chips, sub).transpose(4, 2, 0, 1, 3, 5)
    masked = masked.reshape(n * own_frames, mels * hz * sub)
    masked = lax.all_to_all(masked, "tm", 0, 0, tiled=True)
    mine = ring_gather(masked)
    inputs = [jnp.concatenate([x, to_core(x)], axis=1) for x in mine]

    pre1 = [scatter_chips(conv(x, weights1).astype(bf16)) for x in inputs]

    def per_channel(x, width):
        return jnp.sum(x.reshape(mels, width), axis=0)

    def per_lane(x):
        return jnp.tile(x, mels)[None]

    def rows_sum(x):
        return jnp.sum(x, axis=0)

    def norm_stats(total, square_total):
        average = total / count
        variance = square_total / count - average * average
        return average, lax.rsqrt(variance + 1e-05)

    sums = sum(rows_sum(x * v) for x, v in zip(pre1, valid))
    squares = sum(rows_sum(x * x * v) for x, v in zip(pre1, valid))
    mean1, rstd1 = norm_stats(per_channel(sums, block), per_channel(squares, block))

    both1 = lax.all_gather(jnp.stack([norm1_gain, norm1_bias]), "tm")
    both1 = both1.transpose(1, 0, 2).reshape(2, planes, per_plane, 2, part)
    both1 = lax.dynamic_index_in_dim(both1, plane, 1, keepdims=False)
    both1 = lax.dynamic_index_in_dim(both1, core, 2, keepdims=False).reshape(2, half2)
    both1 = lax.dynamic_slice_in_dim(both1, chip * block, block, 1)
    gain1, bias1 = both1[0], both1[1]

    xhat1 = [(x - per_lane(mean1)) * per_lane(rstd1) for x in pre1]
    z1 = [per_lane(gain1) * x + per_lane(bias1) for x in xhat1]
    act1 = [(v * jax.nn.silu(z)).astype(bf16) for v, z in zip(valid, z1)]

    hidden = {}

    def hidden_of(r):
        if r not in hidden:
            half = gather_chips(act1[r])
            hidden[r] = jnp.concatenate([half, to_core(half)], axis=1)
        return hidden[r]

    pre2 = ring_sum(lambda r: conv(hidden_of(r), weights2))
    v0 = valid[0]
    sums2 = jnp.stack([rows_sum(pre2 * v0), rows_sum(pre2 * pre2 * v0)])
    sums2 = plane_sum(sums2.reshape(2, mels, part).sum(axis=1))
    mean2, rstd2 = norm_stats(sums2[0], sums2[1])
    xhat2 = (pre2 - per_lane(mean2)) * per_lane(rstd2)
    z2 = per_lane(norm2_gain) * xhat2 + per_lane(norm2_bias)
    out_local = (v0 * jax.nn.silu(z2)).astype(bf16)
    block_out = lax.all_to_all(
        out_local.reshape(n, own_frames, mels, part), "tm", 0, 0, tiled=True
    )
    block_out = block_out.transpose(1, 2, 0, 3).reshape(1, own_frames, mels, n * part)

    grad_in = out_grad[0].reshape(own_frames, mels, n, part).transpose(2, 0, 1, 3)
    grad_in = lax.all_to_all(grad_in, "tm", 0, 0, tiled=True).reshape(frames, mels * part)
    dz2 = grad_in.astype(f32) * v0 * silu_slope(z2)
    grads2 = jnp.stack([rows_sum(dz2), rows_sum(dz2 * xhat2)])
    grads2 = plane_sum(grads2.reshape(2, mels, part).sum(axis=1))
    bias2_grad, gain2_grad = grads2[0], grads2[1]
    dpre2 = (
        v0
        * per_lane(norm2_gain * rstd2)
        * (dz2 - (per_lane(bias2_grad) + xhat2 * per_lane(gain2_grad)) / count)
    ).astype(bf16)

    dpre2 = ring_gather(dpre2)
    half_lanes = chips * mels * block

    def back2(r):
        dact = conv_t(dpre2[r], weights2)
        other = to_core(dact[:, half_lanes:].astype(bf16))
        return scatter_chips((dact[:, :half_lanes] + other.astype(f32)).astype(bf16))

    dact1 = [back2(r) for r in groups]
    wgrad2 = [conv_w(hidden_of(r), dpre2[r]) for r in groups]

    def mel_taps(mats, cols, place):
        taps = []
        for a in range(3):
            mat = mats[a]
            for b in range(3):
                total = None
                for mo in range(mels):
                    mi = mo + b - 1
                    if 0 <= mi < mels:
                        term = place(mat, mo, mi)
                        total = term if total is None else total + term
                taps.append(total)
        return taps

    mats2 = [
        sum(wgrad2[r][a] for r in groups).reshape(mels, part, 2, chips, mels, block)
        for a in range(3)
    ]
    conv2_grad = jnp.stack(
        mel_taps(mats2, None, lambda m, mo, mi: m[mo, :, :, :, mi]), axis=1
    )
    conv2_grad = chip_order(core_order(conv2_grad, 2), 3)
    conv2_grad = conv2_grad.reshape(part, 9, 2, per_plane, part).transpose(0, 1, 3, 2, 4)
    conv2_grad = conv2_grad.reshape(part, 9, slice2)

    dz1 = [d * v * silu_slope(z) for d, v, z in zip(dact1, valid, z1)]
    bias1_sum = per_channel(sum(rows_sum(d) for d in dz1), block)
    gain1_sum = per_channel(sum(rows_sum(d * x) for d, x in zip(dz1, xhat1)), block)
    dpre1 = [
        (
            v
            * per_lane(gain1 * rstd1)
            * (d - (per_lane(bias1_sum) + x * per_lane(gain1_sum)) / count)
        ).astype(bf16)
        for v, d, x in zip(valid, dz1, xhat1)
    ]
    both = lax.all_gather(jnp.stack([gain1_sum, bias1_sum]), ("batch", "tm"))
    both = both.reshape(planes, chips, 2, 2, block).transpose(3, 0, 2, 1, 4)
    both = both.reshape(2, planes, 2, per_plane, part).transpose(0, 1, 3, 2, 4)
    both = lax.dynamic_index_in_dim(both.reshape(2, n, part), me, 1, keepdims=False)
    gain1_grad, bias1_grad = both[0], both[1]

    spread = {}

    def spread_of(r):
        if r not in spread:
            spread[r] = gather_chips(dpre1[r])
        return spread[r]

    own_lanes = mels * hz * sub

    def back1(r):
        dx = conv_t(spread_of(r), weights1)
        other = to_core(dx[:, own_lanes:].astype(bf16))
        return dx[:, :own_lanes] + other.astype(f32)

    dx = ring_sum(back1).astype(bf16)
    dx = lax.all_to_all(dx.reshape(n, own_frames, own_lanes), "tm", 0, 0, tiled=True)
    dx = dx.reshape(chips, 2, own_frames, mels, hz, sub).transpose(2, 3, 1, 4, 0, 5)
    input_grad = dx.reshape(1, own_frames, mels, width1) * here_valid[None, :, None, None]

    wgrad1 = [conv_w(inputs[r], spread_of(r)) for r in groups]
    mats1 = [
        sum(wgrad1[r][a] for r in groups).reshape(chips, mels, block, 2, mels, hz, sub)
        for a in range(3)
    ]
    grad1 = jnp.stack(
        mel_taps(mats1, None, lambda m, mo, mi: m[:, mo, :, :, mi]), axis=2
    ).astype(bf16)
    grad1 = chip_order(core_order(grad1, 3), 0)
    grad1 = grad1.transpose(3, 4, 0, 1, 2, 5).reshape(planes, half2, 9, sub)
    grad1 = lax.all_to_all(grad1, "batch", 0, 0, tiled=True)
    grad1 = lax.all_to_all(
        grad1.reshape(chips, part, 9, sub), "tm", 0, 0, tiled=True, axis_index_groups=same_core
    )
    conv1_grad = grad1.transpose(1, 2, 0, 3).reshape(part, 9, chips * sub).astype(f32)

    return (
        block_out,
        input_grad,
        conv1_grad,
        gain1_grad,
        bias1_grad,
        conv2_grad,
        gain2_grad,
        bias2_grad,
    )


def solution(mesh):
    return jax.shard_map(
        per_device,
        mesh=mesh,
        in_specs=(
            P("batch", "tm", None, None),
            P("batch", None),
            P("tm", None, "batch"),
            P("tm"),
            P("tm"),
            P("tm", None, "batch"),
            P("tm"),
            P("tm"),
            P("batch", "tm", None, None),
        ),
        out_specs=(
            P("batch", "tm", None, None),
            P("batch", "tm", None, None),
            P("tm", None, "batch"),
            P("tm"),
            P("tm"),
            P("tm", None, "batch"),
            P("tm"),
            P("tm"),
        ),
        check_vma=False,
    )
```

time: 933 us -> 864 us (0.926)
  waiting for transfers between devices: 576 us -> 226 us
  starting transfers between devices: 7.78 us -> 120 us
  local copies, waits for them, and re-layouts: 104 us -> 188 us
  other arithmetic: 50.5 us -> 118 us
  blocking collectives: 41.9 us -> 75 us
  between operations: 16.4 us -> 4.4 us
    all_gather x4 -> x0, waiting for transfers between devices: 266 us -> none  [the longest x1 109 us: per_device(): lax.all_gather(conv2_weight, 'batch', axis=2, tiled=True)]
    reduce_scatter x3 -> x0, waiting for transfers between devices: 257 us -> none  [the longest x1 162 us: per_device(): lax.psum_scatter(conv2_local.astype(jnp.bfloat16), 'batch', scatter_dimen...]
    ppermute x0 -> x82, waiting for transfers between devices: none -> 224 us  [the longest x12 149 us: to_right(): lax.ppermute(x, 'batch', [(z, (z + 1) % planes) for z in range(planes)])]
    ppermute x0 -> x82, starting transfers between devices: none -> 85.4 us  [the longest x48 63.4 us: to_chip(): return lax.ppermute(x, 'tm', [(i, i ^ 2 * bits) for i in range(n)])]
    all_gather x0 -> x3, blocking collectives: none -> 75 us  [the longest x1 42.4 us: per_device(): both = lax.all_gather(jnp.stack([gain1_sum, bias1_sum]), ('batch', 'tm'))]
    reshape x3 -> x16, local copies, waits for them, and re-layouts: 8.42 us -> 59.5 us  [the longest x3 11.3 us: per_device(): sum((wgrad1[r][a] for r in groups))]
    select_n x0 -> x12, other arithmetic: none -> 47.5 us  [the longest x4 17 us: chip_order(): x = jnp.where(chip // 2 == 1, jnp.flip(x, axis), x)]
    psum x4 -> x0, blocking collectives: 41.9 us -> none  [the longest x1 12.1 us: per_device(): lax.psum((jnp.sum(delta_one * scaled_one, axis=(0, 1)), jnp.sum(delta_one...]
  transfers between devices with their start and end apart: 10 -> 90, of which waited for: 10 -> 36; matrix products, arithmetic and copies ran while one was open for 16% -> 47% of each run, Pallas kernels for 0% -> 0%
where the time goes in v1:
time: 864 us; the launch traced here: 852 us
  waiting for transfers between devices  226 us (26%)
  local copies, waits for them, and re-layouts  188 us (22%)
  starting transfers between devices  120 us (14%)
  matrix products  120 us (14%)
  other arithmetic  118 us (14%)
  blocking collectives  75 us (9%)
    ppermute x12, waiting for transfers between devices, to_right(): lax.ppermute(x, 'batch', [(z, (z + 1) % planes) for z in range(planes)])  149 us
    dot_general x72, matrix products, contract(): lax.dot_general(rows, matrix, (dims, ((), ())), preferred_element_type=f32)  120 us
    ppermute x48, waiting for transfers between devices, to_chip(): return lax.ppermute(x, 'tm', [(i, i ^ 2 * bits) for i in range(n)])  75.2 us
    ppermute x48, starting transfers between devices, to_chip(): return lax.ppermute(x, 'tm', [(i, i ^ 2 * bits) for i in range(n)])  63.4 us
    unnamed x320, local copies, waits for them, and re-layouts  46.3 us
    all_gather x1, blocking collectives, per_device(): both = lax.all_gather(jnp.stack([gain1_sum, bias1_sum]), ('batch', 'tm'))  42.4 us
    another operation x1, local copies, waits for them, and re-layouts, per_device(): jnp.stack(mel_taps(mats2, None, lambda m, mo, mi: m[mo, :, :, :, mi]), ax...  20.8 us
    all_gather x1, blocking collectives, per_device(): both1 = lax.all_gather(jnp.stack([norm1_gain, norm1_bias]), 'tm')  19.9 us
  transfers between devices with their start and end apart: 90, of which 36 were waited for; matrix products, arithmetic and copies ran while one was open for 47% of the time, Pallas kernels for 0%

profile of v1, /device:TPU:0, one launch (start us, length us, event | category | flops | bytes accessed | tf_op | source)
XLA Modules:
  0.0 852.0 jit_solution(3829120238829603194)
XLA Ops:
  0.7 12.7 %all-gather.2 = s32[4,1,24]{2,1,0:T(1,128)S(1)} all-gather(s32[1,1,24]{2,1,0:T(1,128)} %bitcast.389), channel_id=1, replica_groups=mesh['tm'=8,'batch'=4] {'batch'}, dimensions={0}, use_global_device_ids=true | all-gather | bytes 480 | tf_op jit(solution)/shard_map/all_gather | solution.py:193
  16.8 3.7 all-to-all-start
  25.2 3.7 copy.185
  28.9 4.7 reverse_select_fusion.3
  33.6 4.6 fusion.198
  43.2 4.4 all-to-all-start.1
  47.7 19.9 %all-gather.3 = f32[8,2,256]{2,1,0:T(2,128)S(1)} all-gather(f32[1,2,256]{2,1,0:T(2,128)S(1)} %maximum_bitcast_fusion.12), channel_id=2, replica_groups=mesh['tm'=8,'batch'=4] {'tm'}, dimensions={0}, use_global_device_ids=true | all-gather | bytes 18432 | tf_op jit(solution)/shard_map/all_gather | solution.py:233
  69.6 5.1 all-to-all-start.2
  74.8 9.2 %collective-permute-done.4 = bf16[896,256]{1,0:T(8,128)(2,1)} collective-permute-done((bf16[896,256]{1,0:T(8,128)(2,1)S(1)}, bf16[896,256]{1,0:T(8,128)(2,1)}, u32[]{:S(2)}, u32[]{:S(2)}) %collective-permute-start.4) | collective-permute-done | bytes 458784 | tf_op jit(solution)/shard_map/ppermute | solution.py:79
  92.9 19.3 %collective-permute-done.9 = bf16[896,256]{1,0:T(8,128)(2,1)} collective-permute-done((bf16[896,256]{1,0:T(8,128)(2,1)}, bf16[896,256]{1,0:T(8,128)(2,1)}, u32[]{:S(2)}, u32[]{:S(2)}) %collective-permute-start.9) | collective-permute-done | bytes 458784 | tf_op jit(solution)/shard_map/ppermute | solution.py:79
  119.5 6.8 collective-permute-done.14
  129.0 4.2 all-to-all-start.4
  133.2 4.6 reshape.456
  137.8 8.7 %copy.178 = bf16[2,2,64,9,2,2,64]{6,5,4,2,1,0,3:T(2,128)(2,1)} copy(bf16[2,2,64,9,2,2,64]{2,1,0,6,3,5,4:T(2,128)(2,1)} %bitcast.333) | data formatting | bytes 2359296 | tf_op jit(solution)/shard_map/reshape | solution.py:85
  146.5 5.8 broadcast_select_fusion.1
  152.3 3.3 broadcast_select_fusion.3
  155.6 3.7 broadcast_select_fusion.5
  161.8 4.1 maximum_bitcast_fusion
  169.5 3.2 reshape.459
  176.3 3.4 reshape.460
  238.0 4.3 collective-permute-done.8
  242.3 4.3 collective-permute-done.7
  260.0 5.1 collective-permute-done.32
  270.2 4.7 collective-permute-done.28
  280.1 4.6 collective-permute-done.24
  288.6 5.2 collective-permute-done.20
  303.4 20.4 %collective-permute-done.35 = bf16[896,512]{1,0:T(8,128)(2,1)S(1)} collective-permute-done((bf16[896,512]{1,0:T(8,128)(2,1)S(1)}, bf16[896,512]{1,0:T(8,128)(2,1)S(1)}, u32[]{:S(2)}, u32[]{:S(2)}) %collective-permute-start.35) | collective-permute-done | bytes 917536 | tf_op jit(solution)/shard_map/ppermute | solution.py:79
  328.2 20.4 %collective-permute-done.36 = bf16[896,512]{1,0:T(8,128)(2,1)S(1)} collective-permute-done((bf16[896,512]{1,0:T(8,128)(2,1)S(1)}, bf16[896,512]{1,0:T(8,128)(2,1)S(1)}, u32[]{:S(2)}, u32[]{:S(2)}) %collective-permute-start.36) | collective-permute-done | bytes 917536 | tf_op jit(solution)/shard_map/ppermute | solution.py:79
  352.8 19.5 %collective-permute-done.37 = bf16[896,512]{1,0:T(8,128)(2,1)S(1)} collective-permute-done((bf16[896,512]{1,0:T(8,128)(2,1)S(1)}, bf16[896,512]{1,0:T(8,128)(2,1)S(1)}, u32[]{:S(2)}, u32[]{:S(2)}) %collective-permute-start.37) | collective-permute-done | bytes 917536 | tf_op jit(solution)/shard_map/ppermute | solution.py:79
  380.5 4.8 fusion.193
  392.1 4.2 all-to-all-start.3
  397.0 3.6 multiply_convert_fusion
  410.9 4.0 fusion.4
  415.0 3.8 fusion.6
  418.8 3.8 fusion.219
  445.9 3.8 fusion.16
  455.4 11.1 %collective-permute-done.53 = bf16[896,512]{1,0:T(8,128)(2,1)S(1)} collective-permute-done((bf16[896,512]{1,0:T(8,128)(2,1)}, bf16[896,512]{1,0:T(8,128)(2,1)S(1)}, u32[]{:S(2)}, u32[]{:S(2)}) %collective-permute-start.53) | collective-permute-done | bytes 917536 | tf_op jit(solution)/shard_map/ppermute | solution.py:79
  488.9 13.9 %collective-permute-done.58 = bf16[896,512]{1,0:T(8,128)(2,1)S(1)} collective-permute-done((bf16[896,512]{1,0:T(8,128)(2,1)S(1)}, bf16[896,512]{1,0:T(8,128)(2,1)S(1)}, u32[]{:S(2)}, u32[]{:S(2)}) %collective-permute-start.58) | collective-permute-done | bytes 917536 | tf_op jit(solution)/shard_map/ppermute | solution.py:79
  517.8 3.5 reshape.478
  524.3 3.6 reshape.479
  527.8 5.7 add_add_fusion.4
  536.5 3.5 reshape.480
  540.0 5.2 slice_bitcast_fusion.4
  561.7 3.4 multiply_convert_fusion.2
  571.5 20.8 %stack.176 = f32[256,9,2,4,64]{0,1,4,3,2:T(8,128)} concatenate(f32[256,1,2,4,64]{0,1,4,3,2:T(1,128)S(1)} %copy-done.54, f32[256,1,2,4,64]{0,1,4,3,2:T(1,128)S(1)} %copy-done.53, f32[256,1,2,4,64]{0,1,4,3,2:T(1,128)S(1)} %copy-done.52, f32[256,1,2,4,64]{0,1,4,3,2:T(1,128)} %get-tuple-element.111, f32[256,1,2,4,64]{0,1,4,3,2:T(1,128)} %get-tuple-element.110, ...), dimensions={1} | concatenate | bytes 9437184 | tf_op jit(solution)/shard_map/stack | solution.py:306
  600.6 6.2 collective-permute-done.73
  608.2 11.0 %collective-permute-done.72 = bf16[896,128]{1,0:T(8,128)(2,1)S(1)} collective-permute-done((bf16[896,128]{1,0:T(8,128)(2,1)S(1)}, bf16[896,128]{1,0:T(8,128)(2,1)S(1)}, u32[]{:S(2)}, u32[]{:S(2)}) %collective-permute-start.72) | collective-permute-done | bytes 229408 | tf_op jit(solution)/shard_map/ppermute | solution.py:76
  647.7 3.8 reshape.471
  665.0 3.6 reshape.472
  682.2 3.8 reshape.473
  692.0 4.8 broadcast_select_fusion.4
  701.4 4.2 broadcast_select_fusion.2
  705.6 8.7 %copy.209 = bf16[2,2,64,9,2,2,64]{2,1,0,6,3,5,4:T(2,128)(2,1)} copy(bf16[2,2,64,9,2,2,64]{6,5,4,2,1,0,3:T(2,128)(2,1)} %broadcast_select_fusion.2) | data formatting | bytes 2359296 | tf_op jit(solution)/shard_map/jit(_where)/select_n | solution.py:87
  714.3 4.5 reshape.476
  718.8 5.2 all-to-all-start.6
  732.5 25.0 %collective-permute-done.80 = bf16[896,256]{1,0:T(8,128)(2,1)S(1)} collective-permute-done((bf16[896,256]{1,0:T(8,128)(2,1)S(1)}, bf16[896,256]{1,0:T(8,128)(2,1)S(1)}, u32[]{:S(2)}, u32[]{:S(2)}) %collective-permute-start.80) | collective-permute-done | bytes 458784 | tf_op jit(solution)/shard_map/ppermute | solution.py:79
  758.8 4.3 collective-permute-start.81
  764.5 4.9 copy.215
  773.5 3.5 all-to-all-start.5
  777.0 7.2 reverse_select_fusion.2
  785.9 4.3 all-to-all-start.7
  790.2 7.3 reverse_select_fusion.1
  797.5 6.0 copy.218
  803.6 42.4 %all-gather.4 = f32[32,2,64]{2,1,0:T(2,128)S(1)} all-gather(f32[1,2,64]{2,1,0:T(2,128)S(1)} %maximum_bitcast_fusion.13), channel_id=3, replica_groups=mesh['tm'=8,'batch'=4] {'batch','tm'}, dimensions={0}, use_global_device_ids=true | all-gather | bytes 16896 | tf_op jit(solution)/shard_map/all_gather | solution.py:324
  (692 shorter events, 364.3 us)
Async XLA Ops:
  16.8 26.4 %all-to-all-start = ((bf16[8,112,256]{2,1,0:T(8,128)(2,1)}), bf16[8,112,256]{2,1,0:T(8,128)(2,1)S(1)}, u32[]{:S(2)}, u32[]{:S(2)}) async-start(bf16[8,112,256]{2,1,0:T(8,128)(2,1)} %copy.175), calls=%async_computation | async-start | bytes 917504 | tf_op jit(solution)/shard_map/all_to_all | solution.py:209
  43.2 26.4 %all-to-all-start.1 = ((bf16[4,256,9,64]{1,3,2,0:T(8,128)(2,1)}), bf16[4,256,9,64]{1,3,2,0:T(8,128)(2,1)}, u32[]{:S(2)}, u32[]{:S(2)}) async-start(bf16[4,256,9,64]{1,3,2,0:T(8,128)(2,1)} %copy.177), calls=%async_computation.1 | async-start | bytes 2359296 | tf_op jit(solution)/shard_map/all_to_all | solution.py:158
  68.6 15.4 %collective-permute-start.4 = (bf16[896,256]{1,0:T(8,128)(2,1)S(1)}, bf16[896,256]{1,0:T(8,128)(2,1)}, u32[]{:S(2)}, u32[]{:S(2)}) collective-permute-start(bf16[896,256]{1,0:T(8,128)(2,1)S(1)} %bitcast.343), channel_id=1, source_target_pairs={{0,1},{1,2},{2,3},{3,0},{4,5},{5,6},{6,7},{7,4},{8,9},{9,10},{10,1... | collective-permute-start | bytes 1376264 | tf_op jit(solution)/shard_map/ppermute | solution.py:79
  69.6 59.3 %all-to-all-start.2 = ((bf16[4,256,9,64]{1,3,2,0:T(8,128)(2,1)}), bf16[4,256,9,64]{1,3,2,0:T(8,128)(2,1)}, u32[]{:S(2)}, u32[]{:S(2)}) async-start(bf16[4,256,9,64]{1,3,2,0:T(8,128)(2,1)} %all-to-all-done.1), calls=%async_computation.2 | async-start | bytes 2359296 | tf_op jit(solution)/shard_map/all_to_all | solution.py:159
  84.0 28.2 %collective-permute-start.9 = (bf16[896,256]{1,0:T(8,128)(2,1)}, bf16[896,256]{1,0:T(8,128)(2,1)}, u32[]{:S(2)}, u32[]{:S(2)}) collective-permute-start(bf16[896,256]{1,0:T(8,128)(2,1)} %collective-permute-done.4), channel_id=1, source_target_pairs={{0,1},{1,2},{2,3},{3,0},{4,5},{5,6},{6,7},{7,4},{8,9},{9,10},{10,1... | collective-permute-start | bytes 1376264 | tf_op jit(solution)/shard_map/ppermute | solution.py:79
  92.2 24.6 %collective-permute-start = (bf16[896,256]{1,0:T(8,128)(2,1)S(1)}, bf16[896,256]{1,0:T(8,128)(2,1)S(1)}, u32[]{:S(2)}, u32[]{:S(2)}) collective-permute-start(bf16[896,256]{1,0:T(8,128)(2,1)S(1)} %bitcast.344), channel_id=1, source_target_pairs={{0,4},{4,0},{8,12},{12,8},{16,20},{20,16},{24,28},{28,24},{1,5},{5... | collective-permute-start | bytes 1376264 | tf_op jit(solution)/shard_map/ppermute | solution.py:73
  112.2 14.1 %collective-permute-start.14 = (bf16[896,256]{1,0:T(8,128)(2,1)}, bf16[896,256]{1,0:T(8,128)(2,1)}, u32[]{:S(2)}, u32[]{:S(2)}) collective-permute-start(bf16[896,256]{1,0:T(8,128)(2,1)} %collective-permute-done.9), channel_id=1, source_target_pairs={{0,1},{1,2},{2,3},{3,0},{4,5},{5,6},{6,7},{7,4},{8,9},{9,10},{10,1... | collective-permute-start | bytes 1376264 | tf_op jit(solution)/shard_map/ppermute | solution.py:79
  129.0 248.7 %all-to-all-start.4 = ((bf16[8,112,2,256]{3,2,1,0:T(2,128)(2,1)}), bf16[8,112,2,256]{3,2,1,0:T(2,128)(2,1)}, u32[]{:S(2)}, u32[]{:S(2)}) async-start(bf16[8,112,2,256]{3,2,1,0:T(2,128)(2,1)} %bitcast.348), calls=%async_computation.4 | async-start | bytes 1835008 | tf_op jit(solution)/shard_map/all_to_all | solution.py:266
  206.7 13.7 %collective-permute-start.16 = (bf16[896,128]{1,0:T(8,128)(2,1)S(1)}, bf16[896,128]{1,0:T(8,128)(2,1)S(1)}, u32[]{:S(2)}, u32[]{:S(2)}) collective-permute-start(bf16[896,128]{1,0:T(8,128)(2,1)S(1)} %get-tuple-element.137), channel_id=1, source_target_pairs={{0,8},{4,12},{8,0},{12,4},{16,24},{20,28},{24,16},{28,20},{1,9},{5... | collective-permute-start | bytes 688136 | tf_op jit(solution)/shard_map/ppermute | solution.py:76
  207.7 14.9 %collective-permute-start.13 = (bf16[896,128]{1,0:T(8,128)(2,1)S(1)}, bf16[896,128]{1,0:T(8,128)(2,1)S(1)}, u32[]{:S(2)}, u32[]{:S(2)}) collective-permute-start(bf16[896,128]{1,0:T(8,128)(2,1)S(1)} %get-tuple-element.135), channel_id=1, source_target_pairs={{0,24},{4,28},{8,16},{12,20},{16,8},{20,12},{24,0},{28,4},{1,25},{... | collective-permute-start | bytes 688136 | tf_op jit(solution)/shard_map/ppermute | solution.py:76
  210.6 16.9 %collective-permute-start.12 = (bf16[896,128]{1,0:T(8,128)(2,1)S(1)}, bf16[896,128]{1,0:T(8,128)(2,1)S(1)}, u32[]{:S(2)}, u32[]{:S(2)}) collective-permute-start(bf16[896,128]{1,0:T(8,128)(2,1)S(1)} %get-tuple-element.136), channel_id=1, source_target_pairs={{0,16},{4,20},{8,24},{12,28},{16,0},{20,4},{24,8},{28,12},{1,17},{... | collective-permute-start | bytes 688136 | tf_op jit(solution)/shard_map/ppermute | solution.py:76
  215.4 14.7 %collective-permute-start.11 = (bf16[896,128]{1,0:T(8,128)(2,1)S(1)}, bf16[896,128]{1,0:T(8,128)(2,1)S(1)}, u32[]{:S(2)}, u32[]{:S(2)}) collective-permute-start(bf16[896,128]{1,0:T(8,128)(2,1)S(1)} %get-tuple-element.134), channel_id=1, source_target_pairs={{0,8},{4,12},{8,0},{12,4},{16,24},{20,28},{24,16},{28,20},{1,9},{5... | collective-permute-start | bytes 688136 | tf_op jit(solution)/shard_map/ppermute | solution.py:76
  217.7 14.8 %collective-permute-start.3 = (bf16[896,128]{1,0:T(8,128)(2,1)S(1)}, bf16[896,128]{1,0:T(8,128)(2,1)S(1)}, u32[]{:S(2)}, u32[]{:S(2)}) collective-permute-start(bf16[896,128]{1,0:T(8,128)(2,1)S(1)} %get-tuple-element.132), channel_id=1, source_target_pairs={{0,24},{4,28},{8,16},{12,20},{16,8},{20,12},{24,0},{28,4},{1,25},{... | collective-permute-start | bytes 688136 | tf_op jit(solution)/shard_map/ppermute | solution.py:76
  220.3 16.9 %collective-permute-start.2 = (bf16[896,128]{1,0:T(8,128)(2,1)S(1)}, bf16[896,128]{1,0:T(8,128)(2,1)S(1)}, u32[]{:S(2)}, u32[]{:S(2)}) collective-permute-start(bf16[896,128]{1,0:T(8,128)(2,1)S(1)} %get-tuple-element.133), channel_id=1, source_target_pairs={{0,16},{4,20},{8,24},{12,28},{16,0},{20,4},{24,8},{28,12},{1,17},{... | collective-permute-start | bytes 688136 | tf_op jit(solution)/shard_map/ppermute | solution.py:76
  222.6 15.3 %collective-permute-start.1 = (bf16[896,128]{1,0:T(8,128)(2,1)S(1)}, bf16[896,128]{1,0:T(8,128)(2,1)S(1)}, u32[]{:S(2)}, u32[]{:S(2)}) collective-permute-start(bf16[896,128]{1,0:T(8,128)(2,1)S(1)} %get-tuple-element.131), channel_id=1, source_target_pairs={{0,8},{4,12},{8,0},{12,4},{16,24},{20,28},{24,16},{28,20},{1,9},{5... | collective-permute-start | bytes 688136 | tf_op jit(solution)/shard_map/ppermute | solution.py:76
  227.5 14.8 %collective-permute-start.8 = (bf16[896,128]{1,0:T(8,128)(2,1)S(1)}, bf16[896,128]{1,0:T(8,128)(2,1)S(1)}, u32[]{:S(2)}, u32[]{:S(2)}) collective-permute-start(bf16[896,128]{1,0:T(8,128)(2,1)S(1)} %get-tuple-element.129), channel_id=1, source_target_pairs={{0,24},{4,28},{8,16},{12,20},{16,8},{20,12},{24,0},{28,4},{1,25},{... | collective-permute-start | bytes 688136 | tf_op jit(solution)/shard_map/ppermute | solution.py:76
  230.1 16.4 %collective-permute-start.7 = (bf16[896,128]{1,0:T(8,128)(2,1)S(1)}, bf16[896,128]{1,0:T(8,128)(2,1)S(1)}, u32[]{:S(2)}, u32[]{:S(2)}) collective-permute-start(bf16[896,128]{1,0:T(8,128)(2,1)S(1)} %get-tuple-element.130), channel_id=1, source_target_pairs={{0,16},{4,20},{8,24},{12,28},{16,0},{20,4},{24,8},{28,12},{1,17},{... | collective-permute-start | bytes 688136 | tf_op jit(solution)/shard_map/ppermute | solution.py:76
  232.4 14.5 %collective-permute-start.6 = (bf16[896,128]{1,0:T(8,128)(2,1)S(1)}, bf16[896,128]{1,0:T(8,128)(2,1)S(1)}, u32[]{:S(2)}, u32[]{:S(2)}) collective-permute-start(bf16[896,128]{1,0:T(8,128)(2,1)S(1)} %get-tuple-element.128), channel_id=1, source_target_pairs={{0,8},{4,12},{8,0},{12,4},{16,24},{20,28},{24,16},{28,20},{1,9},{5... | collective-permute-start | bytes 688136 | tf_op jit(solution)/shard_map/ppermute | solution.py:76
  255.9 13.0 %collective-permute-start.27 = (bf16[896,128]{1,0:T(8,128)(2,1)S(1)}, bf16[896,128]{1,0:T(8,128)(2,1)S(1)}, u32[]{:S(2)}, u32[]{:S(2)}) collective-permute-start(bf16[896,128]{1,0:T(8,128)(2,1)S(1)} %get-tuple-element.169), channel_id=1, source_target_pairs={{0,8},{4,12},{8,0},{12,4},{16,24},{20,28},{24,16},{28,20},{1,9},{5... | collective-permute-start | bytes 688136 | tf_op jit(solution)/shard_map/ppermute | solution.py:76
  257.4 17.5 %collective-permute-start.28 = (bf16[896,128]{1,0:T(8,128)(2,1)S(1)}, bf16[896,128]{1,0:T(8,128)(2,1)S(1)}, u32[]{:S(2)}, u32[]{:S(2)}) collective-permute-start(bf16[896,128]{1,0:T(8,128)(2,1)S(1)} %get-tuple-element.169), channel_id=1, source_target_pairs={{0,16},{4,20},{8,24},{12,28},{16,0},{20,4},{24,8},{28,12},{1,17},{... | collective-permute-start | bytes 688136 | tf_op jit(solution)/shard_map/ppermute | solution.py:76
  258.8 16.4 %collective-permute-start.29 = (bf16[896,128]{1,0:T(8,128)(2,1)S(1)}, bf16[896,128]{1,0:T(8,128)(2,1)S(1)}, u32[]{:S(2)}, u32[]{:S(2)}) collective-permute-start(bf16[896,128]{1,0:T(8,128)(2,1)S(1)} %get-tuple-element.169), channel_id=1, source_target_pairs={{0,24},{4,28},{8,16},{12,20},{16,8},{20,12},{24,0},{28,4},{1,25},{... | collective-permute-start | bytes 688136 | tf_op jit(solution)/shard_map/ppermute | solution.py:76
  265.1 13.6 %collective-permute-start.23 = (bf16[896,128]{1,0:T(8,128)(2,1)S(1)}, bf16[896,128]{1,0:T(8,128)(2,1)S(1)}, u32[]{:S(2)}, u32[]{:S(2)}) collective-permute-start(bf16[896,128]{1,0:T(8,128)(2,1)S(1)} %get-tuple-element.167), channel_id=1, source_target_pairs={{0,8},{4,12},{8,0},{12,4},{16,24},{20,28},{24,16},{28,20},{1,9},{5... | collective-permute-start | bytes 688136 | tf_op jit(solution)/shard_map/ppermute | solution.py:76
  266.9 17.8 %collective-permute-start.24 = (bf16[896,128]{1,0:T(8,128)(2,1)S(1)}, bf16[896,128]{1,0:T(8,128)(2,1)S(1)}, u32[]{:S(2)}, u32[]{:S(2)}) collective-permute-start(bf16[896,128]{1,0:T(8,128)(2,1)S(1)} %get-tuple-element.167), channel_id=1, source_target_pairs={{0,16},{4,20},{8,24},{12,28},{16,0},{20,4},{24,8},{28,12},{1,17},{... | collective-permute-start | bytes 688136 | tf_op jit(solution)/shard_map/ppermute | solution.py:76
  268.8 15.9 %collective-permute-start.25 = (bf16[896,128]{1,0:T(8,128)(2,1)S(1)}, bf16[896,128]{1,0:T(8,128)(2,1)S(1)}, u32[]{:S(2)}, u32[]{:S(2)}) collective-permute-start(bf16[896,128]{1,0:T(8,128)(2,1)S(1)} %get-tuple-element.167), channel_id=1, source_target_pairs={{0,24},{4,28},{8,16},{12,20},{16,8},{20,12},{24,0},{28,4},{1,25},{... | collective-permute-start | bytes 688136 | tf_op jit(solution)/shard_map/ppermute | solution.py:76
  274.9 13.7 %collective-permute-start.19 = (bf16[896,128]{1,0:T(8,128)(2,1)S(1)}, bf16[896,128]{1,0:T(8,128)(2,1)S(1)}, u32[]{:S(2)}, u32[]{:S(2)}) collective-permute-start(bf16[896,128]{1,0:T(8,128)(2,1)S(1)} %get-tuple-element.77), channel_id=1, source_target_pairs={{0,8},{4,12},{8,0},{12,4},{16,24},{20,28},{24,16},{28,20},{1,9},{5... | collective-permute-start | bytes 688136 | tf_op jit(solution)/shard_map/ppermute | solution.py:76
  275.3 18.5 %collective-permute-start.20 = (bf16[896,128]{1,0:T(8,128)(2,1)S(1)}, bf16[896,128]{1,0:T(8,128)(2,1)S(1)}, u32[]{:S(2)}, u32[]{:S(2)}) collective-permute-start(bf16[896,128]{1,0:T(8,128)(2,1)S(1)} %get-tuple-element.77), channel_id=1, source_target_pairs={{0,16},{4,20},{8,24},{12,28},{16,0},{20,4},{24,8},{28,12},{1,17},{... | collective-permute-start | bytes 688136 | tf_op jit(solution)/shard_map/ppermute | solution.py:76
  278.7 15.1 %collective-permute-start.21 = (bf16[896,128]{1,0:T(8,128)(2,1)S(1)}, bf16[896,128]{1,0:T(8,128)(2,1)S(1)}, u32[]{:S(2)}, u32[]{:S(2)}) collective-permute-start(bf16[896,128]{1,0:T(8,128)(2,1)S(1)} %get-tuple-element.77), channel_id=1, source_target_pairs={{0,24},{4,28},{8,16},{12,20},{16,8},{20,12},{24,0},{28,4},{1,25},{... | collective-permute-start | bytes 688136 | tf_op jit(solution)/shard_map/ppermute | solution.py:76
  284.7 14.9 %collective-permute-start.30 = (bf16[896,512]{1,0:T(8,128)(2,1)S(1)}, bf16[896,512]{1,0:T(8,128)(2,1)S(1)}, u32[]{:S(2)}, u32[]{:S(2)}) collective-permute-start(bf16[896,512]{1,0:T(8,128)(2,1)S(1)} %pad_maximum_fusion.9), channel_id=1, source_target_pairs={{0,4},{4,0},{8,12},{12,8},{16,20},{20,16},{24,28},{28,24},{1,5},{5... | collective-permute-start | bytes 2752520 | tf_op jit(solution)/shard_map/ppermute | solution.py:73
  299.2 24.6 %collective-permute-start.35 = (bf16[896,512]{1,0:T(8,128)(2,1)S(1)}, bf16[896,512]{1,0:T(8,128)(2,1)S(1)}, u32[]{:S(2)}, u32[]{:S(2)}) collective-permute-start(bf16[896,512]{1,0:T(8,128)(2,1)S(1)} %add_convert_fusion.2), channel_id=1, source_target_pairs={{0,1},{1,2},{2,3},{3,0},{4,5},{5,6},{6,7},{7,4},{8,9},{9,10},{10,1... | collective-permute-start | bytes 2752520 | tf_op jit(solution)/shard_map/ppermute | solution.py:79
  324.6 24.0 %collective-permute-start.36 = (bf16[896,512]{1,0:T(8,128)(2,1)S(1)}, bf16[896,512]{1,0:T(8,128)(2,1)S(1)}, u32[]{:S(2)}, u32[]{:S(2)}) collective-permute-start(bf16[896,512]{1,0:T(8,128)(2,1)S(1)} %add_convert_fusion.1), channel_id=1, source_target_pairs={{0,1},{1,2},{2,3},{3,0},{4,5},{5,6},{6,7},{7,4},{8,9},{9,10},{10,1... | collective-permute-start | bytes 2752520 | tf_op jit(solution)/shard_map/ppermute | solution.py:79
  349.3 22.9 %collective-permute-start.37 = (bf16[896,512]{1,0:T(8,128)(2,1)S(1)}, bf16[896,512]{1,0:T(8,128)(2,1)S(1)}, u32[]{:S(2)}, u32[]{:S(2)}) collective-permute-start(bf16[896,512]{1,0:T(8,128)(2,1)S(1)} %add_convert_fusion), channel_id=1, source_target_pairs={{0,1},{1,2},{2,3},{3,0},{4,5},{5,6},{6,7},{7,4},{8,9},{9,10},{10,1... | collective-permute-start | bytes 2752520 | tf_op jit(solution)/shard_map/ppermute | solution.py:79
  392.1 30.6 %all-to-all-start.3 = ((bf16[8,112,2,256]{3,2,1,0:T(2,128)(2,1)}), bf16[8,112,2,256]{3,2,1,0:T(2,128)(2,1)}, u32[]{:S(2)}, u32[]{:S(2)}) async-start(bf16[8,112,2,256]{3,2,1,0:T(2,128)(2,1)} %reshape.466), calls=%async_computation.3 | async-start | bytes 1835008 | tf_op jit(solution)/shard_map/all_to_all | solution.py:260
  400.6 28.3 %collective-permute-start.48 = (bf16[896,512]{1,0:T(8,128)(2,1)}, bf16[896,512]{1,0:T(8,128)(2,1)}, u32[]{:S(2)}, u32[]{:S(2)}) collective-permute-start(bf16[896,512]{1,0:T(8,128)(2,1)} %multiply_convert_fusion), channel_id=1, source_target_pairs={{0,1},{1,2},{2,3},{3,0},{4,5},{5,6},{6,7},{7,4},{8,9},{9,10},{10,1... | collective-permute-start | bytes 2752520 | tf_op jit(solution)/shard_map/ppermute | solution.py:79
  410.9 26.0 %collective-permute-start.44 = (bf16[896,512]{1,0:T(8,128)(2,1)}, bf16[896,512]{1,0:T(8,128)(2,1)}, u32[]{:S(2)}, u32[]{:S(2)}) collective-permute-start(bf16[896,512]{1,0:T(8,128)(2,1)} %slice.898), channel_id=1, source_target_pairs={{0,4},{4,0},{8,12},{12,8},{16,20},{20,16},{24,28},{28,24},{1,5},{5... | collective-permute-start | bytes 2752520 | tf_op jit(solution)/shard_map/ppermute | solution.py:73
  436.6 15.5 %collective-permute-start.49 = (bf16[896,512]{1,0:T(8,128)(2,1)S(1)}, bf16[896,512]{1,0:T(8,128)(2,1)S(1)}, u32[]{:S(2)}, u32[]{:S(2)}) collective-permute-start(bf16[896,512]{1,0:T(8,128)(2,1)S(1)} %slice.897), channel_id=1, source_target_pairs={{0,4},{4,0},{8,12},{12,8},{16,20},{20,16},{24,28},{28,24},{1,5},{5... | collective-permute-start | bytes 2752520 | tf_op jit(solution)/shard_map/ppermute | solution.py:73
  438.6 35.5 %collective-permute-start.47 = (bf16[896,128]{1,0:T(8,128)(2,1)S(1)}, bf16[896,128]{1,0:T(8,128)(2,1)S(1)}, u32[]{:S(2)}, u32[]{:S(2)}) collective-permute-start(bf16[896,128]{1,0:T(8,128)(2,1)S(1)} %get-tuple-element.126), channel_id=1, source_target_pairs={{0,24},{4,28},{8,16},{12,20},{16,8},{20,12},{24,0},{28,4},{1,25},{... | collective-permute-start | bytes 688136 | tf_op jit(solution)/shard_map/ppermute | solution.py:76
  441.5 34.4 %collective-permute-start.46 = (bf16[896,128]{1,0:T(8,128)(2,1)S(1)}, bf16[896,128]{1,0:T(8,128)(2,1)S(1)}, u32[]{:S(2)}, u32[]{:S(2)}) collective-permute-start(bf16[896,128]{1,0:T(8,128)(2,1)S(1)} %get-tuple-element.127), channel_id=1, source_target_pairs={{0,16},{4,20},{8,24},{12,28},{16,0},{20,4},{24,8},{28,12},{1,17},{... | collective-permute-start | bytes 688136 | tf_op jit(solution)/shard_map/ppermute | solution.py:76
  442.0 37.9 %collective-permute-start.45 = (bf16[896,128]{1,0:T(8,128)(2,1)S(1)}, bf16[896,128]{1,0:T(8,128)(2,1)S(1)}, u32[]{:S(2)}, u32[]{:S(2)}) collective-permute-start(bf16[896,128]{1,0:T(8,128)(2,1)S(1)} %get-tuple-element.125), channel_id=1, source_target_pairs={{0,8},{4,12},{8,0},{12,4},{16,24},{20,28},{24,16},{28,20},{1,9},{5... | collective-permute-start | bytes 688136 | tf_op jit(solution)/shard_map/ppermute | solution.py:76
  442.2 24.4 %collective-permute-start.53 = (bf16[896,512]{1,0:T(8,128)(2,1)}, bf16[896,512]{1,0:T(8,128)(2,1)S(1)}, u32[]{:S(2)}, u32[]{:S(2)}) collective-permute-start(bf16[896,512]{1,0:T(8,128)(2,1)} %collective-permute-done.48), channel_id=1, source_target_pairs={{0,1},{1,2},{2,3},{3,0},{4,5},{5,6},{6,7},{7,4},{8,9},{9,10},{10,1... | collective-permute-start | bytes 2752520 | tf_op jit(solution)/shard_map/ppermute | solution.py:79
  452.6 27.5 %collective-permute-start.52 = (bf16[896,128]{1,0:T(8,128)(2,1)S(1)}, bf16[896,128]{1,0:T(8,128)(2,1)S(1)}, u32[]{:S(2)}, u32[]{:S(2)}) collective-permute-start(bf16[896,128]{1,0:T(8,128)(2,1)S(1)} %get-tuple-element.117), channel_id=1, source_target_pairs={{0,24},{4,28},{8,16},{12,20},{16,8},{20,12},{24,0},{28,4},{1,25},{... | collective-permute-start | bytes 688136 | tf_op jit(solution)/shard_map/ppermute | solution.py:76
  470.2 13.9 %collective-permute-start.54 = (bf16[896,512]{1,0:T(8,128)(2,1)S(1)}, bf16[896,512]{1,0:T(8,128)(2,1)S(1)}, u32[]{:S(2)}, u32[]{:S(2)}) collective-permute-start(bf16[896,512]{1,0:T(8,128)(2,1)S(1)} %slice.896), channel_id=1, source_target_pairs={{0,4},{4,0},{8,12},{12,8},{16,20},{20,16},{24,28},{28,24},{1,5},{5... | collective-permute-start | bytes 2752520 | tf_op jit(solution)/shard_map/ppermute | solution.py:73
  480.0 22.9 %collective-permute-start.58 = (bf16[896,512]{1,0:T(8,128)(2,1)S(1)}, bf16[896,512]{1,0:T(8,128)(2,1)S(1)}, u32[]{:S(2)}, u32[]{:S(2)}) collective-permute-start(bf16[896,512]{1,0:T(8,128)(2,1)S(1)} %collective-permute-done.53), channel_id=1, source_target_pairs={{0,1},{1,2},{2,3},{3,0},{4,5},{5,6},{6,7},{7,4},{8,9},{9,10},{10,1... | collective-permute-start | bytes 2752520 | tf_op jit(solution)/shard_map/ppermute | solution.py:79
  485.4 63.7 %collective-permute-start.57 = (bf16[896,128]{1,0:T(8,128)(2,1)}, bf16[896,128]{1,0:T(8,128)(2,1)}, u32[]{:S(2)}, u32[]{:S(2)}) collective-permute-start(bf16[896,128]{1,0:T(8,128)(2,1)} %get-tuple-element.120), channel_id=1, source_target_pairs={{0,24},{4,28},{8,16},{12,20},{16,8},{20,12},{24,0},{28,4},{1,25},{... | collective-permute-start | bytes 688136 | tf_op jit(solution)/shard_map/ppermute | solution.py:76
  486.9 66.5 %collective-permute-start.56 = (bf16[896,128]{1,0:T(8,128)(2,1)}, bf16[896,128]{1,0:T(8,128)(2,1)}, u32[]{:S(2)}, u32[]{:S(2)}) collective-permute-start(bf16[896,128]{1,0:T(8,128)(2,1)} %get-tuple-element.121), channel_id=1, source_target_pairs={{0,16},{4,20},{8,24},{12,28},{16,0},{20,4},{24,8},{28,12},{1,17},{... | collective-permute-start | bytes 688136 | tf_op jit(solution)/shard_map/ppermute | solution.py:76
  488.4 65.1 %collective-permute-start.55 = (bf16[896,128]{1,0:T(8,128)(2,1)}, bf16[896,128]{1,0:T(8,128)(2,1)}, u32[]{:S(2)}, u32[]{:S(2)}) collective-permute-start(bf16[896,128]{1,0:T(8,128)(2,1)} %get-tuple-element.119), channel_id=1, source_target_pairs={{0,8},{4,12},{8,0},{12,4},{16,24},{20,28},{24,16},{28,20},{1,9},{5... | collective-permute-start | bytes 688136 | tf_op jit(solution)/shard_map/ppermute | solution.py:76
  507.4 37.8 %collective-permute-start.59 = (bf16[896,512]{1,0:T(8,128)(2,1)}, bf16[896,512]{1,0:T(8,128)(2,1)}, u32[]{:S(2)}, u32[]{:S(2)}) collective-permute-start(bf16[896,512]{1,0:T(8,128)(2,1)} %slice.895), channel_id=1, source_target_pairs={{0,4},{4,0},{8,12},{12,8},{16,20},{20,16},{24,28},{28,24},{1,5},{5... | collective-permute-start | bytes 2752520 | tf_op jit(solution)/shard_map/ppermute | solution.py:73
  565.1 30.0 %collective-permute-start.69 = (bf16[896,128]{1,0:T(8,128)(2,1)}, bf16[896,128]{1,0:T(8,128)(2,1)}, u32[]{:S(2)}, u32[]{:S(2)}) collective-permute-start(bf16[896,128]{1,0:T(8,128)(2,1)} %get-tuple-element.155), channel_id=1, source_target_pairs={{0,24},{4,28},{8,16},{12,20},{16,8},{20,12},{24,0},{28,4},{1,25},{... | collective-permute-start | bytes 688136 | tf_op jit(solution)/shard_map/ppermute | solution.py:76
  566.6 30.0 %collective-permute-start.68 = (bf16[896,128]{1,0:T(8,128)(2,1)}, bf16[896,128]{1,0:T(8,128)(2,1)}, u32[]{:S(2)}, u32[]{:S(2)}) collective-permute-start(bf16[896,128]{1,0:T(8,128)(2,1)} %get-tuple-element.155), channel_id=1, source_target_pairs={{0,16},{4,20},{8,24},{12,28},{16,0},{20,4},{24,8},{28,12},{1,17},{... | collective-permute-start | bytes 688136 | tf_op jit(solution)/shard_map/ppermute | solution.py:76
  568.0 29.2 %collective-permute-start.67 = (bf16[896,128]{1,0:T(8,128)(2,1)}, bf16[896,128]{1,0:T(8,128)(2,1)}, u32[]{:S(2)}, u32[]{:S(2)}) collective-permute-start(bf16[896,128]{1,0:T(8,128)(2,1)} %get-tuple-element.155), channel_id=1, source_target_pairs={{0,8},{4,12},{8,0},{12,4},{16,24},{20,28},{24,16},{28,20},{1,9},{5... | collective-permute-start | bytes 688136 | tf_op jit(solution)/shard_map/ppermute | solution.py:76
  592.3 51.3 %collective-permute-start.65 = (bf16[896,128]{1,0:T(8,128)(2,1)}, bf16[896,128]{1,0:T(8,128)(2,1)S(1)}, u32[]{:S(2)}, u32[]{:S(2)}) collective-permute-start(bf16[896,128]{1,0:T(8,128)(2,1)} %get-tuple-element.157), channel_id=1, source_target_pairs={{0,24},{4,28},{8,16},{12,20},{16,8},{20,12},{24,0},{28,4},{1,25},{... | collective-permute-start | bytes 688136 | tf_op jit(solution)/shard_map/ppermute | solution.py:76
  593.7 50.0 %collective-permute-start.64 = (bf16[896,128]{1,0:T(8,128)(2,1)}, bf16[896,128]{1,0:T(8,128)(2,1)S(1)}, u32[]{:S(2)}, u32[]{:S(2)}) collective-permute-start(bf16[896,128]{1,0:T(8,128)(2,1)} %get-tuple-element.157), channel_id=1, source_target_pairs={{0,16},{4,20},{8,24},{12,28},{16,0},{20,4},{24,8},{28,12},{1,17},{... | collective-permute-start | bytes 688136 | tf_op jit(solution)/shard_map/ppermute | solution.py:76
  596.6 22.7 %collective-permute-start.72 = (bf16[896,128]{1,0:T(8,128)(2,1)S(1)}, bf16[896,128]{1,0:T(8,128)(2,1)S(1)}, u32[]{:S(2)}, u32[]{:S(2)}) collective-permute-start(bf16[896,128]{1,0:T(8,128)(2,1)S(1)} %copy-done.87), channel_id=1, source_target_pairs={{0,16},{4,20},{8,24},{12,28},{16,0},{20,4},{24,8},{28,12},{1,17},{... | collective-permute-start | bytes 688136 | tf_op jit(solution)/shard_map/ppermute | solution.py:76
  597.2 23.8 %collective-permute-start.71 = (bf16[896,128]{1,0:T(8,128)(2,1)S(1)}, bf16[896,128]{1,0:T(8,128)(2,1)S(1)}, u32[]{:S(2)}, u32[]{:S(2)}) collective-permute-start(bf16[896,128]{1,0:T(8,128)(2,1)S(1)} %copy-done.87), channel_id=1, source_target_pairs={{0,8},{4,12},{8,0},{12,4},{16,24},{20,28},{24,16},{28,20},{1,9},{5... | collective-permute-start | bytes 688136 | tf_op jit(solution)/shard_map/ppermute | solution.py:76
  606.8 15.2 %collective-permute-start.77 = (bf16[896,128]{1,0:T(8,128)(2,1)S(1)}, bf16[896,128]{1,0:T(8,128)(2,1)S(1)}, u32[]{:S(2)}, u32[]{:S(2)}) collective-permute-start(bf16[896,128]{1,0:T(8,128)(2,1)S(1)} %copy-done.84), channel_id=1, source_target_pairs={{0,24},{4,28},{8,16},{12,20},{16,8},{20,12},{24,0},{28,4},{1,25},{... | collective-permute-start | bytes 688136 | tf_op jit(solution)/shard_map/ppermute | solution.py:76
  622.1 21.6 %collective-permute-start.63 = (bf16[896,128]{1,0:T(8,128)(2,1)}, bf16[896,128]{1,0:T(8,128)(2,1)S(1)}, u32[]{:S(2)}, u32[]{:S(2)}) collective-permute-start(bf16[896,128]{1,0:T(8,128)(2,1)} %get-tuple-element.157), channel_id=1, source_target_pairs={{0,8},{4,12},{8,0},{12,4},{16,24},{20,28},{24,16},{28,20},{1,9},{5... | collective-permute-start | bytes 688136 | tf_op jit(solution)/shard_map/ppermute | solution.py:76
  632.5 67.7 %collective-permute-start.78 = (bf16[896,256]{1,0:T(8,128)(2,1)}, bf16[896,256]{1,0:T(8,128)(2,1)}, u32[]{:S(2)}, u32[]{:S(2)}) collective-permute-start(bf16[896,256]{1,0:T(8,128)(2,1)} %slice.899), channel_id=1, source_target_pairs={{0,4},{4,0},{8,12},{12,8},{16,20},{20,16},{24,28},{28,24},{1,5},{5... | collective-permute-start | bytes 1376264 | tf_op jit(solution)/shard_map/ppermute | solution.py:73
  634.7 91.1 %collective-permute-start.74 = (bf16[896,256]{1,0:T(8,128)(2,1)}, bf16[896,256]{1,0:T(8,128)(2,1)}, u32[]{:S(2)}, u32[]{:S(2)}) collective-permute-start(bf16[896,256]{1,0:T(8,128)(2,1)} %slice.900), channel_id=1, source_target_pairs={{0,4},{4,0},{8,12},{12,8},{16,20},{20,16},{24,28},{28,24},{1,5},{5... | collective-permute-start | bytes 1376264 | tf_op jit(solution)/shard_map/ppermute | solution.py:73
  643.5 89.0 %collective-permute-start.70 = (bf16[896,256]{1,0:T(8,128)(2,1)}, bf16[896,256]{1,0:T(8,128)(2,1)}, u32[]{:S(2)}, u32[]{:S(2)}) collective-permute-start(bf16[896,256]{1,0:T(8,128)(2,1)} %slice.901), channel_id=1, source_target_pairs={{0,4},{4,0},{8,12},{12,8},{16,20},{20,16},{24,28},{28,24},{1,5},{5... | collective-permute-start | bytes 1376264 | tf_op jit(solution)/shard_map/ppermute | solution.py:73
  701.4 24.5 %collective-permute-start.79 = (bf16[896,256]{1,0:T(8,128)(2,1)S(1)}, bf16[896,256]{1,0:T(8,128)(2,1)S(1)}, u32[]{:S(2)}, u32[]{:S(2)}) collective-permute-start(bf16[896,256]{1,0:T(8,128)(2,1)S(1)} %fusion.22), channel_id=1, source_target_pairs={{0,1},{1,2},{2,3},{3,0},{4,5},{5,6},{6,7},{7,4},{8,9},{9,10},{10,1... | collective-permute-start | bytes 1376264 | tf_op jit(solution)/shard_map/ppermute | solution.py:79
  718.8 54.6 %all-to-all-start.6 = ((bf16[4,256,9,64]{1,3,2,0:T(8,128)(2,1)}), bf16[4,256,9,64]{1,3,2,0:T(8,128)(2,1)}, u32[]{:S(2)}, u32[]{:S(2)}) async-start(bf16[4,256,9,64]{1,3,2,0:T(8,128)(2,1)} %reshape.476), calls=%async_computation.6 | async-start | bytes 2359296 | tf_op jit(solution)/shard_map/all_to_all | solution.py:359
  728.0 29.5 %collective-permute-start.80 = (bf16[896,256]{1,0:T(8,128)(2,1)S(1)}, bf16[896,256]{1,0:T(8,128)(2,1)S(1)}, u32[]{:S(2)}, u32[]{:S(2)}) collective-permute-start(bf16[896,256]{1,0:T(8,128)(2,1)S(1)} %fusion.24), channel_id=1, source_target_pairs={{0,1},{1,2},{2,3},{3,0},{4,5},{5,6},{6,7},{7,4},{8,9},{9,10},{10,1... | collective-permute-start | bytes 1376264 | tf_op jit(solution)/shard_map/ppermute | solution.py:79
  732.4 37.1 %collective-permute-start.66 = (bf16[896,256]{1,0:T(8,128)(2,1)S(1)}, bf16[896,256]{1,0:T(8,128)(2,1)S(1)}, u32[]{:S(2)}, u32[]{:S(2)}) collective-permute-start(bf16[896,256]{1,0:T(8,128)(2,1)S(1)} %slice.902), channel_id=1, source_target_pairs={{0,4},{4,0},{8,12},{12,8},{16,20},{20,16},{24,28},{28,24},{1,5},{5... | collective-permute-start | bytes 1376264 | tf_op jit(solution)/shard_map/ppermute | solution.py:73
  758.8 13.7 %collective-permute-start.81 = (bf16[896,256]{1,0:T(8,128)(2,1)S(1)}, bf16[896,256]{1,0:T(8,128)(2,1)S(1)}, u32[]{:S(2)}, u32[]{:S(2)}) collective-permute-start(bf16[896,256]{1,0:T(8,128)(2,1)S(1)} %fusion.26), channel_id=1, source_target_pairs={{0,1},{1,2},{2,3},{3,0},{4,5},{5,6},{6,7},{7,4},{8,9},{9,10},{10,1... | collective-permute-start | bytes 1376264 | tf_op jit(solution)/shard_map/ppermute | solution.py:79
  785.9 62.2 %all-to-all-start.7 = ((bf16[4,256,9,64]{1,3,2,0:T(8,128)(2,1)}), bf16[4,256,9,64]{1,3,2,0:T(8,128)(2,1)}, u32[]{:S(2)}, u32[]{:S(2)}) async-start(bf16[4,256,9,64]{1,3,2,0:T(8,128)(2,1)} %all-to-all-done.6), calls=%async_computation.7 | async-start | bytes 2359296 | tf_op jit(solution)/shard_map/all_to_all | solution.py:360
  (163 other events, 1956.3 us)

commit v2 on v0

--- a/solution.py
+++ b/solution.py
@@ -1,7 +1,13 @@
+import functools
+
 import jax
 import jax.numpy as jnp
 from jax import lax
+from jax.experimental import pallas as pl
+from jax.experimental.pallas import tpu as pltpu
 from jax.sharding import PartitionSpec as P
+
+f32, bf16 = jnp.float32, jnp.bfloat16
 
 
 def frame_valid(lengths_row, frame_total, clip_count):
@@ -106,7 +112,7 @@
     return ((before - average) * inv_std, inv_std)
 
 
-def per_device(
+def gathered(
     features,
     lengths,
     conv1_weight,
@@ -225,9 +231,530 @@
     )
 
 
+NT = (((1,), (1,)), ((), ()))
+NN = (((1,), (0,)), ((), ()))
+TN = (((0,), (0,)), ((), ()))
+CHIPS, PLANES, MELS = 4, 4, 2
+
+
+def mxu(a, b, dims):
+    return lax.dot_general(a, b, dims, preferred_element_type=f32)
+
+
+def vmem(mib):
+    return pltpu.CompilerParams(vmem_limit_bytes=mib << 20)
+
+
+def same(*shape):
+    return pl.BlockSpec(shape, lambda *_: (0,) * len(shape))
+
+
+def rolled(value, shift):
+    shift %= value.shape[0]
+    return pltpu.roll(value, shift, 0) if shift else value
+
+
+def taps1_kernel(pos, w, out):
+    def half(tap, rx):
+        low, high = w[0, tap, :64, :], w[0, tap, 64:, :]
+        return jnp.where(pos[2] == rx, low, high)
+
+    for rx in range(2):
+        for mo in range(MELS):
+            for mi in range(MELS):
+                row = rx * 128 + mo * 64
+                out[0, row : row + 64, mi * 128 : mi * 128 + 128] = half(mi - mo + 1, rx)
+
+
+def taps1(pos, w):
+    spec = pltpu.PrefetchScalarGridSpec(
+        num_scalar_prefetch=1,
+        grid=(3, 4),
+        in_specs=[
+            pl.BlockSpec(
+                (1, 3, 128, 128),
+                lambda a, t, p: (2 * (p[1] ^ (t % 2)) + (p[0] ^ (t // 2)), a, 0, 0),
+            )
+        ],
+        out_specs=pl.BlockSpec((1, 256, 256), lambda a, t, p: (a, 0, t)),
+    )
+    return pl.pallas_call(
+        taps1_kernel, grid_spec=spec, out_shape=jax.ShapeDtypeStruct((3, 256, 1024), bf16)
+    )(pos, w)
+
+
+def taps2_kernel(pos, w, out):
+    part = w.shape[1]
+    low = lax.broadcasted_iota(jnp.int32, (part, 128), 1) < 64
+    straight, turned = [], []
+    for tap in range(3):
+        value = w[tap].astype(f32)
+        other = pltpu.roll(value, 64, 1)
+        straight.append(jnp.where(pos[2] == 0, value, other))
+        turned.append(jnp.where(pos[2] == 0, other, value))
+    for mo in range(MELS):
+        first, second = 1 - mo, 2 - mo
+        rows = slice(mo * part, (mo + 1) * part)
+        out[0, rows, :128] = jnp.where(low, straight[first], turned[second]).astype(bf16)
+        out[0, rows, 128:] = jnp.where(low, turned[first], straight[second]).astype(bf16)
+
+
+def taps2(pos, w):
+    part = w.shape[1]
+    spec = pltpu.PrefetchScalarGridSpec(
+        num_scalar_prefetch=1,
+        grid=(3, 4),
+        in_specs=[
+            pl.BlockSpec(
+                (3, part, 128),
+                lambda a, t, p: (a, 0, 2 * (p[0] ^ (t // 2)) + (p[1] ^ (t % 2))),
+            )
+        ],
+        out_specs=pl.BlockSpec((1, MELS * part, 256), lambda a, t, p: (a, 0, t)),
+    )
+    return pl.pallas_call(
+        taps2_kernel, grid_spec=spec, out_shape=jax.ShapeDtypeStruct((3, 2 * part, 1024), bf16)
+    )(pos, w)
+
+
+def conv_kernel(pieces, splits, *refs):
+    xs, w, outs = refs[:pieces], refs[pieces], refs[pieces + 1 :]
+    total = None
+    for a in (1, 0, 2):
+        z, start = None, 0
+        for x in xs:
+            width = x.shape[1]
+            term = mxu(x[...], w[a, :, start : start + width], NT)
+            z, start = term if z is None else z + term, start + width
+        z = rolled(z, 1 - a)
+        total = z if total is None else total + z
+    start = 0
+    for out in outs:
+        out[...] = total[:, start : start + out.shape[1]].astype(out.dtype)
+        start += out.shape[1]
+
+
+def conv(xs, w, kinds, tile):
+    rows, (_, width, depth) = xs[0].shape[0], w.shape
+    lanes = tile // len(kinds)
+    outs = [jax.ShapeDtypeStruct((rows, width // len(kinds)), kind) for kind in kinds]
+    flops = 2 * 3 * rows * width * depth
+    return pl.pallas_call(
+        functools.partial(conv_kernel, len(xs), len(kinds)),
+        grid=(width // tile,),
+        in_specs=[same(*x.shape) for x in xs]
+        + [pl.BlockSpec((3, tile, depth), lambda i: (0, i, 0))],
+        out_specs=[pl.BlockSpec((rows, lanes), lambda i: (0, i)) for _ in kinds],
+        out_shape=outs,
+        compiler_params=vmem(32),
+        cost_estimate=pl.CostEstimate(
+            flops=flops, bytes_accessed=2 * rows * depth + 6 * width * depth, transcendentals=0
+        ),
+    )(*xs, w)
+
+
+def spread_rows(dst, at, value, width, lane):
+    rows, lanes = value.shape
+    wide = value.astype(f32)
+    for a in range(3):
+        moved = value if a == 1 else rolled(wide, a - 1).astype(bf16)
+        dst[at : at + rows, a * width + lane : a * width + lane + lanes] = moved
+
+
+def conv_t_kernel(pieces, *refs):
+    dys, w = refs[:pieces], refs[pieces]
+    keep, send, moved = refs[pieces + 1 :]
+    width = moved.shape[1] // 3
+    step = pl.program_id(0)
+
+    @pl.when(step == 0)
+    def _():
+        lane = 0
+        for dy in dys:
+            spread_rows(moved, 0, dy[...], width, lane)
+            lane += dy.shape[1]
+
+    value = mxu(moved[...], w[...].reshape(3 * width, w.shape[2]), NN)
+
+    @pl.when(step == 0)
+    def _():
+        send[...] = value.astype(send.dtype)
+
+    @pl.when(step == 1)
+    def _():
+        keep[...] = value.astype(keep.dtype)
+
+
+def conv_t(dys, w):
+    rows, (_, width, depth) = dys[0].shape[0], w.shape
+    half = depth // 2
+    return pl.pallas_call(
+        functools.partial(conv_t_kernel, len(dys)),
+        grid=(2,),
+        in_specs=[same(*dy.shape) for dy in dys]
+        + [pl.BlockSpec((3, width, half), lambda i: (0, 0, 1 - i))],
+        out_specs=[same(rows, half), same(rows, half)],
+        out_shape=[
+            jax.ShapeDtypeStruct((rows, half), f32),
+            jax.ShapeDtypeStruct((rows, half), bf16),
+        ],
+        scratch_shapes=[pltpu.VMEM((rows, 3 * width), bf16)],
+        compiler_params=vmem(32),
+        cost_estimate=pl.CostEstimate(
+            flops=6 * rows * width * depth,
+            bytes_accessed=6 * rows * half + 6 * width * depth,
+            transcendentals=0,
+        ),
+    )(*dys, w)
+
+
+def grad2_place(pos, out, a, prod):
+    part = prod.shape[0] // 2
+    low = lax.broadcasted_iota(jnp.int32, (part, 128), 1) < 64
+
+    def pick(mo, mi):
+        block = prod[mo * part : (mo + 1) * part]
+        u, v = block[:, :128], block[:, 128:]
+        u, v = jnp.where(pos[2] == 0, u, v), jnp.where(pos[2] == 0, v, u)
+        if mi == 0:
+            return jnp.where(low, u, pltpu.roll(v, 64, 1))
+        return jnp.where(low, pltpu.roll(u, 64, 1), v)
+
+    out[3 * a] = pick(1, 0)
+    out[3 * a + 1] = pick(0, 0) + pick(1, 1)
+    out[3 * a + 2] = pick(0, 1)
+
+
+def grad1_place(pos, out, a, prod):
+    def pick(rx, mo, mi):
+        return prod[rx * 128 + mo * 64 :][:64, mi * 128 : mi * 128 + 128]
+
+    for tap in range(3):
+        both = []
+        for rx in range(2):
+            terms = [pick(rx, mo, mo + tap - 1) for mo in range(MELS) if 0 <= mo + tap - 1 < MELS]
+            both.append(functools.reduce(lambda x, y: x + y, terms))
+        low = jnp.where(pos[2] == 0, both[0], both[1])
+        high = jnp.where(pos[2] == 0, both[1], both[0])
+        out[0, 3 * a + tap, :64, :] = low.astype(bf16)
+        out[0, 3 * a + tap, 64:, :] = high.astype(bf16)
+
+
+def grad_kernel(place, groups, pieces, columns, pos, *refs):
+    dys = refs[: groups * pieces]
+    xs = refs[groups * pieces : -3]
+    out, moved, x = refs[-3:]
+    width = moved.shape[1] // 3
+    step = pl.program_id(0)
+    rows = dys[0].shape[0]
+    per_group = len(xs) // groups
+    steps_each = 4 // per_group
+
+    @pl.when(step == 0)
+    def _():
+        for r in range(groups):
+            lane = 0
+            for dy in dys[r * pieces : (r + 1) * pieces]:
+                spread_rows(moved, r * rows, dy[...], width, lane)
+                lane += dy.shape[1]
+
+    for k in range(per_group):
+
+        @pl.when(step // steps_each == k)
+        def _():
+            for r in range(groups):
+                x[r * rows : (r + 1) * rows, :] = xs[r * per_group + k][...]
+
+    for a in range(3):
+        place(pos, out, a, mxu(moved[:, a * width : (a + 1) * width], x[...], TN))
+
+
+def weight_grad_own(pos, dys, xs, place, out_shape, out_spec):
+    groups, pieces, per_group = len(dys), len(dys[0]), len(xs[0])
+    rows = dys[0][0].shape[0]
+    width = sum(dy.shape[1] for dy in dys[0])
+    steps_each = 4 // per_group
+
+    def column(k):
+        return lambda t, p: (0, jnp.clip(t - k * steps_each, 0, steps_each - 1))
+
+    spec = pltpu.PrefetchScalarGridSpec(
+        num_scalar_prefetch=1,
+        grid=(4,),
+        in_specs=[same(*dy.shape) for group in dys for dy in group]
+        + [pl.BlockSpec((rows, 256), column(k)) for _ in xs for k in range(per_group)],
+        out_specs=out_spec,
+        scratch_shapes=[
+            pltpu.VMEM((groups * rows, 3 * width), bf16),
+            pltpu.VMEM((groups * rows, 256), bf16),
+        ],
+    )
+    return pl.pallas_call(
+        functools.partial(grad_kernel, place, groups, pieces, 256),
+        grid_spec=spec,
+        out_shape=out_shape,
+        compiler_params=vmem(56),
+        cost_estimate=pl.CostEstimate(
+            flops=6 * groups * rows * width * 1024,
+            bytes_accessed=2 * groups * rows * (width + 1024),
+            transcendentals=0,
+        ),
+    )(pos, *[dy for group in dys for dy in group], *[x for group in xs for x in group])
+
+
+def stationary(
+    features,
+    lengths,
+    conv1_weight,
+    norm1_gain,
+    norm1_bias,
+    conv2_weight,
+    norm2_gain,
+    norm2_bias,
+    out_grad,
+):
+    n = 2 * CHIPS
+    me, plane = lax.axis_index("tm"), lax.axis_index("batch")
+    core, chip = me % 2, me // 2
+    py, px = chip // 2, chip % 2
+    pos = jnp.stack([core, py, px]).astype(jnp.int32)
+    own_frames, _, width1 = features.shape[1:]
+    frames = own_frames * n
+    part = conv2_weight.shape[0]
+    block = part // CHIPS
+    clip_count = lengths.shape[1] // 3
+    same_core = [[c + 2 * p for p in range(CHIPS)] for c in range(2)]
+    groups = range(PLANES)
+    X, Y = 2, 4
+
+    def swap(x, bits):
+        return lax.ppermute(x, "tm", [(i, i ^ bits) for i in range(n)])
+
+    def along(x, shift):
+        return lax.ppermute(x, "batch", [(z, (z + shift) % PLANES) for z in groups])
+
+    def route(x, pairs):
+        flat = [(a * PLANES + b, c * PLANES + d) for (a, b), (c, d) in pairs]
+        return lax.ppermute(x, ("tm", "batch"), flat)
+
+    def plane_sum(x):
+        got = [
+            lax.ppermute(x, "batch", [(z, z ^ s) for z in groups]) for s in range(1, PLANES)
+        ]
+        return (x + got[0]) + (got[1] + got[2])
+
+    def gather_chips(x, x_first):
+        lanes = x.shape[1]
+        if x_first:
+            pair = jnp.concatenate([x, swap(x, X)], axis=1)
+            return jnp.concatenate([pair, swap(pair, Y)], axis=1)
+        other = swap(x, Y)
+        far = swap(jnp.concatenate([x, other], axis=1), X)
+        return jnp.concatenate([x, far[:, :lanes], other, far[:, lanes:]], axis=1)
+
+    def scatter_chips(x, x_first):
+        lanes = x.shape[1] // 4
+        parts = [x[:, k * lanes : (k + 1) * lanes] for k in range(4)]
+        if x_first:
+            keep, send = [parts[0], parts[2]], [parts[1], parts[3]]
+        else:
+            keep, send = [parts[0], parts[1]], [parts[2], parts[3]]
+        got = swap(jnp.concatenate(send, axis=1).astype(bf16), X if x_first else Y)
+        low = keep[0] + got[:, :lanes].astype(f32)
+        high = (keep[1] + got[:, lanes:].astype(f32)).astype(bf16)
+        return low + swap(high, Y if x_first else X).astype(f32)
+
+    w1 = conv1_weight.transpose(1, 0, 2)
+    w1 = w1.reshape(9, 2, part // 2, 2, conv1_weight.shape[2] // 2).transpose(1, 3, 0, 2, 4)
+    w1 = w1.reshape(CHIPS, 9, part // 2, conv1_weight.shape[2] // 2)
+    w1 = lax.all_to_all(w1, "tm", 0, 0, tiled=True, axis_index_groups=same_core)
+    w1 = lax.all_to_all(w1, "batch", 0, 0, tiled=True)
+    weights1 = taps1(pos, w1)
+    weights2 = taps2(pos, conv2_weight.transpose(1, 0, 2))
+
+    group_lengths = [lengths] + [along(lengths, s) for s in range(1, PLANES)]
+    count = sum(jnp.sum(x.astype(f32)) for x in group_lengths) * MELS
+    mask = [frame_valid(x[0], frames, clip_count).astype(f32)[:, None] for x in group_lengths]
+    here_valid = lax.dynamic_slice_in_dim(
+        mask[0].astype(bf16), me * own_frames, own_frames, 0
+    )
+
+    own_norm = jnp.stack([norm1_gain, norm1_bias]).reshape(2, CHIPS, block)
+
+    def norm_block(k):
+        return lax.dynamic_index_in_dim(own_norm, k, 1, keepdims=False)
+
+    both1 = jnp.where(chip == plane, norm_block(chip), 0.0)
+    for s in range(1, CHIPS):
+        both1 += route(
+            norm_block(plane ^ s),
+            [((2 * j + c, j), (2 * (j ^ s) + c, j)) for j in groups for c in range(2)],
+        )
+    gain1, bias1 = both1[0], both1[1]
+
+    lanes1 = width1 // n
+    masked = features[0] * here_valid[:, :, None]
+    masked = masked.reshape(own_frames, MELS, 2, 2, 2, lanes1).transpose(2, 4, 3, 0, 1, 5)
+    masked = masked.reshape(frames, MELS * lanes1)
+    mine = [lax.all_to_all(masked, "tm", 0, 0, tiled=True)]
+    for _ in range(PLANES - 1):
+        mine.append(along(mine[-1], 1))
+    inputs = []
+    for x in mine:
+        near = swap(x, Y)
+        inputs.append([x, near, swap(x, 1), swap(near, 1)])
+
+    pre1 = []
+    for x in inputs:
+        keep, send = conv(x, weights1, (f32, bf16), 256)
+        pre1.append(keep + swap(send, X).astype(f32))
+
+    def per_channel(x):
+        return jnp.sum(x.reshape(MELS, -1), axis=0)
+
+    def per_lane(x):
+        return jnp.tile(x, MELS)[None]
+
+    def rows_sum(x):
+        return jnp.sum(x, axis=0)
+
+    def norm_stats(total, square_total):
+        average = total / count
+        variance = square_total / count - average * average
+        return average, lax.rsqrt(variance + 1e-05)
+
+    sums = sum(rows_sum(x * v) for x, v in zip(pre1, mask))
+    squares = sum(rows_sum(x * x * v) for x, v in zip(pre1, mask))
+    mean1, rstd1 = norm_stats(per_channel(sums), per_channel(squares))
+    xhat1 = [(x - per_lane(mean1)) * per_lane(rstd1) for x in pre1]
+    z1 = [per_lane(gain1) * x + per_lane(bias1) for x in xhat1]
+    act1 = [(v * jax.nn.silu(z)).astype(bf16) for v, z in zip(mask, z1)]
+
+    hidden = [None] * PLANES
+    total = None
+    for r in (1, 2, 3, 0):
+        half = gather_chips(act1[r], r % 2 == 1)
+        hidden[r] = [half, swap(half, 1)]
+        (term,) = conv(hidden[r], weights2, (bf16 if r == 1 else f32,), 512)
+        total = term if r == 1 else term + along(total.astype(bf16), 1).astype(f32)
+    pre2, v0 = total, mask[0]
+
+    sums2 = jnp.stack([rows_sum(pre2 * v0), rows_sum(pre2 * pre2 * v0)])
+    sums2 = plane_sum(sums2.reshape(2, MELS, part).sum(axis=1))
+    mean2, rstd2 = norm_stats(sums2[0], sums2[1])
+    xhat2 = (pre2 - per_lane(mean2)) * per_lane(rstd2)
+    z2 = per_lane(norm2_gain) * xhat2 + per_lane(norm2_bias)
+
+    grad_in = out_grad[0].reshape(own_frames, MELS, n, part).transpose(2, 0, 1, 3)
+    grad_in = lax.all_to_all(grad_in, "tm", 0, 0, tiled=True).reshape(frames, MELS * part)
+    dz2 = grad_in.astype(f32) * v0 * silu_slope(z2)
+    grads2 = jnp.stack([rows_sum(dz2), rows_sum(dz2 * xhat2)])
+    grads2 = plane_sum(grads2.reshape(2, MELS, part).sum(axis=1))
+    bias2_grad, gain2_grad = grads2[0], grads2[1]
+    dpre2 = (
+        v0
+        * per_lane(norm2_gain * rstd2)
+        * (dz2 - (per_lane(bias2_grad) + xhat2 * per_lane(gain2_grad)) / count)
+    ).astype(bf16)
+
+    dpre2, z2_later = lax.optimization_barrier((dpre2, z2))
+    out_local = (v0 * jax.nn.silu(z2_later)).astype(bf16)
+    block_out = lax.all_to_all(
+        out_local.reshape(n, own_frames, MELS, part), "tm", 0, 0, tiled=True
+    )
+    block_out = block_out.transpose(1, 2, 0, 3).reshape(1, own_frames, MELS, n * part)
+
+    grad2 = [dpre2]
+    for _ in range(PLANES - 1):
+        grad2.append(along(grad2[-1], 1))
+    dact1 = []
+    for r in groups:
+        keep, send = conv_t([grad2[r]], weights2)
+        dact1.append(scatter_chips(keep + swap(send, 1).astype(f32), r % 2 == 1))
+
+    dz1 = [d * v * silu_slope(z) for d, v, z in zip(dact1, mask, z1)]
+    bias1_sum = per_channel(sum(rows_sum(d) for d in dz1))
+    gain1_sum = per_channel(sum(rows_sum(d * x) for d, x in zip(dz1, xhat1)))
+    dpre1 = [
+        (
+            v
+            * per_lane(gain1 * rstd1)
+            * (d - (per_lane(bias1_sum) + x * per_lane(gain1_sum)) / count)
+        ).astype(bf16)
+        for v, d, x in zip(mask, dz1, xhat1)
+    ]
+    pairs1, total = [None] * PLANES, None
+    for r in (1, 2, 3, 0):
+        pairs1[r] = [dpre1[r], swap(dpre1[r], X)]
+        keep, send = conv_t(pairs1[r], weights1)
+        half = keep + swap(send, 1).astype(f32)
+        lanes = half.shape[1] // 2
+        term = half[:, :lanes] + swap(half[:, lanes:].astype(bf16), Y).astype(f32)
+        total = term if r == 1 else term + along(total.astype(bf16), 1).astype(f32)
+    dx = total.astype(bf16).reshape(n, own_frames, MELS * lanes1)
+    dx = lax.all_to_all(dx, "tm", 0, 0, tiled=True)
+    dx = dx.reshape(2, 2, 2, own_frames, MELS, lanes1).transpose(3, 4, 0, 2, 1, 5)
+    input_grad = dx.reshape(1, own_frames, MELS, width1) * here_valid[None, :, :, None]
+
+    grad1 = weight_grad_own(
+        pos,
+        pairs1,
+        inputs,
+        grad1_place,
+        jax.ShapeDtypeStruct((PLANES, 9, part // 2, 128), bf16),
+        pl.BlockSpec(
+            (1, 9, part // 2, 128),
+            lambda t, p: (2 * (p[1] ^ (t % 2)) + (p[0] ^ (t // 2)), 0, 0, 0),
+        ),
+    )
+    grad1 = lax.all_to_all(grad1, "batch", 0, 0, tiled=True)
+    grad1_sent = lax.all_to_all(grad1, "tm", 0, 0, tiled=True, axis_index_groups=same_core)
+    conv1_grad = grad1_sent.reshape(2, 2, 9, part // 2, -1).transpose(2, 0, 3, 1, 4)
+    conv1_grad = conv1_grad.reshape(9, part, -1).astype(f32).transpose(1, 0, 2)
+
+    conv2_grad = weight_grad_own(
+        pos,
+        [[g] for g in grad2],
+        hidden,
+        grad2_place,
+        jax.ShapeDtypeStruct((9, part, conv2_weight.shape[2]), f32),
+        pl.BlockSpec(
+            (9, part, 128),
+            lambda t, p: (0, 0, 2 * (p[0] ^ (t // 2)) + (p[1] ^ (t % 2))),
+        ),
+    ).transpose(1, 0, 2)
+
+    mine1 = jnp.stack([gain1_sum, bias1_sum])
+    parts1 = [mine1] + [
+        route(mine1, [((2 * (j ^ s) + c, j), (2 * j + c, j)) for j in groups for c in range(2)])
+        for s in range(1, CHIPS)
+    ]
+    whole1 = jnp.stack(parts1, axis=1).reshape(2, 2, 2, block)
+    whole1 = jnp.where(plane // 2 == 1, jnp.flip(whole1, 1), whole1)
+    whole1 = jnp.where(plane % 2 == 1, jnp.flip(whole1, 2), whole1).reshape(2, part)
+    grads1 = jnp.where(chip == plane, whole1, 0.0)
+    for s in range(1, PLANES):
+        grads1 += route(
+            whole1,
+            [((2 * j + c, j), (2 * j + c, (j + s) % PLANES)) for j in groups for c in range(2)],
+        )
+    gain1_grad, bias1_grad = grads1[0], grads1[1]
+
+    return (
+        block_out,
+        input_grad,
+        conv1_grad,
+        gain1_grad,
+        bias1_grad,
+        conv2_grad,
+        gain2_grad,
+        bias2_grad,
+    )
+
+
 def solution(mesh):
     return jax.shard_map(
-        per_device,
+        stationary if dict(mesh.shape) == {"tm": 8, "batch": 4} else gathered,
         mesh=mesh,
         in_specs=(
             P("batch", "tm", None, None),

time: 933 us -> 532 us (0.57)
  waiting for transfers between devices: 576 us -> 190 us
  matrix products: 128 us -> 0 us
  starting transfers between devices: 7.78 us -> 124 us
  Pallas kernels: 0 us -> 110 us
  local copies, waits for them, and re-layouts: 104 us -> 51.8 us
  blocking collectives: 41.9 us -> 0 us
  between operations: 16.4 us -> 5.11 us
    all_gather x4 -> x0, waiting for transfers between devices: 266 us -> none  [the longest x1 109 us: per_device(): lax.all_gather(conv2_weight, 'batch', axis=2, tiled=True)]
    reduce_scatter x3 -> x0, waiting for transfers between devices: 257 us -> none  [the longest x1 162 us: per_device(): lax.psum_scatter(conv2_local.astype(jnp.bfloat16), 'batch', scatter_dimen...]
    ppermute x0 -> x82, waiting for transfers between devices: none -> 177 us  [the longest x52 92.6 us: swap(): return lax.ppermute(x, 'tm', [(i, i ^ bits) for i in range(n)])]
    dot_general x18 -> x0, matrix products: 128 us -> none  [the longest x6 66.9 us: transposed(): jnp.dot(grad_padded[2 - tap_row:2 - tap_row + row_count], tap_weights(wei...]
    pallas_call x0 -> x20, Pallas kernels: none -> 110 us  [the longest x8 34.9 us: conv_t(): pl.pallas_call(functools.partial(conv_t_kernel, len(dys)), grid=(2,), in_...]
    ppermute x0 -> x82, starting transfers between devices: none -> 88.6 us  [the longest x52 38 us: swap(): return lax.ppermute(x, 'tm', [(i, i ^ bits) for i in range(n)])]
    psum x4 -> x0, blocking collectives: 41.9 us -> none  [the longest x1 12.1 us: per_device(): lax.psum((jnp.sum(delta_one * scaled_one, axis=(0, 1)), jnp.sum(delta_one...]
    all_to_all x2 -> x8, starting transfers between devices: 7.25 us -> 35.5 us  [the longest x1 6.28 us: stationary(): grad1 = lax.all_to_all(grad1, 'batch', 0, 0, tiled=True)]
  transfers between devices with their start and end apart: 10 -> 90, of which waited for: 10 -> 36; matrix products, arithmetic and copies ran while one was open for 16% -> 12% of each run, Pallas kernels for 0% -> 21%
where the time goes in v2:
time: 532 us; the launch traced here: 526 us
  waiting for transfers between devices  190 us (36%)
  starting transfers between devices  124 us (23%)
  Pallas kernels  110 us (21%)
  local copies, waits for them, and re-layouts  51.8 us (10%)
  other arithmetic  44.5 us (8%)
    ppermute x52, waiting for transfers between devices, swap(): return lax.ppermute(x, 'tm', [(i, i ^ bits) for i in range(n)])  92.6 us
    ppermute x15, waiting for transfers between devices, along(): return lax.ppermute(x, 'batch', [(z, (z + shift) % PLANES) for z in groups])  82 us
    ppermute x52, starting transfers between devices, swap(): return lax.ppermute(x, 'tm', [(i, i ^ bits) for i in range(n)])  38 us
    pallas_call x8, Pallas kernels, conv_t(): pl.pallas_call(functools.partial(conv_t_kernel, len(dys)), grid=(2,), in_...  34.9 us
    pallas_call x2, Pallas kernels, weight_grad_own(): pl.pallas_call(functools.partial(grad_kernel, place, groups, pieces, 256)...  34.7 us
    pallas_call x8, Pallas kernels, conv(): pl.pallas_call(functools.partial(conv_kernel, len(xs), len(kinds)), grid=...  23.6 us
    unnamed x145, local copies, waits for them, and re-layouts  23.3 us
    ppermute x9, starting transfers between devices, route(): return lax.ppermute(x, ('tm', 'batch'), flat)  21 us
  transfers between devices with their start and end apart: 90, of which 36 were waited for; matrix products, arithmetic and copies ran while one was open for 12% of the time, Pallas kernels for 21%

profile of v2, /device:TPU:0, one launch (start us, length us, event | category | flops | bytes accessed | tf_op | source)
XLA Modules:
  0.0 526.0 jit_solution(17393353531333158135)
XLA Ops:
  0.6 4.1 collective-permute-start.18
  13.0 3.7 all-to-all-start
  18.4 7.4 %all-to-all-done = bf16[8,112,256]{2,1,0:T(8,128)(2,1)S(1)} async-done(((bf16[8,112,256]{2,1,0:T(8,128)(2,1)}), bf16[8,112,256]{2,1,0:T(8,128)(2,1)S(1)}, u32[]{:S(2)}, u32[]{:S(2)}) %all-to-all-start) | async-done | bytes 458784 | tf_op jit(solution)/shard_map/all_to_all | solution.py:599
  25.8 4.3 all-to-all-start.1
  30.2 12.3 %collective-permute-done.7.refs_0_.refs_12_ = bf16[896,256]{1,0:T(8,128)(2,1)S(1)} collective-permute-done((bf16[896,256]{1,0:T(8,128)(2,1)S(1)}, bf16[896,256]{1,0:T(8,128)(2,1)S(1)}, u32[]{:S(2)}, u32[]{:S(2)}) %collective-permute-start.7) | collective-permute-done | bytes 458784 | tf_op jit(solution)/shard_map/ppermute | solution.py:534
  44.5 5.1 all-to-all-start.2
  49.6 2.8 collective-permute-start
  55.9 3.2 collective-permute-start.14
  59.7 5.2 collective-permute-start.2
  68.5 14.4 %collective-permute-done.19.refs_0_.refs_20_ = bf16[896,256]{1,0:T(8,128)(2,1)S(1)} collective-permute-done((bf16[896,256]{1,0:T(8,128)(2,1)S(1)}, bf16[896,256]{1,0:T(8,128)(2,1)S(1)}, u32[]{:S(2)}, u32[]{:S(2)}) %collective-permute-start.19) | collective-permute-done | bytes 458784 | tf_op jit(solution)/shard_map/ppermute | solution.py:534
  86.9 7.3 %collective-permute-done.20.refs_1_.refs_21_ = bf16[896,256]{1,0:T(8,128)(2,1)} collective-permute-done((bf16[896,256]{1,0:T(8,128)(2,1)S(1)}, bf16[896,256]{1,0:T(8,128)(2,1)}, u32[]{:S(2)}, u32[]{:S(2)}) %collective-permute-start.20) | collective-permute-done | bytes 458784 | tf_op jit(solution)/shard_map/ppermute | solution.py:531
  94.8 8.1 %shard_map.152.refs_4_.refs_2_ = bf16[3,256,1024]{2,1,0:T(8,128)(2,1)} custom-call(s32[3]{0:T(128)} %pad_add_fusion.pos, bf16[4,9,128,128]{3,2,1,0:T(8,128)(2,1)} %all-to-all-done.2.w), custom_call_target="tpu_custom_call" | custom-call | tf_op jit(solution)/shard_map/pallas_call | solution.py:281
  104.4 2.8 shard_map.155
  109.1 2.8 shard_map.154
  112.2 2.8 shard_map.153
  116.9 2.9 shard_map.156
  120.7 4.7 collective-permute-done.6
  125.6 4.0 collective-permute-done.23
  133.1 5.2 collective-permute-done.34
  140.5 11.3 %collective-permute-done.35 = bf16[896,256]{1,0:T(8,128)(2,1)S(1)} collective-permute-done((bf16[896,256]{1,0:T(8,128)(2,1)S(1)}, bf16[896,256]{1,0:T(8,128)(2,1)S(1)}, u32[]{:S(2)}, u32[]{:S(2)}) %collective-permute-start.35) | collective-permute-done | bytes 458784 | tf_op jit(solution)/shard_map/ppermute | solution.py:531
  156.3 9.1 %shard_map.157.refs_2_.refs_1_ = bf16[3,512,1024]{2,1,0:T(8,128)(2,1)} custom-call(s32[3]{0:T(128)} %pad_add_fusion.pos, bf16[9,256,512]{2,1,0:T(8,128)(2,1)} %bitcast.101), custom_call_target="tpu_custom_call" | custom-call | tf_op jit(solution)/shard_map/pallas_call | solution.py:315
  168.6 3.1 shard_map.161
  176.3 15.3 %collective-permute-done.25 = bf16[896,128]{1,0:T(8,128)(2,1)S(1)} collective-permute-done((bf16[896,128]{1,0:T(8,128)(2,1)S(1)}, bf16[896,128]{1,0:T(8,128)(2,1)S(1)}, u32[]{:S(2)}, u32[]{:S(2)}) %collective-permute-start.25) | collective-permute-done | bytes 229408 | tf_op jit(solution)/shard_map/ppermute | solution.py:531
  193.1 3.1 shard_map.160
  199.1 4.1 collective-permute-done.26
  203.5 3.1 shard_map.159
  206.6 14.6 %collective-permute-done.38 = bf16[896,512]{1,0:T(8,128)(2,1)S(1)} collective-permute-done((bf16[896,512]{1,0:T(8,128)(2,1)S(1)}, bf16[896,512]{1,0:T(8,128)(2,1)S(1)}, u32[]{:S(2)}, u32[]{:S(2)}) %collective-permute-start.38) | collective-permute-done | bytes 917536 | tf_op jit(solution)/shard_map/ppermute | solution.py:534
  227.4 4.6 all-to-all-start.3
  236.0 3.1 shard_map.158
  239.1 7.2 %collective-permute-done.39 = bf16[896,512]{1,0:T(8,128)(2,1)} collective-permute-done((bf16[896,512]{1,0:T(8,128)(2,1)}, bf16[896,512]{1,0:T(8,128)(2,1)}, u32[]{:S(2)}, u32[]{:S(2)}) %collective-permute-start.39) | collective-permute-done | bytes 917536 | tf_op jit(solution)/shard_map/ppermute | solution.py:534
  248.5 3.9 collective-permute-start.40
  254.1 4.2 fusion.71
  269.0 4.1 shard_map.162
  274.3 14.1 %collective-permute-done.49.refs_0_.refs_1_ = bf16[896,512]{1,0:T(8,128)(2,1)} collective-permute-done((bf16[896,512]{1,0:T(8,128)(2,1)S(1)}, bf16[896,512]{1,0:T(8,128)(2,1)}, u32[]{:S(2)}, u32[]{:S(2)}) %collective-permute-start.49) | collective-permute-done | bytes 917536 | tf_op jit(solution)/shard_map/ppermute | solution.py:534
  293.5 15.4 %collective-permute-done.53.refs_0_.refs_2_ = bf16[896,512]{1,0:T(8,128)(2,1)} collective-permute-done((bf16[896,512]{1,0:T(8,128)(2,1)}, bf16[896,512]{1,0:T(8,128)(2,1)}, u32[]{:S(2)}, u32[]{:S(2)}) %collective-permute-start.53) | collective-permute-done | bytes 917536 | tf_op jit(solution)/shard_map/ppermute | solution.py:534
  309.6 6.1 %shard_map.163 = (f32[896,512]{1,0:T(8,128)S(1)}, bf16[896,512]{1,0:T(8,128)(2,1)}) custom-call(bf16[896,512]{1,0:T(8,128)(2,1)} %collective-permute-done.49.refs_0_.refs_1_, bf16[3,512,1024]{2,1,0:T(8,128)(2,1)S(1)} %copy-done.5), custom_call_target="tpu_custom_call" | custom-call | flops 2818572288 | bytes 5898240 | tf_op jit(solution)/shard_map/pallas_call | solution.py:391
  318.3 3.1 reshape.393
  321.5 4.4 all-to-all-start.4
  329.1 5.1 shard_map.164
  334.3 5.2 shard_map.165
  346.2 8.9 %collective-permute-done.51 = bf16[896,256]{1,0:T(8,128)(2,1)S(1)} collective-permute-done((bf16[896,256]{1,0:T(8,128)(2,1)S(1)}, bf16[896,256]{1,0:T(8,128)(2,1)S(1)}, u32[]{:S(2)}, u32[]{:S(2)}) %collective-permute-start.51) | collective-permute-done | bytes 458784 | tf_op jit(solution)/shard_map/ppermute | solution.py:531
  357.4 7.5 %collective-permute-done.59 = bf16[896,256]{1,0:T(8,128)(2,1)S(1)} collective-permute-done((bf16[896,256]{1,0:T(8,128)(2,1)S(1)}, bf16[896,256]{1,0:T(8,128)(2,1)S(1)}, u32[]{:S(2)}, u32[]{:S(2)}) %collective-permute-start.59) | collective-permute-done | bytes 458784 | tf_op jit(solution)/shard_map/ppermute | solution.py:531
  366.6 2.7 fusion.72
  373.1 3.0 multiply_convert_fusion.2
  378.8 4.9 collective-permute-done.70.refs_1_.refs_3_
  386.3 3.3 shard_map.169
  393.8 3.1 copy.34
  396.9 3.1 reshape.394
  402.2 4.3 shard_map.168
  408.6 4.5 collective-permute-done.61.refs_1_
  413.9 13.5 %shard_map.170 = bf16[4,9,128,128]{3,2,1,0:T(8,128)(2,1)} custom-call(s32[3]{0:T(128)} %pad_add_fusion.pos, bf16[896,128]{1,0:T(8,128)(2,1)} %get-tuple-element.117.refs_0_, bf16[896,128]{1,0:T(8,128)(2,1)} %copy-done.37, bf16[896,128]{1,0:T(8,128)(2,1)} %copy-done.22, bf16[896,128]{1,0:T(8,128)(2,1)} %copy-done.35, ...), custom_call_target="tpu_custom_call" | custom-call | flops 5637144576 | bytes 9175040 | tf_op jit(solution)/shard_map/pallas_call | solution.py:492
  427.4 6.3 %all-to-all-start.6 = ((bf16[4,9,128,128]{3,2,1,0:T(8,128)(2,1)}), bf16[4,9,128,128]{3,2,1,0:T(8,128)(2,1)}, u32[]{:S(2)}, u32[]{:S(2)}) async-start(bf16[4,9,128,128]{3,2,1,0:T(8,128)(2,1)} %shard_map.170), calls=%async_computation.6 | async-start | bytes 2359296 | tf_op jit(solution)/shard_map/all_to_all | solution.py:710
  435.5 3.3 shard_map.167
  441.4 3.4 shard_map.166
  450.3 4.4 collective-permute-done.72
  461.2 3.4 collective-permute-done.69
  464.6 2.8 collective-permute-done.73
  469.6 2.8 collective-permute-start.74
  472.5 4.8 collective-permute-start.81
  481.7 3.7 all-to-all-start.7
  488.8 21.2 %shard_map.171 = f32[9,256,512]{2,1,0:T(8,128)} custom-call(s32[3]{0:T(128)} %pad_add_fusion.pos, bf16[896,512]{1,0:T(8,128)(2,1)} %copy-done.18, bf16[896,512]{1,0:T(8,128)(2,1)} %collective-permute-done.49.refs_0_.refs_1_, bf16[896,512]{1,0:T(8,128)(2,1)} %collective-permute-done.53.refs_0_.refs_2_, ...), custom_call_target="tpu_custom_call" | custom-call | flops 11274289152 | bytes 11010048 | tf_op jit(solution)/shard_map/pallas_call | solution.py:492
  511.0 3.5 all-to-all-start.5
  517.2 2.9 reshape.403
  520.2 3.3 all-to-all-done.5
  (418 shorter events, 148.9 us)
Async XLA Ops:
  13.0 12.8 %all-to-all-start = ((bf16[8,112,256]{2,1,0:T(8,128)(2,1)}), bf16[8,112,256]{2,1,0:T(8,128)(2,1)S(1)}, u32[]{:S(2)}, u32[]{:S(2)}) async-start(bf16[8,112,256]{2,1,0:T(8,128)(2,1)} %all_to_all.28), calls=%async_computation | async-start | bytes 917504 | tf_op jit(solution)/shard_map/all_to_all | solution.py:599
  25.8 18.7 %all-to-all-start.1 = ((bf16[4,9,128,128]{3,2,1,0:T(8,128)(2,1)}), bf16[4,9,128,128]{3,2,1,0:T(8,128)(2,1)}, u32[]{:S(2)}, u32[]{:S(2)}) async-start(bf16[4,9,128,128]{3,2,1,0:T(8,128)(2,1)} %bitcast.14), calls=%async_computation.1 | async-start | bytes 2359296 | tf_op jit(solution)/shard_map/all_to_all | solution.py:570
  30.1 12.4 %collective-permute-start.7 = (bf16[896,256]{1,0:T(8,128)(2,1)S(1)}, bf16[896,256]{1,0:T(8,128)(2,1)S(1)}, u32[]{:S(2)}, u32[]{:S(2)}) collective-permute-start(bf16[896,256]{1,0:T(8,128)(2,1)S(1)} %bitcast.94), channel_id=1, source_target_pairs={{0,1},{1,2},{2,3},{3,0},{4,5},{5,6},{6,7},{7,4},{8,9},{9,10},{10,1... | collective-permute-start | bytes 1376264 | tf_op jit(solution)/shard_map/ppermute | solution.py:534
  42.5 13.4 %collective-permute-start.13 = (bf16[896,256]{1,0:T(8,128)(2,1)S(1)}, bf16[896,256]{1,0:T(8,128)(2,1)S(1)}, u32[]{:S(2)}, u32[]{:S(2)}) collective-permute-start(bf16[896,256]{1,0:T(8,128)(2,1)S(1)} %collective-permute-done.7.refs_0_.refs_12_), channel_id=1, source_target_pairs={{0,1},{1,2},{2,3},{3,0},{4,5},{5,6},{6,7},{7,4},{8,9},{9,10},{10,1... | collective-permute-start | bytes 1376264 | tf_op jit(solution)/shard_map/ppermute | solution.py:534
  44.5 50.3 %all-to-all-start.2 = ((bf16[4,9,128,128]{3,2,1,0:T(8,128)(2,1)}), bf16[4,9,128,128]{3,2,1,0:T(8,128)(2,1)}, u32[]{:S(2)}, u32[]{:S(2)}) async-start(bf16[4,9,128,128]{3,2,1,0:T(8,128)(2,1)} %all-to-all-done.1), calls=%async_computation.2 | async-start | bytes 2359296 | tf_op jit(solution)/shard_map/all_to_all | solution.py:571
  52.5 12.4 %collective-permute-start.1 = (f32[2,64]{1,0:T(2,128)S(1)}, f32[2,64]{1,0:T(2,128)S(1)}, u32[]{:S(2)}, u32[]{:S(2)}) collective-permute-start(f32[2,64]{1,0:T(2,128)S(1)} %get-tuple-element.112), channel_id=1, source_target_pairs={{0,16},{4,20},{9,25},{13,29},{18,2},{22,6},{27,11},{31,15}} | collective-permute-start | bytes 1544 | tf_op jit(solution)/shard_map/ppermute | solution.py:538
  55.0 13.5 %collective-permute-start.3 = (bf16[896,256]{1,0:T(8,128)(2,1)S(1)}, bf16[896,256]{1,0:T(8,128)(2,1)S(1)}, u32[]{:S(2)}, u32[]{:S(2)}) collective-permute-start(bf16[896,256]{1,0:T(8,128)(2,1)S(1)} %bitcast.95), channel_id=1, source_target_pairs={{0,16},{4,20},{8,24},{12,28},{16,0},{20,4},{24,8},{28,12},{1,17},{... | collective-permute-start | bytes 1376264 | tf_op jit(solution)/shard_map/ppermute | solution.py:531
  55.9 26.9 %collective-permute-start.19 = (bf16[896,256]{1,0:T(8,128)(2,1)S(1)}, bf16[896,256]{1,0:T(8,128)(2,1)S(1)}, u32[]{:S(2)}, u32[]{:S(2)}) collective-permute-start(bf16[896,256]{1,0:T(8,128)(2,1)S(1)} %collective-permute-done.13.refs_0_.refs_16_), channel_id=1, source_target_pairs={{0,1},{1,2},{2,3},{3,0},{4,5},{5,6},{6,7},{7,4},{8,9},{9,10},{10,1... | collective-permute-start | bytes 1376264 | tf_op jit(solution)/shard_map/ppermute | solution.py:534
  55.9 28.2 %collective-permute-start.14 = (bf16[896,256]{1,0:T(8,128)(2,1)S(1)}, bf16[896,256]{1,0:T(8,128)(2,1)S(1)}, u32[]{:S(2)}, u32[]{:S(2)}) collective-permute-start(bf16[896,256]{1,0:T(8,128)(2,1)S(1)} %collective-permute-done.13.refs_0_.refs_16_), channel_id=1, source_target_pairs={{0,16},{4,20},{8,24},{12,28},{16,0},{20,4},{24,8},{28,12},{1,17},{... | collective-permute-start | bytes 1376264 | tf_op jit(solution)/shard_map/ppermute | solution.py:531
  64.9 20.1 %collective-permute-start.8 = (bf16[896,256]{1,0:T(8,128)(2,1)S(1)}, bf16[896,256]{1,0:T(8,128)(2,1)S(1)}, u32[]{:S(2)}, u32[]{:S(2)}) collective-permute-start(bf16[896,256]{1,0:T(8,128)(2,1)S(1)} %collective-permute-done.7.refs_0_.refs_12_), channel_id=1, source_target_pairs={{0,16},{4,20},{8,24},{12,28},{16,0},{20,4},{24,8},{28,12},{1,17},{... | collective-permute-start | bytes 1376264 | tf_op jit(solution)/shard_map/ppermute | solution.py:531
  67.5 18.8 %collective-permute-start.9 = (bf16[896,256]{1,0:T(8,128)(2,1)S(1)}, bf16[896,256]{1,0:T(8,128)(2,1)}, u32[]{:S(2)}, u32[]{:S(2)}) collective-permute-start(bf16[896,256]{1,0:T(8,128)(2,1)S(1)} %collective-permute-done.7.refs_0_.refs_12_), channel_id=1, source_target_pairs={{0,4},{4,0},{8,12},{12,8},{16,20},{20,16},{24,28},{28,24},{1,5},{5... | collective-permute-start | bytes 1376264 | tf_op jit(solution)/shard_map/ppermute | solution.py:531
  68.5 18.4 %collective-permute-start.15 = (bf16[896,256]{1,0:T(8,128)(2,1)S(1)}, bf16[896,256]{1,0:T(8,128)(2,1)}, u32[]{:S(2)}, u32[]{:S(2)}) collective-permute-start(bf16[896,256]{1,0:T(8,128)(2,1)S(1)} %collective-permute-done.13.refs_0_.refs_16_), channel_id=1, source_target_pairs={{0,4},{4,0},{8,12},{12,8},{16,20},{20,16},{24,28},{28,24},{1,5},{5... | collective-permute-start | bytes 1376264 | tf_op jit(solution)/shard_map/ppermute | solution.py:531
  82.8 11.4 %collective-permute-start.20 = (bf16[896,256]{1,0:T(8,128)(2,1)S(1)}, bf16[896,256]{1,0:T(8,128)(2,1)}, u32[]{:S(2)}, u32[]{:S(2)}) collective-permute-start(bf16[896,256]{1,0:T(8,128)(2,1)S(1)} %collective-permute-done.19.refs_0_.refs_20_), channel_id=1, source_target_pairs={{0,16},{4,20},{8,24},{12,28},{16,0},{20,4},{24,8},{28,12},{1,17},{... | collective-permute-start | bytes 1376264 | tf_op jit(solution)/shard_map/ppermute | solution.py:531
  85.0 22.2 %collective-permute-start.10 = (bf16[896,256]{1,0:T(8,128)(2,1)S(1)}, bf16[896,256]{1,0:T(8,128)(2,1)}, u32[]{:S(2)}, u32[]{:S(2)}) collective-permute-start(bf16[896,256]{1,0:T(8,128)(2,1)S(1)} %collective-permute-done.8.refs_1_.refs_13_), channel_id=1, source_target_pairs={{0,4},{4,0},{8,12},{12,8},{16,20},{20,16},{24,28},{28,24},{1,5},{5... | collective-permute-start | bytes 1376264 | tf_op jit(solution)/shard_map/ppermute | solution.py:531
  86.3 25.6 %collective-permute-start.4 = (bf16[896,256]{1,0:T(8,128)(2,1)S(1)}, bf16[896,256]{1,0:T(8,128)(2,1)}, u32[]{:S(2)}, u32[]{:S(2)}) collective-permute-start(bf16[896,256]{1,0:T(8,128)(2,1)S(1)} %bitcast.96), channel_id=1, source_target_pairs={{0,4},{4,0},{8,12},{12,8},{16,20},{20,16},{24,28},{28,24},{1,5},{5... | collective-permute-start | bytes 1376264 | tf_op jit(solution)/shard_map/ppermute | solution.py:531
  86.8 25.3 %collective-permute-start.5 = (bf16[896,256]{1,0:T(8,128)(2,1)S(1)}, bf16[896,256]{1,0:T(8,128)(2,1)}, u32[]{:S(2)}, u32[]{:S(2)}) collective-permute-start(bf16[896,256]{1,0:T(8,128)(2,1)S(1)} %collective-permute-done.3.refs_1_.refs_9_), channel_id=1, source_target_pairs={{0,4},{4,0},{8,12},{12,8},{16,20},{20,16},{24,28},{28,24},{1,5},{5... | collective-permute-start | bytes 1376264 | tf_op jit(solution)/shard_map/ppermute | solution.py:531
  94.3 22.6 %collective-permute-start.21 = (bf16[896,256]{1,0:T(8,128)(2,1)S(1)}, bf16[896,256]{1,0:T(8,128)(2,1)}, u32[]{:S(2)}, u32[]{:S(2)}) collective-permute-start(bf16[896,256]{1,0:T(8,128)(2,1)S(1)} %collective-permute-done.19.refs_0_.refs_20_), channel_id=1, source_target_pairs={{0,4},{4,0},{8,12},{12,8},{16,20},{20,16},{24,28},{28,24},{1,5},{5... | collective-permute-start | bytes 1376264 | tf_op jit(solution)/shard_map/ppermute | solution.py:531
  94.3 22.6 %collective-permute-start.22 = (bf16[896,256]{1,0:T(8,128)(2,1)}, bf16[896,256]{1,0:T(8,128)(2,1)}, u32[]{:S(2)}, u32[]{:S(2)}) collective-permute-start(bf16[896,256]{1,0:T(8,128)(2,1)} %collective-permute-done.20.refs_1_.refs_21_), channel_id=1, source_target_pairs={{0,4},{4,0},{8,12},{12,8},{16,20},{20,16},{24,28},{28,24},{1,5},{5... | collective-permute-start | bytes 1376264 | tf_op jit(solution)/shard_map/ppermute | solution.py:531
  107.2 12.9 %collective-permute-start.17 = (bf16[896,128]{1,0:T(8,128)(2,1)S(1)}, bf16[896,128]{1,0:T(8,128)(2,1)S(1)}, u32[]{:S(2)}, u32[]{:S(2)}) collective-permute-start(bf16[896,128]{1,0:T(8,128)(2,1)S(1)} %get-tuple-element.39), channel_id=1, source_target_pairs={{0,8},{4,12},{8,0},{12,4},{16,24},{20,28},{24,16},{28,20},{1,9},{5... | collective-permute-start | bytes 688136 | tf_op jit(solution)/shard_map/ppermute | solution.py:531
  138.4 13.4 %collective-permute-start.35 = (bf16[896,256]{1,0:T(8,128)(2,1)S(1)}, bf16[896,256]{1,0:T(8,128)(2,1)S(1)}, u32[]{:S(2)}, u32[]{:S(2)}) collective-permute-start(bf16[896,256]{1,0:T(8,128)(2,1)S(1)} %pad_maximum_fusion.7), channel_id=1, source_target_pairs={{0,16},{4,20},{8,24},{12,28},{16,0},{20,4},{24,8},{28,12},{1,17},{... | collective-permute-start | bytes 1376264 | tf_op jit(solution)/shard_map/ppermute | solution.py:531
  138.7 15.5 %collective-permute-start.31 = (bf16[896,128]{1,0:T(8,128)(2,1)S(1)}, bf16[896,128]{1,0:T(8,128)(2,1)S(1)}, u32[]{:S(2)}, u32[]{:S(2)}) collective-permute-start(bf16[896,128]{1,0:T(8,128)(2,1)S(1)} %get-tuple-element.131), channel_id=1, source_target_pairs={{0,16},{4,20},{8,24},{12,28},{16,0},{20,4},{24,8},{28,12},{1,17},{... | collective-permute-start | bytes 688136 | tf_op jit(solution)/shard_map/ppermute | solution.py:531
  151.9 14.6 %collective-permute-start.36 = (bf16[896,512]{1,0:T(8,128)(2,1)S(1)}, bf16[896,512]{1,0:T(8,128)(2,1)S(1)}, u32[]{:S(2)}, u32[]{:S(2)}) collective-permute-start(bf16[896,512]{1,0:T(8,128)(2,1)S(1)} %pad_maximum_fusion.3.refs_0_.refs_6_), channel_id=1, source_target_pairs={{0,4},{4,0},{8,12},{12,8},{16,20},{20,16},{24,28},{28,24},{1,5},{5... | collective-permute-start | bytes 2752520 | tf_op jit(solution)/shard_map/ppermute | solution.py:531
  155.1 11.2 %collective-permute-start.32 = (bf16[896,256]{1,0:T(8,128)(2,1)}, bf16[896,256]{1,0:T(8,128)(2,1)S(1)}, u32[]{:S(2)}, u32[]{:S(2)}) collective-permute-start(bf16[896,256]{1,0:T(8,128)(2,1)} %pad_maximum_fusion.6), channel_id=1, source_target_pairs={{0,8},{4,12},{8,0},{12,4},{16,24},{20,28},{24,16},{28,20},{1,9},{5... | collective-permute-start | bytes 1376264 | tf_op jit(solution)/shard_map/ppermute | solution.py:531
  166.4 26.7 %collective-permute-start.33 = (bf16[896,512]{1,0:T(8,128)(2,1)S(1)}, bf16[896,512]{1,0:T(8,128)(2,1)S(1)}, u32[]{:S(2)}, u32[]{:S(2)}) collective-permute-start(bf16[896,512]{1,0:T(8,128)(2,1)S(1)} %pad_maximum_fusion.2.refs_0_.refs_8_), channel_id=1, source_target_pairs={{0,4},{4,0},{8,12},{12,8},{16,20},{20,16},{24,28},{28,24},{1,5},{5... | collective-permute-start | bytes 2752520 | tf_op jit(solution)/shard_map/ppermute | solution.py:531
  171.7 24.6 %collective-permute-start.37 = (bf16[896,512]{1,0:T(8,128)(2,1)S(1)}, bf16[896,512]{1,0:T(8,128)(2,1)S(1)}, u32[]{:S(2)}, u32[]{:S(2)}) collective-permute-start(bf16[896,512]{1,0:T(8,128)(2,1)S(1)} %shard_map.161), channel_id=1, source_target_pairs={{0,1},{1,2},{2,3},{3,0},{4,5},{5,6},{6,7},{7,4},{8,9},{9,10},{10,1... | collective-permute-start | bytes 2752520 | tf_op jit(solution)/shard_map/ppermute | solution.py:534
  174.2 18.7 %collective-permute-start.29 = (bf16[896,256]{1,0:T(8,128)(2,1)S(1)}, bf16[896,256]{1,0:T(8,128)(2,1)S(1)}, u32[]{:S(2)}, u32[]{:S(2)}) collective-permute-start(bf16[896,256]{1,0:T(8,128)(2,1)S(1)} %pad_maximum_fusion.5), channel_id=1, source_target_pairs={{0,16},{4,20},{8,24},{12,28},{16,0},{20,4},{24,8},{28,12},{1,17},{... | collective-permute-start | bytes 1376264 | tf_op jit(solution)/shard_map/ppermute | solution.py:531
  174.5 17.0 %collective-permute-start.25 = (bf16[896,128]{1,0:T(8,128)(2,1)S(1)}, bf16[896,128]{1,0:T(8,128)(2,1)S(1)}, u32[]{:S(2)}, u32[]{:S(2)}) collective-permute-start(bf16[896,128]{1,0:T(8,128)(2,1)S(1)} %get-tuple-element.129), channel_id=1, source_target_pairs={{0,16},{4,20},{8,24},{12,28},{16,0},{20,4},{24,8},{28,12},{1,17},{... | collective-permute-start | bytes 688136 | tf_op jit(solution)/shard_map/ppermute | solution.py:531
  191.6 11.6 %collective-permute-start.26 = (bf16[896,256]{1,0:T(8,128)(2,1)S(1)}, bf16[896,256]{1,0:T(8,128)(2,1)S(1)}, u32[]{:S(2)}, u32[]{:S(2)}) collective-permute-start(bf16[896,256]{1,0:T(8,128)(2,1)S(1)} %pad_maximum_fusion.4), channel_id=1, source_target_pairs={{0,8},{4,12},{8,0},{12,4},{16,24},{20,28},{24,16},{28,20},{1,9},{5... | collective-permute-start | bytes 1376264 | tf_op jit(solution)/shard_map/ppermute | solution.py:531
  196.6 24.5 %collective-permute-start.38 = (bf16[896,512]{1,0:T(8,128)(2,1)S(1)}, bf16[896,512]{1,0:T(8,128)(2,1)S(1)}, u32[]{:S(2)}, u32[]{:S(2)}) collective-permute-start(bf16[896,512]{1,0:T(8,128)(2,1)S(1)} %add_convert_fusion.1), channel_id=1, source_target_pairs={{0,1},{1,2},{2,3},{3,0},{4,5},{5,6},{6,7},{7,4},{8,9},{9,10},{10,1... | collective-permute-start | bytes 2752520 | tf_op jit(solution)/shard_map/ppermute | solution.py:534
  203.3 28.7 %collective-permute-start.27 = (bf16[896,512]{1,0:T(8,128)(2,1)S(1)}, bf16[896,512]{1,0:T(8,128)(2,1)S(1)}, u32[]{:S(2)}, u32[]{:S(2)}) collective-permute-start(bf16[896,512]{1,0:T(8,128)(2,1)S(1)} %pad_maximum_fusion.refs_0_.refs_4_), channel_id=1, source_target_pairs={{0,4},{4,0},{8,12},{12,8},{16,20},{20,16},{24,28},{28,24},{1,5},{5... | collective-permute-start | bytes 2752520 | tf_op jit(solution)/shard_map/ppermute | solution.py:531
  222.4 23.9 %collective-permute-start.39 = (bf16[896,512]{1,0:T(8,128)(2,1)}, bf16[896,512]{1,0:T(8,128)(2,1)}, u32[]{:S(2)}, u32[]{:S(2)}) collective-permute-start(bf16[896,512]{1,0:T(8,128)(2,1)} %add_convert_fusion), channel_id=1, source_target_pairs={{0,1},{1,2},{2,3},{3,0},{4,5},{5,6},{6,7},{7,4},{8,9},{9,10},{10,1... | collective-permute-start | bytes 2752520 | tf_op jit(solution)/shard_map/ppermute | solution.py:534
  227.4 25.1 %all-to-all-start.3 = ((bf16[8,112,2,256]{3,2,1,0:T(2,128)(2,1)}), bf16[8,112,2,256]{3,2,1,0:T(2,128)(2,1)}, u32[]{:S(2)}, u32[]{:S(2)}) async-start(bf16[8,112,2,256]{3,2,1,0:T(2,128)(2,1)} %bitcast.92), calls=%async_computation.3 | async-start | bytes 1835008 | tf_op jit(solution)/shard_map/all_to_all | solution.py:649
  268.1 20.4 %collective-permute-start.49 = (bf16[896,512]{1,0:T(8,128)(2,1)S(1)}, bf16[896,512]{1,0:T(8,128)(2,1)}, u32[]{:S(2)}, u32[]{:S(2)}) collective-permute-start(bf16[896,512]{1,0:T(8,128)(2,1)S(1)} %multiply_convert_fusion.1.refs_0_), channel_id=1, source_target_pairs={{0,1},{1,2},{2,3},{3,0},{4,5},{5,6},{6,7},{7,4},{8,9},{9,10},{10,1... | collective-permute-start | bytes 2752520 | tf_op jit(solution)/shard_map/ppermute | solution.py:534
  274.3 14.8 %collective-permute-start.46 = (bf16[896,512]{1,0:T(8,128)(2,1)S(1)}, bf16[896,512]{1,0:T(8,128)(2,1)S(1)}, u32[]{:S(2)}, u32[]{:S(2)}) collective-permute-start(bf16[896,512]{1,0:T(8,128)(2,1)S(1)} %get-tuple-element.45), channel_id=1, source_target_pairs={{0,4},{4,0},{8,12},{12,8},{16,20},{20,16},{24,28},{28,24},{1,5},{5... | collective-permute-start | bytes 2752520 | tf_op jit(solution)/shard_map/ppermute | solution.py:531
  288.4 20.5 %collective-permute-start.53 = (bf16[896,512]{1,0:T(8,128)(2,1)}, bf16[896,512]{1,0:T(8,128)(2,1)}, u32[]{:S(2)}, u32[]{:S(2)}) collective-permute-start(bf16[896,512]{1,0:T(8,128)(2,1)} %collective-permute-done.49.refs_0_.refs_1_), channel_id=1, source_target_pairs={{0,1},{1,2},{2,3},{3,0},{4,5},{5,6},{6,7},{7,4},{8,9},{9,10},{10,1... | collective-permute-start | bytes 2752520 | tf_op jit(solution)/shard_map/ppermute | solution.py:534
  293.2 32.6 %collective-permute-start.47 = (bf16[896,256]{1,0:T(8,128)(2,1)}, bf16[896,256]{1,0:T(8,128)(2,1)}, u32[]{:S(2)}, u32[]{:S(2)}) collective-permute-start(bf16[896,256]{1,0:T(8,128)(2,1)} %concatenate.60), channel_id=1, source_target_pairs={{0,16},{4,20},{8,24},{12,28},{16,0},{20,4},{24,8},{28,12},{1,17},{... | collective-permute-start | bytes 1376264 | tf_op jit(solution)/shard_map/ppermute | solution.py:531
  309.0 25.3 %collective-permute-start.57 = (bf16[896,512]{1,0:T(8,128)(2,1)}, bf16[896,512]{1,0:T(8,128)(2,1)}, u32[]{:S(2)}, u32[]{:S(2)}) collective-permute-start(bf16[896,512]{1,0:T(8,128)(2,1)} %collective-permute-done.53.refs_0_.refs_2_), channel_id=1, source_target_pairs={{0,1},{1,2},{2,3},{3,0},{4,5},{5,6},{6,7},{7,4},{8,9},{9,10},{10,1... | collective-permute-start | bytes 2752520 | tf_op jit(solution)/shard_map/ppermute | solution.py:534
  316.9 23.1 %collective-permute-start.50 = (bf16[896,512]{1,0:T(8,128)(2,1)}, bf16[896,512]{1,0:T(8,128)(2,1)}, u32[]{:S(2)}, u32[]{:S(2)}) collective-permute-start(bf16[896,512]{1,0:T(8,128)(2,1)} %get-tuple-element.47), channel_id=1, source_target_pairs={{0,4},{4,0},{8,12},{12,8},{16,20},{20,16},{24,28},{28,24},{1,5},{5... | collective-permute-start | bytes 2752520 | tf_op jit(solution)/shard_map/ppermute | solution.py:531
  321.5 72.3 %all-to-all-start.4 = ((bf16[8,112,2,256]{3,2,1,0:T(2,128)(2,1)}), bf16[8,112,2,256]{3,2,1,0:T(2,128)(2,1)}, u32[]{:S(2)}, u32[]{:S(2)}) async-start(bf16[8,112,2,256]{3,2,1,0:T(2,128)(2,1)} %reshape.393), calls=%async_computation.4 | async-start | bytes 1835008 | tf_op jit(solution)/shard_map/all_to_all | solution.py:662
  327.0 39.5 %collective-permute-start.48 = (bf16[896,128]{1,0:T(8,128)(2,1)S(1)}, bf16[896,128]{1,0:T(8,128)(2,1)S(1)}, u32[]{:S(2)}, u32[]{:S(2)}) collective-permute-start(bf16[896,128]{1,0:T(8,128)(2,1)S(1)} %fusion.19), channel_id=1, source_target_pairs={{0,8},{4,12},{8,0},{12,4},{16,24},{20,28},{24,16},{28,20},{1,9},{5... | collective-permute-start | bytes 688136 | tf_op jit(solution)/shard_map/ppermute | solution.py:531
  341.6 13.4 %collective-permute-start.51 = (bf16[896,256]{1,0:T(8,128)(2,1)S(1)}, bf16[896,256]{1,0:T(8,128)(2,1)S(1)}, u32[]{:S(2)}, u32[]{:S(2)}) collective-permute-start(bf16[896,256]{1,0:T(8,128)(2,1)S(1)} %pad_maximum_fusion.8), channel_id=1, source_target_pairs={{0,8},{4,12},{8,0},{12,4},{16,24},{20,28},{24,16},{28,20},{1,9},{5... | collective-permute-start | bytes 1376264 | tf_op jit(solution)/shard_map/ppermute | solution.py:531
  342.2 14.5 %collective-permute-start.55 = (bf16[896,256]{1,0:T(8,128)(2,1)S(1)}, bf16[896,256]{1,0:T(8,128)(2,1)S(1)}, u32[]{:S(2)}, u32[]{:S(2)}) collective-permute-start(bf16[896,256]{1,0:T(8,128)(2,1)S(1)} %concatenate.59), channel_id=1, source_target_pairs={{0,16},{4,20},{8,24},{12,28},{16,0},{20,4},{24,8},{28,12},{1,17},{... | collective-permute-start | bytes 1376264 | tf_op jit(solution)/shard_map/ppermute | solution.py:531
  344.6 20.3 %collective-permute-start.59 = (bf16[896,256]{1,0:T(8,128)(2,1)S(1)}, bf16[896,256]{1,0:T(8,128)(2,1)S(1)}, u32[]{:S(2)}, u32[]{:S(2)}) collective-permute-start(bf16[896,256]{1,0:T(8,128)(2,1)S(1)} %pad_maximum_fusion.9), channel_id=1, source_target_pairs={{0,8},{4,12},{8,0},{12,4},{16,24},{20,28},{24,16},{28,20},{1,9},{5... | collective-permute-start | bytes 1376264 | tf_op jit(solution)/shard_map/ppermute | solution.py:531
  355.1 11.4 %collective-permute-start.52 = (bf16[896,128]{1,0:T(8,128)(2,1)S(1)}, bf16[896,128]{1,0:T(8,128)(2,1)S(1)}, u32[]{:S(2)}, u32[]{:S(2)}) collective-permute-start(bf16[896,128]{1,0:T(8,128)(2,1)S(1)} %fusion.15), channel_id=1, source_target_pairs={{0,16},{4,20},{8,24},{12,28},{16,0},{20,4},{24,8},{28,12},{1,17},{... | collective-permute-start | bytes 688136 | tf_op jit(solution)/shard_map/ppermute | solution.py:531
  356.8 12.5 %collective-permute-start.56 = (bf16[896,128]{1,0:T(8,128)(2,1)S(1)}, bf16[896,128]{1,0:T(8,128)(2,1)S(1)}, u32[]{:S(2)}, u32[]{:S(2)}) collective-permute-start(bf16[896,128]{1,0:T(8,128)(2,1)S(1)} %fusion.11), channel_id=1, source_target_pairs={{0,8},{4,12},{8,0},{12,4},{16,24},{20,28},{24,16},{28,20},{1,9},{5... | collective-permute-start | bytes 688136 | tf_op jit(solution)/shard_map/ppermute | solution.py:531
  377.3 24.9 %collective-permute-start.67 = (bf16[896,128]{1,0:T(8,128)(2,1)}, bf16[896,128]{1,0:T(8,128)(2,1)}, u32[]{:S(2)}, u32[]{:S(2)}) collective-permute-start(bf16[896,128]{1,0:T(8,128)(2,1)} %get-tuple-element.116.refs_0_.refs_4_), channel_id=1, source_target_pairs={{0,8},{4,12},{8,0},{12,4},{16,24},{20,28},{24,16},{28,20},{1,9},{5... | collective-permute-start | bytes 688136 | tf_op jit(solution)/shard_map/ppermute | solution.py:531
  389.7 49.2 %collective-permute-start.71 = (bf16[896,512]{1,0:T(8,128)(2,1)}, bf16[896,512]{1,0:T(8,128)(2,1)}, u32[]{:S(2)}, u32[]{:S(2)}) collective-permute-start(bf16[896,512]{1,0:T(8,128)(2,1)} %get-tuple-element.59), channel_id=1, source_target_pairs={{0,4},{4,0},{8,12},{12,8},{16,20},{20,16},{24,28},{28,24},{1,5},{5... | collective-permute-start | bytes 2752520 | tf_op jit(solution)/shard_map/ppermute | solution.py:531
  402.1 11.1 %collective-permute-start.61 = (bf16[896,128]{1,0:T(8,128)(2,1)}, bf16[896,128]{1,0:T(8,128)(2,1)S(1)}, u32[]{:S(2)}, u32[]{:S(2)}) collective-permute-start(bf16[896,128]{1,0:T(8,128)(2,1)} %get-tuple-element.117.refs_0_), channel_id=1, source_target_pairs={{0,8},{4,12},{8,0},{12,4},{16,24},{20,28},{24,16},{28,20},{1,9},{5... | collective-permute-start | bytes 688136 | tf_op jit(solution)/shard_map/ppermute | solution.py:531
  407.7 37.1 %collective-permute-start.68 = (bf16[896,512]{1,0:T(8,128)(2,1)}, bf16[896,512]{1,0:T(8,128)(2,1)}, u32[]{:S(2)}, u32[]{:S(2)}) collective-permute-start(bf16[896,512]{1,0:T(8,128)(2,1)} %get-tuple-element.57), channel_id=1, source_target_pairs={{0,4},{4,0},{8,12},{12,8},{16,20},{20,16},{24,28},{28,24},{1,5},{5... | collective-permute-start | bytes 2752520 | tf_op jit(solution)/shard_map/ppermute | solution.py:531
  427.4 54.3 %all-to-all-start.6 = ((bf16[4,9,128,128]{3,2,1,0:T(8,128)(2,1)}), bf16[4,9,128,128]{3,2,1,0:T(8,128)(2,1)}, u32[]{:S(2)}, u32[]{:S(2)}) async-start(bf16[4,9,128,128]{3,2,1,0:T(8,128)(2,1)} %shard_map.170), calls=%async_computation.6 | async-start | bytes 2359296 | tf_op jit(solution)/shard_map/all_to_all | solution.py:710
  438.9 18.1 %collective-permute-start.65 = (bf16[896,512]{1,0:T(8,128)(2,1)}, bf16[896,512]{1,0:T(8,128)(2,1)}, u32[]{:S(2)}, u32[]{:S(2)}) collective-permute-start(bf16[896,512]{1,0:T(8,128)(2,1)} %get-tuple-element.55), channel_id=1, source_target_pairs={{0,4},{4,0},{8,12},{12,8},{16,20},{20,16},{24,28},{28,24},{1,5},{5... | collective-permute-start | bytes 2752520 | tf_op jit(solution)/shard_map/ppermute | solution.py:531
  441.2 13.5 %collective-permute-start.72 = (bf16[896,256]{1,0:T(8,128)(2,1)S(1)}, bf16[896,256]{1,0:T(8,128)(2,1)S(1)}, u32[]{:S(2)}, u32[]{:S(2)}) collective-permute-start(bf16[896,256]{1,0:T(8,128)(2,1)S(1)} %slice.291), channel_id=1, source_target_pairs={{0,16},{4,20},{8,24},{12,28},{16,0},{20,4},{24,8},{28,12},{1,17},{... | collective-permute-start | bytes 1376264 | tf_op jit(solution)/shard_map/ppermute | solution.py:531
  444.8 33.8 %collective-permute-start.62 = (bf16[896,512]{1,0:T(8,128)(2,1)}, bf16[896,512]{1,0:T(8,128)(2,1)S(1)}, u32[]{:S(2)}, u32[]{:S(2)}) collective-permute-start(bf16[896,512]{1,0:T(8,128)(2,1)} %get-tuple-element.53), channel_id=1, source_target_pairs={{0,4},{4,0},{8,12},{12,8},{16,20},{20,16},{24,28},{28,24},{1,5},{5... | collective-permute-start | bytes 2752520 | tf_op jit(solution)/shard_map/ppermute | solution.py:531
  448.3 16.3 %collective-permute-start.69 = (bf16[896,256]{1,0:T(8,128)(2,1)}, bf16[896,256]{1,0:T(8,128)(2,1)}, u32[]{:S(2)}, u32[]{:S(2)}) collective-permute-start(bf16[896,256]{1,0:T(8,128)(2,1)} %slice.292), channel_id=1, source_target_pairs={{0,16},{4,20},{8,24},{12,28},{16,0},{20,4},{24,8},{28,12},{1,17},{... | collective-permute-start | bytes 1376264 | tf_op jit(solution)/shard_map/ppermute | solution.py:531
  454.9 12.6 %collective-permute-start.73 = (bf16[896,256]{1,0:T(8,128)(2,1)S(1)}, bf16[896,256]{1,0:T(8,128)(2,1)}, u32[]{:S(2)}, u32[]{:S(2)}) collective-permute-start(bf16[896,256]{1,0:T(8,128)(2,1)S(1)} %fusion), channel_id=1, source_target_pairs={{0,1},{1,2},{2,3},{3,0},{4,5},{5,6},{6,7},{7,4},{8,9},{9,10},{10,1... | collective-permute-start | bytes 1376264 | tf_op jit(solution)/shard_map/ppermute | solution.py:534
  461.2 24.2 %collective-permute-start.66 = (bf16[896,256]{1,0:T(8,128)(2,1)}, bf16[896,256]{1,0:T(8,128)(2,1)}, u32[]{:S(2)}, u32[]{:S(2)}) collective-permute-start(bf16[896,256]{1,0:T(8,128)(2,1)} %slice.293), channel_id=1, source_target_pairs={{0,16},{4,20},{8,24},{12,28},{16,0},{20,4},{24,8},{28,12},{1,17},{... | collective-permute-start | bytes 1376264 | tf_op jit(solution)/shard_map/ppermute | solution.py:531
  469.6 17.8 %collective-permute-start.74 = (bf16[896,256]{1,0:T(8,128)(2,1)}, bf16[896,256]{1,0:T(8,128)(2,1)}, u32[]{:S(2)}, u32[]{:S(2)}) collective-permute-start(bf16[896,256]{1,0:T(8,128)(2,1)} %fusion.2), channel_id=1, source_target_pairs={{0,1},{1,2},{2,3},{3,0},{4,5},{5,6},{6,7},{7,4},{8,9},{9,10},{10,1... | collective-permute-start | bytes 1376264 | tf_op jit(solution)/shard_map/ppermute | solution.py:534
  472.5 37.5 %collective-permute-start.81 = (f32[2,256]{1,0:T(2,128)S(1)}, f32[2,256]{1,0:T(2,128)S(1)}, u32[]{:S(2)}, u32[]{:S(2)}) collective-permute-start(f32[2,256]{1,0:T(2,128)S(1)} %reshape.399), channel_id=1, source_target_pairs={{0,3},{4,7},{9,8},{13,12},{18,17},{22,21},{27,26},{31,30}} | collective-permute-start | bytes 6152 | tf_op jit(solution)/shard_map/ppermute | solution.py:538
  477.3 32.8 %collective-permute-start.80 = (f32[2,256]{1,0:T(2,128)S(1)}, f32[2,256]{1,0:T(2,128)S(1)}, u32[]{:S(2)}, u32[]{:S(2)}) collective-permute-start(f32[2,256]{1,0:T(2,128)S(1)} %reshape.399), channel_id=1, source_target_pairs={{0,2},{4,6},{9,11},{13,15},{18,16},{22,20},{27,25},{31,29}} | collective-permute-start | bytes 6152 | tf_op jit(solution)/shard_map/ppermute | solution.py:538
  478.6 31.5 %collective-permute-start.79 = (f32[2,256]{1,0:T(2,128)S(1)}, f32[2,256]{1,0:T(2,128)S(1)}, u32[]{:S(2)}, u32[]{:S(2)}) collective-permute-start(f32[2,256]{1,0:T(2,128)S(1)} %reshape.399), channel_id=1, source_target_pairs={{0,1},{4,5},{9,10},{13,14},{18,19},{22,23},{27,24},{31,28}} | collective-permute-start | bytes 6152 | tf_op jit(solution)/shard_map/ppermute | solution.py:538
  481.7 29.3 %all-to-all-start.7 = ((bf16[4,9,128,128]{3,2,1,0:T(8,128)(2,1)}), bf16[4,9,128,128]{3,2,1,0:T(8,128)(2,1)S(1)}, u32[]{:S(2)}, u32[]{:S(2)}) async-start(bf16[4,9,128,128]{3,2,1,0:T(8,128)(2,1)} %all-to-all-done.6), calls=%async_computation.7 | async-start | bytes 2359296 | tf_op jit(solution)/shard_map/all_to_all | solution.py:711
  485.4 24.6 %collective-permute-start.63 = (bf16[896,256]{1,0:T(8,128)(2,1)S(1)}, bf16[896,256]{1,0:T(8,128)(2,1)S(1)}, u32[]{:S(2)}, u32[]{:S(2)}) collective-permute-start(bf16[896,256]{1,0:T(8,128)(2,1)S(1)} %slice.294), channel_id=1, source_target_pairs={{0,16},{4,20},{8,24},{12,28},{16,0},{20,4},{24,8},{28,12},{1,17},{... | collective-permute-start | bytes 1376264 | tf_op jit(solution)/shard_map/ppermute | solution.py:531
  488.8 21.3 %collective-permute-start.75 = (bf16[896,256]{1,0:T(8,128)(2,1)S(1)}, bf16[896,256]{1,0:T(8,128)(2,1)S(1)}, u32[]{:S(2)}, u32[]{:S(2)}) collective-permute-start(bf16[896,256]{1,0:T(8,128)(2,1)S(1)} %fusion.4), channel_id=1, source_target_pairs={{0,1},{1,2},{2,3},{3,0},{4,5},{5,6},{6,7},{7,4},{8,9},{9,10},{10,1... | collective-permute-start | bytes 1376264 | tf_op jit(solution)/shard_map/ppermute | solution.py:534
  511.0 12.5 %all-to-all-start.5 = ((bf16[8,112,256]{2,1,0:T(8,128)(2,1)}), bf16[8,112,256]{2,1,0:T(8,128)(2,1)S(1)}, u32[]{:S(2)}, u32[]{:S(2)}) async-start(bf16[8,112,256]{2,1,0:T(8,128)(2,1)} %bitcast.28), calls=%async_computation.5 | async-start | bytes 917504 | tf_op jit(solution)/shard_map/all_to_all | solution.py:695
  (91 other events, 1208.7 us)

commit v3 on v0

--- a/solution.py
+++ b/solution.py
@@ -1,7 +1,13 @@
+import functools
+
 import jax
 import jax.numpy as jnp
 from jax import lax
+from jax.experimental import pallas as pl
+from jax.experimental.pallas import tpu as pltpu
 from jax.sharding import PartitionSpec as P
+
+f32, bf16 = jnp.float32, jnp.bfloat16
 
 
 def frame_valid(lengths_row, frame_total, clip_count):
@@ -106,7 +112,7 @@
     return ((before - average) * inv_std, inv_std)
 
 
-def per_device(
+def gathered(
     features,
     lengths,
     conv1_weight,
@@ -225,9 +231,687 @@
     )
 
 
+NT = (((1,), (1,)), ((), ()))
+NN = (((1,), (0,)), ((), ()))
+TN = (((0,), (0,)), ((), ()))
+CHIPS, PLANES, MELS = 4, 4, 2
+
+
+def mxu(a, b, dims):
+    return lax.dot_general(a, b, dims, preferred_element_type=f32)
+
+
+def vmem(mib):
+    return pltpu.CompilerParams(vmem_limit_bytes=mib << 20)
+
+
+def same(*shape):
+    return pl.BlockSpec(shape, lambda *_: (0,) * len(shape))
+
+
+def cost(flops, bytes_accessed):
+    return pl.CostEstimate(flops=flops, bytes_accessed=bytes_accessed, transcendentals=0)
+
+
+def rolled(value, shift):
+    shift %= value.shape[0]
+    return pltpu.roll(value, shift, 0) if shift else value
+
+
+def taps1_kernel(pos, own, other, out):
+    for t in range(4):
+        source = 2 * (pos[1] ^ (t // 2)) + t % 2
+        for rx in range(2):
+            for tap in range(9):
+                value = jnp.where(
+                    pos[0] ^ pos[2] == rx, own[source, tap], other[source, tap]
+                )
+                a, b = tap // 3, tap % 3
+                for mo in range(MELS):
+                    mi = mo + b - 1
+                    if 0 <= mi < MELS:
+                        row, lane = rx * 256 + mo * 128, t * 256 + mi * 128
+                        out[a, row : row + 128, lane : lane + 128] = value
+
+
+def taps1(pos, own, other):
+    spec = pltpu.PrefetchScalarGridSpec(
+        num_scalar_prefetch=1,
+        grid=(1,),
+        in_specs=[same(*own.shape), same(*own.shape)],
+        out_specs=same(3, 512, 1024),
+    )
+    return pl.pallas_call(
+        taps1_kernel,
+        grid_spec=spec,
+        out_shape=jax.ShapeDtypeStruct((3, 512, 1024), bf16),
+        compiler_params=vmem(24),
+    )(pos, own, other)
+
+
+def taps2_kernel(pos, own, other, out):
+    part = own.shape[1]
+    for core, w in enumerate((own, other)):
+        for a in range(3):
+            for mo in range(MELS):
+                row = (core * MELS + mo) * part
+                for mi in range(MELS):
+                    lane = mi * 128
+                    out[a, row : row + part, lane : lane + 128] = w[3 * a + mi - mo + 1]
+
+
+def taps2(pos, own, other):
+    part = own.shape[1]
+    source = pl.BlockSpec(
+        (9, part, 128), lambda t, p: (0, 0, 2 * (p[2] ^ (t % 2)) + (p[1] ^ (t // 2)))
+    )
+    spec = pltpu.PrefetchScalarGridSpec(
+        num_scalar_prefetch=1,
+        grid=(4,),
+        in_specs=[source, source],
+        out_specs=pl.BlockSpec((3, 4 * part, 256), lambda t, p: (0, 0, t)),
+    )
+    return pl.pallas_call(
+        taps2_kernel,
+        grid_spec=spec,
+        out_shape=jax.ShapeDtypeStruct((3, 4 * part, 1024), bf16),
+        compiler_params=vmem(24),
+    )(pos, own, other)
+
+
+def quarters_kernel(pos, *refs):
+    quads, out = refs[:4], refs[4]
+    taps, half, lanes = quads[0].shape
+    for k in range(4):
+        row = pl.multiple_of((pos[1] ^ (k // 2)) * half, half)
+        lane = pl.multiple_of((pos[2] ^ (k % 2)) * lanes, lanes)
+        out[:, pl.ds(row, half), pl.ds(lane, lanes)] = quads[k][...].astype(out.dtype)
+
+
+def from_quarters(pos, quads):
+    taps, half, lanes = quads[0].shape
+    spec = pltpu.PrefetchScalarGridSpec(
+        num_scalar_prefetch=1,
+        grid=(3,),
+        in_specs=[pl.BlockSpec((taps // 3, half, lanes), lambda i, p: (i, 0, 0))] * 4,
+        out_specs=pl.BlockSpec((taps // 3, 2 * half, 2 * lanes), lambda i, p: (i, 0, 0)),
+    )
+    return pl.pallas_call(
+        quarters_kernel,
+        grid_spec=spec,
+        out_shape=jax.ShapeDtypeStruct((taps, 2 * half, 2 * lanes), f32),
+    )(pos, *quads)
+
+
+def conv_kernel(pieces, *refs):
+    xs, w, outs = refs[:pieces], refs[pieces], refs[pieces + 1 :]
+    total = None
+    for a in (1, 0, 2):
+        z, start = None, 0
+        for x in xs:
+            width = x.shape[1]
+            term = mxu(x[...], w[a, :, start : start + width], NT)
+            z, start = term if z is None else z + term, start + width
+        z = rolled(z, 1 - a)
+        total = z if total is None else total + z
+    start = 0
+    for out in outs:
+        out[...] = total[:, start : start + out.shape[1]].astype(out.dtype)
+        start += out.shape[1]
+
+
+def conv(xs, w, kinds, tile):
+    rows, (_, width, depth) = xs[0].shape[0], w.shape
+    lanes = tile // len(kinds)
+    return pl.pallas_call(
+        functools.partial(conv_kernel, len(xs)),
+        grid=(width // tile,),
+        in_specs=[same(*x.shape) for x in xs]
+        + [pl.BlockSpec((3, tile, depth), lambda i: (0, i, 0))],
+        out_specs=[pl.BlockSpec((rows, lanes), lambda i: (0, i)) for _ in kinds],
+        out_shape=[jax.ShapeDtypeStruct((rows, width // len(kinds)), kind) for kind in kinds],
+        compiler_params=vmem(32),
+        cost_estimate=cost(6 * rows * width * depth, 2 * rows * depth + 6 * width * depth),
+    )(*xs, w)
+
+
+def spread_rows(dst, at, value, width, lane):
+    rows, lanes = value.shape
+    wide = value.astype(f32)
+    for a in range(3):
+        moved = value if a == 1 else rolled(wide, a - 1).astype(bf16)
+        dst[at : at + rows, a * width + lane : a * width + lane + lanes] = moved
+
+
+def conv_t_kernel(pieces, *refs):
+    dys, w = refs[:pieces], refs[pieces]
+    outs, moved = refs[pieces + 1 : -1], refs[-1]
+    width = moved.shape[1] // 3
+    step = pl.program_id(0)
+
+    @pl.when(step == 0)
+    def _():
+        lane = 0
+        for dy in dys:
+            spread_rows(moved, 0, dy[...], width, lane)
+            lane += dy.shape[1]
+
+    value = mxu(moved[...], w[...].reshape(3 * width, w.shape[2]), NN)
+    for k, out in enumerate(outs):
+
+        @pl.when(step == k)
+        def _():
+            out[...] = value.astype(out.dtype)
+
+
+def conv_t(dys, w, blocks):
+    rows, (_, width, depth) = dys[0].shape[0], w.shape
+    lanes = depth // blocks
+    return pl.pallas_call(
+        functools.partial(conv_t_kernel, len(dys)),
+        grid=(blocks,),
+        in_specs=[same(*dy.shape) for dy in dys]
+        + [pl.BlockSpec((3, width, lanes), lambda i: (0, 0, i))],
+        out_specs=[same(rows, lanes)] * blocks,
+        out_shape=[
+            jax.ShapeDtypeStruct((rows, lanes), bf16 if k else f32) for k in range(blocks)
+        ],
+        scratch_shapes=[pltpu.VMEM((rows, 3 * width), bf16)],
+        compiler_params=vmem(32),
+        cost_estimate=cost(6 * rows * width * depth, 3 * rows * depth + 6 * width * depth),
+    )(*dys, w)
+
+
+def grad2_place(pos, own, send, a, prod):
+    part = prod.shape[0] // 4
+    for core, out in enumerate((own, send)):
+        first = prod[2 * core * part : (2 * core + 1) * part]
+        second = prod[(2 * core + 1) * part : (2 * core + 2) * part]
+        out[3 * a] = second[:, :128].astype(out.dtype)
+        out[3 * a + 1] = (first[:, :128] + second[:, 128:]).astype(out.dtype)
+        out[3 * a + 2] = first[:, 128:].astype(out.dtype)
+
+
+def grad1_place(pos, own, send, a, prod):
+    taps = []
+    for rx in range(2):
+        first, second = prod[rx * 256 : rx * 256 + 128], prod[rx * 256 + 128 :][:128]
+        taps.append([second[:, :128], first[:, :128] + second[:, 128:], first[:, 128:]])
+    for b in range(3):
+        mine = pos[0] == pos[2]
+        own[0, 3 * a + b] = jnp.where(mine, taps[0][b], taps[1][b])
+        send[0, 3 * a + b] = jnp.where(mine, taps[1][b], taps[0][b]).astype(bf16)
+
+
+def grad_kernel(place, groups, pieces, pos, *refs):
+    dys = refs[: groups * pieces]
+    xs = refs[groups * pieces : -4]
+    own, send, moved, x = refs[-4:]
+    width = moved.shape[1] // 3
+    step = pl.program_id(0)
+    rows = dys[0].shape[0]
+    per_group = len(xs) // groups
+    steps_each = 4 // per_group
+
+    @pl.when(step == 0)
+    def _():
+        for r in range(groups):
+            lane = 0
+            for dy in dys[r * pieces : (r + 1) * pieces]:
+                spread_rows(moved, r * rows, dy[...], width, lane)
+                lane += dy.shape[1]
+
+    for k in range(per_group):
+
+        @pl.when(step // steps_each == k)
+        def _():
+            for r in range(groups):
+                x[r * rows : (r + 1) * rows, :] = xs[r * per_group + k][...]
+
+    for a in range(3):
+        place(pos, own, send, a, mxu(moved[:, a * width : (a + 1) * width], x[...], TN))
+
+
+def weight_grad_own(pos, dys, xs, place, shape, out_spec):
+    groups, pieces, per_group = len(dys), len(dys[0]), len(xs[0])
+    rows = dys[0][0].shape[0]
+    width = sum(dy.shape[1] for dy in dys[0])
+    steps_each = 4 // per_group
+
+    def column(k):
+        return lambda t, p: (0, jnp.clip(t - k * steps_each, 0, steps_each - 1))
+
+    spec = pltpu.PrefetchScalarGridSpec(
+        num_scalar_prefetch=1,
+        grid=(4,),
+        in_specs=[same(*dy.shape) for group in dys for dy in group]
+        + [pl.BlockSpec((rows, 256), column(k)) for _ in xs for k in range(per_group)],
+        out_specs=[out_spec, out_spec],
+        scratch_shapes=[
+            pltpu.VMEM((groups * rows, 3 * width), bf16),
+            pltpu.VMEM((groups * rows, 256), bf16),
+        ],
+    )
+    args = [dy for group in dys for dy in group] + [x for group in xs for x in group]
+    return pl.pallas_call(
+        functools.partial(grad_kernel, place, groups, pieces),
+        grid_spec=spec,
+        out_shape=[jax.ShapeDtypeStruct(shape, f32), jax.ShapeDtypeStruct(shape, bf16)],
+        compiler_params=vmem(56),
+        cost_estimate=cost(
+            6 * groups * rows * width * 1024, 2 * groups * rows * (width + 1024)
+        ),
+    )(pos, *args)
+
+
+def clip_places(lengths_row, half_rows):
+    clips = lengths_row.shape[0]
+    each = clips // 3
+
+    def rank(axis):
+        clip = lax.broadcasted_iota(jnp.int32, (clips, clips), axis)
+        kind, place = clip // each, clip % each
+        late = place >= each // 2
+        long = jnp.where(late, place + 2 * each, place)
+        middle = jnp.where(late, place + each + each // 2, place + each // 2)
+        return jnp.where(kind == 2, long, jnp.where(kind == 1, middle, place + each))
+
+    size = lengths_row[None, :] + 1
+    before = jnp.sum(jnp.where(rank(1) < rank(0), size, 0), axis=1)
+    late = before + lengths_row + 1 > half_rows
+    taken = jnp.sum(jnp.where(late, 0, lengths_row + 1))
+    return late.astype(jnp.int32), jnp.where(late, before - taken, before)
+
+
+def halves_fit(lengths_row, half_rows):
+    late, _ = clip_places(lengths_row, half_rows)
+    return jnp.sum(late * (lengths_row + 1)) <= half_rows
+
+
+def row_valid(lengths_row, core, half_rows):
+    half, start = clip_places(lengths_row, half_rows)
+    length = jnp.where(half == core, lengths_row, 0)[None, :]
+    row = lax.broadcasted_iota(jnp.int32, (half_rows, lengths_row.shape[0]), 0)
+    inside = (row >= start[None, :]) & (row < start[None, :] + length)
+    return jnp.sum(inside.astype(f32), axis=1, keepdims=True)
+
+
+def row_picker(lengths_row, core, half_rows, frames):
+    clips = lengths_row.shape[0]
+    clip = lax.broadcasted_iota(jnp.int32, (frames, clips), 1)
+    frame = lax.broadcasted_iota(jnp.int32, (frames, clips), 0)
+    each = clips // 3
+    padded = jnp.where(clip < each, 16, jnp.where(clip < 2 * each, 32, 64))
+    base = jnp.where(
+        clip < each, 0, jnp.where(clip < 2 * each, 16 * each, 48 * each)
+    ) + padded * (clip % each)
+    offset = frame - base
+    inside = (offset >= 0) & (offset < lengths_row[None, :])
+    half, start = clip_places(lengths_row, half_rows)
+    place = jnp.where(half == core, start, start + half_rows)
+    target = jnp.sum(jnp.where(inside, place[None, :] + offset + 1, 0), axis=1)
+    row = lax.broadcasted_iota(jnp.int32, (2 * half_rows, frames), 0)
+    return (row + 1 == target[None, :]).astype(bf16)
+
+
+def after(value, *others):
+    return lax.optimization_barrier((value, *others))[0]
+
+
+def stationary(
+    features,
+    lengths,
+    conv1_weight,
+    norm1_gain,
+    norm1_bias,
+    conv2_weight,
+    norm2_gain,
+    norm2_bias,
+    out_grad,
+):
+    n = 2 * CHIPS
+    own_frames, _, width1 = features.shape[1:]
+    frames, lanes1 = own_frames * n, width1 // n
+
+    sent = features[0].reshape(own_frames, MELS, 2, 2, 2, lanes1).transpose(2, 4, 3, 0, 1, 5)
+    sent = sent.reshape(frames, MELS * lanes1)
+    mine = lax.all_to_all(sent, "tm", 0, 0, tiled=True)
+    every = [lengths[0]] + [
+        lax.ppermute(lengths, "batch", [(z, (z + s) % PLANES) for z in range(PLANES)])[0]
+        for s in range(1, PLANES)
+    ]
+    part, wide = conv1_weight.shape[0], conv1_weight.shape[2]
+    quarters = conv1_weight.transpose(1, 0, 2).reshape(9, 2, part // 2, 2, wide // 2)
+    quarters = quarters.transpose(1, 3, 0, 2, 4).reshape(CHIPS, 9, part // 2, wide // 2)
+    half_rows = frames * 3 // 7
+    fits = functools.reduce(jnp.logical_and, [halves_fit(x, half_rows) for x in every])
+    return lax.cond(
+        fits,
+        functools.partial(on_rows, half_rows),
+        functools.partial(on_rows, frames // 2),
+        mine,
+        jnp.stack(every),
+        quarters,
+        norm1_gain,
+        norm1_bias,
+        conv2_weight,
+        norm2_gain,
+        norm2_bias,
+        out_grad,
+    )
+
+
+def on_rows(
+    rows,
+    mine,
+    every,
+    w1,
+    norm1_gain,
+    norm1_bias,
+    conv2_weight,
+    norm2_gain,
+    norm2_bias,
+    out_grad,
+):
+    n = 2 * CHIPS
+    me, plane = lax.axis_index("tm"), lax.axis_index("batch")
+    core, chip = me % 2, me // 2
+    py, px = chip // 2, chip % 2
+    pos = jnp.stack([core, py, px]).astype(jnp.int32)
+    frames, lanes1 = mine.shape[0], mine.shape[1] // MELS
+    own_frames, width1 = frames // n, n * lanes1
+    part = conv2_weight.shape[0]
+    half = part // 2
+    same_core = [[c + 2 * p for p in range(CHIPS)] for c in range(2)]
+    groups = range(PLANES)
+    X, Y = 2, 4
+
+    def swap(x, bits):
+        return lax.ppermute(x, "tm", [(i, i ^ bits) for i in range(n)])
+
+    def along(x, shift):
+        return lax.ppermute(x, "batch", [(z, (z + shift) % PLANES) for z in groups])
+
+    def route(x, pairs):
+        flat = [(a * PLANES + b, c * PLANES + d) for (a, b), (c, d) in pairs]
+        return lax.ppermute(x, ("tm", "batch"), flat)
+
+    def plane_sum(x):
+        got = [
+            lax.ppermute(x, "batch", [(z, z ^ s) for z in groups]) for s in range(1, PLANES)
+        ]
+        return (x + got[0]) + (got[1] + got[2])
+
+    def per_channel(x):
+        return jnp.sum(x.reshape(MELS, -1), axis=0)
+
+    def per_lane(x):
+        return jnp.tile(x, MELS)[None]
+
+    def rows_sum(x):
+        return jnp.sum(x, axis=0)
+
+    picker = row_picker(every[0], core, rows, frames)
+    mask = [row_valid(every[r], core, rows) for r in groups]
+    count = jnp.sum(every.astype(f32)) * MELS
+    packed = mxu(picker, mine, NN).astype(bf16)
+    other = swap(packed[rows:], 1)
+    first = jnp.where(core == 0, packed[:rows], other)
+    second = jnp.where(core == 0, other, packed[:rows])
+    mine = [jnp.concatenate([first, second], axis=1)]
+
+    w1 = lax.all_to_all(w1, "tm", 0, 0, tiled=True, axis_index_groups=same_core)
+    w2 = conv2_weight.transpose(1, 0, 2)
+    w2_other = swap(after(w2, mine[0]), 1)
+
+    def norm_of_block(own_norm):
+        both = 0.0
+        for y in range(2):
+            for c in range(2):
+                both += route(
+                    own_norm[:, y],
+                    [((2 * j + x, j), (4 * y + 2 * x + c, j)) for j in groups for x in range(2)],
+                )
+        return both
+
+    own_norm = jnp.stack([norm1_gain, norm1_bias]).reshape(2, 2, half)
+    nears, both1, weights2 = [], None, None
+    for r in groups:
+        x = mine[r]
+        ahead = along(x, 1) if r < PLANES - 1 else None
+        nears.append(swap(x, Y))
+        done = [nears[r]]
+        if r == 1:
+            w1 = lax.all_to_all(after(w1, x), "batch", 0, 0, tiled=True)
+            weights2 = taps2(pos, w2, after(w2_other, x))
+            done.append(weights2)
+        if r == 2:
+            both1 = norm_of_block(after(own_norm, x))
+            done.append(both1)
+        if ahead is not None:
+            mine.append(after(ahead, *done))
+    gain1, bias1 = both1[0], both1[1]
+
+    w1 = after(w1, mine[3])
+    weights1 = taps1(pos, w1, swap(w1, 1))
+    inputs, pre1, send = [], [], None
+    for r in groups:
+        inputs.append([mine[r], nears[r] if r < 3 else after(nears[r], send)])
+        xs = inputs[r] if r == 0 else [after(mine[r], send), inputs[r][1]]
+        keep, send = conv(xs, weights1, (f32, bf16), 512)
+        pre1.append(keep + swap(send, X).astype(f32))
+
+    def norm_stats(total, square_total):
+        average = total / count
+        variance = square_total / count - average * average
+        return average, lax.rsqrt(variance + 1e-05)
+
+    def chip_sum(x):
+        return x + swap(x, 1)
+
+    sums = jnp.stack(
+        [
+            per_channel(sum(rows_sum(x * v) for x, v in zip(pre1, mask))),
+            per_channel(sum(rows_sum(x * x * v) for x, v in zip(pre1, mask))),
+        ]
+    )
+    sums = chip_sum(sums)
+    mean1, rstd1 = norm_stats(sums[0], sums[1])
+    xhat1 = [(x - per_lane(mean1)) * per_lane(rstd1) for x in pre1]
+    z1 = [per_lane(gain1) * x + per_lane(bias1) for x in xhat1]
+    act1 = [(v * jax.nn.silu(z)).astype(bf16) for v, z in zip(mask, z1)]
+
+    hidden = [None] * PLANES
+    payload, term, got, grad_in = None, None, None, None
+    for r in (1, 2, 3, 0):
+        x = act1[r] if r == 1 else after(act1[r], *got)
+        got = [swap(x, X), swap(x, Y), swap(x, X + Y)]
+        if r != 1:
+            got[2] = after(got[2], term)
+        hidden[r] = [x, *got]
+        moved = None if r == 1 else along(payload, 1)
+        (term,) = conv(hidden[r], weights2, (bf16 if r == 1 else f32,), 512)
+        if r == 1:
+            payload = term
+            continue
+        if r == 0:
+            grad_in = mxu(picker, grad_in.reshape(frames, MELS * part), NN).astype(bf16)
+            grad_in = jnp.concatenate([grad_in[:rows], swap(grad_in[rows:], 1)], axis=1)
+            moved = after(moved, grad_in)
+        total = term + after(moved, term).astype(f32)
+        payload = total.astype(bf16)
+        if r == 2:
+            grad_in = after(out_grad, payload)[0].reshape(own_frames, MELS, n, part)
+            grad_in = grad_in.transpose(2, 0, 1, 3)
+            grad_in = lax.all_to_all(grad_in, "tm", 0, 0, tiled=True)
+    pre2, v0 = total, mask[0]
+
+    def all_rows(x, y):
+        sums = jnp.stack([rows_sum(x), rows_sum(y)]).reshape(2, 2, MELS, part).sum(axis=2)
+        return plane_sum(sums + swap(jnp.flip(sums, 1), 1))
+
+    def lanes2(x):
+        return jnp.broadcast_to(x[:, None, :], (2, MELS, part)).reshape(1, -1)
+
+    norm2 = jnp.stack([norm2_gain, norm2_bias])
+    norm2 = jnp.stack([norm2, swap(after(norm2, act1[1]), 1)], axis=1)
+    sums2 = all_rows(pre2 * v0, pre2 * pre2 * v0)
+    mean2, rstd2 = norm_stats(sums2[0], sums2[1])
+    xhat2 = (pre2 - lanes2(mean2)) * lanes2(rstd2)
+    z2 = lanes2(norm2[0]) * xhat2 + lanes2(norm2[1])
+    dz2 = grad_in.astype(f32) * v0 * silu_slope(z2)
+    grads2 = all_rows(dz2, dz2 * xhat2)
+    bias2_grad, gain2_grad = grads2[0, 0], grads2[1, 0]
+    dpre2 = (
+        v0
+        * lanes2(norm2[0] * rstd2)
+        * (dz2 - (lanes2(grads2[0]) + xhat2 * lanes2(grads2[1])) / count)
+    ).astype(bf16)
+
+    grad2 = [dpre2]
+    dact1, block_out = [], None
+    for r in groups:
+        ahead = along(grad2[r], 1) if r < PLANES - 1 else None
+        keep, *sends = conv_t([grad2[r]], weights2, CHIPS)
+        got = [swap(v, bits) for v, bits in zip(sends, (X, Y, X + Y))]
+        done = list(got)
+        if r == 0:
+            out_local = (v0 * jax.nn.silu(after(z2, keep))).astype(bf16)
+            lanes = MELS * part
+            out_local = jnp.concatenate(
+                [out_local[:, :lanes], swap(out_local[:, lanes:], 1)], axis=0
+            )
+            out_local = mxu(picker, out_local, TN).astype(bf16)
+            out_local = out_local.reshape(n, own_frames, MELS, part)
+            done.append(out_local)
+        if r == 1:
+            block_out = lax.all_to_all(after(out_local, keep), "tm", 0, 0, tiled=True)
+        if r == 2:
+            block_out = block_out.transpose(1, 2, 0, 3)
+            block_out = block_out.reshape(1, own_frames, MELS, n * part)
+            done.append(block_out)
+        dact1.append(
+            (keep + got[0].astype(f32)) + (got[1].astype(f32) + got[2].astype(f32))
+        )
+        if ahead is not None:
+            ahead, *rest = lax.optimization_barrier((ahead, *done))
+            if r == 0:
+                out_local = rest[-1]
+            if r == 2:
+                block_out = rest[-1]
+            grad2.append(ahead)
+
+    dz1 = [d * v * silu_slope(z) for d, v, z in zip(dact1, mask, z1)]
+    sums = jnp.stack(
+        [
+            per_channel(sum(rows_sum(d) for d in dz1)),
+            per_channel(sum(rows_sum(d * x) for d, x in zip(dz1, xhat1))),
+        ]
+    )
+    grads1 = chip_sum(sums)
+    dpre1 = [
+        (
+            v
+            * per_lane(gain1 * rstd1)
+            * (d - (per_lane(grads1[0]) + x * per_lane(grads1[1])) / count)
+        ).astype(bf16)
+        for v, d, x in zip(mask, dz1, xhat1)
+    ]
+    order = (1, 2, 3, 0)
+    pairs1, terms = [None] * PLANES, {}
+    for k, r in enumerate(order):
+        x = dpre1[r] if k == 0 else after(dpre1[r], pairs1[1][1])
+        pairs1[r] = [x, swap(x, X)]
+    send = None
+    for k, r in enumerate(order):
+        x, near = pairs1[r]
+        if k > 0:
+            near = after(near, send)
+        keep, send = conv_t([x, near], weights1, 2)
+        terms[r] = keep, send
+
+    def dx_term(r):
+        return terms[r][0] + swap(terms[r][1], Y).astype(f32)
+
+    first = dx_term(1).astype(bf16)
+    pairs1[1][0] = after(pairs1[1][0], first, send)
+    grad1_own, grad1_send = weight_grad_own(
+        pos,
+        [pairs1[r] for r in order],
+        [inputs[r] for r in order],
+        grad1_place,
+        (PLANES, 9, half, 128),
+        pl.BlockSpec(
+            (1, 9, half, 128), lambda t, p: (2 * (p[1] ^ (t // 2)) + t % 2, 0, 0, 0)
+        ),
+    )
+    grad1 = (grad1_own + swap(grad1_send, 1).astype(f32)).astype(bf16)
+    second = (dx_term(2) + after(along(first, 1), grad1).astype(f32)).astype(bf16)
+    moved = along(second, 1)
+    grad1_planes = lax.all_to_all(after(grad1, second), "batch", 0, 0, tiled=True)
+    grad2_own, grad2_send = weight_grad_own(
+        pos,
+        [[after(grad2[0], second)]] + [[g] for g in grad2[1:]],
+        hidden,
+        grad2_place,
+        (9, part, conv2_weight.shape[2]),
+        pl.BlockSpec(
+            (9, part, 128), lambda t, p: (0, 0, 2 * (p[2] ^ (t % 2)) + (p[1] ^ (t // 2)))
+        ),
+    )
+    third = (dx_term(3) + after(moved, grad2_send).astype(f32)).astype(bf16)
+    moved = along(third, 1)
+    conv2_grad = grad2_own + swap(after(grad2_send, third), 1).astype(f32)
+    dx = (dx_term(0) + after(moved, conv2_grad).astype(f32)).astype(bf16)
+    conv2_grad = conv2_grad.transpose(1, 0, 2)
+    low, high = dx[:, : MELS * lanes1], dx[:, MELS * lanes1 :]
+    other = swap(jnp.where(core == 0, high, low), 1)
+    dx = jnp.concatenate([jnp.where(core == 0, low, high), other], axis=0)
+    dx = mxu(picker, dx, TN).astype(bf16)
+
+    def quarter(k):
+        return lax.dynamic_index_in_dim(grad1_planes, chip ^ k, 0, keepdims=False)
+
+    quads = [quarter(0)] + [swap(quarter(k), 2 * k) for k in range(1, CHIPS)]
+    dx = lax.all_to_all(dx.reshape(n, own_frames, MELS * lanes1), "tm", 0, 0, tiled=True)
+    dx = dx.reshape(2, 2, 2, own_frames, MELS, lanes1).transpose(3, 4, 0, 2, 1, 5)
+    input_grad = dx.reshape(1, own_frames, MELS, width1)
+    conv1_grad = from_quarters(pos, quads).transpose(1, 0, 2)
+
+    grads1 = after(grads1, grad2_send)
+    whole1 = jnp.concatenate(
+        [
+            route(
+                grads1,
+                [((4 * y + 2 * x, j), (2 * j + x, j)) for j in groups for x in range(2)],
+            )
+            for y in range(2)
+        ],
+        axis=1,
+    )
+    mine1 = jnp.where(chip == plane, whole1, 0.0)
+    for s in range(1, PLANES):
+        mine1 += route(
+            whole1,
+            [((2 * j + c, j), (2 * j + c, (j + s) % PLANES)) for j in groups for c in range(2)],
+        )
+    bias1_grad, gain1_grad = mine1[0], mine1[1]
+
+    return (
+        block_out,
+        input_grad,
+        conv1_grad,
+        gain1_grad,
+        bias1_grad,
+        conv2_grad,
+        gain2_grad,
+        bias2_grad,
+    )
+
+
 def solution(mesh):
     return jax.shard_map(
-        per_device,
+        stationary if dict(mesh.shape) == {"tm": 8, "batch": 4} else gathered,
         mesh=mesh,
         in_specs=(
             P("batch", "tm", None, None),

time: 933 us -> 500 us (0.54)
  waiting for transfers between devices: 576 us -> 168 us
  starting transfers between devices: 7.78 us -> 132 us
  matrix products: 128 us -> 5.5 us
  Pallas kernels: 0 us -> 85.2 us
  local copies, waits for them, and re-layouts: 104 us -> 49.8 us
  blocking collectives: 41.9 us -> 0 us
  other arithmetic: 50.5 us -> 37.4 us
  between operations: 16.4 us -> 4.48 us
  loops' own time: 0 us -> 11.5 us
    all_gather x4 -> x0, waiting for transfers between devices: 266 us -> none  [the longest x1 109 us: per_device(): lax.all_gather(conv2_weight, 'batch', axis=2, tiled=True)]
    reduce_scatter x3 -> x0, waiting for transfers between devices: 257 us -> none  [the longest x1 162 us: per_device(): lax.psum_scatter(conv2_local.astype(jnp.bfloat16), 'batch', scatter_dimen...]
    ppermute x0 -> x86, waiting for transfers between devices: none -> 164 us  [the longest x56 103 us: swap(): return lax.ppermute(x, 'tm', [(i, i ^ bits) for i in range(n)])]
    dot_general x18 -> x4, matrix products: 128 us -> 5.5 us  [mxu(): return lax.dot_general(a, b, dims, preferred_element_type=f32)]
    ppermute x0 -> x86, starting transfers between devices: none -> 103 us  [the longest x56 49.4 us: swap(): return lax.ppermute(x, 'tm', [(i, i ^ bits) for i in range(n)])]
    pallas_call x0 -> x21, Pallas kernels: none -> 85.2 us  [the longest x2 28.1 us: weight_grad_own(): pl.pallas_call(functools.partial(grad_kernel, place, groups, pieces), gri...]
    psum x4 -> x0, blocking collectives: 41.9 us -> none  [the longest x1 12.1 us: per_device(): lax.psum((jnp.sum(delta_one * scaled_one, axis=(0, 1)), jnp.sum(delta_one...]
    convert_element_type x6 -> x0, local copies, waits for them, and re-layouts: 25.8 us -> none  [the longest x1 10.8 us: per_device(): partial_terms.astype(jnp.bfloat16)]
  transfers between devices with their start and end apart: 10 -> 93, of which waited for: 10 -> 46; matrix products, arithmetic and copies ran while one was open for 16% -> 10% of each run, Pallas kernels for 0% -> 13%
where the time goes in v3:
time: 500 us; the launch traced here: 494 us
  waiting for transfers between devices  168 us (34%)
  starting transfers between devices  132 us (26%)
  Pallas kernels  85.2 us (17%)
  local copies, waits for them, and re-layouts  49.8 us (10%)
  other arithmetic  37.4 us (7%)
  loops' own time  11.5 us (2%)
  matrix products  5.5 us (1%)
    ppermute x56, waiting for transfers between devices, swap(): return lax.ppermute(x, 'tm', [(i, i ^ bits) for i in range(n)])  103 us
    ppermute x12, waiting for transfers between devices, along(): return lax.ppermute(x, 'batch', [(z, (z + shift) % PLANES) for z in groups])  54.7 us
    ppermute x56, starting transfers between devices, swap(): return lax.ppermute(x, 'tm', [(i, i ^ bits) for i in range(n)])  49.4 us
    pallas_call x2, Pallas kernels, weight_grad_own(): pl.pallas_call(functools.partial(grad_kernel, place, groups, pieces), gri...  28.1 us
    pallas_call x8, Pallas kernels, conv_t(): pl.pallas_call(functools.partial(conv_t_kernel, len(dys)), grid=(blocks,)...  26 us
    cond x224, local copies, waits for them, and re-layouts  25.6 us
    ppermute x12, starting transfers between devices, along(): return lax.ppermute(x, 'batch', [(z, (z + shift) % PLANES) for z in groups])  21.5 us
    pallas_call x8, Pallas kernels, conv(): pl.pallas_call(functools.partial(conv_kernel, len(xs)), grid=(width // ti...  21.3 us
  transfers between devices with their start and end apart: 93, of which 46 were waited for; matrix products, arithmetic and copies ran while one was open for 10% of the time, Pallas kernels for 13%

profile of v3, /device:TPU:0, one launch (start us, length us, event | category | flops | bytes accessed | tf_op | source)
XLA Modules:
  0.0 494.4 jit_solution(14141318083523817442)
XLA Ops:
  0.7 5.1 %collective-permute-start.168 = (s32[1,24]{1,0:T(1,128)}, s32[1,24]{1,0:T(1,128)S(1)}, u32[]{:S(2)}, u32[]{:S(2)}) collective-permute-start(s32[1,24]{1,0:T(1,128)} %param.12), channel_id=1, source_target_pairs={{0,3},{1,0},{2,1},{3,2},{4,7},{5,4},{6,5},{7,6},{8,11},{9,8},{10,9... | collective-permute-start | bytes 296 | tf_op jit(solution)/shard_map/ppermute | solution.py:580
  9.5 3.7 all-to-all-start.12
  18.7 3.6 all-to-all-done.12
  22.3 471.0 %conditional.1 = (bf16[1,112,2,2048]{3,2,1,0:T(2,128)(2,1)}, bf16[1,112,2,1024]{3,2,1,0:T(2,128)(2,1)}, f32[256,9,256]{2,0,1:T(8,128)}, f32[256]{0:T(256)}, f32[...) conditional(s32[]{:T(128)} %convert_element_type.375, (s32[1,24]{1,0:T(1,128)S(1)}, ...), branch_computations={%region_8.49_spmd, %region_49.90_spmd} | conditional | flops 53263933440 | bytes 630682432 | solution.py:588
  36.3 2.6 copy.73
  38.9 4.4 all-to-all-start.6
  45.2 2.5 collective-permute-start.84
  47.7 19.7 %collective-permute-done.85.refs_1_.refs_15_ = bf16[384,512]{1,0:T(8,128)(2,1)S(1)} collective-permute-done((bf16[384,512]{1,0:T(8,128)(2,1)S(1)}, bf16[384,512]{1,0:T(8,128)(2,1)S(1)}, u32[]{:S(2)}, u32[]{:S(2)}) %collective-permute-start.85) | collective-permute-done | bytes 393248 | tf_op jit(solution)/shard_map/cond/branch_1_fun/ppermute | solution.py:630
  68.2 4.1 all-to-all-start.7
  74.8 4.3 branch_1_fun.21.refs_4_.refs_1_
  79.1 2.7 copy-done.7
  82.9 20.9 %collective-permute-done.86.refs_0_.refs_10_ = bf16[384,512]{1,0:T(8,128)(2,1)} collective-permute-done((bf16[384,512]{1,0:T(8,128)(2,1)}, bf16[384,512]{1,0:T(8,128)(2,1)}, u32[]{:S(2)}, u32[]{:S(2)}) %collective-permute-start.86) | collective-permute-done | bytes 393248 | tf_op jit(solution)/shard_map/cond/branch_1_fun/ppermute | solution.py:633
  104.4 4.4 collective-permute-start.93
  129.9 2.5 branch_1_fun.24
  140.4 4.1 collective-permute-done.98
  144.6 3.0 collective-permute-done.100
  154.8 5.1 %collective-permute-done.105.refs_3_.refs_11_ = bf16[384,256]{1,0:T(8,128)(2,1)S(1)} collective-permute-done((bf16[384,256]{1,0:T(8,128)(2,1)S(1)}, bf16[384,256]{1,0:T(8,128)(2,1)S(1)}, u32[]{:S(2)}, u32[]{:S(2)}) %collective-permute-start.105) | collective-permute-done | bytes 196640 | tf_op jit(solution)/shard_map/cond/branch_1_fun/ppermute | solution.py:630
  159.9 3.8 collective-permute-done.104.refs_2_.refs_10_
  163.7 2.9 copy-done.8
  166.6 3.3 branch_1_fun.27
  170.0 3.1 collective-permute-start.115
  176.6 5.3 %collective-permute-done.108.refs_3_.refs_15_ = bf16[384,256]{1,0:T(8,128)(2,1)S(1)} collective-permute-done((bf16[384,256]{1,0:T(8,128)(2,1)S(1)}, bf16[384,256]{1,0:T(8,128)(2,1)S(1)}, u32[]{:S(2)}, u32[]{:S(2)}) %collective-permute-start.108) | collective-permute-done | bytes 196640 | tf_op jit(solution)/shard_map/cond/branch_1_fun/ppermute | solution.py:630
  181.9 2.5 collective-permute-done.107.refs_2_.refs_14_
  184.5 3.4 branch_1_fun.28
  187.9 3.9 collective-permute-done.115
  196.9 5.1 %collective-permute-done.111.refs_3_.refs_19_ = bf16[384,256]{1,0:T(8,128)(2,1)S(1)} collective-permute-done((bf16[384,256]{1,0:T(8,128)(2,1)S(1)}, bf16[384,256]{1,0:T(8,128)(2,1)S(1)}, u32[]{:S(2)}, u32[]{:S(2)}) %collective-permute-start.111) | collective-permute-done | bytes 196640 | tf_op jit(solution)/shard_map/cond/branch_1_fun/ppermute | solution.py:630
  204.1 3.4 branch_1_fun.29
  209.0 2.8 copy.99
  211.8 4.2 all-to-all-start.8
  221.3 2.9 collective-permute-start.114
  225.5 9.2 %collective-permute-done.114.refs_3_.refs_7_ = bf16[384,256]{1,0:T(8,128)(2,1)S(1)} collective-permute-done((bf16[384,256]{1,0:T(8,128)(2,1)S(1)}, bf16[384,256]{1,0:T(8,128)(2,1)S(1)}, u32[]{:S(2)}, u32[]{:S(2)}) %collective-permute-start.114) | collective-permute-done | bytes 196640 | tf_op jit(solution)/shard_map/cond/branch_1_fun/ppermute | solution.py:630
  234.7 2.8 collective-permute-done.113.refs_2_.refs_6_
  237.6 2.8 copy-done.9
  240.4 3.4 branch_1_fun.30
  247.7 3.4 collective-permute-start.122
  253.1 2.5 collective-permute-done.121
  255.8 2.7 fusion.186
  270.9 2.8 copy-done.10
  273.7 4.4 branch_1_fun.31
  284.4 3.1 reshape.347
  287.5 4.0 collective-permute-done.129
  292.9 2.8 copy-done.11
  295.7 4.4 branch_1_fun.32
  303.7 4.2 all-to-all-start.9
  312.3 3.1 copy-done.12
  315.3 4.4 branch_1_fun.33
  323.4 3.1 copy.69
  326.4 3.1 reshape.348
  331.4 2.8 copy-done.13
  334.2 4.5 branch_1_fun.34
  352.7 5.5 %collective-permute-done.144.refs_1_ = bf16[384,256]{1,0:T(8,128)(2,1)S(1)} collective-permute-done((bf16[384,256]{1,0:T(8,128)(2,1)S(1)}, bf16[384,256]{1,0:T(8,128)(2,1)S(1)}, u32[]{:S(2)}, u32[]{:S(2)}) %collective-permute-start.144) | collective-permute-done | bytes 196640 | tf_op jit(solution)/shard_map/cond/branch_1_fun/ppermute | solution.py:630
  375.0 10.8 %branch_1_fun.39 = (f32[4,9,128,128]{3,2,1,0:T(8,128)}, bf16[4,9,128,128]{3,2,1,0:T(8,128)(2,1)}) custom-call(s32[3]{0:T(128)} %copy-done.41, bf16[384,256]{1,0:T(8,128)(2,1)} %copy-done.33, bf16[384,256]{1,0:T(8,128)(2,1)} %copy-done.85, bf16[384,256]{1,0:T(8,128)(2,1)} %copy-done.32, bf16[384,256]{1,0:T(8,128)(2,1)} %copy-done.86, ...), custom_call_target="tpu_custom_call" | custom-call | flops 4831838208 | bytes 4718592 | tf_op jit(solution)/shard_map/cond/branch_1_fun/pallas_call | solution.py:496
  388.9 3.1 add_convert_fusion.7
  392.0 7.2 %collective-permute-done.152 = bf16[384,512]{1,0:T(8,128)(2,1)S(1)} collective-permute-done((bf16[384,512]{1,0:T(8,128)(2,1)S(1)}, bf16[384,512]{1,0:T(8,128)(2,1)S(1)}, u32[]{:S(2)}, u32[]{:S(2)}) %collective-permute-start.152) | collective-permute-done | bytes 393248 | tf_op jit(solution)/shard_map/cond/branch_1_fun/ppermute | solution.py:633
  400.6 17.3 %branch_1_fun.40 = (f32[9,256,512]{2,1,0:T(8,128)}, bf16[9,256,512]{2,1,0:T(8,128)(2,1)}) custom-call(s32[3]{0:T(128)} %copy-done.41, bf16[384,1024]{1,0:T(8,128)(2,1)} %copy-done.19, bf16[384,1024]{1,0:T(8,128)(2,1)} %copy-done.44, bf16[384,1024]{1,0:T(8,128)(2,1)} %copy-done.45, bf16[384,1024]{1,0:T(8,128)(2,1)} %copy-done.46, ...), custom_call_target="tpu_custom_call" | custom-call | flops 9663676416 | bytes 6291456 | tf_op jit(solution)/shard_map/cond/branch_1_fun/pallas_call | solution.py:496
  418.2 3.9 all-to-all-start.11
  426.1 2.7 collective-permute-start.155
  428.8 6.1 %convert_add_fusion.6 = f32[9,256,512]{2,1,0:T(8,128)} fusion(f32[9,256,512]{2,1,0:T(8,128)} %get-tuple-element.235, bf16[9,256,512]{2,1,0:T(8,128)(2,1)} %collective-permute-done.156), kind=kLoop, calls=%fused_computation.278 | loop fusion | flops 2359296 | bytes 11796480 | tf_op jit(solution)/shard_map/cond/branch_1_fun/add | solution.py:864
  435.0 19.5 %collective-permute-done.155 = bf16[384,512]{1,0:T(8,128)(2,1)S(1)} collective-permute-done((bf16[384,512]{1,0:T(8,128)(2,1)S(1)}, bf16[384,512]{1,0:T(8,128)(2,1)S(1)}, u32[]{:S(2)}, u32[]{:S(2)}) %collective-permute-start.155) | collective-permute-done | bytes 393248 | tf_op jit(solution)/shard_map/cond/branch_1_fun/ppermute | solution.py:633
  457.1 6.1 %collective-permute-start.164 = (f32[2,256]{1,0:T(2,128)S(1)}, f32[2,256]{1,0:T(2,128)S(1)}, u32[]{:S(2)}, u32[]{:S(2)}) collective-permute-start(f32[2,256]{1,0:T(2,128)S(1)} %constant_dynamic-update-slice_fusion.2), channel_id=1, source_target_pairs={{0,2},{4,6},{9,11},{13,15},{18,16},{22,20},{27,25},{31,29}} | collective-permute-start | bytes 6152 | tf_op jit(solution)/shard_map/cond/branch_1_fun/ppermute | solution.py:637
  467.2 4.7 all-to-all-start.10
  475.5 8.5 %collective-permute-done.159.refs_2_ = bf16[9,128,128]{2,1,0:T(8,128)(2,1)S(1)} collective-permute-done((bf16[9,128,128]{2,1,0:T(8,128)(2,1)S(1)}, bf16[9,128,128]{2,1,0:T(8,128)(2,1)S(1)}, u32[]{:S(2)}, u32[]{:S(2)}) %collective-permute-start.159) | collective-permute-done | bytes 294944 | tf_op jit(solution)/shard_map/cond/branch_1_fun/ppermute | solution.py:630
  484.0 2.4 collective-permute-done.158.refs_1_
  487.1 4.2 branch_1_fun.41
  (499 shorter events, 163.2 us)
Async XLA Ops:
  0.7 13.9 %collective-permute-start.168 = (s32[1,24]{1,0:T(1,128)}, s32[1,24]{1,0:T(1,128)S(1)}, u32[]{:S(2)}, u32[]{:S(2)}) collective-permute-start(s32[1,24]{1,0:T(1,128)} %param.12), channel_id=1, source_target_pairs={{0,3},{1,0},{2,1},{3,2},{4,7},{5,4},{6,5},{7,6},{8,11},{9,8},{10,9... | collective-permute-start | bytes 296 | tf_op jit(solution)/shard_map/ppermute | solution.py:580
  5.8 8.8 %collective-permute-start.167 = (s32[1,24]{1,0:T(1,128)}, s32[1,24]{1,0:T(1,128)S(1)}, u32[]{:S(2)}, u32[]{:S(2)}) collective-permute-start(s32[1,24]{1,0:T(1,128)} %param.12), channel_id=1, source_target_pairs={{0,2},{1,3},{2,0},{3,1},{4,6},{5,7},{6,4},{7,5},{8,10},{9,11},{10,... | collective-permute-start | bytes 296 | tf_op jit(solution)/shard_map/ppermute | solution.py:580
  5.8 8.8 %collective-permute-start.166 = (s32[1,24]{1,0:T(1,128)}, s32[1,24]{1,0:T(1,128)S(1)}, u32[]{:S(2)}, u32[]{:S(2)}) collective-permute-start(s32[1,24]{1,0:T(1,128)} %param.12), channel_id=1, source_target_pairs={{0,1},{1,2},{2,3},{3,0},{4,5},{5,6},{6,7},{7,4},{8,9},{9,10},{10,1... | collective-permute-start | bytes 296 | tf_op jit(solution)/shard_map/ppermute | solution.py:580
  9.5 12.8 %all-to-all-start.12 = ((bf16[8,112,256]{2,1,0:T(8,128)(2,1)}), bf16[8,112,256]{2,1,0:T(8,128)(2,1)S(1)}, u32[]{:S(2)}, u32[]{:S(2)}) async-start(bf16[8,112,256]{2,1,0:T(8,128)(2,1)} %all_to_all.44), calls=%async_computation.12 | async-start | bytes 917504 | tf_op jit(solution)/shard_map/all_to_all | solution.py:578
  36.1 38.7 %collective-permute-start.88 = (bf16[9,256,512]{2,1,0:T(8,128)(2,1)}, bf16[9,256,512]{2,1,0:T(8,128)(2,1)S(1)}, u32[]{:S(2)}, u32[]{:S(2)}) collective-permute-start(bf16[9,256,512]{2,1,0:T(8,128)(2,1)} %bitcast.521), channel_id=1, source_target_pairs={{0,4},{4,0},{8,12},{12,8},{16,20},{20,16},{24,28},{28,24},{1,5},{5... | collective-permute-start | bytes 7077896 | tf_op jit(solution)/shard_map/cond/branch_1_fun/ppermute | solution.py:630
  38.9 29.4 %all-to-all-start.6 = ((bf16[4,9,128,128]{3,2,1,0:T(8,128)(2,1)}), bf16[4,9,128,128]{3,2,1,0:T(8,128)(2,1)}, u32[]{:S(2)}, u32[]{:S(2)}) async-start(bf16[4,9,128,128]{3,2,1,0:T(8,128)(2,1)} %bitcast.524), calls=%async_computation.6 | async-start | bytes 2359296 | tf_op jit(solution)/shard_map/cond/branch_1_fun/all_to_all | solution.py:663
  43.3 24.2 %collective-permute-start.85 = (bf16[384,512]{1,0:T(8,128)(2,1)S(1)}, bf16[384,512]{1,0:T(8,128)(2,1)S(1)}, u32[]{:S(2)}, u32[]{:S(2)}) collective-permute-start(bf16[384,512]{1,0:T(8,128)(2,1)S(1)} %pad_maximum_fusion.8.refs_0_.refs_14_), channel_id=1, source_target_pairs={{0,16},{4,20},{8,24},{12,28},{16,0},{20,4},{24,8},{28,12},{1,17},{... | collective-permute-start | bytes 1179656 | tf_op jit(solution)/shard_map/cond/branch_1_fun/ppermute | solution.py:630
  45.2 23.0 %collective-permute-start.84 = (bf16[384,512]{1,0:T(8,128)(2,1)S(1)}, bf16[384,512]{1,0:T(8,128)(2,1)}, u32[]{:S(2)}, u32[]{:S(2)}) collective-permute-start(bf16[384,512]{1,0:T(8,128)(2,1)S(1)} %pad_maximum_fusion.8.refs_0_.refs_14_), channel_id=1, source_target_pairs={{0,1},{1,2},{2,3},{3,0},{4,5},{5,6},{6,7},{7,4},{8,9},{9,10},{10,1... | collective-permute-start | bytes 1179656 | tf_op jit(solution)/shard_map/cond/branch_1_fun/ppermute | solution.py:633
  68.2 49.2 %all-to-all-start.7 = ((bf16[4,9,128,128]{3,2,1,0:T(8,128)(2,1)}), bf16[4,9,128,128]{3,2,1,0:T(8,128)(2,1)S(1)}, u32[]{:S(2)}, u32[]{:S(2)}) async-start(bf16[4,9,128,128]{3,2,1,0:T(8,128)(2,1)} %all-to-all-done.6), calls=%async_computation.7 | async-start | bytes 2359296 | tf_op jit(solution)/shard_map/cond/branch_1_fun/all_to_all | solution.py:685
  72.3 10.6 %collective-permute-start.87 = (bf16[384,512]{1,0:T(8,128)(2,1)}, bf16[384,512]{1,0:T(8,128)(2,1)}, u32[]{:S(2)}, u32[]{:S(2)}) collective-permute-start(bf16[384,512]{1,0:T(8,128)(2,1)} %collective-permute-done.84.refs_0_.refs_8_), channel_id=1, source_target_pairs={{0,16},{4,20},{8,24},{12,28},{16,0},{20,4},{24,8},{28,12},{1,17},{... | collective-permute-start | bytes 1179656 | tf_op jit(solution)/shard_map/cond/branch_1_fun/ppermute | solution.py:630
  72.6 31.2 %collective-permute-start.86 = (bf16[384,512]{1,0:T(8,128)(2,1)}, bf16[384,512]{1,0:T(8,128)(2,1)}, u32[]{:S(2)}, u32[]{:S(2)}) collective-permute-start(bf16[384,512]{1,0:T(8,128)(2,1)} %collective-permute-done.84.refs_0_.refs_8_), channel_id=1, source_target_pairs={{0,1},{1,2},{2,3},{3,0},{4,5},{5,6},{6,7},{7,4},{8,9},{9,10},{10,1... | collective-permute-start | bytes 1179656 | tf_op jit(solution)/shard_map/cond/branch_1_fun/ppermute | solution.py:633
  103.8 12.2 %collective-permute-start.94 = (bf16[384,512]{1,0:T(8,128)(2,1)}, bf16[384,512]{1,0:T(8,128)(2,1)S(1)}, u32[]{:S(2)}, u32[]{:S(2)}) collective-permute-start(bf16[384,512]{1,0:T(8,128)(2,1)} %collective-permute-done.86.refs_0_.refs_10_), channel_id=1, source_target_pairs={{0,16},{4,20},{8,24},{12,28},{16,0},{20,4},{24,8},{28,12},{1,17},{... | collective-permute-start | bytes 1179656 | tf_op jit(solution)/shard_map/cond/branch_1_fun/ppermute | solution.py:630
  104.4 12.1 %collective-permute-start.93 = (bf16[384,512]{1,0:T(8,128)(2,1)}, bf16[384,512]{1,0:T(8,128)(2,1)S(1)}, u32[]{:S(2)}, u32[]{:S(2)}) collective-permute-start(bf16[384,512]{1,0:T(8,128)(2,1)} %collective-permute-done.86.refs_0_.refs_10_), channel_id=1, source_target_pairs={{0,1},{1,2},{2,3},{3,0},{4,5},{5,6},{6,7},{7,4},{8,9},{9,10},{10,1... | collective-permute-start | bytes 1179656 | tf_op jit(solution)/shard_map/cond/branch_1_fun/ppermute | solution.py:633
  123.6 13.4 %collective-permute-start.99 = (bf16[384,512]{1,0:T(8,128)(2,1)S(1)}, bf16[384,512]{1,0:T(8,128)(2,1)S(1)}, u32[]{:S(2)}, u32[]{:S(2)}) collective-permute-start(bf16[384,512]{1,0:T(8,128)(2,1)S(1)} %collective-permute-done.93.refs_0_.refs_12_), channel_id=1, source_target_pairs={{0,16},{4,20},{8,24},{12,28},{16,0},{20,4},{24,8},{28,12},{1,17},{... | collective-permute-start | bytes 1179656 | tf_op jit(solution)/shard_map/cond/branch_1_fun/ppermute | solution.py:630
  127.7 10.9 %collective-permute-start.97 = (bf16[384,256]{1,0:T(8,128)(2,1)S(1)}, bf16[384,256]{1,0:T(8,128)(2,1)S(1)}, u32[]{:S(2)}, u32[]{:S(2)}) collective-permute-start(bf16[384,256]{1,0:T(8,128)(2,1)S(1)} %get-tuple-element.163), channel_id=1, source_target_pairs={{0,8},{4,12},{8,0},{12,4},{16,24},{20,28},{24,16},{28,20},{1,9},{5... | collective-permute-start | bytes 589832 | tf_op jit(solution)/shard_map/cond/branch_1_fun/ppermute | solution.py:630
  134.9 9.6 %collective-permute-start.98 = (bf16[384,256]{1,0:T(8,128)(2,1)S(1)}, bf16[384,256]{1,0:T(8,128)(2,1)S(1)}, u32[]{:S(2)}, u32[]{:S(2)}) collective-permute-start(bf16[384,256]{1,0:T(8,128)(2,1)S(1)} %get-tuple-element.170), channel_id=1, source_target_pairs={{0,8},{4,12},{8,0},{12,4},{16,24},{20,28},{24,16},{28,20},{1,9},{5... | collective-permute-start | bytes 589832 | tf_op jit(solution)/shard_map/cond/branch_1_fun/ppermute | solution.py:630
  138.4 9.2 %collective-permute-start.100 = (bf16[384,256]{1,0:T(8,128)(2,1)S(1)}, bf16[384,256]{1,0:T(8,128)(2,1)S(1)}, u32[]{:S(2)}, u32[]{:S(2)}) collective-permute-start(bf16[384,256]{1,0:T(8,128)(2,1)S(1)} %get-tuple-element.175), channel_id=1, source_target_pairs={{0,8},{4,12},{8,0},{12,4},{16,24},{20,28},{24,16},{28,20},{1,9},{5... | collective-permute-start | bytes 589832 | tf_op jit(solution)/shard_map/cond/branch_1_fun/ppermute | solution.py:630
  151.2 8.7 %collective-permute-start.105 = (bf16[384,256]{1,0:T(8,128)(2,1)S(1)}, bf16[384,256]{1,0:T(8,128)(2,1)S(1)}, u32[]{:S(2)}, u32[]{:S(2)}) collective-permute-start(bf16[384,256]{1,0:T(8,128)(2,1)S(1)} %get-tuple-element.503.refs_0_.refs_8_), channel_id=1, source_target_pairs={{0,24},{4,28},{8,16},{12,20},{16,8},{20,12},{24,0},{28,4},{1,25},{... | collective-permute-start | bytes 589832 | tf_op jit(solution)/shard_map/cond/branch_1_fun/ppermute | solution.py:630
  152.9 10.8 %collective-permute-start.104 = (bf16[384,256]{1,0:T(8,128)(2,1)S(1)}, bf16[384,256]{1,0:T(8,128)(2,1)S(1)}, u32[]{:S(2)}, u32[]{:S(2)}) collective-permute-start(bf16[384,256]{1,0:T(8,128)(2,1)S(1)} %get-tuple-element.503.refs_0_.refs_8_), channel_id=1, source_target_pairs={{0,16},{4,20},{8,24},{12,28},{16,0},{20,4},{24,8},{28,12},{1,17},{... | collective-permute-start | bytes 589832 | tf_op jit(solution)/shard_map/cond/branch_1_fun/ppermute | solution.py:630
  154.5 9.2 %collective-permute-start.103 = (bf16[384,256]{1,0:T(8,128)(2,1)S(1)}, bf16[384,256]{1,0:T(8,128)(2,1)S(1)}, u32[]{:S(2)}, u32[]{:S(2)}) collective-permute-start(bf16[384,256]{1,0:T(8,128)(2,1)S(1)} %get-tuple-element.503.refs_0_.refs_8_), channel_id=1, source_target_pairs={{0,8},{4,12},{8,0},{12,4},{16,24},{20,28},{24,16},{28,20},{1,9},{5... | collective-permute-start | bytes 589832 | tf_op jit(solution)/shard_map/cond/branch_1_fun/ppermute | solution.py:630
  170.0 21.8 %collective-permute-start.115 = (bf16[384,1024]{1,0:T(8,128)(2,1)S(1)}, bf16[384,1024]{1,0:T(8,128)(2,1)S(1)}, u32[]{:S(2)}, u32[]{:S(2)}) collective-permute-start(bf16[384,1024]{1,0:T(8,128)(2,1)S(1)} %branch_1_fun.27), channel_id=1, source_target_pairs={{0,1},{1,2},{2,3},{3,0},{4,5},{5,6},{6,7},{7,4},{8,9},{9,10},{10,1... | collective-permute-start | bytes 2359304 | tf_op jit(solution)/shard_map/cond/branch_1_fun/ppermute | solution.py:633
  173.1 8.8 %collective-permute-start.108 = (bf16[384,256]{1,0:T(8,128)(2,1)S(1)}, bf16[384,256]{1,0:T(8,128)(2,1)S(1)}, u32[]{:S(2)}, u32[]{:S(2)}) collective-permute-start(bf16[384,256]{1,0:T(8,128)(2,1)S(1)} %get-tuple-element.179.refs_0_.refs_12_), channel_id=1, source_target_pairs={{0,24},{4,28},{8,16},{12,20},{16,8},{20,12},{24,0},{28,4},{1,25},{... | collective-permute-start | bytes 589832 | tf_op jit(solution)/shard_map/cond/branch_1_fun/ppermute | solution.py:630
  174.3 10.2 %collective-permute-start.107 = (bf16[384,256]{1,0:T(8,128)(2,1)S(1)}, bf16[384,256]{1,0:T(8,128)(2,1)S(1)}, u32[]{:S(2)}, u32[]{:S(2)}) collective-permute-start(bf16[384,256]{1,0:T(8,128)(2,1)S(1)} %get-tuple-element.179.refs_0_.refs_12_), channel_id=1, source_target_pairs={{0,16},{4,20},{8,24},{12,28},{16,0},{20,4},{24,8},{28,12},{1,17},{... | collective-permute-start | bytes 589832 | tf_op jit(solution)/shard_map/cond/branch_1_fun/ppermute | solution.py:630
  175.7 8.7 %collective-permute-start.106 = (bf16[384,256]{1,0:T(8,128)(2,1)S(1)}, bf16[384,256]{1,0:T(8,128)(2,1)S(1)}, u32[]{:S(2)}, u32[]{:S(2)}) collective-permute-start(bf16[384,256]{1,0:T(8,128)(2,1)S(1)} %get-tuple-element.179.refs_0_.refs_12_), channel_id=1, source_target_pairs={{0,8},{4,12},{8,0},{12,4},{16,24},{20,28},{24,16},{28,20},{1,9},{5... | collective-permute-start | bytes 589832 | tf_op jit(solution)/shard_map/cond/branch_1_fun/ppermute | solution.py:630
  192.9 23.2 %collective-permute-start.116 = (bf16[384,1024]{1,0:T(8,128)(2,1)}, bf16[384,1024]{1,0:T(8,128)(2,1)}, u32[]{:S(2)}, u32[]{:S(2)}) collective-permute-start(bf16[384,1024]{1,0:T(8,128)(2,1)} %add_convert_fusion.9), channel_id=1, source_target_pairs={{0,1},{1,2},{2,3},{3,0},{4,5},{5,6},{6,7},{7,4},{8,9},{9,10},{10,1... | collective-permute-start | bytes 2359304 | tf_op jit(solution)/shard_map/cond/branch_1_fun/ppermute | solution.py:633
  193.4 8.6 %collective-permute-start.111 = (bf16[384,256]{1,0:T(8,128)(2,1)S(1)}, bf16[384,256]{1,0:T(8,128)(2,1)S(1)}, u32[]{:S(2)}, u32[]{:S(2)}) collective-permute-start(bf16[384,256]{1,0:T(8,128)(2,1)S(1)} %get-tuple-element.181.refs_0_.refs_16_), channel_id=1, source_target_pairs={{0,24},{4,28},{8,16},{12,20},{16,8},{20,12},{24,0},{28,4},{1,25},{... | collective-permute-start | bytes 589832 | tf_op jit(solution)/shard_map/cond/branch_1_fun/ppermute | solution.py:630
  194.8 9.2 %collective-permute-start.110 = (bf16[384,256]{1,0:T(8,128)(2,1)S(1)}, bf16[384,256]{1,0:T(8,128)(2,1)S(1)}, u32[]{:S(2)}, u32[]{:S(2)}) collective-permute-start(bf16[384,256]{1,0:T(8,128)(2,1)S(1)} %get-tuple-element.181.refs_0_.refs_16_), channel_id=1, source_target_pairs={{0,16},{4,20},{8,24},{12,28},{16,0},{20,4},{24,8},{28,12},{1,17},{... | collective-permute-start | bytes 589832 | tf_op jit(solution)/shard_map/cond/branch_1_fun/ppermute | solution.py:630
  211.8 32.7 %all-to-all-start.8 = ((bf16[8,112,2,256]{3,2,1,0:T(2,128)(2,1)}), bf16[8,112,2,256]{3,2,1,0:T(2,128)(2,1)}, u32[]{:S(2)}, u32[]{:S(2)}) async-start(bf16[8,112,2,256]{3,2,1,0:T(2,128)(2,1)} %bitcast.514), calls=%async_computation.8 | async-start | bytes 1835008 | tf_op jit(solution)/shard_map/cond/branch_1_fun/all_to_all | solution.py:746
  218.4 27.5 %collective-permute-start.117 = (bf16[384,1024]{1,0:T(8,128)(2,1)}, bf16[384,1024]{1,0:T(8,128)(2,1)S(1)}, u32[]{:S(2)}, u32[]{:S(2)}) collective-permute-start(bf16[384,1024]{1,0:T(8,128)(2,1)} %add_convert_fusion.8), channel_id=1, source_target_pairs={{0,1},{1,2},{2,3},{3,0},{4,5},{5,6},{6,7},{7,4},{8,9},{9,10},{10,1... | collective-permute-start | bytes 2359304 | tf_op jit(solution)/shard_map/cond/branch_1_fun/ppermute | solution.py:633
  221.3 13.4 %collective-permute-start.114 = (bf16[384,256]{1,0:T(8,128)(2,1)S(1)}, bf16[384,256]{1,0:T(8,128)(2,1)S(1)}, u32[]{:S(2)}, u32[]{:S(2)}) collective-permute-start(bf16[384,256]{1,0:T(8,128)(2,1)S(1)} %get-tuple-element.183.refs_0_.refs_4_), channel_id=1, source_target_pairs={{0,24},{4,28},{8,16},{12,20},{16,8},{20,12},{24,0},{28,4},{1,25},{... | collective-permute-start | bytes 589832 | tf_op jit(solution)/shard_map/cond/branch_1_fun/ppermute | solution.py:630
  224.2 13.4 %collective-permute-start.113 = (bf16[384,256]{1,0:T(8,128)(2,1)S(1)}, bf16[384,256]{1,0:T(8,128)(2,1)S(1)}, u32[]{:S(2)}, u32[]{:S(2)}) collective-permute-start(bf16[384,256]{1,0:T(8,128)(2,1)S(1)} %get-tuple-element.183.refs_0_.refs_4_), channel_id=1, source_target_pairs={{0,16},{4,20},{8,24},{12,28},{16,0},{20,4},{24,8},{28,12},{1,17},{... | collective-permute-start | bytes 589832 | tf_op jit(solution)/shard_map/cond/branch_1_fun/ppermute | solution.py:630
  224.7 12.8 %collective-permute-start.112 = (bf16[384,256]{1,0:T(8,128)(2,1)S(1)}, bf16[384,256]{1,0:T(8,128)(2,1)S(1)}, u32[]{:S(2)}, u32[]{:S(2)}) collective-permute-start(bf16[384,256]{1,0:T(8,128)(2,1)S(1)} %get-tuple-element.183.refs_0_.refs_4_), channel_id=1, source_target_pairs={{0,8},{4,12},{8,0},{12,4},{16,24},{20,28},{24,16},{28,20},{1,9},{5... | collective-permute-start | bytes 589832 | tf_op jit(solution)/shard_map/cond/branch_1_fun/ppermute | solution.py:630
  268.8 23.4 %collective-permute-start.127 = (bf16[384,1024]{1,0:T(8,128)(2,1)S(1)}, bf16[384,1024]{1,0:T(8,128)(2,1)S(1)}, u32[]{:S(2)}, u32[]{:S(2)}) collective-permute-start(bf16[384,1024]{1,0:T(8,128)(2,1)S(1)} %multiply_convert_fusion.11.refs_0_), channel_id=1, source_target_pairs={{0,1},{1,2},{2,3},{3,0},{4,5},{5,6},{6,7},{7,4},{8,9},{9,10},{10,1... | collective-permute-start | bytes 2359304 | tf_op jit(solution)/shard_map/cond/branch_1_fun/ppermute | solution.py:633
  278.8 8.7 %collective-permute-start.128 = (bf16[384,256]{1,0:T(8,128)(2,1)S(1)}, bf16[384,256]{1,0:T(8,128)(2,1)S(1)}, u32[]{:S(2)}, u32[]{:S(2)}) collective-permute-start(bf16[384,256]{1,0:T(8,128)(2,1)S(1)} %get-tuple-element.191), channel_id=1, source_target_pairs={{0,8},{4,12},{8,0},{12,4},{16,24},{20,28},{24,16},{28,20},{1,9},{5... | collective-permute-start | bytes 589832 | tf_op jit(solution)/shard_map/cond/branch_1_fun/ppermute | solution.py:630
  280.3 11.2 %collective-permute-start.129 = (bf16[384,256]{1,0:T(8,128)(2,1)S(1)}, bf16[384,256]{1,0:T(8,128)(2,1)S(1)}, u32[]{:S(2)}, u32[]{:S(2)}) collective-permute-start(bf16[384,256]{1,0:T(8,128)(2,1)S(1)} %get-tuple-element.192), channel_id=1, source_target_pairs={{0,16},{4,20},{8,24},{12,28},{16,0},{20,4},{24,8},{28,12},{1,17},{... | collective-permute-start | bytes 589832 | tf_op jit(solution)/shard_map/cond/branch_1_fun/ppermute | solution.py:630
  280.9 10.6 %collective-permute-start.130 = (bf16[384,256]{1,0:T(8,128)(2,1)S(1)}, bf16[384,256]{1,0:T(8,128)(2,1)S(1)}, u32[]{:S(2)}, u32[]{:S(2)}) collective-permute-start(bf16[384,256]{1,0:T(8,128)(2,1)S(1)} %get-tuple-element.193), channel_id=1, source_target_pairs={{0,24},{4,28},{8,16},{12,20},{16,8},{20,12},{24,0},{28,4},{1,25},{... | collective-permute-start | bytes 589832 | tf_op jit(solution)/shard_map/cond/branch_1_fun/ppermute | solution.py:630
  292.2 20.1 %collective-permute-start.132 = (bf16[384,1024]{1,0:T(8,128)(2,1)S(1)}, bf16[384,1024]{1,0:T(8,128)(2,1)S(1)}, u32[]{:S(2)}, u32[]{:S(2)}) collective-permute-start(bf16[384,1024]{1,0:T(8,128)(2,1)S(1)} %collective-permute-done.127.refs_0_.refs_1_), channel_id=1, source_target_pairs={{0,1},{1,2},{2,3},{3,0},{4,5},{5,6},{6,7},{7,4},{8,9},{9,10},{10,1... | collective-permute-start | bytes 2359304 | tf_op jit(solution)/shard_map/cond/branch_1_fun/ppermute | solution.py:633
  300.8 9.5 %collective-permute-start.134 = (bf16[384,256]{1,0:T(8,128)(2,1)S(1)}, bf16[384,256]{1,0:T(8,128)(2,1)S(1)}, u32[]{:S(2)}, u32[]{:S(2)}) collective-permute-start(bf16[384,256]{1,0:T(8,128)(2,1)S(1)} %get-tuple-element.198), channel_id=1, source_target_pairs={{0,16},{4,20},{8,24},{12,28},{16,0},{20,4},{24,8},{28,12},{1,17},{... | collective-permute-start | bytes 589832 | tf_op jit(solution)/shard_map/cond/branch_1_fun/ppermute | solution.py:630
  302.3 8.0 %collective-permute-start.135 = (bf16[384,256]{1,0:T(8,128)(2,1)S(1)}, bf16[384,256]{1,0:T(8,128)(2,1)}, u32[]{:S(2)}, u32[]{:S(2)}) collective-permute-start(bf16[384,256]{1,0:T(8,128)(2,1)S(1)} %get-tuple-element.199), channel_id=1, source_target_pairs={{0,24},{4,28},{8,16},{12,20},{16,8},{20,12},{24,0},{28,4},{1,25},{... | collective-permute-start | bytes 589832 | tf_op jit(solution)/shard_map/cond/branch_1_fun/ppermute | solution.py:630
  303.7 19.7 %all-to-all-start.9 = ((bf16[8,112,2,256]{3,2,1,0:T(2,128)(2,1)}), bf16[8,112,2,256]{3,2,1,0:T(2,128)(2,1)}, u32[]{:S(2)}, u32[]{:S(2)}) async-start(bf16[8,112,2,256]{3,2,1,0:T(2,128)(2,1)} %reshape.347), calls=%async_computation.9 | async-start | bytes 1835008 | tf_op jit(solution)/shard_map/cond/branch_1_fun/all_to_all | solution.py:788
  312.3 19.1 %collective-permute-start.136 = (bf16[384,1024]{1,0:T(8,128)(2,1)S(1)}, bf16[384,1024]{1,0:T(8,128)(2,1)S(1)}, u32[]{:S(2)}, u32[]{:S(2)}) collective-permute-start(bf16[384,1024]{1,0:T(8,128)(2,1)S(1)} %collective-permute-done.132.refs_0_.refs_2_), channel_id=1, source_target_pairs={{0,1},{1,2},{2,3},{3,0},{4,5},{5,6},{6,7},{7,4},{8,9},{9,10},{10,1... | collective-permute-start | bytes 2359304 | tf_op jit(solution)/shard_map/cond/branch_1_fun/ppermute | solution.py:633
  319.8 9.8 %collective-permute-start.137 = (bf16[384,256]{1,0:T(8,128)(2,1)S(1)}, bf16[384,256]{1,0:T(8,128)(2,1)}, u32[]{:S(2)}, u32[]{:S(2)}) collective-permute-start(bf16[384,256]{1,0:T(8,128)(2,1)S(1)} %get-tuple-element.201), channel_id=1, source_target_pairs={{0,8},{4,12},{8,0},{12,4},{16,24},{20,28},{24,16},{28,20},{1,9},{5... | collective-permute-start | bytes 589832 | tf_op jit(solution)/shard_map/cond/branch_1_fun/ppermute | solution.py:630
  320.5 10.0 %collective-permute-start.138 = (bf16[384,256]{1,0:T(8,128)(2,1)S(1)}, bf16[384,256]{1,0:T(8,128)(2,1)}, u32[]{:S(2)}, u32[]{:S(2)}) collective-permute-start(bf16[384,256]{1,0:T(8,128)(2,1)S(1)} %get-tuple-element.202), channel_id=1, source_target_pairs={{0,16},{4,20},{8,24},{12,28},{16,0},{20,4},{24,8},{28,12},{1,17},{... | collective-permute-start | bytes 589832 | tf_op jit(solution)/shard_map/cond/branch_1_fun/ppermute | solution.py:630
  321.9 8.6 %collective-permute-start.139 = (bf16[384,256]{1,0:T(8,128)(2,1)S(1)}, bf16[384,256]{1,0:T(8,128)(2,1)}, u32[]{:S(2)}, u32[]{:S(2)}) collective-permute-start(bf16[384,256]{1,0:T(8,128)(2,1)S(1)} %get-tuple-element.203), channel_id=1, source_target_pairs={{0,24},{4,28},{8,16},{12,20},{16,8},{20,12},{24,0},{28,4},{1,25},{... | collective-permute-start | bytes 589832 | tf_op jit(solution)/shard_map/cond/branch_1_fun/ppermute | solution.py:630
  359.7 10.6 %collective-permute-start.146 = (bf16[384,256]{1,0:T(8,128)(2,1)S(1)}, bf16[384,256]{1,0:T(8,128)(2,1)S(1)}, u32[]{:S(2)}, u32[]{:S(2)}) collective-permute-start(bf16[384,256]{1,0:T(8,128)(2,1)S(1)} %get-tuple-element.215.refs_0_.refs_4_), channel_id=1, source_target_pairs={{0,8},{4,12},{8,0},{12,4},{16,24},{20,28},{24,16},{28,20},{1,9},{5... | collective-permute-start | bytes 589832 | tf_op jit(solution)/shard_map/cond/branch_1_fun/ppermute | solution.py:630
  362.3 12.6 %collective-permute-start.151 = (bf16[384,512]{1,0:T(8,128)(2,1)S(1)}, bf16[384,512]{1,0:T(8,128)(2,1)S(1)}, u32[]{:S(2)}, u32[]{:S(2)}) collective-permute-start(bf16[384,512]{1,0:T(8,128)(2,1)S(1)} %get-tuple-element.217), channel_id=1, source_target_pairs={{0,16},{4,20},{8,24},{12,28},{16,0},{20,4},{24,8},{28,12},{1,17},{... | collective-permute-start | bytes 1179656 | tf_op jit(solution)/shard_map/cond/branch_1_fun/ppermute | solution.py:630
  363.8 9.0 %collective-permute-start.145 = (bf16[384,256]{1,0:T(8,128)(2,1)S(1)}, bf16[384,256]{1,0:T(8,128)(2,1)S(1)}, u32[]{:S(2)}, u32[]{:S(2)}) collective-permute-start(bf16[384,256]{1,0:T(8,128)(2,1)S(1)} %get-tuple-element.214.refs_0_.refs_6_), channel_id=1, source_target_pairs={{0,8},{4,12},{8,0},{12,4},{16,24},{20,28},{24,16},{28,20},{1,9},{5... | collective-permute-start | bytes 589832 | tf_op jit(solution)/shard_map/cond/branch_1_fun/ppermute | solution.py:630
  385.9 13.3 %collective-permute-start.152 = (bf16[384,512]{1,0:T(8,128)(2,1)S(1)}, bf16[384,512]{1,0:T(8,128)(2,1)S(1)}, u32[]{:S(2)}, u32[]{:S(2)}) collective-permute-start(bf16[384,512]{1,0:T(8,128)(2,1)S(1)} %add_convert_fusion.13), channel_id=1, source_target_pairs={{0,1},{1,2},{2,3},{3,0},{4,5},{5,6},{6,7},{7,4},{8,9},{9,10},{10,1... | collective-permute-start | bytes 1179656 | tf_op jit(solution)/shard_map/cond/branch_1_fun/ppermute | solution.py:633
  386.5 12.7 %collective-permute-start.150 = (bf16[384,512]{1,0:T(8,128)(2,1)S(1)}, bf16[384,512]{1,0:T(8,128)(2,1)S(1)}, u32[]{:S(2)}, u32[]{:S(2)}) collective-permute-start(bf16[384,512]{1,0:T(8,128)(2,1)S(1)} %get-tuple-element.219), channel_id=1, source_target_pairs={{0,16},{4,20},{8,24},{12,28},{16,0},{20,4},{24,8},{28,12},{1,17},{... | collective-permute-start | bytes 1179656 | tf_op jit(solution)/shard_map/cond/branch_1_fun/ppermute | solution.py:630
  387.5 30.4 %collective-permute-start.149 = (bf16[384,512]{1,0:T(8,128)(2,1)S(1)}, bf16[384,512]{1,0:T(8,128)(2,1)S(1)}, u32[]{:S(2)}, u32[]{:S(2)}) collective-permute-start(bf16[384,512]{1,0:T(8,128)(2,1)S(1)} %get-tuple-element.221), channel_id=1, source_target_pairs={{0,16},{4,20},{8,24},{12,28},{16,0},{20,4},{24,8},{28,12},{1,17},{... | collective-permute-start | bytes 1179656 | tf_op jit(solution)/shard_map/cond/branch_1_fun/ppermute | solution.py:630
  399.4 18.5 %collective-permute-start.154 = (bf16[384,512]{1,0:T(8,128)(2,1)S(1)}, bf16[384,512]{1,0:T(8,128)(2,1)S(1)}, u32[]{:S(2)}, u32[]{:S(2)}) collective-permute-start(bf16[384,512]{1,0:T(8,128)(2,1)S(1)} %add_convert_fusion.12), channel_id=1, source_target_pairs={{0,1},{1,2},{2,3},{3,0},{4,5},{5,6},{6,7},{7,4},{8,9},{9,10},{10,1... | collective-permute-start | bytes 1179656 | tf_op jit(solution)/shard_map/cond/branch_1_fun/ppermute | solution.py:633
  418.1 10.7 %collective-permute-start.156 = (bf16[9,256,512]{2,1,0:T(8,128)(2,1)}, bf16[9,256,512]{2,1,0:T(8,128)(2,1)}, u32[]{:S(2)}, u32[]{:S(2)}) collective-permute-start(bf16[9,256,512]{2,1,0:T(8,128)(2,1)} %get-tuple-element.236), channel_id=1, source_target_pairs={{0,4},{4,0},{8,12},{12,8},{16,20},{20,16},{24,28},{28,24},{1,5},{5... | collective-permute-start | bytes 7077896 | tf_op jit(solution)/shard_map/cond/branch_1_fun/ppermute | solution.py:630
  418.2 46.3 %all-to-all-start.11 = ((bf16[4,9,128,128]{3,2,1,0:T(8,128)(2,1)}), bf16[4,9,128,128]{3,2,1,0:T(8,128)(2,1)S(1)}, u32[]{:S(2)}, u32[]{:S(2)}) async-start(bf16[4,9,128,128]{3,2,1,0:T(8,128)(2,1)} %add_convert_fusion.7), calls=%async_computation.11 | async-start | bytes 2359296 | tf_op jit(solution)/shard_map/cond/branch_1_fun/all_to_all | solution.py:851
  423.3 31.1 %collective-permute-start.148 = (bf16[384,512]{1,0:T(8,128)(2,1)S(1)}, bf16[384,512]{1,0:T(8,128)(2,1)S(1)}, u32[]{:S(2)}, u32[]{:S(2)}) collective-permute-start(bf16[384,512]{1,0:T(8,128)(2,1)S(1)} %get-tuple-element.224), channel_id=1, source_target_pairs={{0,16},{4,20},{8,24},{12,28},{16,0},{20,4},{24,8},{28,12},{1,17},{... | collective-permute-start | bytes 1179656 | tf_op jit(solution)/shard_map/cond/branch_1_fun/ppermute | solution.py:630
  424.8 29.9 %collective-permute-start.162 = (f32[2,128]{1,0:T(2,128)S(1)}, f32[2,128]{1,0:T(2,128)S(1)}, u32[]{:S(2)}, u32[]{:S(2)}) collective-permute-start(f32[2,128]{1,0:T(2,128)S(1)} %fusion.162), channel_id=1, source_target_pairs={{16,0},{24,4},{17,9},{25,13},{18,18},{26,22},{19,27},{27,31}} | collective-permute-start | bytes 3080 | tf_op jit(solution)/shard_map/cond/branch_1_fun/ppermute | solution.py:637
  426.1 28.3 %collective-permute-start.155 = (bf16[384,512]{1,0:T(8,128)(2,1)S(1)}, bf16[384,512]{1,0:T(8,128)(2,1)S(1)}, u32[]{:S(2)}, u32[]{:S(2)}) collective-permute-start(bf16[384,512]{1,0:T(8,128)(2,1)S(1)} %add_convert_fusion.11), channel_id=1, source_target_pairs={{0,1},{1,2},{2,3},{3,0},{4,5},{5,6},{6,7},{7,4},{8,9},{9,10},{10,1... | collective-permute-start | bytes 1179656 | tf_op jit(solution)/shard_map/cond/branch_1_fun/ppermute | solution.py:633
  454.7 10.7 %collective-permute-start.157 = (bf16[384,256]{1,0:T(8,128)(2,1)S(1)}, bf16[384,256]{1,0:T(8,128)(2,1)S(1)}, u32[]{:S(2)}, u32[]{:S(2)}) collective-permute-start(bf16[384,256]{1,0:T(8,128)(2,1)S(1)} %get-tuple-element.487), channel_id=1, source_target_pairs={{0,4},{4,0},{8,12},{12,8},{16,20},{20,16},{24,28},{28,24},{1,5},{5... | collective-permute-start | bytes 589832 | tf_op jit(solution)/shard_map/cond/branch_1_fun/ppermute | solution.py:630
  454.8 17.2 %collective-permute-start.165 = (f32[2,256]{1,0:T(2,128)S(1)}, f32[2,256]{1,0:T(2,128)S(1)}, u32[]{:S(2)}, u32[]{:S(2)}) collective-permute-start(f32[2,256]{1,0:T(2,128)S(1)} %constant_dynamic-update-slice_fusion.2), channel_id=1, source_target_pairs={{0,3},{4,7},{9,8},{13,12},{18,17},{22,21},{27,26},{31,30}} | collective-permute-start | bytes 6152 | tf_op jit(solution)/shard_map/cond/branch_1_fun/ppermute | solution.py:637
  457.1 17.1 %collective-permute-start.164 = (f32[2,256]{1,0:T(2,128)S(1)}, f32[2,256]{1,0:T(2,128)S(1)}, u32[]{:S(2)}, u32[]{:S(2)}) collective-permute-start(f32[2,256]{1,0:T(2,128)S(1)} %constant_dynamic-update-slice_fusion.2), channel_id=1, source_target_pairs={{0,2},{4,6},{9,11},{13,15},{18,16},{22,20},{27,25},{31,29}} | collective-permute-start | bytes 6152 | tf_op jit(solution)/shard_map/cond/branch_1_fun/ppermute | solution.py:637
  463.2 11.0 %collective-permute-start.163 = (f32[2,256]{1,0:T(2,128)S(1)}, f32[2,256]{1,0:T(2,128)S(1)}, u32[]{:S(2)}, u32[]{:S(2)}) collective-permute-start(f32[2,256]{1,0:T(2,128)S(1)} %constant_dynamic-update-slice_fusion.2), channel_id=1, source_target_pairs={{0,1},{4,5},{9,10},{13,14},{18,19},{22,23},{27,24},{31,28}} | collective-permute-start | bytes 6152 | tf_op jit(solution)/shard_map/cond/branch_1_fun/ppermute | solution.py:637
  465.4 10.1 %collective-permute-start.160 = (bf16[9,128,128]{2,1,0:T(8,128)(2,1)S(1)}, bf16[9,128,128]{2,1,0:T(8,128)(2,1)S(1)}, u32[]{:S(2)}, u32[]{:S(2)}) collective-permute-start(bf16[9,128,128]{2,1,0:T(8,128)(2,1)S(1)} %get-tuple-element.476), channel_id=1, source_target_pairs={{0,24},{4,28},{8,16},{12,20},{16,8},{20,12},{24,0},{28,4},{1,25},{... | collective-permute-start | bytes 884744 | tf_op jit(solution)/shard_map/cond/branch_1_fun/ppermute | solution.py:630
  465.4 18.6 %collective-permute-start.159 = (bf16[9,128,128]{2,1,0:T(8,128)(2,1)S(1)}, bf16[9,128,128]{2,1,0:T(8,128)(2,1)S(1)}, u32[]{:S(2)}, u32[]{:S(2)}) collective-permute-start(bf16[9,128,128]{2,1,0:T(8,128)(2,1)S(1)} %get-tuple-element.477), channel_id=1, source_target_pairs={{0,16},{4,20},{8,24},{12,28},{16,0},{20,4},{24,8},{28,12},{1,17},{... | collective-permute-start | bytes 884744 | tf_op jit(solution)/shard_map/cond/branch_1_fun/ppermute | solution.py:630
  467.2 24.1 %all-to-all-start.10 = ((bf16[8,112,256]{2,1,0:T(8,128)(2,1)}), bf16[8,112,256]{2,1,0:T(8,128)(2,1)S(1)}, u32[]{:S(2)}, u32[]{:S(2)}) async-start(bf16[8,112,256]{2,1,0:T(8,128)(2,1)} %bitcast.140), calls=%async_computation.10 | async-start | bytes 917504 | tf_op jit(solution)/shard_map/cond/branch_1_fun/all_to_all | solution.py:876
  472.0 14.5 %collective-permute-start.158 = (bf16[9,128,128]{2,1,0:T(8,128)(2,1)S(1)}, bf16[9,128,128]{2,1,0:T(8,128)(2,1)S(1)}, u32[]{:S(2)}, u32[]{:S(2)}) collective-permute-start(bf16[9,128,128]{2,1,0:T(8,128)(2,1)S(1)} %get-tuple-element.478), channel_id=1, source_target_pairs={{0,8},{4,12},{8,0},{12,4},{16,24},{20,28},{24,16},{28,20},{1,9},{5... | collective-permute-start | bytes 884744 | tf_op jit(solution)/shard_map/cond/branch_1_fun/ppermute | solution.py:630
  (135 other events, 1305.9 us)

commit v4 on v3

--- a/solution.py
+++ b/solution.py
@@ -319,28 +319,68 @@
     )(pos, own, other)
 
 
-def quarters_kernel(pos, *refs):
-    quads, out = refs[:4], refs[4]
-    taps, half, lanes = quads[0].shape
-    for k in range(4):
+def to_quarters_kernel(pos, w, *outs):
+    half, lanes = outs[0].shape[1:]
+    for k, out in enumerate(outs):
         row = pl.multiple_of((pos[1] ^ (k // 2)) * half, half)
         lane = pl.multiple_of((pos[2] ^ (k % 2)) * lanes, lanes)
-        out[:, pl.ds(row, half), pl.ds(lane, lanes)] = quads[k][...].astype(out.dtype)
-
-
-def from_quarters(pos, quads):
-    taps, half, lanes = quads[0].shape
+        out[...] = w[:, pl.ds(row, half), pl.ds(lane, lanes)]
+
+
+def to_quarters(pos, w):
+    taps, o, c = w.shape
     spec = pltpu.PrefetchScalarGridSpec(
         num_scalar_prefetch=1,
-        grid=(3,),
-        in_specs=[pl.BlockSpec((taps // 3, half, lanes), lambda i, p: (i, 0, 0))] * 4,
-        out_specs=pl.BlockSpec((taps // 3, 2 * half, 2 * lanes), lambda i, p: (i, 0, 0)),
-    )
+        grid=(1,),
+        in_specs=[same(*w.shape)],
+        out_specs=[same(taps, o // 2, c // 2)] * 4,
+    )
+    return pl.pallas_call(
+        to_quarters_kernel,
+        grid_spec=spec,
+        out_shape=[jax.ShapeDtypeStruct((taps, o // 2, c // 2), w.dtype)] * 4,
+        compiler_params=vmem(16),
+    )(pos, w)
+
+
+def by_chip_kernel(pos, *refs):
+    for k in range(4):
+        refs[4][2 * (pos[1] ^ (k // 2)) + (pos[2] ^ (k % 2))] = refs[k][...]
+
+
+def by_chip(pos, pieces):
+    shape = pieces[0].shape
+    spec = pltpu.PrefetchScalarGridSpec(
+        num_scalar_prefetch=1,
+        grid=(1,),
+        in_specs=[same(*shape)] * 4,
+        out_specs=same(4, *shape),
+    )
+    return pl.pallas_call(
+        by_chip_kernel,
+        grid_spec=spec,
+        out_shape=jax.ShapeDtypeStruct((4, *shape), pieces[0].dtype),
+        compiler_params=vmem(16),
+    )(pos, *pieces)
+
+
+def quarters_kernel(quads, out):
+    half, lanes = quads.shape[2:]
+    for k in range(4):
+        row, lane = (k // 2) * half, (k % 2) * lanes
+        out[:, row : row + half, lane : lane + lanes] = quads[k].astype(out.dtype)
+
+
+def from_quarters(quads):
+    _, taps, half, lanes = quads.shape
     return pl.pallas_call(
         quarters_kernel,
-        grid_spec=spec,
+        grid=(1,),
+        in_specs=[same(*quads.shape)],
+        out_specs=same(taps, 2 * half, 2 * lanes),
         out_shape=jax.ShapeDtypeStruct((taps, 2 * half, 2 * lanes), f32),
-    )(pos, *quads)
+        compiler_params=vmem(16),
+    )(quads)
 
 
 def conv_kernel(pieces, *refs):
@@ -370,7 +410,7 @@
         + [pl.BlockSpec((3, tile, depth), lambda i: (0, i, 0))],
         out_specs=[pl.BlockSpec((rows, lanes), lambda i: (0, i)) for _ in kinds],
         out_shape=[jax.ShapeDtypeStruct((rows, width // len(kinds)), kind) for kind in kinds],
-        compiler_params=vmem(32),
+        compiler_params=vmem(16),
         cost_estimate=cost(6 * rows * width * depth, 2 * rows * depth + 6 * width * depth),
     )(*xs, w)
 
@@ -417,9 +457,171 @@
             jax.ShapeDtypeStruct((rows, lanes), bf16 if k else f32) for k in range(blocks)
         ],
         scratch_shapes=[pltpu.VMEM((rows, 3 * width), bf16)],
-        compiler_params=vmem(32),
+        compiler_params=vmem(16),
         cost_estimate=cost(6 * rows * width * depth, 3 * rows * depth + 6 * width * depth),
     )(*dys, w)
+
+
+def to_lanes_kernel(pos, x, *outs):
+    width = x.shape[2]
+    for k, out in enumerate(outs):
+
+        @pl.when(pl.program_id(0) == k)
+        def _():
+            for m in range(MELS):
+                out[:, m * width : (m + 1) * width] = x[:, m, :]
+
+
+def to_lanes(pos, x, count):
+    rows, _, lanes = x.shape
+    width = lanes // count
+    spec = pltpu.PrefetchScalarGridSpec(
+        num_scalar_prefetch=1,
+        grid=(count,),
+        in_specs=[pl.BlockSpec((rows, MELS, width), lambda i, p: (0, 0, p[3] ^ i))],
+        out_specs=[same(rows, MELS * width)] * count,
+    )
+    return pl.pallas_call(
+        to_lanes_kernel,
+        grid_spec=spec,
+        out_shape=[jax.ShapeDtypeStruct((rows, MELS * width), x.dtype)] * count,
+    )(pos, x)
+
+
+def from_lanes_kernel(pos, *refs):
+    out = refs[-1]
+    width = out.shape[2]
+    for k, x in enumerate(refs[:-1]):
+
+        @pl.when(pl.program_id(0) == k)
+        def _():
+            for m in range(MELS):
+                out[:, m, :] = x[:, m * width : (m + 1) * width]
+
+
+def from_lanes(pos, pieces):
+    count = len(pieces)
+    rows, lanes = pieces[0].shape
+    width = lanes // MELS
+    spec = pltpu.PrefetchScalarGridSpec(
+        num_scalar_prefetch=1,
+        grid=(count,),
+        in_specs=[same(rows, lanes)] * count,
+        out_specs=pl.BlockSpec((rows, MELS, width), lambda i, p: (0, 0, p[3] ^ i)),
+    )
+    return pl.pallas_call(
+        from_lanes_kernel,
+        grid_spec=spec,
+        out_shape=jax.ShapeDtypeStruct((rows, MELS, count * width), pieces[0].dtype),
+    )(pos, *pieces)
+
+
+def row_sums(x, y):
+    row = lax.broadcasted_iota(jnp.int32, (8, x.shape[1]), 0)
+    first = jnp.sum(x, axis=0, keepdims=True)
+    second = jnp.sum(y, axis=0, keepdims=True)
+    return jnp.where(row == 0, first, jnp.where(row == 1, second, 0.0))
+
+
+def mel_sums(parts):
+    total = (parts[0][...] + parts[1][...]) + (parts[2][...] + parts[3][...])
+    part = total.shape[1] // 4
+    cores = [
+        total[:, 2 * c * part : (2 * c + 1) * part]
+        + total[:, (2 * c + 1) * part : (2 * c + 2) * part]
+        for c in range(2)
+    ]
+    return jnp.concatenate([cores[0], cores[0], cores[1], cores[1]], axis=1)
+
+
+def norm2_kernel(term, moved, mask, pre, sums):
+    value = term[...] + moved[...].astype(f32)
+    pre[...] = value
+    sums[...] = row_sums(value * mask[...], value * value * mask[...])
+
+
+def back2_kernel(pre, mask, grad, norm, count, t0, t1, t2, t3, xhat, dz, act, scale, sums):
+    total = mel_sums((t0, t1, t2, t3)) / count[0, 0]
+    average = total[0:1]
+    rstd = lax.rsqrt(total[1:2] - average * average + 1e-05)
+    gain, bias = norm[0:1], norm[1:2]
+    scaled = (pre[...] - average) * rstd
+    z = gain * scaled + bias
+    sigma = 1.0 / (1.0 + jnp.exp(-z))
+    act[...] = (mask[...] * (z * sigma)).astype(bf16)
+    delta = grad[...].astype(f32) * mask[...] * (sigma * (1.0 + z * (1.0 - sigma)))
+    xhat[...] = scaled
+    dz[...] = delta
+    scale[...] = jnp.broadcast_to(gain * rstd, scale.shape)
+    sums[...] = row_sums(delta, delta * scaled)
+
+
+def dpre2_kernel(xhat, dz, mask, scale, count, t0, t1, t2, t3, dpre, grads):
+    total = mel_sums((t0, t1, t2, t3))
+    grads[...] = total
+    mean = total / count[0, 0]
+    value = dz[...] - (mean[0:1] + xhat[...] * mean[1:2])
+    dpre[...] = (mask[...] * scale[0:1] * value).astype(bf16)
+
+
+def lanes_kernel(body, args, kinds):
+    rows, lanes = args[0].shape
+    shapes = [(8, lanes) if kind is None else (rows, lanes) for kind in kinds]
+    return pl.pallas_call(
+        body,
+        grid=(1,),
+        in_specs=[
+            pl.BlockSpec(memory_space=pltpu.MemorySpace.SMEM)
+            if x.shape == (1, 1)
+            else same(*x.shape)
+            for x in args
+        ],
+        out_specs=[same(*shape) for shape in shapes],
+        out_shape=[
+            jax.ShapeDtypeStruct(shape, kind or f32) for shape, kind in zip(shapes, kinds)
+        ],
+        compiler_params=vmem(24),
+    )(*args)
+
+
+def conv_t3_kernel(*refs):
+    dys, w, outs, moved = refs[:6], refs[6], refs[7:13], refs[13]
+    rows, width = dys[0].shape[0], moved.shape[1] // 3
+    step = pl.program_id(0)
+
+    @pl.when(step == 0)
+    def _():
+        for r in range(3):
+            for k in range(2):
+                dy = dys[2 * r + k]
+                spread_rows(moved, r * rows, dy[...], width, k * dy.shape[1])
+
+    value = mxu(moved[...], w[...].reshape(3 * width, w.shape[2]), NN)
+    for k in range(2):
+
+        @pl.when(step == k)
+        def _():
+            for r in range(3):
+                out = outs[2 * r + k]
+                out[...] = value[r * rows : (r + 1) * rows].astype(out.dtype)
+
+
+def conv_t3(pairs, w):
+    rows, (_, width, depth) = pairs[0][0].shape[0], w.shape
+    lanes = depth // 2
+    flat = [dy for pair in pairs for dy in pair]
+    out = pl.pallas_call(
+        conv_t3_kernel,
+        grid=(2,),
+        in_specs=[same(*dy.shape) for dy in flat]
+        + [pl.BlockSpec((3, width, lanes), lambda i: (0, 0, i))],
+        out_specs=[same(rows, lanes)] * 6,
+        out_shape=[jax.ShapeDtypeStruct((rows, lanes), kind) for kind in (f32, bf16) * 3],
+        scratch_shapes=[pltpu.VMEM((3 * rows, 3 * width), bf16)],
+        compiler_params=vmem(24),
+        cost_estimate=cost(18 * rows * width * depth, 9 * rows * depth + 6 * width * depth),
+    )(*flat, w)
+    return [out[2 * r : 2 * r + 2] for r in range(3)]
 
 
 def grad2_place(pos, own, send, a, prod):
@@ -472,7 +674,7 @@
         place(pos, own, send, a, mxu(moved[:, a * width : (a + 1) * width], x[...], TN))
 
 
-def weight_grad_own(pos, dys, xs, place, shape, out_spec):
+def weight_grad_own(pos, dys, xs, place, shape, out_spec, grant):
     groups, pieces, per_group = len(dys), len(dys[0]), len(xs[0])
     rows = dys[0][0].shape[0]
     width = sum(dy.shape[1] for dy in dys[0])
@@ -497,61 +699,52 @@
         functools.partial(grad_kernel, place, groups, pieces),
         grid_spec=spec,
         out_shape=[jax.ShapeDtypeStruct(shape, f32), jax.ShapeDtypeStruct(shape, bf16)],
-        compiler_params=vmem(56),
-        cost_estimate=cost(
-            6 * groups * rows * width * 1024, 2 * groups * rows * (width + 1024)
-        ),
+        compiler_params=vmem(grant),
+        cost_estimate=cost(0, 0),
     )(pos, *args)
 
 
-def clip_places(lengths_row, half_rows):
-    clips = lengths_row.shape[0]
+def clip_places(lengths, half_rows):
+    clips = lengths.shape[1]
     each = clips // 3
 
     def rank(axis):
-        clip = lax.broadcasted_iota(jnp.int32, (clips, clips), axis)
+        clip = lax.broadcasted_iota(jnp.int32, (1, clips, clips), axis)
         kind, place = clip // each, clip % each
         late = place >= each // 2
         long = jnp.where(late, place + 2 * each, place)
         middle = jnp.where(late, place + each + each // 2, place + each // 2)
         return jnp.where(kind == 2, long, jnp.where(kind == 1, middle, place + each))
 
-    size = lengths_row[None, :] + 1
-    before = jnp.sum(jnp.where(rank(1) < rank(0), size, 0), axis=1)
-    late = before + lengths_row + 1 > half_rows
-    taken = jnp.sum(jnp.where(late, 0, lengths_row + 1))
-    return late.astype(jnp.int32), jnp.where(late, before - taken, before)
-
-
-def halves_fit(lengths_row, half_rows):
-    late, _ = clip_places(lengths_row, half_rows)
-    return jnp.sum(late * (lengths_row + 1)) <= half_rows
-
-
-def row_valid(lengths_row, core, half_rows):
-    half, start = clip_places(lengths_row, half_rows)
-    length = jnp.where(half == core, lengths_row, 0)[None, :]
-    row = lax.broadcasted_iota(jnp.int32, (half_rows, lengths_row.shape[0]), 0)
-    inside = (row >= start[None, :]) & (row < start[None, :] + length)
-    return jnp.sum(inside.astype(f32), axis=1, keepdims=True)
-
-
-def row_picker(lengths_row, core, half_rows, frames):
+    size = lengths + 1
+    before = jnp.sum(jnp.where(rank(2) < rank(1), size[:, None, :], 0), axis=2)
+    late = (before + size > half_rows).astype(jnp.int32)
+    taken = jnp.sum((1 - late) * size, axis=1, keepdims=True)
+    fits = jnp.max(jnp.sum(late * size, axis=1)) <= half_rows
+    return late, before - late * taken, fits
+
+
+def frame_clips(lengths_row, frames, outward):
     clips = lengths_row.shape[0]
     clip = lax.broadcasted_iota(jnp.int32, (frames, clips), 1)
     frame = lax.broadcasted_iota(jnp.int32, (frames, clips), 0)
+    if outward:
+        device, own = outward
+        frame = ((frame // own) ^ device) * own + frame % own
     each = clips // 3
     padded = jnp.where(clip < each, 16, jnp.where(clip < 2 * each, 32, 64))
     base = jnp.where(
         clip < each, 0, jnp.where(clip < 2 * each, 16 * each, 48 * each)
     ) + padded * (clip % each)
     offset = frame - base
-    inside = (offset >= 0) & (offset < lengths_row[None, :])
-    half, start = clip_places(lengths_row, half_rows)
-    place = jnp.where(half == core, start, start + half_rows)
-    target = jnp.sum(jnp.where(inside, place[None, :] + offset + 1, 0), axis=1)
-    row = lax.broadcasted_iota(jnp.int32, (2 * half_rows, frames), 0)
-    return (row + 1 == target[None, :]).astype(bf16)
+    return jnp.where((offset >= 0) & (offset < lengths_row[None, :]), offset, -1)
+
+
+def row_masks(lengths, late, start, core, rows):
+    length = jnp.where(late == core, lengths, 0)[None]
+    row = lax.broadcasted_iota(jnp.int32, (rows, *lengths.shape), 0)
+    inside = (row >= start[None]) & (row < start[None] + length)
+    return jnp.sum(inside.astype(f32), axis=2)
 
 
 def after(value, *others):
@@ -574,30 +767,55 @@
     frames, lanes1 = own_frames * n, width1 // n
 
     sent = features[0].reshape(own_frames, MELS, 2, 2, 2, lanes1).transpose(2, 4, 3, 0, 1, 5)
-    sent = sent.reshape(frames, MELS * lanes1)
+    sent, lengths = lax.optimization_barrier((sent.reshape(frames, MELS * lanes1), lengths))
     mine = lax.all_to_all(sent, "tm", 0, 0, tiled=True)
-    every = [lengths[0]] + [
-        lax.ppermute(lengths, "batch", [(z, (z + s) % PLANES) for z in range(PLANES)])[0]
-        for s in range(1, PLANES)
+    every = jnp.concatenate(
+        [lengths]
+        + [
+            lax.ppermute(lengths, "batch", [(z, (z + s) % PLANES) for z in range(PLANES)])
+            for s in range(1, PLANES)
+        ]
+    )
+    me = lax.axis_index("tm")
+    pos = jnp.stack([me % 2, me // 4, me // 2 % 2, me]).astype(jnp.int32)
+    quarters = to_quarters(pos, conv1_weight.transpose(1, 0, 2))
+    w2 = conv2_weight.transpose(1, 0, 2)
+    norm2 = jnp.stack([norm2_gain, norm2_bias])
+    flip = [(i, i ^ 1) for i in range(n)]
+    w2_other, norm2_other = lax.ppermute(w2, "tm", flip), lax.ppermute(norm2, "tm", flip)
+    norm2 = jnp.concatenate([norm2, norm2, norm2_other, norm2_other], axis=1)
+    count = jnp.sum(every.astype(f32)).reshape(1, 1) * MELS
+    orders = [
+        frame_clips(lengths[0], frames, None),
+        frame_clips(lengths[0], frames, (me, own_frames)),
     ]
-    part, wide = conv1_weight.shape[0], conv1_weight.shape[2]
-    quarters = conv1_weight.transpose(1, 0, 2).reshape(9, 2, part // 2, 2, wide // 2)
-    quarters = quarters.transpose(1, 3, 0, 2, 4).reshape(CHIPS, 9, part // 2, wide // 2)
-    half_rows = frames * 3 // 7
-    fits = functools.reduce(jnp.logical_and, [halves_fit(x, half_rows) for x in every])
+    core = lax.axis_index("tm") % 2
+
+    def places(half_rows):
+        late, start, fits = clip_places(every, half_rows)
+        row = jnp.where(late[0] == core, start[0], start[0] + half_rows)
+        targets = [jnp.max(jnp.where(x >= 0, row[None, :] + x, -1), axis=1) for x in orders]
+        return late, start, *targets, fits
+
+    *packed, fits = places(frames * 3 // 7)
+    *loose, _ = places(frames // 2)
+    chosen = [jnp.where(fits, x, y) for x, y in zip(packed, loose)]
     return lax.cond(
         fits,
-        functools.partial(on_rows, half_rows),
+        functools.partial(on_rows, frames * 3 // 7),
         functools.partial(on_rows, frames // 2),
         mine,
-        jnp.stack(every),
+        every,
+        chosen,
         quarters,
         norm1_gain,
         norm1_bias,
-        conv2_weight,
-        norm2_gain,
-        norm2_bias,
-        out_grad,
+        w2,
+        w2_other,
+        norm2,
+        out_grad[0],
+        count,
+        pos,
     )
 
 
@@ -605,22 +823,24 @@
     rows,
     mine,
     every,
+    places,
     w1,
     norm1_gain,
     norm1_bias,
-    conv2_weight,
-    norm2_gain,
-    norm2_bias,
+    w2,
+    w2_other,
+    norm2,
     out_grad,
+    count,
+    pos,
 ):
     n = 2 * CHIPS
     me, plane = lax.axis_index("tm"), lax.axis_index("batch")
     core, chip = me % 2, me // 2
     py, px = chip // 2, chip % 2
-    pos = jnp.stack([core, py, px]).astype(jnp.int32)
     frames, lanes1 = mine.shape[0], mine.shape[1] // MELS
     own_frames, width1 = frames // n, n * lanes1
-    part = conv2_weight.shape[0]
+    part = w2.shape[1]
     half = part // 2
     same_core = [[c + 2 * p for p in range(CHIPS)] for c in range(2)]
     groups = range(PLANES)
@@ -651,18 +871,16 @@
     def rows_sum(x):
         return jnp.sum(x, axis=0)
 
-    picker = row_picker(every[0], core, rows, frames)
-    mask = [row_valid(every[r], core, rows) for r in groups]
-    count = jnp.sum(every.astype(f32)) * MELS
+    late, start, target, outward = places
+    picker = lax.broadcasted_iota(jnp.int32, (2 * rows, frames), 0) == target[None, :]
+    picker = picker.astype(bf16)
     packed = mxu(picker, mine, NN).astype(bf16)
     other = swap(packed[rows:], 1)
     first = jnp.where(core == 0, packed[:rows], other)
     second = jnp.where(core == 0, other, packed[:rows])
     mine = [jnp.concatenate([first, second], axis=1)]
-
-    w1 = lax.all_to_all(w1, "tm", 0, 0, tiled=True, axis_index_groups=same_core)
-    w2 = conv2_weight.transpose(1, 0, 2)
-    w2_other = swap(after(w2, mine[0]), 1)
+    outward = lax.broadcasted_iota(jnp.int32, (2 * rows, frames), 0) == outward[None, :]
+    outward = outward.astype(bf16)
 
     def norm_of_block(own_norm):
         both = 0.0
@@ -675,35 +893,52 @@
         return both
 
     own_norm = jnp.stack([norm1_gain, norm1_bias]).reshape(2, 2, half)
-    nears, both1, weights2 = [], None, None
+    nears, both1, weights2, mask = [], None, None, None
     for r in groups:
         x = mine[r]
         ahead = along(x, 1) if r < PLANES - 1 else None
         nears.append(swap(x, Y))
-        done = [nears[r]]
+        if r == 0:
+            w1 = [w1[0]] + [swap(w1[k], 2 * k) for k in range(1, CHIPS)]
+            mask = row_masks(every, after(late, x), start, core, rows)
+            mask = [mask[:, k : k + 1] for k in groups]
+            ahead, *mask = lax.optimization_barrier((ahead, *mask))
         if r == 1:
-            w1 = lax.all_to_all(after(w1, x), "batch", 0, 0, tiled=True)
+            w1 = by_chip(pos, [after(w1[0], x)] + w1[1:])
+            w1 = lax.all_to_all(w1, "batch", 0, 0, tiled=True)
             weights2 = taps2(pos, w2, after(w2_other, x))
-            done.append(weights2)
+            grad_in = list(to_lanes(pos, after(out_grad, x), n))
+            sent = [swap(grad_in[k], k) for k in (1, 2, 3, 4, 5)]
+            ahead, nears[0], nears[1], _, *sent = lax.optimization_barrier(
+                (ahead, nears[0], nears[1], weights2, *sent)
+            )
+            grad_in[1:6] = sent
         if r == 2:
             both1 = norm_of_block(after(own_norm, x))
-            done.append(both1)
+            sent = [swap(after(grad_in[k], x), k) for k in (6, 7)]
+            ahead, nears[2], both1, *sent = lax.optimization_barrier(
+                (ahead, nears[2], both1, *sent)
+            )
+            grad_in[6:] = sent
         if ahead is not None:
-            mine.append(after(ahead, *done))
+            mine.append(ahead)
     gain1, bias1 = both1[0], both1[1]
 
-    w1 = after(w1, mine[3])
-    weights1 = taps1(pos, w1, swap(w1, 1))
+    w1_other = swap(after(w1, mine[3]), 1)
+    weights1 = taps1(pos, w1, w1_other)
     inputs, pre1, send = [], [], None
     for r in groups:
-        inputs.append([mine[r], nears[r] if r < 3 else after(nears[r], send)])
+        near = nears[r]
+        if r == 3:
+            near = after(near, send)
+        inputs.append([mine[r], near])
         xs = inputs[r] if r == 0 else [after(mine[r], send), inputs[r][1]]
         keep, send = conv(xs, weights1, (f32, bf16), 512)
         pre1.append(keep + swap(send, X).astype(f32))
 
     def norm_stats(total, square_total):
-        average = total / count
-        variance = square_total / count - average * average
+        average = total / count[0, 0]
+        variance = square_total / count[0, 0] - average * average
         return average, lax.rsqrt(variance + 1e-05)
 
     def chip_sum(x):
@@ -722,7 +957,7 @@
     act1 = [(v * jax.nn.silu(z)).astype(bf16) for v, z in zip(mask, z1)]
 
     hidden = [None] * PLANES
-    payload, term, got, grad_in = None, None, None, None
+    payload, term, got = None, None, None
     for r in (1, 2, 3, 0):
         x = act1[r] if r == 1 else after(act1[r], *got)
         got = [swap(x, X), swap(x, Y), swap(x, X + Y)]
@@ -733,73 +968,46 @@
         (term,) = conv(hidden[r], weights2, (bf16 if r == 1 else f32,), 512)
         if r == 1:
             payload = term
-            continue
-        if r == 0:
-            grad_in = mxu(picker, grad_in.reshape(frames, MELS * part), NN).astype(bf16)
+        elif r != 0:
+            payload = (term + after(moved, term).astype(f32)).astype(bf16)
+        else:
+            grad_in = jnp.concatenate(grad_in, axis=0)
+            grad_in = mxu(outward, after(grad_in, payload), NN).astype(bf16)
             grad_in = jnp.concatenate([grad_in[:rows], swap(grad_in[rows:], 1)], axis=1)
-            moved = after(moved, grad_in)
-        total = term + after(moved, term).astype(f32)
-        payload = total.astype(bf16)
-        if r == 2:
-            grad_in = after(out_grad, payload)[0].reshape(own_frames, MELS, n, part)
-            grad_in = grad_in.transpose(2, 0, 1, 3)
-            grad_in = lax.all_to_all(grad_in, "tm", 0, 0, tiled=True)
-    pre2, v0 = total, mask[0]
-
-    def all_rows(x, y):
-        sums = jnp.stack([rows_sum(x), rows_sum(y)]).reshape(2, 2, MELS, part).sum(axis=2)
-        return plane_sum(sums + swap(jnp.flip(sums, 1), 1))
-
-    def lanes2(x):
-        return jnp.broadcast_to(x[:, None, :], (2, MELS, part)).reshape(1, -1)
-
-    norm2 = jnp.stack([norm2_gain, norm2_bias])
-    norm2 = jnp.stack([norm2, swap(after(norm2, act1[1]), 1)], axis=1)
-    sums2 = all_rows(pre2 * v0, pre2 * pre2 * v0)
-    mean2, rstd2 = norm_stats(sums2[0], sums2[1])
-    xhat2 = (pre2 - lanes2(mean2)) * lanes2(rstd2)
-    z2 = lanes2(norm2[0]) * xhat2 + lanes2(norm2[1])
-    dz2 = grad_in.astype(f32) * v0 * silu_slope(z2)
-    grads2 = all_rows(dz2, dz2 * xhat2)
-    bias2_grad, gain2_grad = grads2[0, 0], grads2[1, 0]
-    dpre2 = (
-        v0
-        * lanes2(norm2[0] * rstd2)
-        * (dz2 - (lanes2(grads2[0]) + xhat2 * lanes2(grads2[1])) / count)
-    ).astype(bf16)
+            moved, grad_in, _ = lax.optimization_barrier((moved, grad_in, term))
+
+    lanes2 = 2 * MELS * part
+
+    def to_planes(sums):
+        got = swap(sums, 1)
+        turned = jnp.concatenate([got[:, lanes2 // 2 :], got[:, : lanes2 // 2]], axis=1)
+        sums = sums + turned
+        return [sums] + [
+            lax.ppermute(sums, "batch", [(z, z ^ s) for z in groups]) for s in range(1, PLANES)
+        ]
+
+    v0 = mask[0]
+    pre2, sums = lanes_kernel(norm2_kernel, [term, moved, v0], [f32, None])
+    xhat2, dz2, out_local, scale2, sums = lanes_kernel(
+        back2_kernel,
+        [pre2, v0, grad_in, norm2, count, *to_planes(sums)],
+        [f32, f32, bf16, None, None],
+    )
+    dpre2, grads2 = lanes_kernel(
+        dpre2_kernel, [xhat2, dz2, v0, scale2, count, *to_planes(sums)], [bf16, None]
+    )
 
     grad2 = [dpre2]
-    dact1, block_out = [], None
+    dact1 = []
     for r in groups:
         ahead = along(grad2[r], 1) if r < PLANES - 1 else None
         keep, *sends = conv_t([grad2[r]], weights2, CHIPS)
         got = [swap(v, bits) for v, bits in zip(sends, (X, Y, X + Y))]
-        done = list(got)
-        if r == 0:
-            out_local = (v0 * jax.nn.silu(after(z2, keep))).astype(bf16)
-            lanes = MELS * part
-            out_local = jnp.concatenate(
-                [out_local[:, :lanes], swap(out_local[:, lanes:], 1)], axis=0
-            )
-            out_local = mxu(picker, out_local, TN).astype(bf16)
-            out_local = out_local.reshape(n, own_frames, MELS, part)
-            done.append(out_local)
-        if r == 1:
-            block_out = lax.all_to_all(after(out_local, keep), "tm", 0, 0, tiled=True)
-        if r == 2:
-            block_out = block_out.transpose(1, 2, 0, 3)
-            block_out = block_out.reshape(1, own_frames, MELS, n * part)
-            done.append(block_out)
         dact1.append(
             (keep + got[0].astype(f32)) + (got[1].astype(f32) + got[2].astype(f32))
         )
         if ahead is not None:
-            ahead, *rest = lax.optimization_barrier((ahead, *done))
-            if r == 0:
-                out_local = rest[-1]
-            if r == 2:
-                block_out = rest[-1]
-            grad2.append(ahead)
+            grad2.append(after(ahead, *got))
 
     dz1 = [d * v * silu_slope(z) for d, v, z in zip(dact1, mask, z1)]
     sums = jnp.stack(
@@ -813,28 +1021,34 @@
         (
             v
             * per_lane(gain1 * rstd1)
-            * (d - (per_lane(grads1[0]) + x * per_lane(grads1[1])) / count)
+            * (d - (per_lane(grads1[0]) + x * per_lane(grads1[1])) / count[0, 0])
         ).astype(bf16)
         for v, d, x in zip(mask, dz1, xhat1)
     ]
     order = (1, 2, 3, 0)
-    pairs1, terms = [None] * PLANES, {}
-    for k, r in enumerate(order):
-        x = dpre1[r] if k == 0 else after(dpre1[r], pairs1[1][1])
-        pairs1[r] = [x, swap(x, X)]
-    send = None
-    for k, r in enumerate(order):
-        x, near = pairs1[r]
-        if k > 0:
-            near = after(near, send)
-        keep, send = conv_t([x, near], weights1, 2)
-        terms[r] = keep, send
-
-    def dx_term(r):
-        return terms[r][0] + swap(terms[r][1], Y).astype(f32)
-
-    first = dx_term(1).astype(bf16)
-    pairs1[1][0] = after(pairs1[1][0], first, send)
+    pairs1, terms, nears = [None] * PLANES, {}, {}
+    pairs1[1] = [dpre1[1], swap(dpre1[1], X)]
+    later = jnp.concatenate([dpre1[r] for r in order[1:]], axis=0)
+    later_near = swap(after(later, pairs1[1][1]), X)
+    terms[1] = conv_t(pairs1[1], weights1, 2)
+    first = (terms[1][0] + swap(terms[1][1], Y).astype(f32)).astype(bf16)
+    out_local = after(out_local, terms[1][1])
+    out_local = jnp.concatenate(
+        [out_local[:, : lanes2 // 2], swap(out_local[:, lanes2 // 2 :], 1)], axis=0
+    )
+    out_local = mxu(outward, out_local, TN).astype(bf16)
+    out_local = after(out_local, first).reshape(n, own_frames, MELS * part)
+    out_pieces = [out_local[k] for k in range(n)]
+    sent = [swap(out_pieces[k], k) for k in (1, 2, 3)]
+    later_near, *sent = lax.optimization_barrier((later_near, *sent))
+    out_pieces[1:4] = sent
+    for k, r in enumerate(order[1:]):
+        pairs1[r] = [dpre1[r], later_near[k * rows : (k + 1) * rows]]
+    terms[2], terms[3], terms[0] = conv_t3([pairs1[r] for r in order[1:]], weights1)
+    for r in order[1:]:
+        nears[r] = swap(terms[r][1], Y)
+
+    moved = along(first, 1)
     grad1_own, grad1_send = weight_grad_own(
         pos,
         [pairs1[r] for r in order],
@@ -844,40 +1058,26 @@
         pl.BlockSpec(
             (1, 9, half, 128), lambda t, p: (2 * (p[1] ^ (t // 2)) + t % 2, 0, 0, 0)
         ),
-    )
+        36,
+    )
+    grad1_send, moved, nears[2] = lax.optimization_barrier((grad1_send, moved, nears[2]))
+    second = ((terms[2][0] + nears[2].astype(f32)) + moved.astype(f32)).astype(bf16)
+    moved = along(second, 1)
     grad1 = (grad1_own + swap(grad1_send, 1).astype(f32)).astype(bf16)
-    second = (dx_term(2) + after(along(first, 1), grad1).astype(f32)).astype(bf16)
-    moved = along(second, 1)
-    grad1_planes = lax.all_to_all(after(grad1, second), "batch", 0, 0, tiled=True)
+    grad1_planes = lax.all_to_all(grad1, "batch", 0, 0, tiled=True)
+    grad2_first = after(grad2[0], grad1)
+    sent = [swap(after(out_pieces[k], grad1), k) for k in (4, 5)]
     grad2_own, grad2_send = weight_grad_own(
         pos,
-        [[after(grad2[0], second)]] + [[g] for g in grad2[1:]],
+        [[grad2_first]] + [[g] for g in grad2[1:]],
         hidden,
         grad2_place,
-        (9, part, conv2_weight.shape[2]),
+        w2.shape,
         pl.BlockSpec(
             (9, part, 128), lambda t, p: (0, 0, 2 * (p[2] ^ (t % 2)) + (p[1] ^ (t // 2)))
         ),
-    )
-    third = (dx_term(3) + after(moved, grad2_send).astype(f32)).astype(bf16)
-    moved = along(third, 1)
-    conv2_grad = grad2_own + swap(after(grad2_send, third), 1).astype(f32)
-    dx = (dx_term(0) + after(moved, conv2_grad).astype(f32)).astype(bf16)
-    conv2_grad = conv2_grad.transpose(1, 0, 2)
-    low, high = dx[:, : MELS * lanes1], dx[:, MELS * lanes1 :]
-    other = swap(jnp.where(core == 0, high, low), 1)
-    dx = jnp.concatenate([jnp.where(core == 0, low, high), other], axis=0)
-    dx = mxu(picker, dx, TN).astype(bf16)
-
-    def quarter(k):
-        return lax.dynamic_index_in_dim(grad1_planes, chip ^ k, 0, keepdims=False)
-
-    quads = [quarter(0)] + [swap(quarter(k), 2 * k) for k in range(1, CHIPS)]
-    dx = lax.all_to_all(dx.reshape(n, own_frames, MELS * lanes1), "tm", 0, 0, tiled=True)
-    dx = dx.reshape(2, 2, 2, own_frames, MELS, lanes1).transpose(3, 4, 0, 2, 1, 5)
-    input_grad = dx.reshape(1, own_frames, MELS, width1)
-    conv1_grad = from_quarters(pos, quads).transpose(1, 0, 2)
-
+        60,
+    )
     grads1 = after(grads1, grad2_send)
     whole1 = jnp.concatenate(
         [
@@ -889,13 +1089,45 @@
         ],
         axis=1,
     )
+    grad2_send, nears[0], *sent = lax.optimization_barrier((grad2_send, nears[0], *sent))
+    sent += [swap(after(out_pieces[k], grad2_send), k) for k in (6, 7)]
+    moved, nears[3], grad2_send, grad1_planes, whole1, *sent = lax.optimization_barrier(
+        (moved, nears[3], grad2_send, grad1_planes, whole1, *sent)
+    )
+    out_pieces[4:] = sent
+    third = ((terms[3][0] + nears[3].astype(f32)) + moved.astype(f32)).astype(bf16)
+    whole1, grad1_planes = after(whole1, third), after(grad1_planes, third)
+    moved = along(third, 1)
+    grad2_got = swap(grad2_send, 1)
+
+    grad1_chips = lax.all_to_all(
+        grad1_planes, "tm", 0, 0, tiled=True, axis_index_groups=same_core
+    )
     mine1 = jnp.where(chip == plane, whole1, 0.0)
     for s in range(1, PLANES):
         mine1 += route(
             whole1,
             [((2 * j + c, j), (2 * j + c, (j + s) % PLANES)) for j in groups for c in range(2)],
         )
+
+    moved, grad2_got, mine1 = lax.optimization_barrier((moved, grad2_got, mine1))
     bias1_grad, gain1_grad = mine1[0], mine1[1]
+    moved, grad1_chips = lax.optimization_barrier((moved, grad1_chips))
+    dx = ((terms[0][0] + nears[0].astype(f32)) + moved.astype(f32)).astype(bf16)
+    low, high = dx[:, : MELS * lanes1], dx[:, MELS * lanes1 :]
+    other = swap(jnp.where(core == 0, high, low), 1)
+    dx = jnp.concatenate([jnp.where(core == 0, low, high), other], axis=0)
+    dx = mxu(picker, dx, TN).astype(bf16)
+    dx, grad2_got, grad1_chips, out_pieces[0] = lax.optimization_barrier(
+        (dx, grad2_got, grad1_chips, out_pieces[0])
+    )
+
+    dx = lax.all_to_all(dx.reshape(n, own_frames, MELS * lanes1), "tm", 0, 0, tiled=True)
+    dx = dx.reshape(2, 2, 2, own_frames, MELS, lanes1).transpose(3, 4, 0, 2, 1, 5)
+    input_grad = dx.reshape(1, own_frames, MELS, width1)
+    conv1_grad = from_quarters(grad1_chips).transpose(1, 0, 2)
+    block_out = from_lanes(pos, out_pieces)[None]
+    conv2_grad = (grad2_own + grad2_got.astype(f32)).transpose(1, 0, 2)
 
     return (
         block_out,
@@ -904,8 +1136,8 @@
         gain1_grad,
         bias1_grad,
         conv2_grad,
-        gain2_grad,
-        bias2_grad,
+        grads2[1, :part],
+        grads2[0, :part],
     )
 
 

time: 500 us -> 458 us (0.916)
  local copies, waits for them, and re-layouts: 49.8 us -> 19.1 us
  other arithmetic: 37.4 us -> 18.1 us
  waiting for transfers between devices: 168 us -> 180 us
  Pallas kernels: 85.2 us -> 95.6 us
  starting transfers between devices: 132 us -> 125 us
    pallas_call x1 -> x9, Pallas kernels: 4.2 us -> 23.7 us  [the longest x1 6.53 us: to_lanes(): pl.pallas_call(to_lanes_kernel, grid_spec=spec, out_shape=[jax.ShapeDtype...]
    cond x224 -> x155, local copies, waits for them, and re-layouts: 25.6 us -> 12.4 us
    ppermute x56 -> x66, starting transfers between devices: 49.4 us -> 61.2 us  [swap(): return lax.ppermute(x, 'tm', [(i, i ^ bits) for i in range(n)])]
    all_to_all x5 -> x3, starting transfers between devices: 20.8 us -> 11.5 us  [the longest x1 4.4 us: on_rows(): grad1_planes = lax.all_to_all(grad1, 'batch', 0, 0, tiled=True)]
    ppermute x12, starting transfers between devices: 21.5 us -> 12.4 us  [along(): return lax.ppermute(x, 'batch', [(z, (z + shift) % PLANES) for z in groups])]
    reshape x3 -> x0, local copies, waits for them, and re-layouts: 7.47 us -> none  [the longest x1 3.14 us: on_rows(): block_out = block_out.reshape(1, own_frames, MELS, n * part)]
    transpose x0 -> x1, other arithmetic: none -> 6.15 us  [on_rows(): conv2_grad = (grad2_own + grad2_got.astype(f32)).transpose(1, 0, 2)]
    add x6 -> x7, other arithmetic: 6.17 us -> 0.04 us  [the longest x2 0.02 us: to_planes(): sums = sums + turned]
  transfers between devices with their start and end apart: 93 -> 103, of which waited for: 46 -> 57; matrix products, arithmetic and copies ran while one was open for 10% -> 4% of each run, Pallas kernels for 13% -> 18%
where the time goes in v4:
time: 458 us; the launch traced here: 452 us
  waiting for transfers between devices  180 us (39%)
  starting transfers between devices  125 us (27%)
  Pallas kernels  95.6 us (21%)
  local copies, waits for them, and re-layouts  19.1 us (4%)
  other arithmetic  18.1 us (4%)
  loops' own time  6.94 us (2%)
    ppermute x66, waiting for transfers between devices, swap(): return lax.ppermute(x, 'tm', [(i, i ^ bits) for i in range(n)])  107 us
    ppermute x66, starting transfers between devices, swap(): return lax.ppermute(x, 'tm', [(i, i ^ bits) for i in range(n)])  61.2 us
    ppermute x12, waiting for transfers between devices, along(): return lax.ppermute(x, 'batch', [(z, (z + shift) % PLANES) for z in groups])  52.5 us
    pallas_call x2, Pallas kernels, weight_grad_own(): pl.pallas_call(functools.partial(grad_kernel, place, groups, pieces), gri...  25.7 us
    pallas_call x8, Pallas kernels, conv(): pl.pallas_call(functools.partial(conv_kernel, len(xs)), grid=(width // ti...  20.4 us
    pallas_call x5, Pallas kernels, conv_t(): pl.pallas_call(functools.partial(conv_t_kernel, len(dys)), grid=(blocks,)...  19.9 us
    ppermute x9, starting transfers between devices, route(): return lax.ppermute(x, ('tm', 'batch'), flat)  15.9 us
    cond x155, local copies, waits for them, and re-layouts  12.4 us
  transfers between devices with their start and end apart: 103, of which 57 were waited for; matrix products, arithmetic and copies ran while one was open for 4% of the time, Pallas kernels for 18%

profile of v4, /device:TPU:0, one launch (start us, length us, event | category | flops | bytes accessed | tf_op | source)
XLA Modules:
  0.0 451.7 jit_solution(16079146249876754891)
XLA Ops:
  3.3 3.0 collective-permute-start.186
  6.3 2.6 collective-permute-start.187
  10.9 3.7 all-to-all-start.8
  18.4 5.2 %all-to-all-done.8 = bf16[8,112,256]{2,1,0:T(8,128)(2,1)S(1)} async-done(((bf16[8,112,256]{2,1,0:T(8,128)(2,1)}), bf16[8,112,256]{2,1,0:T(8,128)(2,1)S(1)}, u32[]{:S(2)}, u32[]{:S(2)}) %all-to-all-start.8) | async-done | bytes 458784 | tf_op jit(solution)/shard_map/all_to_all | solution.py:771
  23.7 426.6 %conditional.1 = (bf16[1,112,2,2048]{3,2,1,0:T(2,128)(2,1)}, bf16[1,112,2,1024]{3,2,1,0:T(2,128)(2,1)}, f32[256,9,256]{2,0,1:T(8,128)}, f32[256]{0:T(256)}, f32[...) conditional(s32[]{:T(128)} %convert_element_type.298, (pred[]{:T(512)}, ...), branch_computations={%region_10.32_spmd, %region_32.54_spmd} | conditional | flops 36335312896 | bytes 479695616 | solution.py:803
  34.8 11.5 %collective-permute-done.94.refs_0_.refs_8_ = bf16[384,512]{1,0:T(8,128)(2,1)S(1)} collective-permute-done((bf16[384,512]{1,0:T(8,128)(2,1)S(1)}, bf16[384,512]{1,0:T(8,128)(2,1)S(1)}, u32[]{:S(2)}, u32[]{:S(2)}) %collective-permute-start.94) | collective-permute-done | bytes 393248 | tf_op jit(solution)/shard_map/cond/branch_1_fun/ppermute | solution.py:853
  48.0 3.5 all-to-all-start.4
  55.6 6.5 %branch_1_fun.26 = (bf16[112,512]{1,0:T(8,128)(2,1)}, bf16[112,512]{1,0:T(8,128)(2,1)}, bf16[112,512]{1,0:T(8,128)(2,1)}, bf16[112,512]{1,0:T(8,128)(2,1)}, bf16...) custom-call(s32[4]{0:T(128)S(1)} %get-tuple-element.227.pos, ...), custom_call_target="tpu_custom_call" | custom-call | tf_op jit(solution)/shard_map/cond/branch_1_fun/pallas_call | solution.py:484
  65.0 2.8 collective-permute-done.100
  68.0 6.3 %collective-permute-done.101 = bf16[112,512]{1,0:T(8,128)(2,1)} collective-permute-done((bf16[112,512]{1,0:T(8,128)(2,1)}, bf16[112,512]{1,0:T(8,128)(2,1)}, u32[]{:S(2)}, u32[]{:S(2)}) %collective-permute-start.101) | collective-permute-done | bytes 114720 | tf_op jit(solution)/shard_map/cond/branch_1_fun/ppermute | solution.py:850
  75.7 4.6 %branch_1_fun.25.refs_4_.refs_1_ = bf16[3,1024,1024]{2,1,0:T(8,128)(2,1)S(1)} custom-call(s32[4]{0:T(128)S(1)} %get-tuple-element.227.pos, bf16[9,256,512]{2,1,0:T(8,128)(2,1)} %get-tuple-element.236.own, bf16[9,256,512]{2,1,0:T(8,128)(2,1)} %get-tuple-element.238.other), custom_call_target="tpu_custom_call" | custom-call | tf_op jit(solution)/shard_map/cond/branch_1_fun/pallas_call | solution.py:314
  80.3 2.6 copy-done
  83.8 4.0 collective-permute-start.103
  90.6 3.9 collective-permute-start.106
  97.7 2.5 collective-permute-start.109
  100.2 3.6 collective-permute-done.110
  103.8 2.7 collective-permute-done.109
  108.1 2.6 collective-permute-done.114.other
  119.7 2.5 branch_1_fun.32
  125.8 3.9 collective-permute-done.117
  129.9 3.2 collective-permute-done.119
  136.2 2.7 collective-permute-start.123
  138.9 4.2 collective-permute-done.121.refs_1_.refs_9_
  143.2 3.9 collective-permute-done.122.refs_2_.refs_10_
  147.1 2.8 copy-done.1
  149.9 3.4 branch_1_fun.33
  158.5 5.2 %collective-permute-done.126.refs_3_.refs_15_ = bf16[384,256]{1,0:T(8,128)(2,1)S(1)} collective-permute-done((bf16[384,256]{1,0:T(8,128)(2,1)S(1)}, bf16[384,256]{1,0:T(8,128)(2,1)S(1)}, u32[]{:S(2)}, u32[]{:S(2)}) %collective-permute-start.126) | collective-permute-done | bytes 196640 | tf_op jit(solution)/shard_map/cond/branch_1_fun/ppermute | solution.py:850
  163.7 2.4 collective-permute-done.124.refs_1_.refs_13_
  166.2 3.4 branch_1_fun.34
  169.7 4.4 collective-permute-done.133
  180.0 4.9 %collective-permute-done.129.refs_3_.refs_19_ = bf16[384,256]{1,0:T(8,128)(2,1)S(1)} collective-permute-done((bf16[384,256]{1,0:T(8,128)(2,1)S(1)}, bf16[384,256]{1,0:T(8,128)(2,1)S(1)}, u32[]{:S(2)}, u32[]{:S(2)}) %collective-permute-start.129) | collective-permute-done | bytes 196640 | tf_op jit(solution)/shard_map/cond/branch_1_fun/ppermute | solution.py:850
  184.9 2.4 collective-permute-done.127.refs_1_.refs_17_
  190.9 3.4 branch_1_fun.35
  198.8 3.4 branch_1_fun.36.term
  202.3 11.9 %collective-permute-done.135.moved = bf16[384,1024]{1,0:T(8,128)(2,1)S(1)} collective-permute-done((bf16[384,1024]{1,0:T(8,128)(2,1)S(1)}, bf16[384,1024]{1,0:T(8,128)(2,1)S(1)}, u32[]{:S(2)}, u32[]{:S(2)}) %collective-permute-start.135) | collective-permute-done | bytes 786464 | tf_op jit(solution)/shard_map/cond/branch_1_fun/ppermute | solution.py:853
  218.0 2.4 collective-permute-start.140
  220.9 2.8 collective-permute-done.140.t3
  226.3 2.9 collective-permute-start.143
  231.1 3.7 collective-permute-done.144.t3
  235.3 4.5 branch_1_fun.40
  243.3 3.9 collective-permute-done.146
  250.5 4.5 collective-permute-done.145.refs_0_.refs_1_
  255.0 4.5 branch_1_fun.41
  263.0 3.0 collective-permute-done.150
  269.2 4.5 %collective-permute-done.149.refs_0_.refs_2_ = bf16[384,1024]{1,0:T(8,128)(2,1)S(1)} collective-permute-done((bf16[384,1024]{1,0:T(8,128)(2,1)S(1)}, bf16[384,1024]{1,0:T(8,128)(2,1)S(1)}, u32[]{:S(2)}, u32[]{:S(2)}) %collective-permute-start.149) | collective-permute-done | bytes 786464 | tf_op jit(solution)/shard_map/cond/branch_1_fun/ppermute | solution.py:853
  274.0 4.5 branch_1_fun.42
  287.5 4.3 collective-permute-done.156.refs_0_.refs_3_
  291.8 4.5 branch_1_fun.43
  309.2 5.6 %collective-permute-done.161.refs_1_ = bf16[384,256]{1,0:T(8,128)(2,1)S(1)} collective-permute-done((bf16[384,256]{1,0:T(8,128)(2,1)S(1)}, bf16[384,256]{1,0:T(8,128)(2,1)S(1)}, u32[]{:S(2)}, u32[]{:S(2)}) %collective-permute-start.161) | collective-permute-done | bytes 196640 | tf_op jit(solution)/shard_map/cond/branch_1_fun/ppermute | solution.py:850
  319.8 7.5 %collective-permute-done.164 = bf16[384,512]{1,0:T(8,128)(2,1)S(1)} collective-permute-done((bf16[384,512]{1,0:T(8,128)(2,1)S(1)}, bf16[384,512]{1,0:T(8,128)(2,1)S(1)}, u32[]{:S(2)}, u32[]{:S(2)}) %collective-permute-start.164) | collective-permute-done | bytes 393248 | tf_op jit(solution)/shard_map/cond/branch_1_fun/ppermute | solution.py:850
  331.3 5.3 %collective-permute-done.166.refs_2_ = bf16[112,512]{1,0:T(8,128)(2,1)S(1)} collective-permute-done((bf16[112,512]{1,0:T(8,128)(2,1)S(1)}, bf16[112,512]{1,0:T(8,128)(2,1)S(1)}, u32[]{:S(2)}, u32[]{:S(2)}) %collective-permute-start.166) | collective-permute-done | bytes 114720 | tf_op jit(solution)/shard_map/cond/branch_1_fun/ppermute | solution.py:850
  338.4 5.0 %branch_1_fun.45 = (f32[384,512]{1,0:T(8,128)S(1)}, bf16[384,512]{1,0:T(8,128)(2,1)S(1)}, f32[384,512]{1,0:T(8,128)S(1)}, bf16[384,512]{1,0:T(8,128)(2,1)S(1)}, ...) custom-call(bf16[384,256]{1,0:T(8,128)(2,1)S(1)} %get-tuple-element.699.refs_0_.refs_2_, ...), custom_call_target="tpu_custom_call" | custom-call | flops 3623878656 | bytes 6684672 | tf_op jit(solution)/shard_map/cond/branch_1_fun/pallas_call | solution.py:613
  346.1 8.5 %branch_1_fun.46 = (f32[4,9,128,128]{3,2,1,0:T(8,128)S(1)}, bf16[4,9,128,128]{3,2,1,0:T(8,128)(2,1)S(1)}) custom-call(s32[4]{0:T(128)S(1)} %get-tuple-element.227.pos, bf16[384,256]{1,0:T(8,128)(2,1)S(1)} %get-tuple-element.698.refs_0_, bf16[384,256]{1,0:T(8,128)(2,1)S(1)} %collective-permute-done.161.refs_1_, ...), custom_call_target="tpu_custom_call" | custom-call | tf_op jit(solution)/shard_map/cond/branch_1_fun/pallas_call | solution.py:698
  356.4 2.8 collective-permute-done.170
  360.7 4.4 all-to-all-start.5
  372.3 17.2 %branch_1_fun.47 = (f32[9,256,512]{2,1,0:T(8,128)}, bf16[9,256,512]{2,1,0:T(8,128)(2,1)}) custom-call(s32[4]{0:T(128)S(1)} %get-tuple-element.227.pos, bf16[384,1024]{1,0:T(8,128)(2,1)} %copy-done.23, bf16[384,1024]{1,0:T(8,128)(2,1)} %copy-done.24, bf16[384,1024]{1,0:T(8,128)(2,1)} %copy-done.25, bf16[384,1024]{1,0:T(8,128)(2,1)} %copy-done.26, ...), custom_call_target="tpu_custom_call" | custom-call | tf_op jit(solution)/shard_map/cond/branch_1_fun/pallas_call | solution.py:698
  394.8 4.2 collective-permute-done.177
  399.0 3.7 all-to-all-done.5
  405.6 3.5 all-to-all-start.6
  409.1 3.8 collective-permute-start.182
  416.9 11.2 %collective-permute-done.180 = bf16[384,512]{1,0:T(8,128)(2,1)S(1)} collective-permute-done((bf16[384,512]{1,0:T(8,128)(2,1)S(1)}, bf16[384,512]{1,0:T(8,128)(2,1)S(1)}, u32[]{:S(2)}, u32[]{:S(2)}) %collective-permute-start.180) | collective-permute-done | bytes 393248 | tf_op jit(solution)/shard_map/cond/branch_1_fun/ppermute | solution.py:853
  433.1 3.5 all-to-all-start.7
  436.6 5.5 %branch_1_fun.48 = bf16[112,2,2048]{2,1,0:T(2,128)(2,1)} custom-call(s32[4]{0:T(128)S(1)} %get-tuple-element.227.pos, bf16[112,512]{1,0:T(8,128)(2,1)} %get-tuple-element.368.refs_0_, bf16[112,512]{1,0:T(8,128)(2,1)} %copy-done.131, bf16[112,512]{1,0:T(8,128)(2,1)} %copy-done.133, bf16[112,512]{1,0:T(8,128)(2,1)} %copy-done.135, ...), custom_call_target="tpu_custom_call" | custom-call | tf_op jit(solution)/shard_map/cond/branch_1_fun/pallas_call | solution.py:512
  442.1 6.1 %add_bitcast_fusion.1 = f32[256,9,512]{2,0,1:T(8,128)} fusion(f32[9,256,512]{2,1,0:T(8,128)} %get-tuple-element.379, bf16[9,256,512]{2,1,0:T(8,128)(2,1)} %collective-permute-done.181), kind=kLoop, calls=%fused_computation.134 | loop fusion | flops 2359296 | bytes 11796480 | tf_op jit(solution)/shard_map/cond/branch_1_fun/transpose | solution.py:1130
  (438 shorter events, 154.1 us)
Async XLA Ops:
  3.3 13.4 %collective-permute-start.186 = (s32[1,24]{1,0:T(1,128)S(1)}, s32[1,24]{1,0:T(1,128)S(1)}, u32[]{:S(2)}, u32[]{:S(2)}) collective-permute-start(s32[1,24]{1,0:T(1,128)S(1)} %copy-done.155), channel_id=1, source_target_pairs={{0,1},{1,2},{2,3},{3,0},{4,5},{5,6},{6,7},{7,4},{8,9},{9,10},{10,1... | collective-permute-start | bytes 296 | tf_op jit(solution)/shard_map/ppermute | solution.py:775
  6.3 10.4 %collective-permute-start.187 = (s32[1,24]{1,0:T(1,128)S(1)}, s32[1,24]{1,0:T(1,128)S(1)}, u32[]{:S(2)}, u32[]{:S(2)}) collective-permute-start(s32[1,24]{1,0:T(1,128)S(1)} %copy-done.155), channel_id=1, source_target_pairs={{0,2},{1,3},{2,0},{3,1},{4,6},{5,7},{6,4},{7,5},{8,10},{9,11},{10,... | collective-permute-start | bytes 296 | tf_op jit(solution)/shard_map/ppermute | solution.py:775
  8.9 7.8 %collective-permute-start.188 = (s32[1,24]{1,0:T(1,128)S(1)}, s32[1,24]{1,0:T(1,128)S(1)}, u32[]{:S(2)}, u32[]{:S(2)}) collective-permute-start(s32[1,24]{1,0:T(1,128)S(1)} %copy-done.155), channel_id=1, source_target_pairs={{0,3},{1,0},{2,1},{3,2},{4,7},{5,4},{6,5},{7,6},{8,11},{9,8},{10,9... | collective-permute-start | bytes 296 | tf_op jit(solution)/shard_map/ppermute | solution.py:775
  10.3 8.1 %collective-permute-start.190 = (f32[2,256]{1,0:T(2,128)S(1)}, f32[2,256]{1,0:T(2,128)S(1)}, u32[]{:S(2)}, u32[]{:S(2)}) collective-permute-start(f32[2,256]{1,0:T(2,128)S(1)} %pad_maximum_fusion.15), channel_id=1, source_target_pairs={{0,4},{4,0},{8,12},{12,8},{16,20},{20,16},{24,28},{28,24},{1,5},{5... | collective-permute-start | bytes 6152 | tf_op jit(solution)/shard_map/ppermute | solution.py:785
  10.4 13.3 %collective-permute-start.189 = (bf16[9,256,512]{2,1,0:T(8,128)(2,1)}, bf16[9,256,512]{2,1,0:T(8,128)(2,1)}, u32[]{:S(2)}, u32[]{:S(2)}) collective-permute-start(bf16[9,256,512]{2,1,0:T(8,128)(2,1)} %bitcast.150), channel_id=1, source_target_pairs={{0,4},{4,0},{8,12},{12,8},{16,20},{20,16},{24,28},{28,24},{1,5},{5... | collective-permute-start | bytes 7077896 | tf_op jit(solution)/shard_map/ppermute | solution.py:785
  10.9 12.8 %all-to-all-start.8 = ((bf16[8,112,256]{2,1,0:T(8,128)(2,1)}), bf16[8,112,256]{2,1,0:T(8,128)(2,1)S(1)}, u32[]{:S(2)}, u32[]{:S(2)}) async-start(bf16[8,112,256]{2,1,0:T(8,128)(2,1)} %bitcast.80), calls=%async_computation.8 | async-start | bytes 917504 | tf_op jit(solution)/shard_map/all_to_all | solution.py:771
  30.1 16.1 %collective-permute-start.111 = (bf16[9,128,128]{2,1,0:T(8,128)(2,1)}, bf16[9,128,128]{2,1,0:T(8,128)(2,1)S(1)}, u32[]{:S(2)}, u32[]{:S(2)}) collective-permute-start(bf16[9,128,128]{2,1,0:T(8,128)(2,1)} %get-tuple-element.258), channel_id=1, source_target_pairs={{0,8},{4,12},{8,0},{12,4},{16,24},{20,28},{24,16},{28,20},{1,9},{5... | collective-permute-start | bytes 884744 | tf_op jit(solution)/shard_map/cond/branch_1_fun/ppermute | solution.py:850
  30.8 15.6 %collective-permute-start.112 = (bf16[9,128,128]{2,1,0:T(8,128)(2,1)}, bf16[9,128,128]{2,1,0:T(8,128)(2,1)S(1)}, u32[]{:S(2)}, u32[]{:S(2)}) collective-permute-start(bf16[9,128,128]{2,1,0:T(8,128)(2,1)} %get-tuple-element.259), channel_id=1, source_target_pairs={{0,16},{4,20},{8,24},{12,28},{16,0},{20,4},{24,8},{28,12},{1,17},{... | collective-permute-start | bytes 884744 | tf_op jit(solution)/shard_map/cond/branch_1_fun/ppermute | solution.py:850
  31.3 15.0 %collective-permute-start.113 = (bf16[9,128,128]{2,1,0:T(8,128)(2,1)}, bf16[9,128,128]{2,1,0:T(8,128)(2,1)S(1)}, u32[]{:S(2)}, u32[]{:S(2)}) collective-permute-start(bf16[9,128,128]{2,1,0:T(8,128)(2,1)} %get-tuple-element.260), channel_id=1, source_target_pairs={{0,24},{4,28},{8,16},{12,20},{16,8},{20,12},{24,0},{28,4},{1,25},{... | collective-permute-start | bytes 884744 | tf_op jit(solution)/shard_map/cond/branch_1_fun/ppermute | solution.py:850
  33.8 12.5 %collective-permute-start.94 = (bf16[384,512]{1,0:T(8,128)(2,1)S(1)}, bf16[384,512]{1,0:T(8,128)(2,1)S(1)}, u32[]{:S(2)}, u32[]{:S(2)}) collective-permute-start(bf16[384,512]{1,0:T(8,128)(2,1)S(1)} %pad_maximum_fusion.9.refs_0_.refs_14_), channel_id=1, source_target_pairs={{0,1},{1,2},{2,3},{3,0},{4,5},{5,6},{6,7},{7,4},{8,9},{9,10},{10,1... | collective-permute-start | bytes 1179656 | tf_op jit(solution)/shard_map/cond/branch_1_fun/ppermute | solution.py:853
  48.0 59.8 %all-to-all-start.4 = ((bf16[4,9,128,128]{3,2,1,0:T(8,128)(2,1)}), bf16[4,9,128,128]{3,2,1,0:T(8,128)(2,1)S(1)}, u32[]{:S(2)}, u32[]{:S(2)}) async-start(bf16[4,9,128,128]{3,2,1,0:T(8,128)(2,1)} %branch_1_fun.27), calls=%async_computation.4 | async-start | bytes 2359296 | tf_op jit(solution)/shard_map/cond/branch_1_fun/all_to_all | solution.py:908
  51.6 12.1 %collective-permute-start.96 = (bf16[384,512]{1,0:T(8,128)(2,1)S(1)}, bf16[384,512]{1,0:T(8,128)(2,1)S(1)}, u32[]{:S(2)}, u32[]{:S(2)}) collective-permute-start(bf16[384,512]{1,0:T(8,128)(2,1)S(1)} %pad_maximum_fusion.9.refs_0_.refs_14_), channel_id=1, source_target_pairs={{0,16},{4,20},{8,24},{12,28},{16,0},{20,4},{24,8},{28,12},{1,17},{... | collective-permute-start | bytes 1179656 | tf_op jit(solution)/shard_map/cond/branch_1_fun/ppermute | solution.py:850
  52.8 30.3 %collective-permute-start.95 = (bf16[384,512]{1,0:T(8,128)(2,1)S(1)}, bf16[384,512]{1,0:T(8,128)(2,1)S(1)}, u32[]{:S(2)}, u32[]{:S(2)}) collective-permute-start(bf16[384,512]{1,0:T(8,128)(2,1)S(1)} %collective-permute-done.94.refs_0_.refs_8_), channel_id=1, source_target_pairs={{0,1},{1,2},{2,3},{3,0},{4,5},{5,6},{6,7},{7,4},{8,9},{9,10},{10,1... | collective-permute-start | bytes 1179656 | tf_op jit(solution)/shard_map/cond/branch_1_fun/ppermute | solution.py:853
  54.7 28.4 %collective-permute-start.97 = (bf16[384,512]{1,0:T(8,128)(2,1)S(1)}, bf16[384,512]{1,0:T(8,128)(2,1)S(1)}, u32[]{:S(2)}, u32[]{:S(2)}) collective-permute-start(bf16[384,512]{1,0:T(8,128)(2,1)S(1)} %collective-permute-done.94.refs_0_.refs_8_), channel_id=1, source_target_pairs={{0,16},{4,20},{8,24},{12,28},{16,0},{20,4},{24,8},{28,12},{1,17},{... | collective-permute-start | bytes 1179656 | tf_op jit(solution)/shard_map/cond/branch_1_fun/ppermute | solution.py:850
  62.1 12.2 %collective-permute-start.101 = (bf16[112,512]{1,0:T(8,128)(2,1)}, bf16[112,512]{1,0:T(8,128)(2,1)}, u32[]{:S(2)}, u32[]{:S(2)}) collective-permute-start(bf16[112,512]{1,0:T(8,128)(2,1)} %get-tuple-element.244), channel_id=1, source_target_pairs={{0,16},{4,20},{8,24},{12,28},{16,0},{20,4},{24,8},{28,12},{1,17},{... | collective-permute-start | bytes 344072 | tf_op jit(solution)/shard_map/cond/branch_1_fun/ppermute | solution.py:850
  63.7 19.2 %collective-permute-start.102 = (bf16[112,512]{1,0:T(8,128)(2,1)}, bf16[112,512]{1,0:T(8,128)(2,1)S(1)}, u32[]{:S(2)}, u32[]{:S(2)}) collective-permute-start(bf16[112,512]{1,0:T(8,128)(2,1)} %get-tuple-element.245), channel_id=1, source_target_pairs={{0,20},{4,16},{8,28},{12,24},{16,4},{20,0},{24,12},{28,8},{1,21},{... | collective-permute-start | bytes 344072 | tf_op jit(solution)/shard_map/cond/branch_1_fun/ppermute | solution.py:850
  67.8 15.1 %collective-permute-start.98 = (bf16[112,512]{1,0:T(8,128)(2,1)}, bf16[112,512]{1,0:T(8,128)(2,1)S(1)}, u32[]{:S(2)}, u32[]{:S(2)}) collective-permute-start(bf16[112,512]{1,0:T(8,128)(2,1)} %get-tuple-element.241), channel_id=1, source_target_pairs={{0,4},{4,0},{8,12},{12,8},{16,20},{20,16},{24,28},{28,24},{1,5},{5... | collective-permute-start | bytes 344072 | tf_op jit(solution)/shard_map/cond/branch_1_fun/ppermute | solution.py:850
  74.3 8.7 %collective-permute-start.99 = (bf16[112,512]{1,0:T(8,128)(2,1)}, bf16[112,512]{1,0:T(8,128)(2,1)S(1)}, u32[]{:S(2)}, u32[]{:S(2)}) collective-permute-start(bf16[112,512]{1,0:T(8,128)(2,1)} %get-tuple-element.242), channel_id=1, source_target_pairs={{0,8},{4,12},{8,0},{12,4},{16,24},{20,28},{24,16},{28,20},{1,9},{5... | collective-permute-start | bytes 344072 | tf_op jit(solution)/shard_map/cond/branch_1_fun/ppermute | solution.py:850
  83.8 22.7 %collective-permute-start.103 = (bf16[384,512]{1,0:T(8,128)(2,1)S(1)}, bf16[384,512]{1,0:T(8,128)(2,1)}, u32[]{:S(2)}, u32[]{:S(2)}) collective-permute-start(bf16[384,512]{1,0:T(8,128)(2,1)S(1)} %collective-permute-done.95.refs_0_.refs_10_), channel_id=1, source_target_pairs={{0,1},{1,2},{2,3},{3,0},{4,5},{5,6},{6,7},{7,4},{8,9},{9,10},{10,1... | collective-permute-start | bytes 1179656 | tf_op jit(solution)/shard_map/cond/branch_1_fun/ppermute | solution.py:853
  87.8 18.7 %collective-permute-start.104 = (bf16[384,512]{1,0:T(8,128)(2,1)S(1)}, bf16[384,512]{1,0:T(8,128)(2,1)S(1)}, u32[]{:S(2)}, u32[]{:S(2)}) collective-permute-start(bf16[384,512]{1,0:T(8,128)(2,1)S(1)} %collective-permute-done.95.refs_0_.refs_10_), channel_id=1, source_target_pairs={{0,16},{4,20},{8,24},{12,28},{16,0},{20,4},{24,8},{28,12},{1,17},{... | collective-permute-start | bytes 1179656 | tf_op jit(solution)/shard_map/cond/branch_1_fun/ppermute | solution.py:850
  97.7 8.8 %collective-permute-start.109 = (bf16[112,512]{1,0:T(8,128)(2,1)S(1)}, bf16[112,512]{1,0:T(8,128)(2,1)S(1)}, u32[]{:S(2)}, u32[]{:S(2)}) collective-permute-start(bf16[112,512]{1,0:T(8,128)(2,1)S(1)} %copy-done.157), channel_id=1, source_target_pairs={{0,24},{4,28},{8,16},{12,20},{16,8},{20,12},{24,0},{28,4},{1,25},{... | collective-permute-start | bytes 344072 | tf_op jit(solution)/shard_map/cond/branch_1_fun/ppermute | solution.py:850
  107.9 11.8 %collective-permute-start.118 = (bf16[384,512]{1,0:T(8,128)(2,1)}, bf16[384,512]{1,0:T(8,128)(2,1)}, u32[]{:S(2)}, u32[]{:S(2)}) collective-permute-start(bf16[384,512]{1,0:T(8,128)(2,1)} %collective-permute-done.103.refs_0_.refs_12_), channel_id=1, source_target_pairs={{0,16},{4,20},{8,24},{12,28},{16,0},{20,4},{24,8},{28,12},{1,17},{... | collective-permute-start | bytes 1179656 | tf_op jit(solution)/shard_map/cond/branch_1_fun/ppermute | solution.py:850
  113.5 12.2 %collective-permute-start.115 = (bf16[384,256]{1,0:T(8,128)(2,1)S(1)}, bf16[384,256]{1,0:T(8,128)(2,1)S(1)}, u32[]{:S(2)}, u32[]{:S(2)}) collective-permute-start(bf16[384,256]{1,0:T(8,128)(2,1)S(1)} %get-tuple-element.264), channel_id=1, source_target_pairs={{0,8},{4,12},{8,0},{12,4},{16,24},{20,28},{24,16},{28,20},{1,9},{5... | collective-permute-start | bytes 589832 | tf_op jit(solution)/shard_map/cond/branch_1_fun/ppermute | solution.py:850
  115.0 10.5 %collective-permute-start.116 = (bf16[384,256]{1,0:T(8,128)(2,1)S(1)}, bf16[384,256]{1,0:T(8,128)(2,1)S(1)}, u32[]{:S(2)}, u32[]{:S(2)}) collective-permute-start(bf16[384,256]{1,0:T(8,128)(2,1)S(1)} %get-tuple-element.269), channel_id=1, source_target_pairs={{0,8},{4,12},{8,0},{12,4},{16,24},{20,28},{24,16},{28,20},{1,9},{5... | collective-permute-start | bytes 589832 | tf_op jit(solution)/shard_map/cond/branch_1_fun/ppermute | solution.py:850
  118.5 11.2 %collective-permute-start.117 = (bf16[384,256]{1,0:T(8,128)(2,1)S(1)}, bf16[384,256]{1,0:T(8,128)(2,1)S(1)}, u32[]{:S(2)}, u32[]{:S(2)}) collective-permute-start(bf16[384,256]{1,0:T(8,128)(2,1)S(1)} %get-tuple-element.274), channel_id=1, source_target_pairs={{0,8},{4,12},{8,0},{12,4},{16,24},{20,28},{24,16},{28,20},{1,9},{5... | collective-permute-start | bytes 589832 | tf_op jit(solution)/shard_map/cond/branch_1_fun/ppermute | solution.py:850
  122.3 10.9 %collective-permute-start.119 = (bf16[384,256]{1,0:T(8,128)(2,1)S(1)}, bf16[384,256]{1,0:T(8,128)(2,1)S(1)}, u32[]{:S(2)}, u32[]{:S(2)}) collective-permute-start(bf16[384,256]{1,0:T(8,128)(2,1)S(1)} %get-tuple-element.278), channel_id=1, source_target_pairs={{0,8},{4,12},{8,0},{12,4},{16,24},{20,28},{24,16},{28,20},{1,9},{5... | collective-permute-start | bytes 589832 | tf_op jit(solution)/shard_map/cond/branch_1_fun/ppermute | solution.py:850
  135.4 7.8 %collective-permute-start.121 = (bf16[384,256]{1,0:T(8,128)(2,1)S(1)}, bf16[384,256]{1,0:T(8,128)(2,1)S(1)}, u32[]{:S(2)}, u32[]{:S(2)}) collective-permute-start(bf16[384,256]{1,0:T(8,128)(2,1)S(1)} %get-tuple-element.706.refs_0_.refs_8_), channel_id=1, source_target_pairs={{0,8},{4,12},{8,0},{12,4},{16,24},{20,28},{24,16},{28,20},{1,9},{5... | collective-permute-start | bytes 589832 | tf_op jit(solution)/shard_map/cond/branch_1_fun/ppermute | solution.py:850
  135.7 11.3 %collective-permute-start.122 = (bf16[384,256]{1,0:T(8,128)(2,1)S(1)}, bf16[384,256]{1,0:T(8,128)(2,1)S(1)}, u32[]{:S(2)}, u32[]{:S(2)}) collective-permute-start(bf16[384,256]{1,0:T(8,128)(2,1)S(1)} %get-tuple-element.706.refs_0_.refs_8_), channel_id=1, source_target_pairs={{0,16},{4,20},{8,24},{12,28},{16,0},{20,4},{24,8},{28,12},{1,17},{... | collective-permute-start | bytes 589832 | tf_op jit(solution)/shard_map/cond/branch_1_fun/ppermute | solution.py:850
  136.2 10.8 %collective-permute-start.123 = (bf16[384,256]{1,0:T(8,128)(2,1)S(1)}, bf16[384,256]{1,0:T(8,128)(2,1)S(1)}, u32[]{:S(2)}, u32[]{:S(2)}) collective-permute-start(bf16[384,256]{1,0:T(8,128)(2,1)S(1)} %get-tuple-element.706.refs_0_.refs_8_), channel_id=1, source_target_pairs={{0,24},{4,28},{8,16},{12,20},{16,8},{20,12},{24,0},{28,4},{1,25},{... | collective-permute-start | bytes 589832 | tf_op jit(solution)/shard_map/cond/branch_1_fun/ppermute | solution.py:850
  153.3 20.8 %collective-permute-start.133 = (bf16[384,1024]{1,0:T(8,128)(2,1)S(1)}, bf16[384,1024]{1,0:T(8,128)(2,1)S(1)}, u32[]{:S(2)}, u32[]{:S(2)}) collective-permute-start(bf16[384,1024]{1,0:T(8,128)(2,1)S(1)} %branch_1_fun.33), channel_id=1, source_target_pairs={{0,1},{1,2},{2,3},{3,0},{4,5},{5,6},{6,7},{7,4},{8,9},{9,10},{10,1... | collective-permute-start | bytes 2359304 | tf_op jit(solution)/shard_map/cond/branch_1_fun/ppermute | solution.py:853
  154.9 8.8 %collective-permute-start.126 = (bf16[384,256]{1,0:T(8,128)(2,1)S(1)}, bf16[384,256]{1,0:T(8,128)(2,1)S(1)}, u32[]{:S(2)}, u32[]{:S(2)}) collective-permute-start(bf16[384,256]{1,0:T(8,128)(2,1)S(1)} %get-tuple-element.281.refs_0_.refs_12_), channel_id=1, source_target_pairs={{0,24},{4,28},{8,16},{12,20},{16,8},{20,12},{24,0},{28,4},{1,25},{... | collective-permute-start | bytes 589832 | tf_op jit(solution)/shard_map/cond/branch_1_fun/ppermute | solution.py:850
  156.5 9.7 %collective-permute-start.124 = (bf16[384,256]{1,0:T(8,128)(2,1)S(1)}, bf16[384,256]{1,0:T(8,128)(2,1)S(1)}, u32[]{:S(2)}, u32[]{:S(2)}) collective-permute-start(bf16[384,256]{1,0:T(8,128)(2,1)S(1)} %get-tuple-element.281.refs_0_.refs_12_), channel_id=1, source_target_pairs={{0,8},{4,12},{8,0},{12,4},{16,24},{20,28},{24,16},{28,20},{1,9},{5... | collective-permute-start | bytes 589832 | tf_op jit(solution)/shard_map/cond/branch_1_fun/ppermute | solution.py:850
  157.7 8.5 %collective-permute-start.125 = (bf16[384,256]{1,0:T(8,128)(2,1)S(1)}, bf16[384,256]{1,0:T(8,128)(2,1)S(1)}, u32[]{:S(2)}, u32[]{:S(2)}) collective-permute-start(bf16[384,256]{1,0:T(8,128)(2,1)S(1)} %get-tuple-element.281.refs_0_.refs_12_), channel_id=1, source_target_pairs={{0,16},{4,20},{8,24},{12,28},{16,0},{20,4},{24,8},{28,12},{1,17},{... | collective-permute-start | bytes 589832 | tf_op jit(solution)/shard_map/cond/branch_1_fun/ppermute | solution.py:850
  174.4 20.0 %collective-permute-start.134 = (bf16[384,1024]{1,0:T(8,128)(2,1)S(1)}, bf16[384,1024]{1,0:T(8,128)(2,1)S(1)}, u32[]{:S(2)}, u32[]{:S(2)}) collective-permute-start(bf16[384,1024]{1,0:T(8,128)(2,1)S(1)} %add_convert_fusion.9), channel_id=1, source_target_pairs={{0,1},{1,2},{2,3},{3,0},{4,5},{5,6},{6,7},{7,4},{8,9},{9,10},{10,1... | collective-permute-start | bytes 2359304 | tf_op jit(solution)/shard_map/cond/branch_1_fun/ppermute | solution.py:853
  176.4 8.5 %collective-permute-start.129 = (bf16[384,256]{1,0:T(8,128)(2,1)S(1)}, bf16[384,256]{1,0:T(8,128)(2,1)S(1)}, u32[]{:S(2)}, u32[]{:S(2)}) collective-permute-start(bf16[384,256]{1,0:T(8,128)(2,1)S(1)} %get-tuple-element.283.refs_0_.refs_16_), channel_id=1, source_target_pairs={{0,24},{4,28},{8,16},{12,20},{16,8},{20,12},{24,0},{28,4},{1,25},{... | collective-permute-start | bytes 589832 | tf_op jit(solution)/shard_map/cond/branch_1_fun/ppermute | solution.py:850
  177.8 9.6 %collective-permute-start.127 = (bf16[384,256]{1,0:T(8,128)(2,1)S(1)}, bf16[384,256]{1,0:T(8,128)(2,1)S(1)}, u32[]{:S(2)}, u32[]{:S(2)}) collective-permute-start(bf16[384,256]{1,0:T(8,128)(2,1)S(1)} %get-tuple-element.283.refs_0_.refs_16_), channel_id=1, source_target_pairs={{0,8},{4,12},{8,0},{12,4},{16,24},{20,28},{24,16},{28,20},{1,9},{5... | collective-permute-start | bytes 589832 | tf_op jit(solution)/shard_map/cond/branch_1_fun/ppermute | solution.py:850
  179.5 7.9 %collective-permute-start.128 = (bf16[384,256]{1,0:T(8,128)(2,1)S(1)}, bf16[384,256]{1,0:T(8,128)(2,1)S(1)}, u32[]{:S(2)}, u32[]{:S(2)}) collective-permute-start(bf16[384,256]{1,0:T(8,128)(2,1)S(1)} %get-tuple-element.283.refs_0_.refs_16_), channel_id=1, source_target_pairs={{0,16},{4,20},{8,24},{12,28},{16,0},{20,4},{24,8},{28,12},{1,17},{... | collective-permute-start | bytes 589832 | tf_op jit(solution)/shard_map/cond/branch_1_fun/ppermute | solution.py:850
  187.4 9.7 %collective-permute-start.132 = (bf16[384,256]{1,0:T(8,128)(2,1)S(1)}, bf16[384,256]{1,0:T(8,128)(2,1)S(1)}, u32[]{:S(2)}, u32[]{:S(2)}) collective-permute-start(bf16[384,256]{1,0:T(8,128)(2,1)S(1)} %get-tuple-element.285.refs_0_.refs_4_), channel_id=1, source_target_pairs={{0,24},{4,28},{8,16},{12,20},{16,8},{20,12},{24,0},{28,4},{1,25},{... | collective-permute-start | bytes 589832 | tf_op jit(solution)/shard_map/cond/branch_1_fun/ppermute | solution.py:850
  188.6 10.2 %collective-permute-start.130 = (bf16[384,256]{1,0:T(8,128)(2,1)S(1)}, bf16[384,256]{1,0:T(8,128)(2,1)S(1)}, u32[]{:S(2)}, u32[]{:S(2)}) collective-permute-start(bf16[384,256]{1,0:T(8,128)(2,1)S(1)} %get-tuple-element.285.refs_0_.refs_4_), channel_id=1, source_target_pairs={{0,8},{4,12},{8,0},{12,4},{16,24},{20,28},{24,16},{28,20},{1,9},{5... | collective-permute-start | bytes 589832 | tf_op jit(solution)/shard_map/cond/branch_1_fun/ppermute | solution.py:850
  190.3 8.5 %collective-permute-start.131 = (bf16[384,256]{1,0:T(8,128)(2,1)S(1)}, bf16[384,256]{1,0:T(8,128)(2,1)S(1)}, u32[]{:S(2)}, u32[]{:S(2)}) collective-permute-start(bf16[384,256]{1,0:T(8,128)(2,1)S(1)} %get-tuple-element.285.refs_0_.refs_4_), channel_id=1, source_target_pairs={{0,16},{4,20},{8,24},{12,28},{16,0},{20,4},{24,8},{28,12},{1,17},{... | collective-permute-start | bytes 589832 | tf_op jit(solution)/shard_map/cond/branch_1_fun/ppermute | solution.py:850
  194.7 19.5 %collective-permute-start.135 = (bf16[384,1024]{1,0:T(8,128)(2,1)S(1)}, bf16[384,1024]{1,0:T(8,128)(2,1)S(1)}, u32[]{:S(2)}, u32[]{:S(2)}) collective-permute-start(bf16[384,1024]{1,0:T(8,128)(2,1)S(1)} %add_convert_fusion.8), channel_id=1, source_target_pairs={{0,1},{1,2},{2,3},{3,0},{4,5},{5,6},{6,7},{7,4},{8,9},{9,10},{10,1... | collective-permute-start | bytes 2359304 | tf_op jit(solution)/shard_map/cond/branch_1_fun/ppermute | solution.py:853
  235.2 19.7 %collective-permute-start.145 = (bf16[384,1024]{1,0:T(8,128)(2,1)S(1)}, bf16[384,1024]{1,0:T(8,128)(2,1)S(1)}, u32[]{:S(2)}, u32[]{:S(2)}) collective-permute-start(bf16[384,1024]{1,0:T(8,128)(2,1)S(1)} %get-tuple-element.340.refs_0_), channel_id=1, source_target_pairs={{0,1},{1,2},{2,3},{3,0},{4,5},{5,6},{6,7},{7,4},{8,9},{9,10},{10,1... | collective-permute-start | bytes 2359304 | tf_op jit(solution)/shard_map/cond/branch_1_fun/ppermute | solution.py:853
  241.0 7.7 %collective-permute-start.147 = (bf16[384,256]{1,0:T(8,128)(2,1)S(1)}, bf16[384,256]{1,0:T(8,128)(2,1)S(1)}, u32[]{:S(2)}, u32[]{:S(2)}) collective-permute-start(bf16[384,256]{1,0:T(8,128)(2,1)S(1)} %get-tuple-element.310), channel_id=1, source_target_pairs={{0,16},{4,20},{8,24},{12,28},{16,0},{20,4},{24,8},{28,12},{1,17},{... | collective-permute-start | bytes 589832 | tf_op jit(solution)/shard_map/cond/branch_1_fun/ppermute | solution.py:850
  241.9 8.6 %collective-permute-start.148 = (bf16[384,256]{1,0:T(8,128)(2,1)S(1)}, bf16[384,256]{1,0:T(8,128)(2,1)S(1)}, u32[]{:S(2)}, u32[]{:S(2)}) collective-permute-start(bf16[384,256]{1,0:T(8,128)(2,1)S(1)} %get-tuple-element.311), channel_id=1, source_target_pairs={{0,24},{4,28},{8,16},{12,20},{16,8},{20,12},{24,0},{28,4},{1,25},{... | collective-permute-start | bytes 589832 | tf_op jit(solution)/shard_map/cond/branch_1_fun/ppermute | solution.py:850
  255.0 18.8 %collective-permute-start.149 = (bf16[384,1024]{1,0:T(8,128)(2,1)S(1)}, bf16[384,1024]{1,0:T(8,128)(2,1)S(1)}, u32[]{:S(2)}, u32[]{:S(2)}) collective-permute-start(bf16[384,1024]{1,0:T(8,128)(2,1)S(1)} %collective-permute-done.145.refs_0_.refs_1_), channel_id=1, source_target_pairs={{0,1},{1,2},{2,3},{3,0},{4,5},{5,6},{6,7},{7,4},{8,9},{9,10},{10,1... | collective-permute-start | bytes 2359304 | tf_op jit(solution)/shard_map/cond/branch_1_fun/ppermute | solution.py:853
  261.5 7.7 %collective-permute-start.152 = (bf16[384,256]{1,0:T(8,128)(2,1)S(1)}, bf16[384,256]{1,0:T(8,128)(2,1)S(1)}, u32[]{:S(2)}, u32[]{:S(2)}) collective-permute-start(bf16[384,256]{1,0:T(8,128)(2,1)S(1)} %get-tuple-element.315), channel_id=1, source_target_pairs={{0,24},{4,28},{8,16},{12,20},{16,8},{20,12},{24,0},{28,4},{1,25},{... | collective-permute-start | bytes 589832 | tf_op jit(solution)/shard_map/cond/branch_1_fun/ppermute | solution.py:850
  273.8 18.0 %collective-permute-start.156 = (bf16[384,1024]{1,0:T(8,128)(2,1)S(1)}, bf16[384,1024]{1,0:T(8,128)(2,1)S(1)}, u32[]{:S(2)}, u32[]{:S(2)}) collective-permute-start(bf16[384,1024]{1,0:T(8,128)(2,1)S(1)} %collective-permute-done.149.refs_0_.refs_2_), channel_id=1, source_target_pairs={{0,1},{1,2},{2,3},{3,0},{4,5},{5,6},{6,7},{7,4},{8,9},{9,10},{10,1... | collective-permute-start | bytes 2359304 | tf_op jit(solution)/shard_map/cond/branch_1_fun/ppermute | solution.py:853
  316.9 10.4 %collective-permute-start.164 = (bf16[384,512]{1,0:T(8,128)(2,1)S(1)}, bf16[384,512]{1,0:T(8,128)(2,1)S(1)}, u32[]{:S(2)}, u32[]{:S(2)}) collective-permute-start(bf16[384,512]{1,0:T(8,128)(2,1)S(1)} %get-tuple-element.330), channel_id=1, source_target_pairs={{0,16},{4,20},{8,24},{12,28},{16,0},{20,4},{24,8},{28,12},{1,17},{... | collective-permute-start | bytes 1179656 | tf_op jit(solution)/shard_map/cond/branch_1_fun/ppermute | solution.py:850
  317.8 9.6 %collective-permute-start.163 = (bf16[384,512]{1,0:T(8,128)(2,1)S(1)}, bf16[384,512]{1,0:T(8,128)(2,1)S(1)}, u32[]{:S(2)}, u32[]{:S(2)}) collective-permute-start(bf16[384,512]{1,0:T(8,128)(2,1)S(1)} %get-tuple-element.676), channel_id=1, source_target_pairs={{0,4},{4,0},{8,12},{12,8},{16,20},{20,16},{24,28},{28,24},{1,5},{5... | collective-permute-start | bytes 1179656 | tf_op jit(solution)/shard_map/cond/branch_1_fun/ppermute | solution.py:850
  318.0 20.3 %collective-permute-start.162 = (bf16[1152,256]{1,0:T(8,128)(2,1)S(1)}, bf16[1152,256]{1,0:T(8,128)(2,1)S(1)}, u32[]{:S(2)}, u32[]{:S(2)}) collective-permute-start(bf16[1152,256]{1,0:T(8,128)(2,1)S(1)} %pad_maximum_fusion.8), channel_id=1, source_target_pairs={{0,8},{4,12},{8,0},{12,4},{16,24},{20,28},{24,16},{28,20},{1,9},{5... | collective-permute-start | bytes 1769480 | tf_op jit(solution)/shard_map/cond/branch_1_fun/ppermute | solution.py:850
  330.6 7.7 %collective-permute-start.167 = (bf16[112,512]{1,0:T(8,128)(2,1)S(1)}, bf16[112,512]{1,0:T(8,128)(2,1)S(1)}, u32[]{:S(2)}, u32[]{:S(2)}) collective-permute-start(bf16[112,512]{1,0:T(8,128)(2,1)S(1)} %get-tuple-element.672), channel_id=1, source_target_pairs={{0,12},{4,8},{8,4},{12,0},{16,28},{20,24},{24,20},{28,16},{1,13},{... | collective-permute-start | bytes 344072 | tf_op jit(solution)/shard_map/cond/branch_1_fun/ppermute | solution.py:850
  331.1 23.6 %collective-permute-start.168 = (bf16[384,512]{1,0:T(8,128)(2,1)S(1)}, bf16[384,512]{1,0:T(8,128)(2,1)S(1)}, u32[]{:S(2)}, u32[]{:S(2)}) collective-permute-start(bf16[384,512]{1,0:T(8,128)(2,1)S(1)} %add_convert_fusion.13), channel_id=1, source_target_pairs={{0,1},{1,2},{2,3},{3,0},{4,5},{5,6},{6,7},{7,4},{8,9},{9,10},{10,1... | collective-permute-start | bytes 1179656 | tf_op jit(solution)/shard_map/cond/branch_1_fun/ppermute | solution.py:853
  344.9 11.5 %collective-permute-start.169 = (bf16[384,512]{1,0:T(8,128)(2,1)S(1)}, bf16[384,512]{1,0:T(8,128)(2,1)S(1)}, u32[]{:S(2)}, u32[]{:S(2)}) collective-permute-start(bf16[384,512]{1,0:T(8,128)(2,1)S(1)} %get-tuple-element.338), channel_id=1, source_target_pairs={{0,16},{4,20},{8,24},{12,28},{16,0},{20,4},{24,8},{28,12},{1,17},{... | collective-permute-start | bytes 1179656 | tf_op jit(solution)/shard_map/cond/branch_1_fun/ppermute | solution.py:850
  360.7 42.0 %all-to-all-start.5 = ((bf16[4,9,128,128]{3,2,1,0:T(8,128)(2,1)}), bf16[4,9,128,128]{3,2,1,0:T(8,128)(2,1)}, u32[]{:S(2)}, u32[]{:S(2)}) async-start(bf16[4,9,128,128]{3,2,1,0:T(8,128)(2,1)} %add_convert_fusion.7), calls=%async_computation.5 | async-start | bytes 2359296 | tf_op jit(solution)/shard_map/cond/branch_1_fun/all_to_all | solution.py:1067
  365.1 24.4 %collective-permute-start.171 = (bf16[384,512]{1,0:T(8,128)(2,1)S(1)}, bf16[384,512]{1,0:T(8,128)(2,1)S(1)}, u32[]{:S(2)}, u32[]{:S(2)}) collective-permute-start(bf16[384,512]{1,0:T(8,128)(2,1)S(1)} %copy-done.81), channel_id=1, source_target_pairs={{0,16},{4,20},{8,24},{12,28},{16,0},{20,4},{24,8},{28,12},{1,17},{... | collective-permute-start | bytes 1179656 | tf_op jit(solution)/shard_map/cond/branch_1_fun/ppermute | solution.py:850
  366.4 32.6 %collective-permute-start.175 = (bf16[384,512]{1,0:T(8,128)(2,1)S(1)}, bf16[384,512]{1,0:T(8,128)(2,1)}, u32[]{:S(2)}, u32[]{:S(2)}) collective-permute-start(bf16[384,512]{1,0:T(8,128)(2,1)S(1)} %copy-done.79), channel_id=1, source_target_pairs={{0,16},{4,20},{8,24},{12,28},{16,0},{20,4},{24,8},{28,12},{1,17},{... | collective-permute-start | bytes 1179656 | tf_op jit(solution)/shard_map/cond/branch_1_fun/ppermute | solution.py:850
  369.2 29.8 %collective-permute-start.174 = (bf16[384,512]{1,0:T(8,128)(2,1)}, bf16[384,512]{1,0:T(8,128)(2,1)S(1)}, u32[]{:S(2)}, u32[]{:S(2)}) collective-permute-start(bf16[384,512]{1,0:T(8,128)(2,1)} %add_convert_fusion.12), channel_id=1, source_target_pairs={{0,1},{1,2},{2,3},{3,0},{4,5},{5,6},{6,7},{7,4},{8,9},{9,10},{10,1... | collective-permute-start | bytes 1179656 | tf_op jit(solution)/shard_map/cond/branch_1_fun/ppermute | solution.py:853
  371.1 18.4 %collective-permute-start.173 = (bf16[112,512]{1,0:T(8,128)(2,1)}, bf16[112,512]{1,0:T(8,128)(2,1)S(1)}, u32[]{:S(2)}, u32[]{:S(2)}) collective-permute-start(bf16[112,512]{1,0:T(8,128)(2,1)} %get-tuple-element.344), channel_id=1, source_target_pairs={{0,20},{4,16},{8,28},{12,24},{16,4},{20,0},{24,12},{28,8},{1,21},{... | collective-permute-start | bytes 344072 | tf_op jit(solution)/shard_map/cond/branch_1_fun/ppermute | solution.py:850
  371.1 18.5 %collective-permute-start.172 = (bf16[112,512]{1,0:T(8,128)(2,1)}, bf16[112,512]{1,0:T(8,128)(2,1)S(1)}, u32[]{:S(2)}, u32[]{:S(2)}) collective-permute-start(bf16[112,512]{1,0:T(8,128)(2,1)} %get-tuple-element.343), channel_id=1, source_target_pairs={{0,16},{4,20},{8,24},{12,28},{16,0},{20,4},{24,8},{28,12},{1,17},{... | collective-permute-start | bytes 344072 | tf_op jit(solution)/shard_map/cond/branch_1_fun/ppermute | solution.py:850
  389.7 9.3 %collective-permute-start.179 = (bf16[112,512]{1,0:T(8,128)(2,1)S(1)}, bf16[112,512]{1,0:T(8,128)(2,1)S(1)}, u32[]{:S(2)}, u32[]{:S(2)}) collective-permute-start(bf16[112,512]{1,0:T(8,128)(2,1)S(1)} %copy-done.102), channel_id=1, source_target_pairs={{0,28},{4,24},{8,20},{12,16},{16,12},{20,8},{24,4},{28,0},{1,29},{... | collective-permute-start | bytes 344072 | tf_op jit(solution)/shard_map/cond/branch_1_fun/ppermute | solution.py:850
  402.7 25.4 %collective-permute-start.181 = (bf16[9,256,512]{2,1,0:T(8,128)(2,1)}, bf16[9,256,512]{2,1,0:T(8,128)(2,1)}, u32[]{:S(2)}, u32[]{:S(2)}) collective-permute-start(bf16[9,256,512]{2,1,0:T(8,128)(2,1)} %get-tuple-element.359), channel_id=1, source_target_pairs={{0,4},{4,0},{8,12},{12,8},{16,20},{20,16},{24,28},{28,24},{1,5},{5... | collective-permute-start | bytes 7077896 | tf_op jit(solution)/shard_map/cond/branch_1_fun/ppermute | solution.py:850
  405.6 22.6 %all-to-all-start.6 = ((bf16[4,9,128,128]{3,2,1,0:T(8,128)(2,1)}), bf16[4,9,128,128]{3,2,1,0:T(8,128)(2,1)S(1)}, u32[]{:S(2)}, u32[]{:S(2)}) async-start(bf16[4,9,128,128]{3,2,1,0:T(8,128)(2,1)} %all-to-all-done.5), calls=%async_computation.6 | async-start | bytes 2359296 | tf_op jit(solution)/shard_map/cond/branch_1_fun/all_to_all | solution.py:1103
  415.6 12.5 %collective-permute-start.180 = (bf16[384,512]{1,0:T(8,128)(2,1)S(1)}, bf16[384,512]{1,0:T(8,128)(2,1)S(1)}, u32[]{:S(2)}, u32[]{:S(2)}) collective-permute-start(bf16[384,512]{1,0:T(8,128)(2,1)S(1)} %add_convert_fusion.11), channel_id=1, source_target_pairs={{0,1},{1,2},{2,3},{3,0},{4,5},{5,6},{6,7},{7,4},{8,9},{9,10},{10,1... | collective-permute-start | bytes 1179656 | tf_op jit(solution)/shard_map/cond/branch_1_fun/ppermute | solution.py:853
  433.1 15.1 %all-to-all-start.7 = ((bf16[8,112,256]{2,1,0:T(8,128)(2,1)}), bf16[8,112,256]{2,1,0:T(8,128)(2,1)S(1)}, u32[]{:S(2)}, u32[]{:S(2)}) async-start(bf16[8,112,256]{2,1,0:T(8,128)(2,1)} %bitcast.71), calls=%async_computation.7 | async-start | bytes 917504 | tf_op jit(solution)/shard_map/cond/branch_1_fun/all_to_all | solution.py:1125
  (119 other events, 1097.9 us)

commit v5 on v4

--- a/solution.py
+++ b/solution.py
@@ -364,23 +364,29 @@
     )(pos, *pieces)
 
 
-def quarters_kernel(quads, out):
-    half, lanes = quads.shape[2:]
+def quarters_kernel(pos, *refs):
+    quads, out = refs[:4], refs[4]
+    taps, half, lanes = quads[0].shape
     for k in range(4):
-        row, lane = (k // 2) * half, (k % 2) * lanes
-        out[:, row : row + half, lane : lane + lanes] = quads[k].astype(out.dtype)
-
-
-def from_quarters(quads):
-    _, taps, half, lanes = quads.shape
+        row = pl.multiple_of((pos[1] ^ (k // 2)) * half, half)
+        lane = pl.multiple_of((pos[2] ^ (k % 2)) * lanes, lanes)
+        out[:, pl.ds(row, half), pl.ds(lane, lanes)] = quads[k][...].astype(out.dtype)
+
+
+def from_quarters(pos, quads):
+    taps, half, lanes = quads[0].shape
+    spec = pltpu.PrefetchScalarGridSpec(
+        num_scalar_prefetch=1,
+        grid=(1,),
+        in_specs=[same(*quads[0].shape)] * 4,
+        out_specs=same(taps, 2 * half, 2 * lanes),
+    )
     return pl.pallas_call(
         quarters_kernel,
-        grid=(1,),
-        in_specs=[same(*quads.shape)],
-        out_specs=same(taps, 2 * half, 2 * lanes),
+        grid_spec=spec,
         out_shape=jax.ShapeDtypeStruct((taps, 2 * half, 2 * lanes), f32),
         compiler_params=vmem(16),
-    )(quads)
+    )(pos, *quads)
 
 
 def conv_kernel(pieces, *refs):
@@ -704,7 +710,7 @@
     )(pos, *args)
 
 
-def clip_places(lengths, half_rows):
+def clip_places(lengths, sizes):
     clips = lengths.shape[1]
     each = clips // 3
 
@@ -716,12 +722,14 @@
         middle = jnp.where(late, place + each + each // 2, place + each // 2)
         return jnp.where(kind == 2, long, jnp.where(kind == 1, middle, place + each))
 
+    sizes = jnp.array(sizes, jnp.int32)[:, None, None]
     size = lengths + 1
     before = jnp.sum(jnp.where(rank(2) < rank(1), size[:, None, :], 0), axis=2)
-    late = (before + size > half_rows).astype(jnp.int32)
-    taken = jnp.sum((1 - late) * size, axis=1, keepdims=True)
-    fits = jnp.max(jnp.sum(late * size, axis=1)) <= half_rows
-    return late, before - late * taken, fits
+    late = ((before + size)[None] > sizes).astype(jnp.int32)
+    taken = jnp.sum((1 - late) * size[None], axis=2, keepdims=True)
+    rest = jnp.sum(late * size[None], axis=2)
+    small = jnp.sum((jnp.max(rest, axis=1) > sizes[:, 0, 0]).astype(jnp.int32))
+    return late, before[None] - late * taken, small
 
 
 def frame_clips(lengths_row, frames, outward):
@@ -778,7 +786,8 @@
     )
     me = lax.axis_index("tm")
     pos = jnp.stack([me % 2, me // 4, me // 2 % 2, me]).astype(jnp.int32)
-    quarters = to_quarters(pos, conv1_weight.transpose(1, 0, 2))
+    mine, quarters = lax.optimization_barrier((mine, conv1_weight))
+    quarters = to_quarters(pos, quarters.transpose(1, 0, 2))
     w2 = conv2_weight.transpose(1, 0, 2)
     norm2 = jnp.stack([norm2_gain, norm2_bias])
     flip = [(i, i ^ 1) for i in range(n)]
@@ -791,22 +800,21 @@
     ]
     core = lax.axis_index("tm") % 2
 
-    def places(half_rows):
-        late, start, fits = clip_places(every, half_rows)
-        row = jnp.where(late[0] == core, start[0], start[0] + half_rows)
-        targets = [jnp.max(jnp.where(x >= 0, row[None, :] + x, -1), axis=1) for x in orders]
-        return late, start, *targets, fits
-
-    *packed, fits = places(frames * 3 // 7)
-    *loose, _ = places(frames // 2)
-    chosen = [jnp.where(fits, x, y) for x, y in zip(packed, loose)]
-    return lax.cond(
-        fits,
-        functools.partial(on_rows, frames * 3 // 7),
-        functools.partial(on_rows, frames // 2),
+    sizes = [frames * 23 // 56, frames * 3 // 7, frames // 2]
+    late, start, small = clip_places(every, sizes)
+    away = jnp.array(sizes, jnp.int32)[:, None]
+    row = jnp.where(late[:, 0] == core, start[:, 0], start[:, 0] + away)
+    targets = [
+        jnp.max(jnp.where(x[None] >= 0, row[:, None, :] + x[None], -1), axis=2) for x in orders
+    ]
+    late, start, targets, small = lax.optimization_barrier((late, start, targets, small))
+    packings = [(late[k], start[k], *[x[k] for x in targets]) for k in range(len(sizes))]
+    return lax.switch(
+        small,
+        [functools.partial(on_rows, size, k) for k, size in enumerate(sizes)],
         mine,
         every,
-        chosen,
+        packings,
         quarters,
         norm1_gain,
         norm1_bias,
@@ -821,6 +829,7 @@
 
 def on_rows(
     rows,
+    size,
     mine,
     every,
     places,
@@ -871,7 +880,7 @@
     def rows_sum(x):
         return jnp.sum(x, axis=0)
 
-    late, start, target, outward = places
+    late, start, target, outward = places[size]
     picker = lax.broadcasted_iota(jnp.int32, (2 * rows, frames), 0) == target[None, :]
     picker = picker.astype(bf16)
     packed = mxu(picker, mine, NN).astype(bf16)
@@ -899,7 +908,7 @@
         ahead = along(x, 1) if r < PLANES - 1 else None
         nears.append(swap(x, Y))
         if r == 0:
-            w1 = [w1[0]] + [swap(w1[k], 2 * k) for k in range(1, CHIPS)]
+            w1 = [w1[0]] + [swap(after(w1[k], x), 2 * k) for k in range(1, CHIPS)]
             mask = row_masks(every, after(late, x), start, core, rows)
             mask = [mask[:, k : k + 1] for k in groups]
             ahead, *mask = lax.optimization_barrier((ahead, *mask))
@@ -908,18 +917,18 @@
             w1 = lax.all_to_all(w1, "batch", 0, 0, tiled=True)
             weights2 = taps2(pos, w2, after(w2_other, x))
             grad_in = list(to_lanes(pos, after(out_grad, x), n))
-            sent = [swap(grad_in[k], k) for k in (1, 2, 3, 4, 5)]
+            sent = [swap(after(grad_in[k], weights2), k) for k in (1, 2, 3)]
             ahead, nears[0], nears[1], _, *sent = lax.optimization_barrier(
                 (ahead, nears[0], nears[1], weights2, *sent)
             )
-            grad_in[1:6] = sent
+            grad_in[1:4] = sent
         if r == 2:
             both1 = norm_of_block(after(own_norm, x))
-            sent = [swap(after(grad_in[k], x), k) for k in (6, 7)]
+            sent = [swap(after(grad_in[k], x), k) for k in (4, 5, 6, 7)]
             ahead, nears[2], both1, *sent = lax.optimization_barrier(
                 (ahead, nears[2], both1, *sent)
             )
-            grad_in[6:] = sent
+            grad_in[4:] = sent
         if ahead is not None:
             mine.append(ahead)
     gain1, bias1 = both1[0], both1[1]
@@ -1030,8 +1039,30 @@
     pairs1[1] = [dpre1[1], swap(dpre1[1], X)]
     later = jnp.concatenate([dpre1[r] for r in order[1:]], axis=0)
     later_near = swap(after(later, pairs1[1][1]), X)
+    grads1 = after(grads1, dpre1[1])
+    whole1 = jnp.concatenate(
+        [
+            route(
+                grads1,
+                [((4 * y + 2 * x, j), (2 * j + x, j)) for j in groups for x in range(2)],
+            )
+            for y in range(2)
+        ],
+        axis=1,
+    )
+    pairs1[1][1], whole1 = lax.optimization_barrier((pairs1[1][1], whole1))
     terms[1] = conv_t(pairs1[1], weights1, 2)
-    first = (terms[1][0] + swap(terms[1][1], Y).astype(f32)).astype(bf16)
+    whole1 = after(whole1, terms[1][1])
+    mine1 = jnp.where(chip == plane, whole1, 0.0)
+    for s in range(1, PLANES):
+        mine1 += route(
+            whole1,
+            [((2 * j + c, j), (2 * j + c, (j + s) % PLANES)) for j in groups for c in range(2)],
+        )
+
+    near, mine1 = lax.optimization_barrier((swap(terms[1][1], Y), mine1))
+    bias1_grad, gain1_grad = mine1[0], mine1[1]
+    first = (terms[1][0] + near.astype(f32)).astype(bf16)
     out_local = after(out_local, terms[1][1])
     out_local = jnp.concatenate(
         [out_local[:, : lanes2 // 2], swap(out_local[:, lanes2 // 2 :], 1)], axis=0
@@ -1039,16 +1070,16 @@
     out_local = mxu(outward, out_local, TN).astype(bf16)
     out_local = after(out_local, first).reshape(n, own_frames, MELS * part)
     out_pieces = [out_local[k] for k in range(n)]
-    sent = [swap(out_pieces[k], k) for k in (1, 2, 3)]
-    later_near, *sent = lax.optimization_barrier((later_near, *sent))
-    out_pieces[1:4] = sent
+    later_near = after(later_near, first)
     for k, r in enumerate(order[1:]):
         pairs1[r] = [dpre1[r], later_near[k * rows : (k + 1) * rows]]
     terms[2], terms[3], terms[0] = conv_t3([pairs1[r] for r in order[1:]], weights1)
     for r in order[1:]:
         nears[r] = swap(terms[r][1], Y)
 
-    moved = along(first, 1)
+    second = ((terms[2][0] + nears[2].astype(f32)) + along(first, 1).astype(f32)).astype(bf16)
+    moved = along(second, 1)
+    pairs1[1][0] = after(pairs1[1][0], second)
     grad1_own, grad1_send = weight_grad_own(
         pos,
         [pairs1[r] for r in order],
@@ -1060,13 +1091,13 @@
         ),
         36,
     )
-    grad1_send, moved, nears[2] = lax.optimization_barrier((grad1_send, moved, nears[2]))
-    second = ((terms[2][0] + nears[2].astype(f32)) + moved.astype(f32)).astype(bf16)
-    moved = along(second, 1)
+    grad1_send, moved, nears[3] = lax.optimization_barrier((grad1_send, moved, nears[3]))
+    third = ((terms[3][0] + nears[3].astype(f32)) + moved.astype(f32)).astype(bf16)
+    moved = along(third, 1)
     grad1 = (grad1_own + swap(grad1_send, 1).astype(f32)).astype(bf16)
     grad1_planes = lax.all_to_all(grad1, "batch", 0, 0, tiled=True)
-    grad2_first = after(grad2[0], grad1)
-    sent = [swap(after(out_pieces[k], grad1), k) for k in (4, 5)]
+    grad2_first = after(grad2[0], third, grad1)
+    sent = [swap(after(out_pieces[k], grad1), k) for k in (4, 5, 6)]
     grad2_own, grad2_send = weight_grad_own(
         pos,
         [[grad2_first]] + [[g] for g in grad2[1:]],
@@ -1078,54 +1109,29 @@
         ),
         60,
     )
-    grads1 = after(grads1, grad2_send)
-    whole1 = jnp.concatenate(
-        [
-            route(
-                grads1,
-                [((4 * y + 2 * x, j), (2 * j + x, j)) for j in groups for x in range(2)],
-            )
-            for y in range(2)
-        ],
-        axis=1,
-    )
     grad2_send, nears[0], *sent = lax.optimization_barrier((grad2_send, nears[0], *sent))
-    sent += [swap(after(out_pieces[k], grad2_send), k) for k in (6, 7)]
-    moved, nears[3], grad2_send, grad1_planes, whole1, *sent = lax.optimization_barrier(
-        (moved, nears[3], grad2_send, grad1_planes, whole1, *sent)
-    )
-    out_pieces[4:] = sent
-    third = ((terms[3][0] + nears[3].astype(f32)) + moved.astype(f32)).astype(bf16)
-    whole1, grad1_planes = after(whole1, third), after(grad1_planes, third)
-    moved = along(third, 1)
-    grad2_got = swap(grad2_send, 1)
-
-    grad1_chips = lax.all_to_all(
-        grad1_planes, "tm", 0, 0, tiled=True, axis_index_groups=same_core
-    )
-    mine1 = jnp.where(chip == plane, whole1, 0.0)
-    for s in range(1, PLANES):
-        mine1 += route(
-            whole1,
-            [((2 * j + c, j), (2 * j + c, (j + s) % PLANES)) for j in groups for c in range(2)],
-        )
-
-    moved, grad2_got, mine1 = lax.optimization_barrier((moved, grad2_got, mine1))
-    bias1_grad, gain1_grad = mine1[0], mine1[1]
-    moved, grad1_chips = lax.optimization_barrier((moved, grad1_chips))
+    later = [swap(after(out_pieces[k], grad2_send), k) for k in (7, 1, 2, 3)]
+    moved, grad1_planes, *later = lax.optimization_barrier((moved, grad1_planes, *later))
+    out_pieces = out_pieces[:1] + later[1:] + sent + later[:1]
+
+    def quarter(k):
+        return lax.dynamic_index_in_dim(grad1_planes, chip ^ k, 0, keepdims=False)
+
+    quads = [quarter(0)] + [swap(quarter(k), 2 * k) for k in range(1, CHIPS)]
+    grad2_got = swap(after(grad2_send, moved), 1)
     dx = ((terms[0][0] + nears[0].astype(f32)) + moved.astype(f32)).astype(bf16)
     low, high = dx[:, : MELS * lanes1], dx[:, MELS * lanes1 :]
     other = swap(jnp.where(core == 0, high, low), 1)
     dx = jnp.concatenate([jnp.where(core == 0, low, high), other], axis=0)
     dx = mxu(picker, dx, TN).astype(bf16)
-    dx, grad2_got, grad1_chips, out_pieces[0] = lax.optimization_barrier(
-        (dx, grad2_got, grad1_chips, out_pieces[0])
+    dx, grad2_got, quads[0], *out_pieces = lax.optimization_barrier(
+        (dx, grad2_got, quads[0], *out_pieces)
     )
 
     dx = lax.all_to_all(dx.reshape(n, own_frames, MELS * lanes1), "tm", 0, 0, tiled=True)
     dx = dx.reshape(2, 2, 2, own_frames, MELS, lanes1).transpose(3, 4, 0, 2, 1, 5)
     input_grad = dx.reshape(1, own_frames, MELS, width1)
-    conv1_grad = from_quarters(grad1_chips).transpose(1, 0, 2)
+    conv1_grad = from_quarters(pos, quads).transpose(1, 0, 2)
     block_out = from_lanes(pos, out_pieces)[None]
     conv2_grad = (grad2_own + grad2_got.astype(f32)).transpose(1, 0, 2)
 

time: 458 us -> 449 us (0.980)
  waiting for transfers between devices: 180 us -> 161 us
  other arithmetic: 18.1 us -> 24.2 us
    ppermute x12, waiting for transfers between devices: 52.5 us -> 44 us  [along(): return lax.ppermute(x, 'batch', [(z, (z + shift) % PLANES) for z in groups])]
    ppermute x66 -> x69, waiting for transfers between devices: 107 us -> 99.7 us  [swap(): return lax.ppermute(x, 'tm', [(i, i ^ bits) for i in range(n)])]
    cond x155 -> x219, local copies, waits for them, and re-layouts: 12.4 us -> 11.7 us
    ppermute x66 -> x69, starting transfers between devices: 61.2 us -> 61.3 us  [swap(): return lax.ppermute(x, 'tm', [(i, i ^ bits) for i in range(n)])]
  transfers between devices with their start and end apart: 103 -> 105, of which waited for: 57 -> 59; matrix products, arithmetic and copies ran while one was open for 4% -> 6% of each run, Pallas kernels for 18% -> 18%
where the time goes in v5:
time: 449 us; the launch traced here: 442 us
  waiting for transfers between devices  161 us (36%)
  starting transfers between devices  123 us (27%)
  Pallas kernels  95.2 us (21%)
  other arithmetic  24.2 us (5%)
  local copies, waits for them, and re-layouts  20.7 us (5%)
  loops' own time  11.2 us (2%)
    ppermute x69, waiting for transfers between devices, swap(): return lax.ppermute(x, 'tm', [(i, i ^ bits) for i in range(n)])  99.7 us
    ppermute x69, starting transfers between devices, swap(): return lax.ppermute(x, 'tm', [(i, i ^ bits) for i in range(n)])  61.3 us
    ppermute x12, waiting for transfers between devices, along(): return lax.ppermute(x, 'batch', [(z, (z + shift) % PLANES) for z in groups])  44 us
    pallas_call x2, Pallas kernels, weight_grad_own(): pl.pallas_call(functools.partial(grad_kernel, place, groups, pieces), gri...  25.6 us
    pallas_call x5, Pallas kernels, conv_t(): pl.pallas_call(functools.partial(conv_t_kernel, len(dys)), grid=(blocks,)...  20.1 us
    pallas_call x8, Pallas kernels, conv(): pl.pallas_call(functools.partial(conv_kernel, len(xs)), grid=(width // ti...  19.7 us
    ppermute x9, starting transfers between devices, route(): return lax.ppermute(x, ('tm', 'batch'), flat)  16.6 us
    ppermute x12, starting transfers between devices, along(): return lax.ppermute(x, 'batch', [(z, (z + shift) % PLANES) for z in groups])  13.2 us
  transfers between devices with their start and end apart: 105, of which 59 were waited for; matrix products, arithmetic and copies ran while one was open for 6% of the time, Pallas kernels for 18%

profile of v5, /device:TPU:0, one launch (start us, length us, event | category | flops | bytes accessed | tf_op | source)
XLA Modules:
  0.0 442.4 jit_solution(10748492964476031364)
XLA Ops:
  3.2 3.0 collective-permute-start.288
  6.2 2.6 collective-permute-start.289
  10.2 3.7 all-to-all-start.9
  18.7 4.3 all-to-all-done.9
  24.4 416.9 %conditional.1 = (bf16[1,112,2,2048]{3,2,1,0:T(2,128)(2,1)}, bf16[1,112,2,1024]{3,2,1,0:T(2,128)(2,1)}, f32[256,9,256]{2,0,1:T(8,128)}, f32[256]{0:T(256)}, f32[...) conditional(s32[]{:T(128)} %clamp.3, (s32[3,896]{1,0:T(4,128)S(1)}, ...), branch_computations={%region_8.30_spmd, %region_30.52_spmd, %region_52.74_spmd} | conditional | flops 36335017984 | bytes 513623136 | solution.py:812
  28.5 2.4 collective-permute-start.20
  31.7 7.6 %collective-permute-done.1.refs_0_.refs_8_ = bf16[368,512]{1,0:T(8,128)(2,1)S(1)} collective-permute-done((bf16[368,512]{1,0:T(8,128)(2,1)S(1)}, bf16[368,512]{1,0:T(8,128)(2,1)S(1)}, u32[]{:S(2)}, u32[]{:S(2)}) %collective-permute-start.1) | collective-permute-done | bytes 376864 | tf_op jit(solution)/shard_map/cond/branch_0_fun/ppermute | solution.py:862
  39.3 3.4 collective-permute-done.19.refs_2_
  44.4 4.4 all-to-all-start
  52.9 6.5 %branch_0_fun.26 = (bf16[112,512]{1,0:T(8,128)(2,1)}, bf16[112,512]{1,0:T(8,128)(2,1)}, bf16[112,512]{1,0:T(8,128)(2,1)}, bf16[112,512]{1,0:T(8,128)(2,1)}, bf16...) custom-call(s32[4]{0:T(128)S(1)} %get-tuple-element.123.pos, ...), custom_call_target="tpu_custom_call" | custom-call | tf_op jit(solution)/shard_map/cond/branch_0_fun/pallas_call | solution.py:490
  59.5 4.6 %branch_0_fun.25.refs_4_.refs_1_ = bf16[3,1024,1024]{2,1,0:T(8,128)(2,1)S(1)} custom-call(s32[4]{0:T(128)S(1)} %get-tuple-element.123.pos, bf16[9,256,512]{2,1,0:T(8,128)(2,1)} %get-tuple-element.132.own, bf16[9,256,512]{2,1,0:T(8,128)(2,1)} %get-tuple-element.134.other), custom_call_target="tpu_custom_call" | custom-call | tf_op jit(solution)/shard_map/cond/branch_0_fun/pallas_call | solution.py:314
  64.1 2.7 copy-done
  72.2 2.5 collective-permute-done.6
  74.7 4.4 collective-permute-done.2.refs_0_.refs_10_
  79.8 4.0 collective-permute-start.8
  86.6 3.9 collective-permute-start.11
  96.7 3.2 collective-permute-done.16
  99.9 2.4 collective-permute-done.15
  118.3 2.4 branch_0_fun.32
  124.3 3.7 collective-permute-done.24
  128.2 3.1 collective-permute-done.26
  137.1 4.0 collective-permute-done.28.refs_1_.refs_9_
  141.1 4.5 %collective-permute-done.29.refs_2_.refs_10_ = bf16[368,256]{1,0:T(8,128)(2,1)S(1)} collective-permute-done((bf16[368,256]{1,0:T(8,128)(2,1)S(1)}, bf16[368,256]{1,0:T(8,128)(2,1)S(1)}, u32[]{:S(2)}, u32[]{:S(2)}) %collective-permute-start.29) | collective-permute-done | bytes 188448 | tf_op jit(solution)/shard_map/cond/branch_0_fun/ppermute | solution.py:859
  145.6 2.9 copy-done.1
  148.4 3.3 branch_0_fun.33
  151.8 2.6 collective-permute-start.40
  158.8 5.0 %collective-permute-done.33.refs_3_.refs_15_ = bf16[368,256]{1,0:T(8,128)(2,1)S(1)} collective-permute-done((bf16[368,256]{1,0:T(8,128)(2,1)S(1)}, bf16[368,256]{1,0:T(8,128)(2,1)S(1)}, u32[]{:S(2)}, u32[]{:S(2)}) %collective-permute-start.33) | collective-permute-done | bytes 188448 | tf_op jit(solution)/shard_map/cond/branch_0_fun/ppermute | solution.py:859
  166.3 3.3 branch_0_fun.34
  169.6 2.3 collective-permute-done.40
  177.0 4.6 %collective-permute-done.36.refs_3_.refs_19_ = bf16[368,256]{1,0:T(8,128)(2,1)S(1)} collective-permute-done((bf16[368,256]{1,0:T(8,128)(2,1)S(1)}, bf16[368,256]{1,0:T(8,128)(2,1)S(1)}, u32[]{:S(2)}, u32[]{:S(2)}) %collective-permute-start.36) | collective-permute-done | bytes 188448 | tf_op jit(solution)/shard_map/cond/branch_0_fun/ppermute | solution.py:859
  187.1 3.3 branch_0_fun.35
  194.1 3.3 branch_0_fun.36.term
  197.6 12.6 %collective-permute-done.42.moved = bf16[368,1024]{1,0:T(8,128)(2,1)S(1)} collective-permute-done((bf16[368,1024]{1,0:T(8,128)(2,1)S(1)}, bf16[368,1024]{1,0:T(8,128)(2,1)S(1)}, u32[]{:S(2)}, u32[]{:S(2)}) %collective-permute-start.42) | collective-permute-done | bytes 753696 | tf_op jit(solution)/shard_map/cond/branch_0_fun/ppermute | solution.py:862
  212.5 3.8 collective-permute-start.47
  221.3 3.8 collective-permute-start.50
  227.0 3.8 collective-permute-done.51.t3
  231.2 4.3 branch_0_fun.40
  239.2 3.8 collective-permute-done.53
  242.9 2.9 collective-permute-done.54
  245.8 4.4 collective-permute-done.52.refs_0_.refs_1_
  250.2 4.3 branch_0_fun.41
  258.1 2.9 collective-permute-done.57
  261.0 2.9 collective-permute-done.58
  263.8 4.4 %collective-permute-done.56.refs_0_.refs_2_ = bf16[368,1024]{1,0:T(8,128)(2,1)S(1)} collective-permute-done((bf16[368,1024]{1,0:T(8,128)(2,1)S(1)}, bf16[368,1024]{1,0:T(8,128)(2,1)S(1)}, u32[]{:S(2)}, u32[]{:S(2)}) %collective-permute-start.56) | collective-permute-done | bytes 753696 | tf_op jit(solution)/shard_map/cond/branch_0_fun/ppermute | solution.py:862
  268.5 4.3 branch_0_fun.42
  278.5 3.3 collective-permute-done.61
  281.8 3.8 collective-permute-done.63.refs_0_.refs_3_
  285.6 4.3 branch_0_fun.43
  295.6 3.3 collective-permute-done.65
  305.5 4.2 collective-permute-done.71
  310.2 2.7 branch_0_fun.44
  315.1 3.3 collective-permute-start.73
  326.2 3.7 collective-permute-done.69
  331.1 4.8 %branch_0_fun.45 = (f32[368,512]{1,0:T(8,128)S(1)}, bf16[368,512]{1,0:T(8,128)(2,1)S(1)}, f32[368,512]{1,0:T(8,128)S(1)}, bf16[368,512]{1,0:T(8,128)(2,1)S(1)}, ...) custom-call(bf16[368,256]{1,0:T(8,128)(2,1)S(1)} %copy-done.21, ...), custom_call_target="tpu_custom_call" | custom-call | flops 3472883712 | bytes 6537216 | tf_op jit(solution)/shard_map/cond/branch_0_fun/pallas_call | solution.py:619
  338.6 9.1 %collective-permute-done.76 = bf16[368,512]{1,0:T(8,128)(2,1)S(1)} collective-permute-done((bf16[368,512]{1,0:T(8,128)(2,1)S(1)}, bf16[368,512]{1,0:T(8,128)(2,1)S(1)}, u32[]{:S(2)}, u32[]{:S(2)}) %collective-permute-start.76) | collective-permute-done | bytes 376864 | tf_op jit(solution)/shard_map/cond/branch_0_fun/ppermute | solution.py:859
  348.1 8.4 %branch_0_fun.46 = (f32[4,9,128,128]{3,2,1,0:T(8,128)S(1)}, bf16[4,9,128,128]{3,2,1,0:T(8,128)(2,1)S(1)}) custom-call(s32[4]{0:T(128)S(1)} %copy-done.200, bf16[368,256]{1,0:T(8,128)(2,1)S(1)} %copy-done.77, bf16[368,256]{1,0:T(8,128)(2,1)S(1)} %copy-done.167, bf16[368,256]{1,0:T(8,128)(2,1)S(1)} %copy-done.21, ...), custom_call_target="tpu_custom_call" | custom-call | tf_op jit(solution)/shard_map/cond/branch_0_fun/pallas_call | solution.py:704
  358.4 2.8 collective-permute-done.80
  362.7 4.1 all-to-all-start.1
  375.9 17.1 %branch_0_fun.47 = (f32[9,256,512]{2,1,0:T(8,128)}, bf16[9,256,512]{2,1,0:T(8,128)(2,1)}) custom-call(s32[4]{0:T(128)S(1)} %copy-done.200, bf16[368,1024]{1,0:T(8,128)(2,1)} %copy-done.69, bf16[368,1024]{1,0:T(8,128)(2,1)} %copy-done.70, bf16[368,1024]{1,0:T(8,128)(2,1)} %copy-done.73, bf16[368,1024]{1,0:T(8,128)(2,1)} %copy-done.74, ...), custom_call_target="tpu_custom_call" | custom-call | tf_op jit(solution)/shard_map/cond/branch_0_fun/pallas_call | solution.py:704
  395.1 2.7 collective-permute-start.87
  398.7 2.7 collective-permute-done.89.refs_2_
  411.3 3.5 all-to-all-start.2
  414.8 5.5 %branch_0_fun.48 = bf16[112,2,2048]{2,1,0:T(2,128)(2,1)} custom-call(s32[4]{0:T(128)S(1)} %copy-done.200, bf16[112,512]{1,0:T(8,128)(2,1)} %get-tuple-element.277.refs_0_, bf16[112,512]{1,0:T(8,128)(2,1)} %copy-done.259, bf16[112,512]{1,0:T(8,128)(2,1)} %copy-done.256, bf16[112,512]{1,0:T(8,128)(2,1)} %copy-done.253, ...), custom_call_target="tpu_custom_call" | custom-call | tf_op jit(solution)/shard_map/cond/branch_0_fun/pallas_call | solution.py:518
  424.6 6.1 %add_bitcast_fusion = f32[256,9,512]{2,0,1:T(8,128)} fusion(f32[9,256,512]{2,1,0:T(8,128)} %get-tuple-element.288, bf16[9,256,512]{2,1,0:T(8,128)(2,1)} %collective-permute-done.92), kind=kLoop, calls=%fused_computation | loop fusion | flops 2359296 | bytes 11796480 | tf_op jit(solution)/shard_map/cond/branch_0_fun/transpose | solution.py:1136
  (505 shorter events, 160.8 us)
Async XLA Ops:
  3.2 11.9 %collective-permute-start.288 = (s32[1,24]{1,0:T(1,128)S(1)}, s32[1,24]{1,0:T(1,128)S(1)}, u32[]{:S(2)}, u32[]{:S(2)}) collective-permute-start(s32[1,24]{1,0:T(1,128)S(1)} %copy-done.283), channel_id=1, source_target_pairs={{0,1},{1,2},{2,3},{3,0},{4,5},{5,6},{6,7},{7,4},{8,9},{9,10},{10,1... | collective-permute-start | bytes 296 | tf_op jit(solution)/shard_map/ppermute | solution.py:783
  6.2 8.9 %collective-permute-start.289 = (s32[1,24]{1,0:T(1,128)S(1)}, s32[1,24]{1,0:T(1,128)S(1)}, u32[]{:S(2)}, u32[]{:S(2)}) collective-permute-start(s32[1,24]{1,0:T(1,128)S(1)} %copy-done.283), channel_id=1, source_target_pairs={{0,2},{1,3},{2,0},{3,1},{4,6},{5,7},{6,4},{7,5},{8,10},{9,11},{10,... | collective-permute-start | bytes 296 | tf_op jit(solution)/shard_map/ppermute | solution.py:783
  10.2 12.8 %all-to-all-start.9 = ((bf16[8,112,256]{2,1,0:T(8,128)(2,1)}), bf16[8,112,256]{2,1,0:T(8,128)(2,1)S(1)}, u32[]{:S(2)}, u32[]{:S(2)}) async-start(bf16[8,112,256]{2,1,0:T(8,128)(2,1)} %bitcast.140), calls=%async_computation.9 | async-start | bytes 917504 | tf_op jit(solution)/shard_map/all_to_all | solution.py:779
  14.5 9.9 %collective-permute-start.291 = (bf16[9,256,512]{2,1,0:T(8,128)(2,1)}, bf16[9,256,512]{2,1,0:T(8,128)(2,1)}, u32[]{:S(2)}, u32[]{:S(2)}) collective-permute-start(bf16[9,256,512]{2,1,0:T(8,128)(2,1)} %bitcast.264), channel_id=1, source_target_pairs={{0,4},{4,0},{8,12},{12,8},{16,20},{20,16},{24,28},{28,24},{1,5},{5... | collective-permute-start | bytes 7077896 | tf_op jit(solution)/shard_map/ppermute | solution.py:794
  26.7 12.7 %collective-permute-start.1 = (bf16[368,512]{1,0:T(8,128)(2,1)S(1)}, bf16[368,512]{1,0:T(8,128)(2,1)S(1)}, u32[]{:S(2)}, u32[]{:S(2)}) collective-permute-start(bf16[368,512]{1,0:T(8,128)(2,1)S(1)} %pad_maximum_fusion.2.refs_0_.refs_14_), channel_id=1, source_target_pairs={{0,1},{1,2},{2,3},{3,0},{4,5},{5,6},{6,7},{7,4},{8,9},{9,10},{10,1... | collective-permute-start | bytes 1130504 | tf_op jit(solution)/shard_map/cond/branch_0_fun/ppermute | solution.py:862
  27.4 11.9 %collective-permute-start.18 = (bf16[9,128,128]{2,1,0:T(8,128)(2,1)S(1)}, bf16[9,128,128]{2,1,0:T(8,128)(2,1)S(1)}, u32[]{:S(2)}, u32[]{:S(2)}) collective-permute-start(bf16[9,128,128]{2,1,0:T(8,128)(2,1)S(1)} %get-tuple-element.160), channel_id=1, source_target_pairs={{0,8},{4,12},{8,0},{12,4},{16,24},{20,28},{24,16},{28,20},{1,9},{5... | collective-permute-start | bytes 884744 | tf_op jit(solution)/shard_map/cond/branch_0_fun/ppermute | solution.py:859
  28.0 14.8 %collective-permute-start.19 = (bf16[9,128,128]{2,1,0:T(8,128)(2,1)S(1)}, bf16[9,128,128]{2,1,0:T(8,128)(2,1)S(1)}, u32[]{:S(2)}, u32[]{:S(2)}) collective-permute-start(bf16[9,128,128]{2,1,0:T(8,128)(2,1)S(1)} %get-tuple-element.162), channel_id=1, source_target_pairs={{0,16},{4,20},{8,24},{12,28},{16,0},{20,4},{24,8},{28,12},{1,17},{... | collective-permute-start | bytes 884744 | tf_op jit(solution)/shard_map/cond/branch_0_fun/ppermute | solution.py:859
  28.5 14.3 %collective-permute-start.20 = (bf16[9,128,128]{2,1,0:T(8,128)(2,1)S(1)}, bf16[9,128,128]{2,1,0:T(8,128)(2,1)S(1)}, u32[]{:S(2)}, u32[]{:S(2)}) collective-permute-start(bf16[9,128,128]{2,1,0:T(8,128)(2,1)S(1)} %copy-done.299), channel_id=1, source_target_pairs={{0,24},{4,28},{8,16},{12,20},{16,8},{20,12},{24,0},{28,4},{1,25},{... | collective-permute-start | bytes 884744 | tf_op jit(solution)/shard_map/cond/branch_0_fun/ppermute | solution.py:859
  44.4 62.3 %all-to-all-start = ((bf16[4,9,128,128]{3,2,1,0:T(8,128)(2,1)}), bf16[4,9,128,128]{3,2,1,0:T(8,128)(2,1)S(1)}, u32[]{:S(2)}, u32[]{:S(2)}) async-start(bf16[4,9,128,128]{3,2,1,0:T(8,128)(2,1)} %branch_0_fun.27), calls=%async_computation | async-start | bytes 2359296 | tf_op jit(solution)/shard_map/cond/branch_0_fun/all_to_all | solution.py:917
  48.8 19.5 %collective-permute-start.3 = (bf16[368,512]{1,0:T(8,128)(2,1)S(1)}, bf16[368,512]{1,0:T(8,128)(2,1)S(1)}, u32[]{:S(2)}, u32[]{:S(2)}) collective-permute-start(bf16[368,512]{1,0:T(8,128)(2,1)S(1)} %pad_maximum_fusion.2.refs_0_.refs_14_), channel_id=1, source_target_pairs={{0,16},{4,20},{8,24},{12,28},{16,0},{20,4},{24,8},{28,12},{1,17},{... | collective-permute-start | bytes 1130504 | tf_op jit(solution)/shard_map/cond/branch_0_fun/ppermute | solution.py:859
  50.0 29.1 %collective-permute-start.2 = (bf16[368,512]{1,0:T(8,128)(2,1)S(1)}, bf16[368,512]{1,0:T(8,128)(2,1)S(1)}, u32[]{:S(2)}, u32[]{:S(2)}) collective-permute-start(bf16[368,512]{1,0:T(8,128)(2,1)S(1)} %collective-permute-done.1.refs_0_.refs_8_), channel_id=1, source_target_pairs={{0,1},{1,2},{2,3},{3,0},{4,5},{5,6},{6,7},{7,4},{8,9},{9,10},{10,1... | collective-permute-start | bytes 1130504 | tf_op jit(solution)/shard_map/cond/branch_0_fun/ppermute | solution.py:862
  52.0 27.1 %collective-permute-start.4 = (bf16[368,512]{1,0:T(8,128)(2,1)S(1)}, bf16[368,512]{1,0:T(8,128)(2,1)S(1)}, u32[]{:S(2)}, u32[]{:S(2)}) collective-permute-start(bf16[368,512]{1,0:T(8,128)(2,1)S(1)} %collective-permute-done.1.refs_0_.refs_8_), channel_id=1, source_target_pairs={{0,16},{4,20},{8,24},{12,28},{16,0},{20,4},{24,8},{28,12},{1,17},{... | collective-permute-start | bytes 1130504 | tf_op jit(solution)/shard_map/cond/branch_0_fun/ppermute | solution.py:859
  66.8 7.9 %collective-permute-start.6 = (bf16[112,512]{1,0:T(8,128)(2,1)S(1)}, bf16[112,512]{1,0:T(8,128)(2,1)S(1)}, u32[]{:S(2)}, u32[]{:S(2)}) collective-permute-start(bf16[112,512]{1,0:T(8,128)(2,1)S(1)} %copy-done.317), channel_id=1, source_target_pairs={{0,8},{4,12},{8,0},{12,4},{16,24},{20,28},{24,16},{28,20},{1,9},{5... | collective-permute-start | bytes 344072 | tf_op jit(solution)/shard_map/cond/branch_0_fun/ppermute | solution.py:859
  79.8 24.8 %collective-permute-start.8 = (bf16[368,512]{1,0:T(8,128)(2,1)S(1)}, bf16[368,512]{1,0:T(8,128)(2,1)S(1)}, u32[]{:S(2)}, u32[]{:S(2)}) collective-permute-start(bf16[368,512]{1,0:T(8,128)(2,1)S(1)} %collective-permute-done.2.refs_0_.refs_10_), channel_id=1, source_target_pairs={{0,1},{1,2},{2,3},{3,0},{4,5},{5,6},{6,7},{7,4},{8,9},{9,10},{10,1... | collective-permute-start | bytes 1130504 | tf_op jit(solution)/shard_map/cond/branch_0_fun/ppermute | solution.py:862
  83.8 21.4 %collective-permute-start.9 = (bf16[368,512]{1,0:T(8,128)(2,1)S(1)}, bf16[368,512]{1,0:T(8,128)(2,1)S(1)}, u32[]{:S(2)}, u32[]{:S(2)}) collective-permute-start(bf16[368,512]{1,0:T(8,128)(2,1)S(1)} %collective-permute-done.2.refs_0_.refs_10_), channel_id=1, source_target_pairs={{0,16},{4,20},{8,24},{12,28},{16,0},{20,4},{24,8},{28,12},{1,17},{... | collective-permute-start | bytes 1130504 | tf_op jit(solution)/shard_map/cond/branch_0_fun/ppermute | solution.py:859
  85.9 10.2 %collective-permute-start.17 = (bf16[112,512]{1,0:T(8,128)(2,1)S(1)}, bf16[112,512]{1,0:T(8,128)(2,1)S(1)}, u32[]{:S(2)}, u32[]{:S(2)}) collective-permute-start(bf16[112,512]{1,0:T(8,128)(2,1)S(1)} %copy-done.311), channel_id=1, source_target_pairs={{0,28},{4,24},{8,20},{12,16},{16,12},{20,8},{24,4},{28,0},{1,29},{... | collective-permute-start | bytes 344072 | tf_op jit(solution)/shard_map/cond/branch_0_fun/ppermute | solution.py:859
  96.1 8.5 %collective-permute-start.14 = (bf16[112,512]{1,0:T(8,128)(2,1)S(1)}, bf16[112,512]{1,0:T(8,128)(2,1)S(1)}, u32[]{:S(2)}, u32[]{:S(2)}) collective-permute-start(bf16[112,512]{1,0:T(8,128)(2,1)S(1)} %copy-done.302), channel_id=1, source_target_pairs={{0,16},{4,20},{8,24},{12,28},{16,0},{20,4},{24,8},{28,12},{1,17},{... | collective-permute-start | bytes 344072 | tf_op jit(solution)/shard_map/cond/branch_0_fun/ppermute | solution.py:859
  106.8 11.5 %collective-permute-start.25 = (bf16[368,512]{1,0:T(8,128)(2,1)}, bf16[368,512]{1,0:T(8,128)(2,1)}, u32[]{:S(2)}, u32[]{:S(2)}) collective-permute-start(bf16[368,512]{1,0:T(8,128)(2,1)} %copy-done.120), channel_id=1, source_target_pairs={{0,16},{4,20},{8,24},{12,28},{16,0},{20,4},{24,8},{28,12},{1,17},{... | collective-permute-start | bytes 1130504 | tf_op jit(solution)/shard_map/cond/branch_0_fun/ppermute | solution.py:859
  112.3 11.8 %collective-permute-start.22 = (bf16[368,256]{1,0:T(8,128)(2,1)S(1)}, bf16[368,256]{1,0:T(8,128)(2,1)S(1)}, u32[]{:S(2)}, u32[]{:S(2)}) collective-permute-start(bf16[368,256]{1,0:T(8,128)(2,1)S(1)} %get-tuple-element.168), channel_id=1, source_target_pairs={{0,8},{4,12},{8,0},{12,4},{16,24},{20,28},{24,16},{28,20},{1,9},{5... | collective-permute-start | bytes 565256 | tf_op jit(solution)/shard_map/cond/branch_0_fun/ppermute | solution.py:859
  114.8 9.2 %collective-permute-start.23 = (bf16[368,256]{1,0:T(8,128)(2,1)S(1)}, bf16[368,256]{1,0:T(8,128)(2,1)S(1)}, u32[]{:S(2)}, u32[]{:S(2)}) collective-permute-start(bf16[368,256]{1,0:T(8,128)(2,1)S(1)} %get-tuple-element.173), channel_id=1, source_target_pairs={{0,8},{4,12},{8,0},{12,4},{16,24},{20,28},{24,16},{28,20},{1,9},{5... | collective-permute-start | bytes 565256 | tf_op jit(solution)/shard_map/cond/branch_0_fun/ppermute | solution.py:859
  117.2 10.8 %collective-permute-start.24 = (bf16[368,256]{1,0:T(8,128)(2,1)S(1)}, bf16[368,256]{1,0:T(8,128)(2,1)S(1)}, u32[]{:S(2)}, u32[]{:S(2)}) collective-permute-start(bf16[368,256]{1,0:T(8,128)(2,1)S(1)} %get-tuple-element.178), channel_id=1, source_target_pairs={{0,8},{4,12},{8,0},{12,4},{16,24},{20,28},{24,16},{28,20},{1,9},{5... | collective-permute-start | bytes 565256 | tf_op jit(solution)/shard_map/cond/branch_0_fun/ppermute | solution.py:859
  120.7 10.5 %collective-permute-start.26 = (bf16[368,256]{1,0:T(8,128)(2,1)S(1)}, bf16[368,256]{1,0:T(8,128)(2,1)S(1)}, u32[]{:S(2)}, u32[]{:S(2)}) collective-permute-start(bf16[368,256]{1,0:T(8,128)(2,1)S(1)} %get-tuple-element.182), channel_id=1, source_target_pairs={{0,8},{4,12},{8,0},{12,4},{16,24},{20,28},{24,16},{28,20},{1,9},{5... | collective-permute-start | bytes 565256 | tf_op jit(solution)/shard_map/cond/branch_0_fun/ppermute | solution.py:859
  134.7 10.9 %collective-permute-start.29 = (bf16[368,256]{1,0:T(8,128)(2,1)S(1)}, bf16[368,256]{1,0:T(8,128)(2,1)S(1)}, u32[]{:S(2)}, u32[]{:S(2)}) collective-permute-start(bf16[368,256]{1,0:T(8,128)(2,1)S(1)} %get-tuple-element.835.refs_0_.refs_8_), channel_id=1, source_target_pairs={{0,16},{4,20},{8,24},{12,28},{16,0},{20,4},{24,8},{28,12},{1,17},{... | collective-permute-start | bytes 565256 | tf_op jit(solution)/shard_map/cond/branch_0_fun/ppermute | solution.py:859
  135.9 9.7 %collective-permute-start.30 = (bf16[368,256]{1,0:T(8,128)(2,1)S(1)}, bf16[368,256]{1,0:T(8,128)(2,1)S(1)}, u32[]{:S(2)}, u32[]{:S(2)}) collective-permute-start(bf16[368,256]{1,0:T(8,128)(2,1)S(1)} %get-tuple-element.835.refs_0_.refs_8_), channel_id=1, source_target_pairs={{0,24},{4,28},{8,16},{12,20},{16,8},{20,12},{24,0},{28,4},{1,25},{... | collective-permute-start | bytes 565256 | tf_op jit(solution)/shard_map/cond/branch_0_fun/ppermute | solution.py:859
  151.8 20.2 %collective-permute-start.40 = (bf16[368,1024]{1,0:T(8,128)(2,1)S(1)}, bf16[368,1024]{1,0:T(8,128)(2,1)S(1)}, u32[]{:S(2)}, u32[]{:S(2)}) collective-permute-start(bf16[368,1024]{1,0:T(8,128)(2,1)S(1)} %branch_0_fun.33), channel_id=1, source_target_pairs={{0,1},{1,2},{2,3},{3,0},{4,5},{5,6},{6,7},{7,4},{8,9},{9,10},{10,1... | collective-permute-start | bytes 2261000 | tf_op jit(solution)/shard_map/cond/branch_0_fun/ppermute | solution.py:862
  155.2 8.7 %collective-permute-start.33 = (bf16[368,256]{1,0:T(8,128)(2,1)S(1)}, bf16[368,256]{1,0:T(8,128)(2,1)S(1)}, u32[]{:S(2)}, u32[]{:S(2)}) collective-permute-start(bf16[368,256]{1,0:T(8,128)(2,1)S(1)} %get-tuple-element.185.refs_0_.refs_12_), channel_id=1, source_target_pairs={{0,24},{4,28},{8,16},{12,20},{16,8},{20,12},{24,0},{28,4},{1,25},{... | collective-permute-start | bytes 565256 | tf_op jit(solution)/shard_map/cond/branch_0_fun/ppermute | solution.py:859
  157.1 8.4 %collective-permute-start.31 = (bf16[368,256]{1,0:T(8,128)(2,1)S(1)}, bf16[368,256]{1,0:T(8,128)(2,1)S(1)}, u32[]{:S(2)}, u32[]{:S(2)}) collective-permute-start(bf16[368,256]{1,0:T(8,128)(2,1)S(1)} %get-tuple-element.185.refs_0_.refs_12_), channel_id=1, source_target_pairs={{0,8},{4,12},{8,0},{12,4},{16,24},{20,28},{24,16},{28,20},{1,9},{5... | collective-permute-start | bytes 565256 | tf_op jit(solution)/shard_map/cond/branch_0_fun/ppermute | solution.py:859
  157.4 8.8 %collective-permute-start.32 = (bf16[368,256]{1,0:T(8,128)(2,1)S(1)}, bf16[368,256]{1,0:T(8,128)(2,1)S(1)}, u32[]{:S(2)}, u32[]{:S(2)}) collective-permute-start(bf16[368,256]{1,0:T(8,128)(2,1)S(1)} %get-tuple-element.185.refs_0_.refs_12_), channel_id=1, source_target_pairs={{0,16},{4,20},{8,24},{12,28},{16,0},{20,4},{24,8},{28,12},{1,17},{... | collective-permute-start | bytes 565256 | tf_op jit(solution)/shard_map/cond/branch_0_fun/ppermute | solution.py:859
  172.2 19.4 %collective-permute-start.41 = (bf16[368,1024]{1,0:T(8,128)(2,1)S(1)}, bf16[368,1024]{1,0:T(8,128)(2,1)S(1)}, u32[]{:S(2)}, u32[]{:S(2)}) collective-permute-start(bf16[368,1024]{1,0:T(8,128)(2,1)S(1)} %add_convert_fusion.2), channel_id=1, source_target_pairs={{0,1},{1,2},{2,3},{3,0},{4,5},{5,6},{6,7},{7,4},{8,9},{9,10},{10,1... | collective-permute-start | bytes 2261000 | tf_op jit(solution)/shard_map/cond/branch_0_fun/ppermute | solution.py:862
  173.4 8.2 %collective-permute-start.36 = (bf16[368,256]{1,0:T(8,128)(2,1)S(1)}, bf16[368,256]{1,0:T(8,128)(2,1)S(1)}, u32[]{:S(2)}, u32[]{:S(2)}) collective-permute-start(bf16[368,256]{1,0:T(8,128)(2,1)S(1)} %get-tuple-element.187.refs_0_.refs_16_), channel_id=1, source_target_pairs={{0,24},{4,28},{8,16},{12,20},{16,8},{20,12},{24,0},{28,4},{1,25},{... | collective-permute-start | bytes 565256 | tf_op jit(solution)/shard_map/cond/branch_0_fun/ppermute | solution.py:859
  175.0 7.9 %collective-permute-start.34 = (bf16[368,256]{1,0:T(8,128)(2,1)S(1)}, bf16[368,256]{1,0:T(8,128)(2,1)S(1)}, u32[]{:S(2)}, u32[]{:S(2)}) collective-permute-start(bf16[368,256]{1,0:T(8,128)(2,1)S(1)} %get-tuple-element.187.refs_0_.refs_16_), channel_id=1, source_target_pairs={{0,8},{4,12},{8,0},{12,4},{16,24},{20,28},{24,16},{28,20},{1,9},{5... | collective-permute-start | bytes 565256 | tf_op jit(solution)/shard_map/cond/branch_0_fun/ppermute | solution.py:859
  175.7 7.9 %collective-permute-start.35 = (bf16[368,256]{1,0:T(8,128)(2,1)S(1)}, bf16[368,256]{1,0:T(8,128)(2,1)S(1)}, u32[]{:S(2)}, u32[]{:S(2)}) collective-permute-start(bf16[368,256]{1,0:T(8,128)(2,1)S(1)} %get-tuple-element.187.refs_0_.refs_16_), channel_id=1, source_target_pairs={{0,16},{4,20},{8,24},{12,28},{16,0},{20,4},{24,8},{28,12},{1,17},{... | collective-permute-start | bytes 565256 | tf_op jit(solution)/shard_map/cond/branch_0_fun/ppermute | solution.py:859
  183.6 9.7 %collective-permute-start.39 = (bf16[368,256]{1,0:T(8,128)(2,1)S(1)}, bf16[368,256]{1,0:T(8,128)(2,1)S(1)}, u32[]{:S(2)}, u32[]{:S(2)}) collective-permute-start(bf16[368,256]{1,0:T(8,128)(2,1)S(1)} %get-tuple-element.189.refs_0_.refs_4_), channel_id=1, source_target_pairs={{0,24},{4,28},{8,16},{12,20},{16,8},{20,12},{24,0},{28,4},{1,25},{... | collective-permute-start | bytes 565256 | tf_op jit(solution)/shard_map/cond/branch_0_fun/ppermute | solution.py:859
  184.7 8.6 %collective-permute-start.37 = (bf16[368,256]{1,0:T(8,128)(2,1)S(1)}, bf16[368,256]{1,0:T(8,128)(2,1)S(1)}, u32[]{:S(2)}, u32[]{:S(2)}) collective-permute-start(bf16[368,256]{1,0:T(8,128)(2,1)S(1)} %get-tuple-element.189.refs_0_.refs_4_), channel_id=1, source_target_pairs={{0,8},{4,12},{8,0},{12,4},{16,24},{20,28},{24,16},{28,20},{1,9},{5... | collective-permute-start | bytes 565256 | tf_op jit(solution)/shard_map/cond/branch_0_fun/ppermute | solution.py:859
  185.8 8.3 %collective-permute-start.38 = (bf16[368,256]{1,0:T(8,128)(2,1)S(1)}, bf16[368,256]{1,0:T(8,128)(2,1)S(1)}, u32[]{:S(2)}, u32[]{:S(2)}) collective-permute-start(bf16[368,256]{1,0:T(8,128)(2,1)S(1)} %get-tuple-element.189.refs_0_.refs_4_), channel_id=1, source_target_pairs={{0,16},{4,20},{8,24},{12,28},{16,0},{20,4},{24,8},{28,12},{1,17},{... | collective-permute-start | bytes 565256 | tf_op jit(solution)/shard_map/cond/branch_0_fun/ppermute | solution.py:859
  191.9 18.3 %collective-permute-start.42 = (bf16[368,1024]{1,0:T(8,128)(2,1)S(1)}, bf16[368,1024]{1,0:T(8,128)(2,1)S(1)}, u32[]{:S(2)}, u32[]{:S(2)}) collective-permute-start(bf16[368,1024]{1,0:T(8,128)(2,1)S(1)} %add_convert_fusion.1), channel_id=1, source_target_pairs={{0,1},{1,2},{2,3},{3,0},{4,5},{5,6},{6,7},{7,4},{8,9},{9,10},{10,1... | collective-permute-start | bytes 2261000 | tf_op jit(solution)/shard_map/cond/branch_0_fun/ppermute | solution.py:862
  231.2 19.0 %collective-permute-start.52 = (bf16[368,1024]{1,0:T(8,128)(2,1)S(1)}, bf16[368,1024]{1,0:T(8,128)(2,1)S(1)}, u32[]{:S(2)}, u32[]{:S(2)}) collective-permute-start(bf16[368,1024]{1,0:T(8,128)(2,1)S(1)} %get-tuple-element.252.refs_0_), channel_id=1, source_target_pairs={{0,1},{1,2},{2,3},{3,0},{4,5},{5,6},{6,7},{7,4},{8,9},{9,10},{10,1... | collective-permute-start | bytes 2261000 | tf_op jit(solution)/shard_map/cond/branch_0_fun/ppermute | solution.py:862
  237.0 8.8 %collective-permute-start.54 = (bf16[368,256]{1,0:T(8,128)(2,1)S(1)}, bf16[368,256]{1,0:T(8,128)(2,1)S(1)}, u32[]{:S(2)}, u32[]{:S(2)}) collective-permute-start(bf16[368,256]{1,0:T(8,128)(2,1)S(1)} %get-tuple-element.214), channel_id=1, source_target_pairs={{0,16},{4,20},{8,24},{12,28},{16,0},{20,4},{24,8},{28,12},{1,17},{... | collective-permute-start | bytes 565256 | tf_op jit(solution)/shard_map/cond/branch_0_fun/ppermute | solution.py:859
  237.0 8.8 %collective-permute-start.55 = (bf16[368,256]{1,0:T(8,128)(2,1)S(1)}, bf16[368,256]{1,0:T(8,128)(2,1)S(1)}, u32[]{:S(2)}, u32[]{:S(2)}) collective-permute-start(bf16[368,256]{1,0:T(8,128)(2,1)S(1)} %get-tuple-element.215), channel_id=1, source_target_pairs={{0,24},{4,28},{8,16},{12,20},{16,8},{20,12},{24,0},{28,4},{1,25},{... | collective-permute-start | bytes 565256 | tf_op jit(solution)/shard_map/cond/branch_0_fun/ppermute | solution.py:859
  250.2 18.1 %collective-permute-start.56 = (bf16[368,1024]{1,0:T(8,128)(2,1)S(1)}, bf16[368,1024]{1,0:T(8,128)(2,1)S(1)}, u32[]{:S(2)}, u32[]{:S(2)}) collective-permute-start(bf16[368,1024]{1,0:T(8,128)(2,1)S(1)} %collective-permute-done.52.refs_0_.refs_1_), channel_id=1, source_target_pairs={{0,1},{1,2},{2,3},{3,0},{4,5},{5,6},{6,7},{7,4},{8,9},{9,10},{10,1... | collective-permute-start | bytes 2261000 | tf_op jit(solution)/shard_map/cond/branch_0_fun/ppermute | solution.py:862
  255.9 7.9 %collective-permute-start.58 = (bf16[368,256]{1,0:T(8,128)(2,1)S(1)}, bf16[368,256]{1,0:T(8,128)(2,1)S(1)}, u32[]{:S(2)}, u32[]{:S(2)}) collective-permute-start(bf16[368,256]{1,0:T(8,128)(2,1)S(1)} %get-tuple-element.218), channel_id=1, source_target_pairs={{0,16},{4,20},{8,24},{12,28},{16,0},{20,4},{24,8},{28,12},{1,17},{... | collective-permute-start | bytes 565256 | tf_op jit(solution)/shard_map/cond/branch_0_fun/ppermute | solution.py:859
  255.9 7.9 %collective-permute-start.59 = (bf16[368,256]{1,0:T(8,128)(2,1)S(1)}, bf16[368,256]{1,0:T(8,128)(2,1)S(1)}, u32[]{:S(2)}, u32[]{:S(2)}) collective-permute-start(bf16[368,256]{1,0:T(8,128)(2,1)S(1)} %get-tuple-element.219), channel_id=1, source_target_pairs={{0,24},{4,28},{8,16},{12,20},{16,8},{20,12},{24,0},{28,4},{1,25},{... | collective-permute-start | bytes 565256 | tf_op jit(solution)/shard_map/cond/branch_0_fun/ppermute | solution.py:859
  268.3 17.3 %collective-permute-start.63 = (bf16[368,1024]{1,0:T(8,128)(2,1)S(1)}, bf16[368,1024]{1,0:T(8,128)(2,1)S(1)}, u32[]{:S(2)}, u32[]{:S(2)}) collective-permute-start(bf16[368,1024]{1,0:T(8,128)(2,1)S(1)} %collective-permute-done.56.refs_0_.refs_2_), channel_id=1, source_target_pairs={{0,1},{1,2},{2,3},{3,0},{4,5},{5,6},{6,7},{7,4},{8,9},{9,10},{10,1... | collective-permute-start | bytes 2261000 | tf_op jit(solution)/shard_map/cond/branch_0_fun/ppermute | solution.py:862
  274.2 7.6 %collective-permute-start.61 = (bf16[368,256]{1,0:T(8,128)(2,1)S(1)}, bf16[368,256]{1,0:T(8,128)(2,1)S(1)}, u32[]{:S(2)}, u32[]{:S(2)}) collective-permute-start(bf16[368,256]{1,0:T(8,128)(2,1)S(1)} %get-tuple-element.223), channel_id=1, source_target_pairs={{0,16},{4,20},{8,24},{12,28},{16,0},{20,4},{24,8},{28,12},{1,17},{... | collective-permute-start | bytes 565256 | tf_op jit(solution)/shard_map/cond/branch_0_fun/ppermute | solution.py:859
  274.2 7.6 %collective-permute-start.62 = (bf16[368,256]{1,0:T(8,128)(2,1)S(1)}, bf16[368,256]{1,0:T(8,128)(2,1)S(1)}, u32[]{:S(2)}, u32[]{:S(2)}) collective-permute-start(bf16[368,256]{1,0:T(8,128)(2,1)S(1)} %get-tuple-element.224), channel_id=1, source_target_pairs={{0,24},{4,28},{8,16},{12,20},{16,8},{20,12},{24,0},{28,4},{1,25},{... | collective-permute-start | bytes 565256 | tf_op jit(solution)/shard_map/cond/branch_0_fun/ppermute | solution.py:859
  291.3 7.6 %collective-permute-start.65 = (bf16[368,256]{1,0:T(8,128)(2,1)S(1)}, bf16[368,256]{1,0:T(8,128)(2,1)S(1)}, u32[]{:S(2)}, u32[]{:S(2)}) collective-permute-start(bf16[368,256]{1,0:T(8,128)(2,1)S(1)} %get-tuple-element.230), channel_id=1, source_target_pairs={{0,16},{4,20},{8,24},{12,28},{16,0},{20,4},{24,8},{28,12},{1,17},{... | collective-permute-start | bytes 565256 | tf_op jit(solution)/shard_map/cond/branch_0_fun/ppermute | solution.py:859
  291.4 7.6 %collective-permute-start.66 = (bf16[368,256]{1,0:T(8,128)(2,1)S(1)}, bf16[368,256]{1,0:T(8,128)(2,1)S(1)}, u32[]{:S(2)}, u32[]{:S(2)}) collective-permute-start(bf16[368,256]{1,0:T(8,128)(2,1)S(1)} %get-tuple-element.231), channel_id=1, source_target_pairs={{0,24},{4,28},{8,16},{12,20},{16,8},{20,12},{24,0},{28,4},{1,25},{... | collective-permute-start | bytes 565256 | tf_op jit(solution)/shard_map/cond/branch_0_fun/ppermute | solution.py:859
  312.9 11.8 %collective-permute-start.72 = (bf16[368,512]{1,0:T(8,128)(2,1)}, bf16[368,512]{1,0:T(8,128)(2,1)}, u32[]{:S(2)}, u32[]{:S(2)}) collective-permute-start(bf16[368,512]{1,0:T(8,128)(2,1)} %get-tuple-element.236), channel_id=1, source_target_pairs={{0,16},{4,20},{8,24},{12,28},{16,0},{20,4},{24,8},{28,12},{1,17},{... | collective-permute-start | bytes 1130504 | tf_op jit(solution)/shard_map/cond/branch_0_fun/ppermute | solution.py:859
  314.1 15.8 %collective-permute-start.69 = (bf16[1104,256]{1,0:T(8,128)(2,1)}, bf16[1104,256]{1,0:T(8,128)(2,1)}, u32[]{:S(2)}, u32[]{:S(2)}) collective-permute-start(bf16[1104,256]{1,0:T(8,128)(2,1)} %pad_maximum_fusion.1), channel_id=1, source_target_pairs={{0,8},{4,12},{8,0},{12,4},{16,24},{20,28},{24,16},{28,20},{1,9},{5... | collective-permute-start | bytes 1695752 | tf_op jit(solution)/shard_map/cond/branch_0_fun/ppermute | solution.py:859
  326.1 12.5 %collective-permute-start.77 = (bf16[368,512]{1,0:T(8,128)(2,1)S(1)}, bf16[368,512]{1,0:T(8,128)(2,1)S(1)}, u32[]{:S(2)}, u32[]{:S(2)}) collective-permute-start(bf16[368,512]{1,0:T(8,128)(2,1)S(1)} %add_convert_fusion.6), channel_id=1, source_target_pairs={{0,1},{1,2},{2,3},{3,0},{4,5},{5,6},{6,7},{7,4},{8,9},{9,10},{10,1... | collective-permute-start | bytes 1130504 | tf_op jit(solution)/shard_map/cond/branch_0_fun/ppermute | solution.py:862
  336.0 11.7 %collective-permute-start.76 = (bf16[368,512]{1,0:T(8,128)(2,1)S(1)}, bf16[368,512]{1,0:T(8,128)(2,1)S(1)}, u32[]{:S(2)}, u32[]{:S(2)}) collective-permute-start(bf16[368,512]{1,0:T(8,128)(2,1)S(1)} %get-tuple-element.244), channel_id=1, source_target_pairs={{0,16},{4,20},{8,24},{12,28},{16,0},{20,4},{24,8},{28,12},{1,17},{... | collective-permute-start | bytes 1130504 | tf_op jit(solution)/shard_map/cond/branch_0_fun/ppermute | solution.py:859
  337.6 18.9 %collective-permute-start.79 = (bf16[368,512]{1,0:T(8,128)(2,1)S(1)}, bf16[368,512]{1,0:T(8,128)(2,1)S(1)}, u32[]{:S(2)}, u32[]{:S(2)}) collective-permute-start(bf16[368,512]{1,0:T(8,128)(2,1)S(1)} %get-tuple-element.247), channel_id=1, source_target_pairs={{0,16},{4,20},{8,24},{12,28},{16,0},{20,4},{24,8},{28,12},{1,17},{... | collective-permute-start | bytes 1130504 | tf_op jit(solution)/shard_map/cond/branch_0_fun/ppermute | solution.py:859
  347.9 10.5 %collective-permute-start.78 = (bf16[368,512]{1,0:T(8,128)(2,1)S(1)}, bf16[368,512]{1,0:T(8,128)(2,1)S(1)}, u32[]{:S(2)}, u32[]{:S(2)}) collective-permute-start(bf16[368,512]{1,0:T(8,128)(2,1)S(1)} %add_convert_fusion.5), channel_id=1, source_target_pairs={{0,1},{1,2},{2,3},{3,0},{4,5},{5,6},{6,7},{7,4},{8,9},{9,10},{10,1... | collective-permute-start | bytes 1130504 | tf_op jit(solution)/shard_map/cond/branch_0_fun/ppermute | solution.py:862
  362.7 41.2 %all-to-all-start.1 = ((bf16[4,9,128,128]{3,2,1,0:T(8,128)(2,1)}), bf16[4,9,128,128]{3,2,1,0:T(8,128)(2,1)S(1)}, u32[]{:S(2)}, u32[]{:S(2)}) async-start(bf16[4,9,128,128]{3,2,1,0:T(8,128)(2,1)} %add_convert_fusion), calls=%async_computation.1 | async-start | bytes 2359296 | tf_op jit(solution)/shard_map/cond/branch_0_fun/all_to_all | solution.py:1098
  369.6 23.4 %collective-permute-start.81 = (bf16[368,512]{1,0:T(8,128)(2,1)S(1)}, bf16[368,512]{1,0:T(8,128)(2,1)S(1)}, u32[]{:S(2)}, u32[]{:S(2)}) collective-permute-start(bf16[368,512]{1,0:T(8,128)(2,1)S(1)} %copy-done.174), channel_id=1, source_target_pairs={{0,16},{4,20},{8,24},{12,28},{16,0},{20,4},{24,8},{28,12},{1,17},{... | collective-permute-start | bytes 1130504 | tf_op jit(solution)/shard_map/cond/branch_0_fun/ppermute | solution.py:859
  371.2 27.5 %collective-permute-start.86 = (bf16[368,512]{1,0:T(8,128)(2,1)S(1)}, bf16[368,512]{1,0:T(8,128)(2,1)S(1)}, u32[]{:S(2)}, u32[]{:S(2)}) collective-permute-start(bf16[368,512]{1,0:T(8,128)(2,1)S(1)} %add_convert_fusion.4), channel_id=1, source_target_pairs={{0,1},{1,2},{2,3},{3,0},{4,5},{5,6},{6,7},{7,4},{8,9},{9,10},{10,1... | collective-permute-start | bytes 1130504 | tf_op jit(solution)/shard_map/cond/branch_0_fun/ppermute | solution.py:862
  374.0 19.1 %collective-permute-start.85 = (bf16[112,512]{1,0:T(8,128)(2,1)}, bf16[112,512]{1,0:T(8,128)(2,1)}, u32[]{:S(2)}, u32[]{:S(2)}) collective-permute-start(bf16[112,512]{1,0:T(8,128)(2,1)} %get-tuple-element.260), channel_id=1, source_target_pairs={{0,24},{4,28},{8,16},{12,20},{16,8},{20,12},{24,0},{28,4},{1,25},{... | collective-permute-start | bytes 344072 | tf_op jit(solution)/shard_map/cond/branch_0_fun/ppermute | solution.py:859
  374.2 18.9 %collective-permute-start.84 = (bf16[112,512]{1,0:T(8,128)(2,1)}, bf16[112,512]{1,0:T(8,128)(2,1)}, u32[]{:S(2)}, u32[]{:S(2)}) collective-permute-start(bf16[112,512]{1,0:T(8,128)(2,1)} %get-tuple-element.259), channel_id=1, source_target_pairs={{0,20},{4,16},{8,28},{12,24},{16,4},{20,0},{24,12},{28,8},{1,21},{... | collective-permute-start | bytes 344072 | tf_op jit(solution)/shard_map/cond/branch_0_fun/ppermute | solution.py:859
  374.8 18.3 %collective-permute-start.83 = (bf16[112,512]{1,0:T(8,128)(2,1)}, bf16[112,512]{1,0:T(8,128)(2,1)}, u32[]{:S(2)}, u32[]{:S(2)}) collective-permute-start(bf16[112,512]{1,0:T(8,128)(2,1)} %get-tuple-element.258), channel_id=1, source_target_pairs={{0,16},{4,20},{8,24},{12,28},{16,0},{20,4},{24,8},{28,12},{1,17},{... | collective-permute-start | bytes 344072 | tf_op jit(solution)/shard_map/cond/branch_0_fun/ppermute | solution.py:859
  395.1 8.6 %collective-permute-start.87 = (bf16[112,512]{1,0:T(8,128)(2,1)S(1)}, bf16[112,512]{1,0:T(8,128)(2,1)}, u32[]{:S(2)}, u32[]{:S(2)}) collective-permute-start(bf16[112,512]{1,0:T(8,128)(2,1)S(1)} %get-tuple-element.263), channel_id=1, source_target_pairs={{0,28},{4,24},{8,20},{12,16},{16,12},{20,8},{24,4},{28,0},{1,29},{... | collective-permute-start | bytes 344072 | tf_op jit(solution)/shard_map/cond/branch_0_fun/ppermute | solution.py:859
  405.4 14.8 %collective-permute-start.93 = (bf16[9,128,128]{2,1,0:T(8,128)(2,1)S(1)}, bf16[9,128,128]{2,1,0:T(8,128)(2,1)S(1)}, u32[]{:S(2)}, u32[]{:S(2)}) collective-permute-start(bf16[9,128,128]{2,1,0:T(8,128)(2,1)S(1)} %get-tuple-element.792), channel_id=1, source_target_pairs={{0,8},{4,12},{8,0},{12,4},{16,24},{20,28},{24,16},{28,20},{1,9},{5... | collective-permute-start | bytes 884744 | tf_op jit(solution)/shard_map/cond/branch_0_fun/ppermute | solution.py:859
  406.5 15.3 %collective-permute-start.94 = (bf16[9,128,128]{2,1,0:T(8,128)(2,1)S(1)}, bf16[9,128,128]{2,1,0:T(8,128)(2,1)S(1)}, u32[]{:S(2)}, u32[]{:S(2)}) collective-permute-start(bf16[9,128,128]{2,1,0:T(8,128)(2,1)S(1)} %get-tuple-element.791), channel_id=1, source_target_pairs={{0,16},{4,20},{8,24},{12,28},{16,0},{20,4},{24,8},{28,12},{1,17},{... | collective-permute-start | bytes 884744 | tf_op jit(solution)/shard_map/cond/branch_0_fun/ppermute | solution.py:859
  407.6 14.9 %collective-permute-start.95 = (bf16[9,128,128]{2,1,0:T(8,128)(2,1)S(1)}, bf16[9,128,128]{2,1,0:T(8,128)(2,1)S(1)}, u32[]{:S(2)}, u32[]{:S(2)}) collective-permute-start(bf16[9,128,128]{2,1,0:T(8,128)(2,1)S(1)} %get-tuple-element.790), channel_id=1, source_target_pairs={{0,24},{4,28},{8,16},{12,20},{16,8},{20,12},{24,0},{28,4},{1,25},{... | collective-permute-start | bytes 884744 | tf_op jit(solution)/shard_map/cond/branch_0_fun/ppermute | solution.py:859
  411.3 19.5 %all-to-all-start.2 = ((bf16[8,112,256]{2,1,0:T(8,128)(2,1)}), bf16[8,112,256]{2,1,0:T(8,128)(2,1)S(1)}, u32[]{:S(2)}, u32[]{:S(2)}) async-start(bf16[8,112,256]{2,1,0:T(8,128)(2,1)} %bitcast.34), calls=%async_computation.2 | async-start | bytes 917504 | tf_op jit(solution)/shard_map/cond/branch_0_fun/all_to_all | solution.py:1131
  (152 other events, 2326.4 us)

commit v6 on v5

--- a/solution.py
+++ b/solution.py
@@ -588,46 +588,6 @@
         ],
         compiler_params=vmem(24),
     )(*args)
-
-
-def conv_t3_kernel(*refs):
-    dys, w, outs, moved = refs[:6], refs[6], refs[7:13], refs[13]
-    rows, width = dys[0].shape[0], moved.shape[1] // 3
-    step = pl.program_id(0)
-
-    @pl.when(step == 0)
-    def _():
-        for r in range(3):
-            for k in range(2):
-                dy = dys[2 * r + k]
-                spread_rows(moved, r * rows, dy[...], width, k * dy.shape[1])
-
-    value = mxu(moved[...], w[...].reshape(3 * width, w.shape[2]), NN)
-    for k in range(2):
-
-        @pl.when(step == k)
-        def _():
-            for r in range(3):
-                out = outs[2 * r + k]
-                out[...] = value[r * rows : (r + 1) * rows].astype(out.dtype)
-
-
-def conv_t3(pairs, w):
-    rows, (_, width, depth) = pairs[0][0].shape[0], w.shape
-    lanes = depth // 2
-    flat = [dy for pair in pairs for dy in pair]
-    out = pl.pallas_call(
-        conv_t3_kernel,
-        grid=(2,),
-        in_specs=[same(*dy.shape) for dy in flat]
-        + [pl.BlockSpec((3, width, lanes), lambda i: (0, 0, i))],
-        out_specs=[same(rows, lanes)] * 6,
-        out_shape=[jax.ShapeDtypeStruct((rows, lanes), kind) for kind in (f32, bf16) * 3],
-        scratch_shapes=[pltpu.VMEM((3 * rows, 3 * width), bf16)],
-        compiler_params=vmem(24),
-        cost_estimate=cost(18 * rows * width * depth, 9 * rows * depth + 6 * width * depth),
-    )(*flat, w)
-    return [out[2 * r : 2 * r + 2] for r in range(3)]
 
 
 def grad2_place(pos, own, send, a, prod):
@@ -1073,9 +1033,14 @@
     later_near = after(later_near, first)
     for k, r in enumerate(order[1:]):
         pairs1[r] = [dpre1[r], later_near[k * rows : (k + 1) * rows]]
-    terms[2], terms[3], terms[0] = conv_t3([pairs1[r] for r in order[1:]], weights1)
-    for r in order[1:]:
+    terms[2] = conv_t(pairs1[2], weights1, 2)
+    nears[2] = swap(terms[2][1], Y)
+    before = terms[2][1]
+    for r in (3, 0):
+        pairs1[r][1] = after(pairs1[r][1], before)
+        terms[r] = conv_t(pairs1[r], weights1, 2)
         nears[r] = swap(terms[r][1], Y)
+        before = terms[r][1]
 
     second = ((terms[2][0] + nears[2].astype(f32)) + along(first, 1).astype(f32)).astype(bf16)
     moved = along(second, 1)
@@ -1107,7 +1072,7 @@
         pl.BlockSpec(
             (9, part, 128), lambda t, p: (0, 0, 2 * (p[2] ^ (t % 2)) + (p[1] ^ (t // 2)))
         ),
-        60,
+        36,
     )
     grad2_send, nears[0], *sent = lax.optimization_barrier((grad2_send, nears[0], *sent))
     later = [swap(after(out_pieces[k], grad2_send), k) for k in (7, 1, 2, 3)]

time: 449 us -> 451 us (level)
    pallas_call x5 -> x8, Pallas kernels: 20.1 us -> 26.1 us  [conv_t(): pl.pallas_call(functools.partial(conv_t_kernel, len(dys)), grid=(blocks,)...]
    pallas_call x1 -> x0, Pallas kernels: 4.85 us -> none  [conv_t3(): pl.pallas_call(conv_t3_kernel, grid=(2,), in_specs=[same(*dy.shape) for d...]
    cond x219 -> x275, local copies, waits for them, and re-layouts: 11.7 us -> 12.6 us
  transfers between devices with their start and end apart: 105 -> 105, of which waited for: 59 -> 57; matrix products, arithmetic and copies ran while one was open for 6% -> 7% of each run, Pallas kernels for 18% -> 18%
where the time goes in v6:
time: 451 us; the launch traced here: 445 us
  waiting for transfers between devices  161 us (36%)
  starting transfers between devices  124 us (27%)
  Pallas kernels  93.7 us (21%)
  other arithmetic  24.2 us (5%)
  local copies, waits for them, and re-layouts  23.9 us (5%)
  loops' own time  11.6 us (3%)
    ppermute x69, waiting for transfers between devices, swap(): return lax.ppermute(x, 'tm', [(i, i ^ bits) for i in range(n)])  99.5 us
    ppermute x69, starting transfers between devices, swap(): return lax.ppermute(x, 'tm', [(i, i ^ bits) for i in range(n)])  61.4 us
    ppermute x12, waiting for transfers between devices, along(): return lax.ppermute(x, 'batch', [(z, (z + shift) % PLANES) for z in groups])  44.1 us
    pallas_call x8, Pallas kernels, conv_t(): pl.pallas_call(functools.partial(conv_t_kernel, len(dys)), grid=(blocks,)...  26.1 us
    pallas_call x2, Pallas kernels, weight_grad_own(): pl.pallas_call(functools.partial(grad_kernel, place, groups, pieces), gri...  22.9 us
    pallas_call x8, Pallas kernels, conv(): pl.pallas_call(functools.partial(conv_kernel, len(xs)), grid=(width // ti...  19.7 us
    ppermute x9, starting transfers between devices, route(): return lax.ppermute(x, ('tm', 'batch'), flat)  16.4 us
    ppermute x12, starting transfers between devices, along(): return lax.ppermute(x, 'batch', [(z, (z + shift) % PLANES) for z in groups])  13.2 us
  transfers between devices with their start and end apart: 105, of which 57 were waited for; matrix products, arithmetic and copies ran while one was open for 7% of the time, Pallas kernels for 18%

profile of v6, /device:TPU:0, one launch (start us, length us, event | category | flops | bytes accessed | tf_op | source)
XLA Modules:
  0.0 444.8 jit_solution(14975948810176976520)
XLA Ops:
  3.2 3.0 collective-permute-start.288
  6.2 2.6 collective-permute-start.289
  10.2 3.7 all-to-all-start.9
  18.7 4.3 all-to-all-done.9
  24.4 419.2 %conditional.1 = (bf16[1,112,2,2048]{3,2,1,0:T(2,128)(2,1)}, bf16[1,112,2,1024]{3,2,1,0:T(2,128)(2,1)}, f32[256,9,256]{2,0,1:T(8,128)}, f32[256]{0:T(256)}, f32[...) conditional(s32[]{:T(128)} %clamp.3, (s32[3,896]{1,0:T(4,128)S(1)}, ...), branch_computations={%region_8.30_spmd, %region_30.52_spmd, %region_52.74_spmd} | conditional | flops 36335017984 | bytes 563562304 | solution.py:772
  28.5 2.4 collective-permute-start.20
  31.7 7.6 %collective-permute-done.1.refs_0_.refs_8_ = bf16[368,512]{1,0:T(8,128)(2,1)S(1)} collective-permute-done((bf16[368,512]{1,0:T(8,128)(2,1)S(1)}, bf16[368,512]{1,0:T(8,128)(2,1)S(1)}, u32[]{:S(2)}, u32[]{:S(2)}) %collective-permute-start.1) | collective-permute-done | bytes 376864 | tf_op jit(solution)/shard_map/cond/branch_0_fun/ppermute | solution.py:822
  39.3 3.5 collective-permute-done.19.refs_2_
  44.4 4.4 all-to-all-start
  52.9 6.5 %branch_0_fun.28 = (bf16[112,512]{1,0:T(8,128)(2,1)}, bf16[112,512]{1,0:T(8,128)(2,1)}, bf16[112,512]{1,0:T(8,128)(2,1)}, bf16[112,512]{1,0:T(8,128)(2,1)}, bf16...) custom-call(s32[4]{0:T(128)S(1)} %get-tuple-element.123.pos, ...), custom_call_target="tpu_custom_call" | custom-call | tf_op jit(solution)/shard_map/cond/branch_0_fun/pallas_call | solution.py:490
  59.4 4.6 %branch_0_fun.27.refs_4_.refs_1_ = bf16[3,1024,1024]{2,1,0:T(8,128)(2,1)S(1)} custom-call(s32[4]{0:T(128)S(1)} %get-tuple-element.123.pos, bf16[9,256,512]{2,1,0:T(8,128)(2,1)} %get-tuple-element.132.own, bf16[9,256,512]{2,1,0:T(8,128)(2,1)} %get-tuple-element.134.other), custom_call_target="tpu_custom_call" | custom-call | tf_op jit(solution)/shard_map/cond/branch_0_fun/pallas_call | solution.py:314
  64.1 2.6 copy-done
  72.1 2.5 collective-permute-done.6
  74.6 4.4 collective-permute-done.2.refs_0_.refs_10_
  79.8 4.0 collective-permute-start.8
  86.6 3.9 collective-permute-start.11
  96.7 3.2 collective-permute-done.16
  99.8 2.4 collective-permute-done.15
  118.4 2.4 branch_0_fun.34
  124.2 3.7 collective-permute-done.24
  128.1 3.1 collective-permute-done.26
  137.0 4.0 collective-permute-done.28.refs_1_.refs_9_
  141.1 4.6 %collective-permute-done.29.refs_2_.refs_10_ = bf16[368,256]{1,0:T(8,128)(2,1)S(1)} collective-permute-done((bf16[368,256]{1,0:T(8,128)(2,1)S(1)}, bf16[368,256]{1,0:T(8,128)(2,1)S(1)}, u32[]{:S(2)}, u32[]{:S(2)}) %collective-permute-start.29) | collective-permute-done | bytes 188448 | tf_op jit(solution)/shard_map/cond/branch_0_fun/ppermute | solution.py:819
  145.7 2.9 copy-done.1
  148.5 3.3 branch_0_fun.35
  151.8 2.6 collective-permute-start.40
  158.8 5.1 %collective-permute-done.33.refs_3_.refs_15_ = bf16[368,256]{1,0:T(8,128)(2,1)S(1)} collective-permute-done((bf16[368,256]{1,0:T(8,128)(2,1)S(1)}, bf16[368,256]{1,0:T(8,128)(2,1)S(1)}, u32[]{:S(2)}, u32[]{:S(2)}) %collective-permute-start.33) | collective-permute-done | bytes 188448 | tf_op jit(solution)/shard_map/cond/branch_0_fun/ppermute | solution.py:819
  166.3 3.3 branch_0_fun.36
  169.7 2.3 collective-permute-done.40
  177.0 4.6 %collective-permute-done.36.refs_3_.refs_19_ = bf16[368,256]{1,0:T(8,128)(2,1)S(1)} collective-permute-done((bf16[368,256]{1,0:T(8,128)(2,1)S(1)}, bf16[368,256]{1,0:T(8,128)(2,1)S(1)}, u32[]{:S(2)}, u32[]{:S(2)}) %collective-permute-start.36) | collective-permute-done | bytes 188448 | tf_op jit(solution)/shard_map/cond/branch_0_fun/ppermute | solution.py:819
  187.1 3.3 branch_0_fun.37
  194.2 3.3 branch_0_fun.38.term
  197.7 12.6 %collective-permute-done.42.moved = bf16[368,1024]{1,0:T(8,128)(2,1)S(1)} collective-permute-done((bf16[368,1024]{1,0:T(8,128)(2,1)S(1)}, bf16[368,1024]{1,0:T(8,128)(2,1)S(1)}, u32[]{:S(2)}, u32[]{:S(2)}) %collective-permute-start.42) | collective-permute-done | bytes 753696 | tf_op jit(solution)/shard_map/cond/branch_0_fun/ppermute | solution.py:822
  212.7 3.7 collective-permute-start.47
  221.4 3.8 collective-permute-start.50
  227.1 3.8 collective-permute-done.51.t3
  231.3 4.3 branch_0_fun.42
  239.2 3.7 collective-permute-done.52
  243.0 2.9 collective-permute-done.53
  245.9 4.4 collective-permute-done.55.refs_0_.refs_1_
  250.3 4.3 branch_0_fun.43
  258.2 2.8 collective-permute-done.56
  261.0 2.9 collective-permute-done.57
  263.9 4.4 collective-permute-done.59.refs_0_.refs_2_
  268.6 4.4 branch_0_fun.44
  278.6 3.3 collective-permute-done.61
  281.9 3.8 collective-permute-done.63.refs_0_.refs_3_
  285.7 4.3 branch_0_fun.45
  295.7 3.3 collective-permute-done.65
  305.6 4.2 collective-permute-done.71
  310.3 2.7 branch_0_fun.46
  315.2 3.2 collective-permute-start.73
  326.3 3.7 collective-permute-done.69
  338.7 6.1 %collective-permute-done.76 = bf16[368,512]{1,0:T(8,128)(2,1)S(1)} collective-permute-done((bf16[368,512]{1,0:T(8,128)(2,1)S(1)}, bf16[368,512]{1,0:T(8,128)(2,1)S(1)}, u32[]{:S(2)}, u32[]{:S(2)}) %collective-permute-start.76) | collective-permute-done | bytes 376864 | tf_op jit(solution)/shard_map/cond/branch_0_fun/ppermute | solution.py:819
  345.2 8.4 %branch_0_fun.50 = (f32[4,9,128,128]{3,2,1,0:T(8,128)S(1)}, bf16[4,9,128,128]{3,2,1,0:T(8,128)(2,1)S(1)}) custom-call(s32[4]{0:T(128)S(1)} %copy-done.269, bf16[368,256]{1,0:T(8,128)(2,1)S(1)} %copy-done.107, bf16[368,256]{1,0:T(8,128)(2,1)S(1)} %copy-done.233, bf16[368,256]{1,0:T(8,128)(2,1)S(1)} %copy-done.24, ...), custom_call_target="tpu_custom_call" | custom-call | tf_op jit(solution)/shard_map/cond/branch_0_fun/pallas_call | solution.py:664
  355.5 2.8 collective-permute-done.80
  359.8 4.8 %all-to-all-start.1 = ((bf16[4,9,128,128]{3,2,1,0:T(8,128)(2,1)}), bf16[4,9,128,128]{3,2,1,0:T(8,128)(2,1)}, u32[]{:S(2)}, u32[]{:S(2)}) async-start(bf16[4,9,128,128]{3,2,1,0:T(8,128)(2,1)} %add_convert_fusion), calls=%async_computation.1 | async-start | bytes 2359296 | tf_op jit(solution)/shard_map/cond/branch_0_fun/all_to_all | solution.py:1063
  377.1 14.5 %branch_0_fun.51 = (f32[9,256,512]{2,1,0:T(8,128)S(1)}, bf16[9,256,512]{2,1,0:T(8,128)(2,1)}) custom-call(s32[4]{0:T(128)S(1)} %copy-done.270, bf16[368,1024]{1,0:T(8,128)(2,1)S(1)} %copy-done.97, bf16[368,1024]{1,0:T(8,128)(2,1)S(1)} %copy-done.99, bf16[368,1024]{1,0:T(8,128)(2,1)S(1)} %copy-done.102, bf16[368,1024]{1,0:T(8,128)(2,1)S(1)} %copy-done.104, ...), custom_call_target="tpu_custom_call" | custom-call | tf_op jit(solution)/shard_map/cond/branch_0_fun/pallas_call | solution.py:664
  395.9 2.6 collective-permute-start.87
  399.2 2.9 collective-permute-done.89.refs_2_
  413.0 3.5 all-to-all-start.2
  416.5 5.5 %branch_0_fun.52 = bf16[112,2,2048]{2,1,0:T(2,128)(2,1)} custom-call(s32[4]{0:T(128)S(1)} %copy-done.270, bf16[112,512]{1,0:T(8,128)(2,1)} %get-tuple-element.279.refs_0_, bf16[112,512]{1,0:T(8,128)(2,1)} %copy-done.335, bf16[112,512]{1,0:T(8,128)(2,1)} %copy-done.332, bf16[112,512]{1,0:T(8,128)(2,1)} %copy-done.329, bf16[112,512]{1,0:T(8,128)(2,1)} %copy-done.326, ...), custom_call_target="tpu_custom_call" | custom-call | tf_op jit(solution)/shard_map/cond/branch_0_fun/pallas_call | solution.py:518
  421.9 2.9 collective-permute-done.94.refs_2_
  427.0 6.1 %add_bitcast_fusion = f32[256,9,512]{2,0,1:T(8,128)} fusion(f32[9,256,512]{2,1,0:T(8,128)} %copy-done.6, bf16[9,256,512]{2,1,0:T(8,128)(2,1)} %collective-permute-done.92), kind=kLoop, calls=%fused_computation | loop fusion | flops 2359296 | bytes 11796480 | tf_op jit(solution)/shard_map/cond/branch_0_fun/transpose | solution.py:1101
  (563 shorter events, 169.6 us)
Async XLA Ops:
  3.2 11.9 %collective-permute-start.288 = (s32[1,24]{1,0:T(1,128)S(1)}, s32[1,24]{1,0:T(1,128)S(1)}, u32[]{:S(2)}, u32[]{:S(2)}) collective-permute-start(s32[1,24]{1,0:T(1,128)S(1)} %copy-done.360), channel_id=1, source_target_pairs={{0,1},{1,2},{2,3},{3,0},{4,5},{5,6},{6,7},{7,4},{8,9},{9,10},{10,1... | collective-permute-start | bytes 296 | tf_op jit(solution)/shard_map/ppermute | solution.py:743
  6.2 8.9 %collective-permute-start.289 = (s32[1,24]{1,0:T(1,128)S(1)}, s32[1,24]{1,0:T(1,128)S(1)}, u32[]{:S(2)}, u32[]{:S(2)}) collective-permute-start(s32[1,24]{1,0:T(1,128)S(1)} %copy-done.360), channel_id=1, source_target_pairs={{0,2},{1,3},{2,0},{3,1},{4,6},{5,7},{6,4},{7,5},{8,10},{9,11},{10,... | collective-permute-start | bytes 296 | tf_op jit(solution)/shard_map/ppermute | solution.py:743
  10.2 12.8 %all-to-all-start.9 = ((bf16[8,112,256]{2,1,0:T(8,128)(2,1)}), bf16[8,112,256]{2,1,0:T(8,128)(2,1)S(1)}, u32[]{:S(2)}, u32[]{:S(2)}) async-start(bf16[8,112,256]{2,1,0:T(8,128)(2,1)} %bitcast.140), calls=%async_computation.9 | async-start | bytes 917504 | tf_op jit(solution)/shard_map/all_to_all | solution.py:739
  14.5 9.9 %collective-permute-start.291 = (bf16[9,256,512]{2,1,0:T(8,128)(2,1)}, bf16[9,256,512]{2,1,0:T(8,128)(2,1)}, u32[]{:S(2)}, u32[]{:S(2)}) collective-permute-start(bf16[9,256,512]{2,1,0:T(8,128)(2,1)} %bitcast.264), channel_id=1, source_target_pairs={{0,4},{4,0},{8,12},{12,8},{16,20},{20,16},{24,28},{28,24},{1,5},{5... | collective-permute-start | bytes 7077896 | tf_op jit(solution)/shard_map/ppermute | solution.py:754
  26.6 12.7 %collective-permute-start.1 = (bf16[368,512]{1,0:T(8,128)(2,1)S(1)}, bf16[368,512]{1,0:T(8,128)(2,1)S(1)}, u32[]{:S(2)}, u32[]{:S(2)}) collective-permute-start(bf16[368,512]{1,0:T(8,128)(2,1)S(1)} %pad_maximum_fusion.2.refs_0_.refs_14_), channel_id=1, source_target_pairs={{0,1},{1,2},{2,3},{3,0},{4,5},{5,6},{6,7},{7,4},{8,9},{9,10},{10,1... | collective-permute-start | bytes 1130504 | tf_op jit(solution)/shard_map/cond/branch_0_fun/ppermute | solution.py:822
  27.4 11.9 %collective-permute-start.18 = (bf16[9,128,128]{2,1,0:T(8,128)(2,1)S(1)}, bf16[9,128,128]{2,1,0:T(8,128)(2,1)S(1)}, u32[]{:S(2)}, u32[]{:S(2)}) collective-permute-start(bf16[9,128,128]{2,1,0:T(8,128)(2,1)S(1)} %get-tuple-element.160), channel_id=1, source_target_pairs={{0,8},{4,12},{8,0},{12,4},{16,24},{20,28},{24,16},{28,20},{1,9},{5... | collective-permute-start | bytes 884744 | tf_op jit(solution)/shard_map/cond/branch_0_fun/ppermute | solution.py:819
  27.9 14.8 %collective-permute-start.19 = (bf16[9,128,128]{2,1,0:T(8,128)(2,1)S(1)}, bf16[9,128,128]{2,1,0:T(8,128)(2,1)S(1)}, u32[]{:S(2)}, u32[]{:S(2)}) collective-permute-start(bf16[9,128,128]{2,1,0:T(8,128)(2,1)S(1)} %get-tuple-element.162), channel_id=1, source_target_pairs={{0,16},{4,20},{8,24},{12,28},{16,0},{20,4},{24,8},{28,12},{1,17},{... | collective-permute-start | bytes 884744 | tf_op jit(solution)/shard_map/cond/branch_0_fun/ppermute | solution.py:819
  28.5 14.3 %collective-permute-start.20 = (bf16[9,128,128]{2,1,0:T(8,128)(2,1)S(1)}, bf16[9,128,128]{2,1,0:T(8,128)(2,1)S(1)}, u32[]{:S(2)}, u32[]{:S(2)}) collective-permute-start(bf16[9,128,128]{2,1,0:T(8,128)(2,1)S(1)} %copy-done.376), channel_id=1, source_target_pairs={{0,24},{4,28},{8,16},{12,20},{16,8},{20,12},{24,0},{28,4},{1,25},{... | collective-permute-start | bytes 884744 | tf_op jit(solution)/shard_map/cond/branch_0_fun/ppermute | solution.py:819
  44.4 62.3 %all-to-all-start = ((bf16[4,9,128,128]{3,2,1,0:T(8,128)(2,1)}), bf16[4,9,128,128]{3,2,1,0:T(8,128)(2,1)S(1)}, u32[]{:S(2)}, u32[]{:S(2)}) async-start(bf16[4,9,128,128]{3,2,1,0:T(8,128)(2,1)} %branch_0_fun.29), calls=%async_computation | async-start | bytes 2359296 | tf_op jit(solution)/shard_map/cond/branch_0_fun/all_to_all | solution.py:877
  48.8 19.5 %collective-permute-start.3 = (bf16[368,512]{1,0:T(8,128)(2,1)S(1)}, bf16[368,512]{1,0:T(8,128)(2,1)S(1)}, u32[]{:S(2)}, u32[]{:S(2)}) collective-permute-start(bf16[368,512]{1,0:T(8,128)(2,1)S(1)} %pad_maximum_fusion.2.refs_0_.refs_14_), channel_id=1, source_target_pairs={{0,16},{4,20},{8,24},{12,28},{16,0},{20,4},{24,8},{28,12},{1,17},{... | collective-permute-start | bytes 1130504 | tf_op jit(solution)/shard_map/cond/branch_0_fun/ppermute | solution.py:819
  50.0 29.1 %collective-permute-start.2 = (bf16[368,512]{1,0:T(8,128)(2,1)S(1)}, bf16[368,512]{1,0:T(8,128)(2,1)S(1)}, u32[]{:S(2)}, u32[]{:S(2)}) collective-permute-start(bf16[368,512]{1,0:T(8,128)(2,1)S(1)} %collective-permute-done.1.refs_0_.refs_8_), channel_id=1, source_target_pairs={{0,1},{1,2},{2,3},{3,0},{4,5},{5,6},{6,7},{7,4},{8,9},{9,10},{10,1... | collective-permute-start | bytes 1130504 | tf_op jit(solution)/shard_map/cond/branch_0_fun/ppermute | solution.py:822
  52.0 27.1 %collective-permute-start.4 = (bf16[368,512]{1,0:T(8,128)(2,1)S(1)}, bf16[368,512]{1,0:T(8,128)(2,1)S(1)}, u32[]{:S(2)}, u32[]{:S(2)}) collective-permute-start(bf16[368,512]{1,0:T(8,128)(2,1)S(1)} %collective-permute-done.1.refs_0_.refs_8_), channel_id=1, source_target_pairs={{0,16},{4,20},{8,24},{12,28},{16,0},{20,4},{24,8},{28,12},{1,17},{... | collective-permute-start | bytes 1130504 | tf_op jit(solution)/shard_map/cond/branch_0_fun/ppermute | solution.py:819
  66.7 7.9 %collective-permute-start.6 = (bf16[112,512]{1,0:T(8,128)(2,1)S(1)}, bf16[112,512]{1,0:T(8,128)(2,1)S(1)}, u32[]{:S(2)}, u32[]{:S(2)}) collective-permute-start(bf16[112,512]{1,0:T(8,128)(2,1)S(1)} %copy-done.394), channel_id=1, source_target_pairs={{0,8},{4,12},{8,0},{12,4},{16,24},{20,28},{24,16},{28,20},{1,9},{5... | collective-permute-start | bytes 344072 | tf_op jit(solution)/shard_map/cond/branch_0_fun/ppermute | solution.py:819
  79.8 24.8 %collective-permute-start.8 = (bf16[368,512]{1,0:T(8,128)(2,1)S(1)}, bf16[368,512]{1,0:T(8,128)(2,1)S(1)}, u32[]{:S(2)}, u32[]{:S(2)}) collective-permute-start(bf16[368,512]{1,0:T(8,128)(2,1)S(1)} %collective-permute-done.2.refs_0_.refs_10_), channel_id=1, source_target_pairs={{0,1},{1,2},{2,3},{3,0},{4,5},{5,6},{6,7},{7,4},{8,9},{9,10},{10,1... | collective-permute-start | bytes 1130504 | tf_op jit(solution)/shard_map/cond/branch_0_fun/ppermute | solution.py:822
  83.8 21.4 %collective-permute-start.9 = (bf16[368,512]{1,0:T(8,128)(2,1)S(1)}, bf16[368,512]{1,0:T(8,128)(2,1)S(1)}, u32[]{:S(2)}, u32[]{:S(2)}) collective-permute-start(bf16[368,512]{1,0:T(8,128)(2,1)S(1)} %collective-permute-done.2.refs_0_.refs_10_), channel_id=1, source_target_pairs={{0,16},{4,20},{8,24},{12,28},{16,0},{20,4},{24,8},{28,12},{1,17},{... | collective-permute-start | bytes 1130504 | tf_op jit(solution)/shard_map/cond/branch_0_fun/ppermute | solution.py:819
  85.9 10.2 %collective-permute-start.17 = (bf16[112,512]{1,0:T(8,128)(2,1)S(1)}, bf16[112,512]{1,0:T(8,128)(2,1)S(1)}, u32[]{:S(2)}, u32[]{:S(2)}) collective-permute-start(bf16[112,512]{1,0:T(8,128)(2,1)S(1)} %copy-done.388), channel_id=1, source_target_pairs={{0,28},{4,24},{8,20},{12,16},{16,12},{20,8},{24,4},{28,0},{1,29},{... | collective-permute-start | bytes 344072 | tf_op jit(solution)/shard_map/cond/branch_0_fun/ppermute | solution.py:819
  96.1 8.5 %collective-permute-start.14 = (bf16[112,512]{1,0:T(8,128)(2,1)S(1)}, bf16[112,512]{1,0:T(8,128)(2,1)S(1)}, u32[]{:S(2)}, u32[]{:S(2)}) collective-permute-start(bf16[112,512]{1,0:T(8,128)(2,1)S(1)} %copy-done.379), channel_id=1, source_target_pairs={{0,16},{4,20},{8,24},{12,28},{16,0},{20,4},{24,8},{28,12},{1,17},{... | collective-permute-start | bytes 344072 | tf_op jit(solution)/shard_map/cond/branch_0_fun/ppermute | solution.py:819
  106.8 11.6 %collective-permute-start.25 = (bf16[368,512]{1,0:T(8,128)(2,1)}, bf16[368,512]{1,0:T(8,128)(2,1)}, u32[]{:S(2)}, u32[]{:S(2)}) collective-permute-start(bf16[368,512]{1,0:T(8,128)(2,1)} %copy-done.150), channel_id=1, source_target_pairs={{0,16},{4,20},{8,24},{12,28},{16,0},{20,4},{24,8},{28,12},{1,17},{... | collective-permute-start | bytes 1130504 | tf_op jit(solution)/shard_map/cond/branch_0_fun/ppermute | solution.py:819
  112.2 11.8 %collective-permute-start.22 = (bf16[368,256]{1,0:T(8,128)(2,1)S(1)}, bf16[368,256]{1,0:T(8,128)(2,1)S(1)}, u32[]{:S(2)}, u32[]{:S(2)}) collective-permute-start(bf16[368,256]{1,0:T(8,128)(2,1)S(1)} %get-tuple-element.168), channel_id=1, source_target_pairs={{0,8},{4,12},{8,0},{12,4},{16,24},{20,28},{24,16},{28,20},{1,9},{5... | collective-permute-start | bytes 565256 | tf_op jit(solution)/shard_map/cond/branch_0_fun/ppermute | solution.py:819
  114.8 9.1 %collective-permute-start.23 = (bf16[368,256]{1,0:T(8,128)(2,1)S(1)}, bf16[368,256]{1,0:T(8,128)(2,1)S(1)}, u32[]{:S(2)}, u32[]{:S(2)}) collective-permute-start(bf16[368,256]{1,0:T(8,128)(2,1)S(1)} %get-tuple-element.172), channel_id=1, source_target_pairs={{0,8},{4,12},{8,0},{12,4},{16,24},{20,28},{24,16},{28,20},{1,9},{5... | collective-permute-start | bytes 565256 | tf_op jit(solution)/shard_map/cond/branch_0_fun/ppermute | solution.py:819
  117.2 10.8 %collective-permute-start.24 = (bf16[368,256]{1,0:T(8,128)(2,1)S(1)}, bf16[368,256]{1,0:T(8,128)(2,1)S(1)}, u32[]{:S(2)}, u32[]{:S(2)}) collective-permute-start(bf16[368,256]{1,0:T(8,128)(2,1)S(1)} %get-tuple-element.177), channel_id=1, source_target_pairs={{0,8},{4,12},{8,0},{12,4},{16,24},{20,28},{24,16},{28,20},{1,9},{5... | collective-permute-start | bytes 565256 | tf_op jit(solution)/shard_map/cond/branch_0_fun/ppermute | solution.py:819
  120.8 10.4 %collective-permute-start.26 = (bf16[368,256]{1,0:T(8,128)(2,1)S(1)}, bf16[368,256]{1,0:T(8,128)(2,1)S(1)}, u32[]{:S(2)}, u32[]{:S(2)}) collective-permute-start(bf16[368,256]{1,0:T(8,128)(2,1)S(1)} %get-tuple-element.182), channel_id=1, source_target_pairs={{0,8},{4,12},{8,0},{12,4},{16,24},{20,28},{24,16},{28,20},{1,9},{5... | collective-permute-start | bytes 565256 | tf_op jit(solution)/shard_map/cond/branch_0_fun/ppermute | solution.py:819
  134.8 10.9 %collective-permute-start.29 = (bf16[368,256]{1,0:T(8,128)(2,1)S(1)}, bf16[368,256]{1,0:T(8,128)(2,1)S(1)}, u32[]{:S(2)}, u32[]{:S(2)}) collective-permute-start(bf16[368,256]{1,0:T(8,128)(2,1)S(1)} %get-tuple-element.841.refs_0_.refs_8_), channel_id=1, source_target_pairs={{0,16},{4,20},{8,24},{12,28},{16,0},{20,4},{24,8},{28,12},{1,17},{... | collective-permute-start | bytes 565256 | tf_op jit(solution)/shard_map/cond/branch_0_fun/ppermute | solution.py:819
  136.0 9.7 %collective-permute-start.30 = (bf16[368,256]{1,0:T(8,128)(2,1)S(1)}, bf16[368,256]{1,0:T(8,128)(2,1)S(1)}, u32[]{:S(2)}, u32[]{:S(2)}) collective-permute-start(bf16[368,256]{1,0:T(8,128)(2,1)S(1)} %get-tuple-element.841.refs_0_.refs_8_), channel_id=1, source_target_pairs={{0,24},{4,28},{8,16},{12,20},{16,8},{20,12},{24,0},{28,4},{1,25},{... | collective-permute-start | bytes 565256 | tf_op jit(solution)/shard_map/cond/branch_0_fun/ppermute | solution.py:819
  151.8 20.2 %collective-permute-start.40 = (bf16[368,1024]{1,0:T(8,128)(2,1)S(1)}, bf16[368,1024]{1,0:T(8,128)(2,1)S(1)}, u32[]{:S(2)}, u32[]{:S(2)}) collective-permute-start(bf16[368,1024]{1,0:T(8,128)(2,1)S(1)} %branch_0_fun.35), channel_id=1, source_target_pairs={{0,1},{1,2},{2,3},{3,0},{4,5},{5,6},{6,7},{7,4},{8,9},{9,10},{10,1... | collective-permute-start | bytes 2261000 | tf_op jit(solution)/shard_map/cond/branch_0_fun/ppermute | solution.py:822
  155.2 8.7 %collective-permute-start.33 = (bf16[368,256]{1,0:T(8,128)(2,1)S(1)}, bf16[368,256]{1,0:T(8,128)(2,1)S(1)}, u32[]{:S(2)}, u32[]{:S(2)}) collective-permute-start(bf16[368,256]{1,0:T(8,128)(2,1)S(1)} %get-tuple-element.185.refs_0_.refs_12_), channel_id=1, source_target_pairs={{0,24},{4,28},{8,16},{12,20},{16,8},{20,12},{24,0},{28,4},{1,25},{... | collective-permute-start | bytes 565256 | tf_op jit(solution)/shard_map/cond/branch_0_fun/ppermute | solution.py:819
  157.1 8.3 %collective-permute-start.31 = (bf16[368,256]{1,0:T(8,128)(2,1)S(1)}, bf16[368,256]{1,0:T(8,128)(2,1)S(1)}, u32[]{:S(2)}, u32[]{:S(2)}) collective-permute-start(bf16[368,256]{1,0:T(8,128)(2,1)S(1)} %get-tuple-element.185.refs_0_.refs_12_), channel_id=1, source_target_pairs={{0,8},{4,12},{8,0},{12,4},{16,24},{20,28},{24,16},{28,20},{1,9},{5... | collective-permute-start | bytes 565256 | tf_op jit(solution)/shard_map/cond/branch_0_fun/ppermute | solution.py:819
  157.4 8.9 %collective-permute-start.32 = (bf16[368,256]{1,0:T(8,128)(2,1)S(1)}, bf16[368,256]{1,0:T(8,128)(2,1)S(1)}, u32[]{:S(2)}, u32[]{:S(2)}) collective-permute-start(bf16[368,256]{1,0:T(8,128)(2,1)S(1)} %get-tuple-element.185.refs_0_.refs_12_), channel_id=1, source_target_pairs={{0,16},{4,20},{8,24},{12,28},{16,0},{20,4},{24,8},{28,12},{1,17},{... | collective-permute-start | bytes 565256 | tf_op jit(solution)/shard_map/cond/branch_0_fun/ppermute | solution.py:819
  172.2 19.4 %collective-permute-start.41 = (bf16[368,1024]{1,0:T(8,128)(2,1)S(1)}, bf16[368,1024]{1,0:T(8,128)(2,1)S(1)}, u32[]{:S(2)}, u32[]{:S(2)}) collective-permute-start(bf16[368,1024]{1,0:T(8,128)(2,1)S(1)} %add_convert_fusion.2), channel_id=1, source_target_pairs={{0,1},{1,2},{2,3},{3,0},{4,5},{5,6},{6,7},{7,4},{8,9},{9,10},{10,1... | collective-permute-start | bytes 2261000 | tf_op jit(solution)/shard_map/cond/branch_0_fun/ppermute | solution.py:822
  173.4 8.2 %collective-permute-start.36 = (bf16[368,256]{1,0:T(8,128)(2,1)S(1)}, bf16[368,256]{1,0:T(8,128)(2,1)S(1)}, u32[]{:S(2)}, u32[]{:S(2)}) collective-permute-start(bf16[368,256]{1,0:T(8,128)(2,1)S(1)} %get-tuple-element.187.refs_0_.refs_16_), channel_id=1, source_target_pairs={{0,24},{4,28},{8,16},{12,20},{16,8},{20,12},{24,0},{28,4},{1,25},{... | collective-permute-start | bytes 565256 | tf_op jit(solution)/shard_map/cond/branch_0_fun/ppermute | solution.py:819
  175.0 7.7 %collective-permute-start.34 = (bf16[368,256]{1,0:T(8,128)(2,1)S(1)}, bf16[368,256]{1,0:T(8,128)(2,1)S(1)}, u32[]{:S(2)}, u32[]{:S(2)}) collective-permute-start(bf16[368,256]{1,0:T(8,128)(2,1)S(1)} %get-tuple-element.187.refs_0_.refs_16_), channel_id=1, source_target_pairs={{0,8},{4,12},{8,0},{12,4},{16,24},{20,28},{24,16},{28,20},{1,9},{5... | collective-permute-start | bytes 565256 | tf_op jit(solution)/shard_map/cond/branch_0_fun/ppermute | solution.py:819
  175.6 8.1 %collective-permute-start.35 = (bf16[368,256]{1,0:T(8,128)(2,1)S(1)}, bf16[368,256]{1,0:T(8,128)(2,1)S(1)}, u32[]{:S(2)}, u32[]{:S(2)}) collective-permute-start(bf16[368,256]{1,0:T(8,128)(2,1)S(1)} %get-tuple-element.187.refs_0_.refs_16_), channel_id=1, source_target_pairs={{0,16},{4,20},{8,24},{12,28},{16,0},{20,4},{24,8},{28,12},{1,17},{... | collective-permute-start | bytes 565256 | tf_op jit(solution)/shard_map/cond/branch_0_fun/ppermute | solution.py:819
  183.6 9.7 %collective-permute-start.39 = (bf16[368,256]{1,0:T(8,128)(2,1)S(1)}, bf16[368,256]{1,0:T(8,128)(2,1)S(1)}, u32[]{:S(2)}, u32[]{:S(2)}) collective-permute-start(bf16[368,256]{1,0:T(8,128)(2,1)S(1)} %get-tuple-element.189.refs_0_.refs_4_), channel_id=1, source_target_pairs={{0,24},{4,28},{8,16},{12,20},{16,8},{20,12},{24,0},{28,4},{1,25},{... | collective-permute-start | bytes 565256 | tf_op jit(solution)/shard_map/cond/branch_0_fun/ppermute | solution.py:819
  184.8 8.6 %collective-permute-start.37 = (bf16[368,256]{1,0:T(8,128)(2,1)S(1)}, bf16[368,256]{1,0:T(8,128)(2,1)S(1)}, u32[]{:S(2)}, u32[]{:S(2)}) collective-permute-start(bf16[368,256]{1,0:T(8,128)(2,1)S(1)} %get-tuple-element.189.refs_0_.refs_4_), channel_id=1, source_target_pairs={{0,8},{4,12},{8,0},{12,4},{16,24},{20,28},{24,16},{28,20},{1,9},{5... | collective-permute-start | bytes 565256 | tf_op jit(solution)/shard_map/cond/branch_0_fun/ppermute | solution.py:819
  185.7 8.5 %collective-permute-start.38 = (bf16[368,256]{1,0:T(8,128)(2,1)S(1)}, bf16[368,256]{1,0:T(8,128)(2,1)S(1)}, u32[]{:S(2)}, u32[]{:S(2)}) collective-permute-start(bf16[368,256]{1,0:T(8,128)(2,1)S(1)} %get-tuple-element.189.refs_0_.refs_4_), channel_id=1, source_target_pairs={{0,16},{4,20},{8,24},{12,28},{16,0},{20,4},{24,8},{28,12},{1,17},{... | collective-permute-start | bytes 565256 | tf_op jit(solution)/shard_map/cond/branch_0_fun/ppermute | solution.py:819
  191.9 18.4 %collective-permute-start.42 = (bf16[368,1024]{1,0:T(8,128)(2,1)S(1)}, bf16[368,1024]{1,0:T(8,128)(2,1)S(1)}, u32[]{:S(2)}, u32[]{:S(2)}) collective-permute-start(bf16[368,1024]{1,0:T(8,128)(2,1)S(1)} %add_convert_fusion.1), channel_id=1, source_target_pairs={{0,1},{1,2},{2,3},{3,0},{4,5},{5,6},{6,7},{7,4},{8,9},{9,10},{10,1... | collective-permute-start | bytes 2261000 | tf_op jit(solution)/shard_map/cond/branch_0_fun/ppermute | solution.py:822
  231.2 19.0 %collective-permute-start.55 = (bf16[368,1024]{1,0:T(8,128)(2,1)S(1)}, bf16[368,1024]{1,0:T(8,128)(2,1)S(1)}, u32[]{:S(2)}, u32[]{:S(2)}) collective-permute-start(bf16[368,1024]{1,0:T(8,128)(2,1)S(1)} %get-tuple-element.254.refs_0_), channel_id=1, source_target_pairs={{0,1},{1,2},{2,3},{3,0},{4,5},{5,6},{6,7},{7,4},{8,9},{9,10},{10,1... | collective-permute-start | bytes 2261000 | tf_op jit(solution)/shard_map/cond/branch_0_fun/ppermute | solution.py:822
  237.0 8.8 %collective-permute-start.53 = (bf16[368,256]{1,0:T(8,128)(2,1)S(1)}, bf16[368,256]{1,0:T(8,128)(2,1)S(1)}, u32[]{:S(2)}, u32[]{:S(2)}) collective-permute-start(bf16[368,256]{1,0:T(8,128)(2,1)S(1)} %get-tuple-element.215), channel_id=1, source_target_pairs={{0,16},{4,20},{8,24},{12,28},{16,0},{20,4},{24,8},{28,12},{1,17},{... | collective-permute-start | bytes 565256 | tf_op jit(solution)/shard_map/cond/branch_0_fun/ppermute | solution.py:819
  237.0 8.8 %collective-permute-start.54 = (bf16[368,256]{1,0:T(8,128)(2,1)S(1)}, bf16[368,256]{1,0:T(8,128)(2,1)S(1)}, u32[]{:S(2)}, u32[]{:S(2)}) collective-permute-start(bf16[368,256]{1,0:T(8,128)(2,1)S(1)} %get-tuple-element.216), channel_id=1, source_target_pairs={{0,24},{4,28},{8,16},{12,20},{16,8},{20,12},{24,0},{28,4},{1,25},{... | collective-permute-start | bytes 565256 | tf_op jit(solution)/shard_map/cond/branch_0_fun/ppermute | solution.py:819
  250.3 18.1 %collective-permute-start.59 = (bf16[368,1024]{1,0:T(8,128)(2,1)S(1)}, bf16[368,1024]{1,0:T(8,128)(2,1)S(1)}, u32[]{:S(2)}, u32[]{:S(2)}) collective-permute-start(bf16[368,1024]{1,0:T(8,128)(2,1)S(1)} %collective-permute-done.55.refs_0_.refs_1_), channel_id=1, source_target_pairs={{0,1},{1,2},{2,3},{3,0},{4,5},{5,6},{6,7},{7,4},{8,9},{9,10},{10,1... | collective-permute-start | bytes 2261000 | tf_op jit(solution)/shard_map/cond/branch_0_fun/ppermute | solution.py:822
  256.0 8.0 %collective-permute-start.57 = (bf16[368,256]{1,0:T(8,128)(2,1)S(1)}, bf16[368,256]{1,0:T(8,128)(2,1)S(1)}, u32[]{:S(2)}, u32[]{:S(2)}) collective-permute-start(bf16[368,256]{1,0:T(8,128)(2,1)S(1)} %get-tuple-element.220), channel_id=1, source_target_pairs={{0,16},{4,20},{8,24},{12,28},{16,0},{20,4},{24,8},{28,12},{1,17},{... | collective-permute-start | bytes 565256 | tf_op jit(solution)/shard_map/cond/branch_0_fun/ppermute | solution.py:819
  256.0 8.0 %collective-permute-start.58 = (bf16[368,256]{1,0:T(8,128)(2,1)S(1)}, bf16[368,256]{1,0:T(8,128)(2,1)S(1)}, u32[]{:S(2)}, u32[]{:S(2)}) collective-permute-start(bf16[368,256]{1,0:T(8,128)(2,1)S(1)} %get-tuple-element.221), channel_id=1, source_target_pairs={{0,24},{4,28},{8,16},{12,20},{16,8},{20,12},{24,0},{28,4},{1,25},{... | collective-permute-start | bytes 565256 | tf_op jit(solution)/shard_map/cond/branch_0_fun/ppermute | solution.py:819
  268.4 17.3 %collective-permute-start.63 = (bf16[368,1024]{1,0:T(8,128)(2,1)S(1)}, bf16[368,1024]{1,0:T(8,128)(2,1)S(1)}, u32[]{:S(2)}, u32[]{:S(2)}) collective-permute-start(bf16[368,1024]{1,0:T(8,128)(2,1)S(1)} %collective-permute-done.59.refs_0_.refs_2_), channel_id=1, source_target_pairs={{0,1},{1,2},{2,3},{3,0},{4,5},{5,6},{6,7},{7,4},{8,9},{9,10},{10,1... | collective-permute-start | bytes 2261000 | tf_op jit(solution)/shard_map/cond/branch_0_fun/ppermute | solution.py:822
  274.3 7.6 %collective-permute-start.61 = (bf16[368,256]{1,0:T(8,128)(2,1)S(1)}, bf16[368,256]{1,0:T(8,128)(2,1)S(1)}, u32[]{:S(2)}, u32[]{:S(2)}) collective-permute-start(bf16[368,256]{1,0:T(8,128)(2,1)S(1)} %get-tuple-element.225), channel_id=1, source_target_pairs={{0,16},{4,20},{8,24},{12,28},{16,0},{20,4},{24,8},{28,12},{1,17},{... | collective-permute-start | bytes 565256 | tf_op jit(solution)/shard_map/cond/branch_0_fun/ppermute | solution.py:819
  291.4 7.6 %collective-permute-start.65 = (bf16[368,256]{1,0:T(8,128)(2,1)S(1)}, bf16[368,256]{1,0:T(8,128)(2,1)S(1)}, u32[]{:S(2)}, u32[]{:S(2)}) collective-permute-start(bf16[368,256]{1,0:T(8,128)(2,1)S(1)} %get-tuple-element.230), channel_id=1, source_target_pairs={{0,16},{4,20},{8,24},{12,28},{16,0},{20,4},{24,8},{28,12},{1,17},{... | collective-permute-start | bytes 565256 | tf_op jit(solution)/shard_map/cond/branch_0_fun/ppermute | solution.py:819
  291.4 7.6 %collective-permute-start.66 = (bf16[368,256]{1,0:T(8,128)(2,1)S(1)}, bf16[368,256]{1,0:T(8,128)(2,1)S(1)}, u32[]{:S(2)}, u32[]{:S(2)}) collective-permute-start(bf16[368,256]{1,0:T(8,128)(2,1)S(1)} %get-tuple-element.231), channel_id=1, source_target_pairs={{0,24},{4,28},{8,16},{12,20},{16,8},{20,12},{24,0},{28,4},{1,25},{... | collective-permute-start | bytes 565256 | tf_op jit(solution)/shard_map/cond/branch_0_fun/ppermute | solution.py:819
  313.0 11.8 %collective-permute-start.72 = (bf16[368,512]{1,0:T(8,128)(2,1)}, bf16[368,512]{1,0:T(8,128)(2,1)}, u32[]{:S(2)}, u32[]{:S(2)}) collective-permute-start(bf16[368,512]{1,0:T(8,128)(2,1)} %get-tuple-element.236), channel_id=1, source_target_pairs={{0,16},{4,20},{8,24},{12,28},{16,0},{20,4},{24,8},{28,12},{1,17},{... | collective-permute-start | bytes 1130504 | tf_op jit(solution)/shard_map/cond/branch_0_fun/ppermute | solution.py:819
  314.1 15.8 %collective-permute-start.69 = (bf16[1104,256]{1,0:T(8,128)(2,1)}, bf16[1104,256]{1,0:T(8,128)(2,1)}, u32[]{:S(2)}, u32[]{:S(2)}) collective-permute-start(bf16[1104,256]{1,0:T(8,128)(2,1)} %pad_maximum_fusion.1), channel_id=1, source_target_pairs={{0,8},{4,12},{8,0},{12,4},{16,24},{20,28},{24,16},{28,20},{1,9},{5... | collective-permute-start | bytes 1695752 | tf_op jit(solution)/shard_map/cond/branch_0_fun/ppermute | solution.py:819
  326.2 12.5 %collective-permute-start.77 = (bf16[368,512]{1,0:T(8,128)(2,1)S(1)}, bf16[368,512]{1,0:T(8,128)(2,1)S(1)}, u32[]{:S(2)}, u32[]{:S(2)}) collective-permute-start(bf16[368,512]{1,0:T(8,128)(2,1)S(1)} %add_convert_fusion.6), channel_id=1, source_target_pairs={{0,1},{1,2},{2,3},{3,0},{4,5},{5,6},{6,7},{7,4},{8,9},{9,10},{10,1... | collective-permute-start | bytes 1130504 | tf_op jit(solution)/shard_map/cond/branch_0_fun/ppermute | solution.py:822
  333.1 11.7 %collective-permute-start.76 = (bf16[368,512]{1,0:T(8,128)(2,1)S(1)}, bf16[368,512]{1,0:T(8,128)(2,1)S(1)}, u32[]{:S(2)}, u32[]{:S(2)}) collective-permute-start(bf16[368,512]{1,0:T(8,128)(2,1)S(1)} %get-tuple-element.241), channel_id=1, source_target_pairs={{0,16},{4,20},{8,24},{12,28},{16,0},{20,4},{24,8},{28,12},{1,17},{... | collective-permute-start | bytes 1130504 | tf_op jit(solution)/shard_map/cond/branch_0_fun/ppermute | solution.py:819
  336.8 16.8 %collective-permute-start.79 = (bf16[368,512]{1,0:T(8,128)(2,1)S(1)}, bf16[368,512]{1,0:T(8,128)(2,1)S(1)}, u32[]{:S(2)}, u32[]{:S(2)}) collective-permute-start(bf16[368,512]{1,0:T(8,128)(2,1)S(1)} %get-tuple-element.243), channel_id=1, source_target_pairs={{0,16},{4,20},{8,24},{12,28},{16,0},{20,4},{24,8},{28,12},{1,17},{... | collective-permute-start | bytes 1130504 | tf_op jit(solution)/shard_map/cond/branch_0_fun/ppermute | solution.py:819
  345.0 10.6 %collective-permute-start.78 = (bf16[368,512]{1,0:T(8,128)(2,1)S(1)}, bf16[368,512]{1,0:T(8,128)(2,1)S(1)}, u32[]{:S(2)}, u32[]{:S(2)}) collective-permute-start(bf16[368,512]{1,0:T(8,128)(2,1)S(1)} %add_convert_fusion.5), channel_id=1, source_target_pairs={{0,1},{1,2},{2,3},{3,0},{4,5},{5,6},{6,7},{7,4},{8,9},{9,10},{10,1... | collective-permute-start | bytes 1130504 | tf_op jit(solution)/shard_map/cond/branch_0_fun/ppermute | solution.py:822
  359.8 44.6 %all-to-all-start.1 = ((bf16[4,9,128,128]{3,2,1,0:T(8,128)(2,1)}), bf16[4,9,128,128]{3,2,1,0:T(8,128)(2,1)}, u32[]{:S(2)}, u32[]{:S(2)}) async-start(bf16[4,9,128,128]{3,2,1,0:T(8,128)(2,1)} %add_convert_fusion), calls=%async_computation.1 | async-start | bytes 2359296 | tf_op jit(solution)/shard_map/cond/branch_0_fun/all_to_all | solution.py:1063
  370.6 23.1 %collective-permute-start.81 = (bf16[368,512]{1,0:T(8,128)(2,1)S(1)}, bf16[368,512]{1,0:T(8,128)(2,1)S(1)}, u32[]{:S(2)}, u32[]{:S(2)}) collective-permute-start(bf16[368,512]{1,0:T(8,128)(2,1)S(1)} %get-tuple-element.256), channel_id=1, source_target_pairs={{0,16},{4,20},{8,24},{12,28},{16,0},{20,4},{24,8},{28,12},{1,17},{... | collective-permute-start | bytes 1130504 | tf_op jit(solution)/shard_map/cond/branch_0_fun/ppermute | solution.py:819
  372.2 26.3 %collective-permute-start.86 = (bf16[368,512]{1,0:T(8,128)(2,1)S(1)}, bf16[368,512]{1,0:T(8,128)(2,1)S(1)}, u32[]{:S(2)}, u32[]{:S(2)}) collective-permute-start(bf16[368,512]{1,0:T(8,128)(2,1)S(1)} %add_convert_fusion.4), channel_id=1, source_target_pairs={{0,1},{1,2},{2,3},{3,0},{4,5},{5,6},{6,7},{7,4},{8,9},{9,10},{10,1... | collective-permute-start | bytes 1130504 | tf_op jit(solution)/shard_map/cond/branch_0_fun/ppermute | solution.py:822
  375.0 18.8 %collective-permute-start.85 = (bf16[112,512]{1,0:T(8,128)(2,1)S(1)}, bf16[112,512]{1,0:T(8,128)(2,1)S(1)}, u32[]{:S(2)}, u32[]{:S(2)}) collective-permute-start(bf16[112,512]{1,0:T(8,128)(2,1)S(1)} %get-tuple-element.262), channel_id=1, source_target_pairs={{0,24},{4,28},{8,16},{12,20},{16,8},{20,12},{24,0},{28,4},{1,25},{... | collective-permute-start | bytes 344072 | tf_op jit(solution)/shard_map/cond/branch_0_fun/ppermute | solution.py:819
  375.0 18.8 %collective-permute-start.84 = (bf16[112,512]{1,0:T(8,128)(2,1)S(1)}, bf16[112,512]{1,0:T(8,128)(2,1)S(1)}, u32[]{:S(2)}, u32[]{:S(2)}) collective-permute-start(bf16[112,512]{1,0:T(8,128)(2,1)S(1)} %get-tuple-element.261), channel_id=1, source_target_pairs={{0,20},{4,16},{8,28},{12,24},{16,4},{20,0},{24,12},{28,8},{1,21},{... | collective-permute-start | bytes 344072 | tf_op jit(solution)/shard_map/cond/branch_0_fun/ppermute | solution.py:819
  375.7 18.0 %collective-permute-start.83 = (bf16[112,512]{1,0:T(8,128)(2,1)S(1)}, bf16[112,512]{1,0:T(8,128)(2,1)S(1)}, u32[]{:S(2)}, u32[]{:S(2)}) collective-permute-start(bf16[112,512]{1,0:T(8,128)(2,1)S(1)} %get-tuple-element.260), channel_id=1, source_target_pairs={{0,16},{4,20},{8,24},{12,28},{16,0},{20,4},{24,8},{28,12},{1,17},{... | collective-permute-start | bytes 344072 | tf_op jit(solution)/shard_map/cond/branch_0_fun/ppermute | solution.py:819
  395.9 8.5 %collective-permute-start.87 = (bf16[112,512]{1,0:T(8,128)(2,1)S(1)}, bf16[112,512]{1,0:T(8,128)(2,1)S(1)}, u32[]{:S(2)}, u32[]{:S(2)}) collective-permute-start(bf16[112,512]{1,0:T(8,128)(2,1)S(1)} %get-tuple-element.265), channel_id=1, source_target_pairs={{0,28},{4,24},{8,20},{12,16},{16,12},{20,8},{24,4},{28,0},{1,29},{... | collective-permute-start | bytes 344072 | tf_op jit(solution)/shard_map/cond/branch_0_fun/ppermute | solution.py:819
  404.4 8.6 %collective-permute-start.92 = (bf16[9,256,512]{2,1,0:T(8,128)(2,1)}, bf16[9,256,512]{2,1,0:T(8,128)(2,1)}, u32[]{:S(2)}, u32[]{:S(2)}) collective-permute-start(bf16[9,256,512]{2,1,0:T(8,128)(2,1)} %get-tuple-element.270), channel_id=1, source_target_pairs={{0,4},{4,0},{8,12},{12,8},{16,20},{20,16},{24,28},{28,24},{1,5},{5... | collective-permute-start | bytes 7077896 | tf_op jit(solution)/shard_map/cond/branch_0_fun/ppermute | solution.py:819
  407.1 14.8 %collective-permute-start.93 = (bf16[9,128,128]{2,1,0:T(8,128)(2,1)S(1)}, bf16[9,128,128]{2,1,0:T(8,128)(2,1)S(1)}, u32[]{:S(2)}, u32[]{:S(2)}) collective-permute-start(bf16[9,128,128]{2,1,0:T(8,128)(2,1)S(1)} %get-tuple-element.798), channel_id=1, source_target_pairs={{0,8},{4,12},{8,0},{12,4},{16,24},{20,28},{24,16},{28,20},{1,9},{5... | collective-permute-start | bytes 884744 | tf_op jit(solution)/shard_map/cond/branch_0_fun/ppermute | solution.py:819
  408.4 16.5 %collective-permute-start.94 = (bf16[9,128,128]{2,1,0:T(8,128)(2,1)S(1)}, bf16[9,128,128]{2,1,0:T(8,128)(2,1)S(1)}, u32[]{:S(2)}, u32[]{:S(2)}) collective-permute-start(bf16[9,128,128]{2,1,0:T(8,128)(2,1)S(1)} %get-tuple-element.797), channel_id=1, source_target_pairs={{0,16},{4,20},{8,24},{12,28},{16,0},{20,4},{24,8},{28,12},{1,17},{... | collective-permute-start | bytes 884744 | tf_op jit(solution)/shard_map/cond/branch_0_fun/ppermute | solution.py:819
  409.5 15.4 %collective-permute-start.95 = (bf16[9,128,128]{2,1,0:T(8,128)(2,1)S(1)}, bf16[9,128,128]{2,1,0:T(8,128)(2,1)S(1)}, u32[]{:S(2)}, u32[]{:S(2)}) collective-permute-start(bf16[9,128,128]{2,1,0:T(8,128)(2,1)S(1)} %get-tuple-element.796), channel_id=1, source_target_pairs={{0,24},{4,28},{8,16},{12,20},{16,8},{20,12},{24,0},{28,4},{1,25},{... | collective-permute-start | bytes 884744 | tf_op jit(solution)/shard_map/cond/branch_0_fun/ppermute | solution.py:819
  413.0 20.1 %all-to-all-start.2 = ((bf16[8,112,256]{2,1,0:T(8,128)(2,1)}), bf16[8,112,256]{2,1,0:T(8,128)(2,1)S(1)}, u32[]{:S(2)}, u32[]{:S(2)}) async-start(bf16[8,112,256]{2,1,0:T(8,128)(2,1)} %bitcast.34), calls=%async_computation.2 | async-start | bytes 917504 | tf_op jit(solution)/shard_map/cond/branch_0_fun/all_to_all | solution.py:1096
  (180 other events, 2469.8 us)
